TPU v7x, 32 devices: a whole 2x2x4 slice. The times are simulated.
32 devices in a mesh: replica: 4 (over x, core), fsdp: 8 (over z, y).
Axes of the slice: x: 2, y: 2, z: 4, core: 2. Of those that a mesh axis runs over, the one named last changes fastest.
Arguments:
- pseudo_grad: bfloat16 [4, 256, 8192], P('replica', 'fsdp'), may hold values from -400 to 400
- params: float32 [256, 8192], P('fsdp'), may hold values from -6 to 6
- momentum: float32 [256, 8192], P('fsdp'), may hold values from -6 to 6
Outputs:
- new_params: float32 [256, 8192], P('fsdp')
- new_momentum: float32 [256, 8192], P('fsdp')
All inputs are finite; a program needn't handle non-finite values.
Results may differ from a plain program's by a relative error of at most 0.0003.
Values may be sent and summed in bfloat16 or wider, within the bound.
No kernel may reach another device: no remote copies, remote signals or barrier semaphores. Data moves between devices by JAX's collectives and lax.ppermute only.
A program may use at most 64 MiB of HBM per device.

v0:
```python
import jax
import jax.numpy as jnp
from jax import lax
from jax.sharding import PartitionSpec as P


def square_total(average):
    return jnp.sum(jnp.sum(average * average, axis=1))


def outer_update(average, square_sum, count, params_part, momentum_part):
    rms = jnp.sqrt(square_sum / jnp.float32(count) + 1e-06)
    factor = 0.2 / rms
    clipped = factor * average
    fresh_momentum = 0.9 * momentum_part + clipped
    fresh_params = params_part - 0.7 * (clipped + 0.9 * fresh_momentum)
    return (fresh_params, fresh_momentum)


def per_device(pseudo_grad, params, momentum):
    groups = lax.axis_size("replica")
    count = params.shape[0] * lax.axis_size("fsdp") * params.shape[1]
    terms = pseudo_grad[0].astype(jnp.float32)
    total = lax.psum_scatter(terms, "replica", scatter_dimension=1, tiled=True)
    average = total / jnp.float32(groups)
    square_sum = lax.psum(square_total(average), ("replica", "fsdp"))
    width = total.shape[1]
    start = lax.axis_index("replica") * width
    params_part = lax.dynamic_slice_in_dim(params, start, width, 1)
    momentum_part = lax.dynamic_slice_in_dim(momentum, start, width, 1)
    fresh_params, fresh_momentum = outer_update(
        average, square_sum, count, params_part, momentum_part
    )
    new_params, new_momentum = (
        lax.all_gather(fresh_params, "replica", axis=1, tiled=True),
        lax.all_gather(fresh_momentum, "replica", axis=1, tiled=True),
    )
    return (new_params, new_momentum)


def solution(mesh):
    placed = (P("replica", "fsdp", None), P("fsdp", None), P("fsdp", None))
    return jax.shard_map(
        per_device,
        mesh=mesh,
        in_specs=placed,
        out_specs=(P("fsdp", None), P("fsdp", None)),
        check_vma=False,
    )
```

profile of v0, /device:TPU:0, one launch (start us, length us, event | category | flops | bytes accessed | tf_op | source)
XLA Modules:
  0.0 129.1 jit_solution(12121519586915933696)
XLA Ops:
  7.2 0.0 reduce-scatter.2.cloned.1.call-start
  7.2 2.1 %bitcast_convert_fusion = f32[32,8192]{1,0:T(8,128)} fusion(bf16[1,32,8192]{2,1,0:T(8,128)(2,1)} %param.3), kind=kLoop, calls=%fused_computation | loop fusion | flops 262144 | bytes 1572864 | tf_op jit(solution)/shard_map/convert_element_type | solution.py:23
  9.3 0.0 reduce-scatter.2.cloned.1.call-update
  9.3 0.0 all-gather.5.cloned.1.call-start
  9.4 29.3 %reduce-scatter.2.cloned.1.call-done = f32[32,2048]{1,0:T(8,128)} async-done(((f32[32,8192]{1,0:T(8,128)}), f32[32,2048]{1,0:T(8,128)}) %reduce-scatter.2.cloned.1.call-update) | async-done | bytes 262160 | tf_op jit(solution)/shard_map/reduce_scatter | solution.py:24
  38.7 0.0 copy-start.1
  38.7 1.7 %multiply_reduce_fusion = f32[]{:T(128)} fusion(f32[32,2048]{1,0:T(8,128)} %reduce-scatter.2.cloned.1.call-done), kind=kLoop, calls=%fused_computation.3 | loop fusion | flops 196607 | bytes 262148 | tf_op jit(solution)/shard_map/reduce_sum | solution.py:8
  40.4 39.5 %psum.7 = f32[]{:T(128)} all-reduce(f32[]{:T(128)} %multiply_reduce_fusion), channel_id=1, replica_groups=mesh['replica'=4,'fsdp'=8] {'replica','fsdp'}, use_global_device_ids=true, to_apply=%region_2.0 | all-reduce | flops 1 | bytes 8 | tf_op jit(solution)/shard_map/psum | solution.py:26
  80.6 0.0 copy-done.1
  80.6 1.9 %multiply_add_fusion = (f32[32,2048]{1,0:T(8,128)}, f32[32,2048]{1,0:T(8,128)}) fusion(f32[32,8192]{1,0:T(8,128)} %param.5, s32[]{:T(128)S(6)} %select_n.4, f32[32,2048]{1,0:T(8,128)S(1)} %copy-done.1, f32[]{:T(128)S(6)} %mul.28, f32[32,8192]{1,0:T(8,128)} %param.4), kind=kLoop, calls=%fused_computation.2 | loop fusion | flops 458752 | bytes 1310728 | tf_op jit(solution)/shard_map/add | solution.py:15
  82.5 0.0 all-gather.5.cloned.1.call-update
  82.6 0.0 all-gather.3.cloned.1.call-start
  82.6 0.7 all-gather.3.cloned.1.call-update
  83.3 17.1 %all-gather.5.cloned.1.call-done = f32[32,8192]{1,0:T(8,128)} async-done(((f32[32,2048]{1,0:T(8,128)}), f32[32,8192]{1,0:T(8,128)}) %all-gather.5.cloned.1.call-update) | async-done | bytes 1048592 | tf_op jit(solution)/shard_map/all_gather | solution.py:36
  100.4 0.0 copy-start
  100.4 19.0 %all-gather.3.cloned.1.call-done = f32[32,8192]{1,0:T(8,128)} async-done(((f32[32,2048]{1,0:T(8,128)}), f32[32,8192]{1,0:T(8,128)}) %all-gather.3.cloned.1.call-update) | async-done | bytes 1048592 | tf_op jit(solution)/shard_map/all_gather | solution.py:35
  119.3 2.3 %copy.7 = f32[32,8192]{1,0:T(8,128)} copy(f32[32,8192]{1,0:T(8,128)} %all-gather.3.cloned.1.call-done) | data formatting | bytes 2097152
  121.6 0.0 copy-done
  121.6 1.0 copy.8
Async XLA Ops:
  7.2 31.5 %reduce-scatter.2.cloned.1.call-start = ((), (), s32[]{:S(2)}) async-start(), calls=%async_computation.1 | async-start | bytes 1310720 | tf_op jit(solution)/shard_map/reduce_scatter | solution.py:24
  9.3 91.1 %all-gather.5.cloned.1.call-start = ((), (), s32[]{:S(2)}) async-start(), calls=%async_computation.3 | async-start | bytes 1310720 | tf_op jit(solution)/shard_map/all_gather | solution.py:36
  38.7 41.9 %copy-start.1 = (f32[32,2048]{1,0:T(8,128)S(1)}, f32[32,2048]{1,0:T(8,128)}, u32[]{:S(2)}) copy-start(f32[32,2048]{1,0:T(8,128)} %reduce-scatter.2.cloned.1.call-done) | copy-start | bytes 786436
  82.6 36.8 %all-gather.3.cloned.1.call-start = ((), (), s32[]{:S(2)}) async-start(), calls=%async_computation.2 | async-start | bytes 1310720 | tf_op jit(solution)/shard_map/all_gather | solution.py:35
  100.4 21.2 %copy-start = (f32[32,8192]{1,0:T(8,128)S(1)}, f32[32,8192]{1,0:T(8,128)}, u32[]{:S(2)}) copy-start(f32[32,8192]{1,0:T(8,128)} %all-gather.5.cloned.1.call-done) | copy-start | bytes 3145732
Sparse Core Ops, SparseCore 0:
  11.1 27.5 reduce-scatter.1
  82.7 17.6 all-gather.4
  102.6 16.7 all-gather.2
where the time goes:
time: 129 us
  waiting for transfers between devices  66.1 us (51%)
  blocking collectives  39.5 us (31%)
  between operations  14.5 us (11%)
  other arithmetic  5.66 us (4%)
  local copies, waits for them, and re-layouts  3.24 us (3%)
    psum x1, blocking collectives, per_device(): square_sum = lax.psum(square_total(average), ('replica', 'fsdp'))  39.5 us
    reduce_scatter x1, waiting for transfers between devices, per_device(): total = lax.psum_scatter(terms, 'replica', scatter_dimension=1, tiled=True)  29.3 us
    all_gather x1, waiting for transfers between devices, per_device(): lax.all_gather(fresh_params, 'replica', axis=1, tiled=True)  19 us
    all_gather x1, waiting for transfers between devices, per_device(): lax.all_gather(fresh_momentum, 'replica', axis=1, tiled=True)  17.1 us
    unnamed x6, local copies, waits for them, and re-layouts  3.24 us
  transfers between devices with their start and end apart: 3, of which 3 were waited for; matrix products, arithmetic and copies ran while one was open for 0% of the time, Pallas kernels for 0%

commit v1 on v0

v1 whole, which is shorter than its diff:
```python
import jax
import jax.numpy as jnp
from jax import lax
from jax.sharding import PartitionSpec as P


def swapped(value, axis, flip):
    size = lax.axis_size(axis)
    return lax.ppermute(value, axis, [(i, i ^ flip) for i in range(size)])


def replica_total(grad):
    size = lax.axis_size("replica")
    wide = jnp.float32
    if size & (size - 1):
        return lax.psum(grad.astype(wide), "replica")
    if size == 1:
        return grad.astype(wide)
    mate = swapped(grad, "replica", 1)
    total = grad.astype(wide) + mate.astype(wide)
    if size >= 4:
        across = swapped(grad, "replica", 2)
        beyond = swapped(across, "replica", 1)
        total = total + (across.astype(wide) + beyond.astype(wide))
    step = 4
    while step < size:
        total = total + swapped(total, "replica", step)
        step *= 2
    return total


def fsdp_sum(value):
    size = lax.axis_size("fsdp")
    if size & (size - 1):
        return lax.psum(value, "fsdp")
    step = 1
    while step < size:
        radix = min(8, size // step)
        parts = [value] + [swapped(value, "fsdp", step * k) for k in range(1, radix)]
        while len(parts) > 1:
            parts = [parts[i] + parts[i + 1] for i in range(0, len(parts), 2)]
        value = parts[0]
        step *= radix
    return value


def per_device(pseudo_grad, params, momentum):
    groups = lax.axis_size("replica")
    count = params.shape[0] * lax.axis_size("fsdp") * params.shape[1]
    average = replica_total(pseudo_grad[0]) / jnp.float32(groups)
    square_sum = fsdp_sum(jnp.sum(jnp.sum(average * average, axis=1)))
    rms = jnp.sqrt(square_sum / jnp.float32(count) + 1e-06)
    clipped = (0.2 / rms) * average
    new_momentum = 0.9 * momentum + clipped
    new_params = params - 0.7 * (clipped + 0.9 * new_momentum)
    return (new_params, new_momentum)


def solution(mesh):
    placed = (P("replica", "fsdp", None), P("fsdp", None), P("fsdp", None))
    return jax.shard_map(
        per_device,
        mesh=mesh,
        in_specs=placed,
        out_specs=(P("fsdp", None), P("fsdp", None)),
        check_vma=False,
    )
```

time: 129 us -> 40.1 us (0.31)
  waiting for transfers between devices: 66.1 us -> 14.9 us
  blocking collectives: 39.5 us -> 0 us
  starting transfers between devices: 0.12 us -> 14.2 us
  between operations: 14.5 us -> 5.73 us
  local copies, waits for them, and re-layouts: 3.24 us -> 0.01 us
    psum x1 -> x0, blocking collectives: 39.5 us -> none  [per_device(): square_sum = lax.psum(square_total(average), ('replica', 'fsdp'))]
    all_gather x2 -> x0, waiting for transfers between devices: 36.1 us -> none  [the longest x1 19 us: per_device(): lax.all_gather(fresh_params, 'replica', axis=1, tiled=True)]
    reduce_scatter x1 -> x0, waiting for transfers between devices: 29.3 us -> none  [per_device(): total = lax.psum_scatter(terms, 'replica', scatter_dimension=1, tiled=True)]
    ppermute x0 -> x10, waiting for transfers between devices: none -> 14.9 us  [swapped(): return lax.ppermute(value, axis, [(i, i ^ flip) for i in range(size)])]
    ppermute x0 -> x10, starting transfers between devices: none -> 14.2 us  [swapped(): return lax.ppermute(value, axis, [(i, i ^ flip) for i in range(size)])]
    unnamed x6 -> x4, local copies, waits for them, and re-layouts: 3.24 us -> 0.01 us
    sub x0 -> x1, other arithmetic: none -> 3.02 us  [per_device(): new_params = params - 0.7 * (clipped + 0.9 * new_momentum)]
    convert_element_type x1 -> x0, other arithmetic: 2.08 us -> none  [per_device(): terms = pseudo_grad[0].astype(jnp.float32)]
  transfers between devices with their start and end apart: 3 -> 10, of which waited for: 3 -> 3; matrix products, arithmetic and copies ran while one was open for 0% -> 0% of each run, Pallas kernels for 0% -> 0%
where the time goes in v1:
time: 40.1 us; the launch traced here: 39.8 us
  waiting for transfers between devices  14.9 us (37%)
  starting transfers between devices  14.2 us (35%)
  between operations  5.73 us (14%)
  other arithmetic  5 us (12%)
    ppermute x10, waiting for transfers between devices, swapped(): return lax.ppermute(value, axis, [(i, i ^ flip) for i in range(size)])  14.9 us
    ppermute x10, starting transfers between devices, swapped(): return lax.ppermute(value, axis, [(i, i ^ flip) for i in range(size)])  14.2 us
    sub x1, other arithmetic, per_device(): new_params = params - 0.7 * (clipped + 0.9 * new_momentum)  3.02 us
    reduce_sum x1, other arithmetic, per_device(): square_sum = fsdp_sum(jnp.sum(jnp.sum(average * average, axis=1)))  1.99 us
  transfers between devices with their start and end apart: 10, of which 3 were waited for; matrix products, arithmetic and copies ran while one was open for 0% of the time, Pallas kernels for 0%

profile of v1, /device:TPU:0, one launch (start us, length us, event | category | flops | bytes accessed | tf_op | source)
XLA Modules:
  0.0 39.8 jit_solution(801747347944844548)
XLA Ops:
  0.6 0.0 copy-start
  0.6 0.0 copy-start.1
  0.6 3.0 %collective-permute-start.1 = (bf16[32,8192]{1,0:T(8,128)(2,1)}, bf16[32,8192]{1,0:T(8,128)(2,1)S(1)}, u32[]{:S(2)}, u32[]{:S(2)}) collective-permute-start(bf16[32,8192]{1,0:T(8,128)(2,1)} %bitcast.9), channel_id=1, source_target_pairs={{0,16},{8,24},{16,0},{24,8},{1,17},{9,25},{17,1},{25,9},{2,18},{10... | collective-permute-start | bytes 1572872 | tf_op jit(solution)/shard_map/ppermute | solution.py:9
  3.7 0.0 collective-permute-start
  3.7 12.1 %collective-permute-done.1 = bf16[32,8192]{1,0:T(8,128)(2,1)S(1)} collective-permute-done((bf16[32,8192]{1,0:T(8,128)(2,1)}, bf16[32,8192]{1,0:T(8,128)(2,1)S(1)}, u32[]{:S(2)}, u32[]{:S(2)}) %collective-permute-start.1) | collective-permute-done | bytes 524320 | tf_op jit(solution)/shard_map/ppermute | solution.py:9
  15.8 0.0 collective-permute-start.2
  15.8 0.0 collective-permute-done
  15.8 1.9 %collective-permute-done.2 = bf16[32,8192]{1,0:T(8,128)(2,1)S(1)} collective-permute-done((bf16[32,8192]{1,0:T(8,128)(2,1)S(1)}, bf16[32,8192]{1,0:T(8,128)(2,1)S(1)}, u32[]{:S(2)}, u32[]{:S(2)}) %collective-permute-start.2) | collective-permute-done | bytes 524320 | tf_op jit(solution)/shard_map/ppermute | solution.py:9
  17.7 2.0 %multiply_reduce_fusion = f32[]{:T(128)} fusion(bf16[32,8192]{1,0:T(8,128)(2,1)S(1)} %collective-permute-done.2, bf16[32,8192]{1,0:T(8,128)(2,1)S(1)} %collective-permute-done.1, bf16[32,8192]{1,0:T(8,128)(2,1)S(1)} %collective-permute-done, bf16[1,32,8192]{2,1,0:T(8,128)(2,1)} %param.3), kind=kLoop, calls=%fused_computation.2 | loop fusion | flops 2621439 | bytes 2097156 | tf_op jit(solution)/shard_map/reduce_sum | solution.py:51
  19.7 4.8 %collective-permute-start.9 = (f32[]{:T(128)}, f32[]{:T(128)}, u32[]{:S(2)}, u32[]{:S(2)}) collective-permute-start(f32[]{:T(128)} %multiply_reduce_fusion), channel_id=1, source_target_pairs={{0,7},{1,6},{2,5},{3,4},{4,3},{5,2},{6,1},{7,0},{8,15},{9,14},{10,... | collective-permute-start | bytes 20 | tf_op jit(solution)/shard_map/ppermute | solution.py:9
  24.5 0.2 collective-permute-start.8
  24.7 0.7 %collective-permute-start.7 = (f32[]{:T(128)}, f32[]{:T(128)}, u32[]{:S(2)}, u32[]{:S(2)}) collective-permute-start(f32[]{:T(128)} %multiply_reduce_fusion), channel_id=1, source_target_pairs={{0,5},{1,4},{2,7},{3,6},{4,1},{5,0},{6,3},{7,2},{8,13},{9,12},{10,... | collective-permute-start | bytes 20 | tf_op jit(solution)/shard_map/ppermute | solution.py:9
  25.4 2.0 %collective-permute-start.6 = (f32[]{:T(128)}, f32[]{:T(128)}, u32[]{:S(2)}, u32[]{:S(2)}) collective-permute-start(f32[]{:T(128)} %multiply_reduce_fusion), channel_id=1, source_target_pairs={{0,4},{1,5},{2,6},{3,7},{4,0},{5,1},{6,2},{7,3},{8,12},{9,13},{10,... | collective-permute-start | bytes 20 | tf_op jit(solution)/shard_map/ppermute | solution.py:9
  27.4 2.4 %collective-permute-start.5 = (f32[]{:T(128)}, f32[]{:T(128)}, u32[]{:S(2)}, u32[]{:S(2)}) collective-permute-start(f32[]{:T(128)} %multiply_reduce_fusion), channel_id=1, source_target_pairs={{0,3},{1,2},{2,1},{3,0},{4,7},{5,6},{6,5},{7,4},{8,11},{9,10},{10,... | collective-permute-start | bytes 20 | tf_op jit(solution)/shard_map/ppermute | solution.py:9
  29.8 0.0 collective-permute-done.9
  29.8 0.8 %collective-permute-start.4 = (f32[]{:T(128)}, f32[]{:T(128)}, u32[]{:S(2)}, u32[]{:S(2)}) collective-permute-start(f32[]{:T(128)} %multiply_reduce_fusion), channel_id=1, source_target_pairs={{0,2},{1,3},{2,0},{3,1},{4,6},{5,7},{6,4},{7,5},{8,10},{9,11},{10,... | collective-permute-start | bytes 20 | tf_op jit(solution)/shard_map/ppermute | solution.py:9
  30.6 0.0 collective-permute-done.8
  30.6 0.3 collective-permute-start.3
  32.1 0.0 collective-permute-done.7
  32.1 0.0 collective-permute-done.6
  33.4 0.8 %collective-permute-done.3 = f32[]{:T(128)} collective-permute-done((f32[]{:T(128)}, f32[]{:T(128)}, u32[]{:S(2)}, u32[]{:S(2)}) %collective-permute-start.3) | collective-permute-done | bytes 36 | tf_op jit(solution)/shard_map/ppermute | solution.py:9
  35.5 0.0 collective-permute-done.5
  35.5 0.0 collective-permute-done.4
  36.8 0.0 copy-done
  36.8 0.0 copy-done.1
  36.8 3.0 %multiply_subtract_fusion = (f32[32,8192]{1,0:T(8,128)}, f32[32,8192]{1,0:T(8,128)}) fusion(f32[32,8192]{1,0:T(8,128)S(1)} %copy-done.1, f32[]{:T(128)S(6)} %mul.24, bf16[32,8192]{1,0:T(8,128)(2,1)S(1)} %collective-permute-done.2, bf16[32,8192]{1,0:T(8,128)(2,1)S(1)} %collective-permute-done.1, bf16[32,8192]{1,0:T(8,128)(2,1)S(1)} %collective-permute-done, ...), kind=kLoop, calls=%fused_computation | loop fusion | flops 3670016 | bytes 6291460 | tf_op jit(solution)/shard_map/sub | solution.py:55
Async XLA Ops:
  0.6 36.2 %copy-start = (bf16[1,32,8192]{2,1,0:T(8,128)(2,1)S(1)}, bf16[1,32,8192]{2,1,0:T(8,128)(2,1)}, u32[]{:S(2)}) copy-start(bf16[1,32,8192]{2,1,0:T(8,128)(2,1)} %param.3) | copy-start | bytes 1572868
  0.6 36.2 %copy-start.1 = (f32[32,8192]{1,0:T(8,128)S(1)}, f32[32,8192]{1,0:T(8,128)}, u32[]{:S(2)}) copy-start(f32[32,8192]{1,0:T(8,128)} %param.4) | copy-start | bytes 3145732
  0.6 15.1 %collective-permute-start.1 = (bf16[32,8192]{1,0:T(8,128)(2,1)}, bf16[32,8192]{1,0:T(8,128)(2,1)S(1)}, u32[]{:S(2)}, u32[]{:S(2)}) collective-permute-start(bf16[32,8192]{1,0:T(8,128)(2,1)} %bitcast.9), channel_id=1, source_target_pairs={{0,16},{8,24},{16,0},{24,8},{1,17},{9,25},{17,1},{25,9},{2,18},{10... | collective-permute-start | bytes 1572872 | tf_op jit(solution)/shard_map/ppermute | solution.py:9
  3.7 12.1 %collective-permute-start = (bf16[32,8192]{1,0:T(8,128)(2,1)}, bf16[32,8192]{1,0:T(8,128)(2,1)S(1)}, u32[]{:S(2)}, u32[]{:S(2)}) collective-permute-start(bf16[32,8192]{1,0:T(8,128)(2,1)} %bitcast.10), channel_id=1, source_target_pairs={{0,8},{8,0},{16,24},{24,16},{1,9},{9,1},{17,25},{25,17},{2,10},{10... | collective-permute-start | bytes 1572872 | tf_op jit(solution)/shard_map/ppermute | solution.py:9
  15.8 1.9 %collective-permute-start.2 = (bf16[32,8192]{1,0:T(8,128)(2,1)S(1)}, bf16[32,8192]{1,0:T(8,128)(2,1)S(1)}, u32[]{:S(2)}, u32[]{:S(2)}) collective-permute-start(bf16[32,8192]{1,0:T(8,128)(2,1)S(1)} %collective-permute-done.1), channel_id=1, source_target_pairs={{0,8},{8,0},{16,24},{24,16},{1,9},{9,1},{17,25},{25,17},{2,10},{10... | collective-permute-start | bytes 1572872 | tf_op jit(solution)/shard_map/ppermute | solution.py:9
  19.7 10.1 %collective-permute-start.9 = (f32[]{:T(128)}, f32[]{:T(128)}, u32[]{:S(2)}, u32[]{:S(2)}) collective-permute-start(f32[]{:T(128)} %multiply_reduce_fusion), channel_id=1, source_target_pairs={{0,7},{1,6},{2,5},{3,4},{4,3},{5,2},{6,1},{7,0},{8,15},{9,14},{10,... | collective-permute-start | bytes 20 | tf_op jit(solution)/shard_map/ppermute | solution.py:9
  24.5 6.1 %collective-permute-start.8 = (f32[]{:T(128)}, f32[]{:T(128)}, u32[]{:S(2)}, u32[]{:S(2)}) collective-permute-start(f32[]{:T(128)} %multiply_reduce_fusion), channel_id=1, source_target_pairs={{0,6},{1,7},{2,4},{3,5},{4,2},{5,3},{6,0},{7,1},{8,14},{9,15},{10,... | collective-permute-start | bytes 20 | tf_op jit(solution)/shard_map/ppermute | solution.py:9
  24.7 7.4 %collective-permute-start.7 = (f32[]{:T(128)}, f32[]{:T(128)}, u32[]{:S(2)}, u32[]{:S(2)}) collective-permute-start(f32[]{:T(128)} %multiply_reduce_fusion), channel_id=1, source_target_pairs={{0,5},{1,4},{2,7},{3,6},{4,1},{5,0},{6,3},{7,2},{8,13},{9,12},{10,... | collective-permute-start | bytes 20 | tf_op jit(solution)/shard_map/ppermute | solution.py:9
  25.4 6.7 %collective-permute-start.6 = (f32[]{:T(128)}, f32[]{:T(128)}, u32[]{:S(2)}, u32[]{:S(2)}) collective-permute-start(f32[]{:T(128)} %multiply_reduce_fusion), channel_id=1, source_target_pairs={{0,4},{1,5},{2,6},{3,7},{4,0},{5,1},{6,2},{7,3},{8,12},{9,13},{10,... | collective-permute-start | bytes 20 | tf_op jit(solution)/shard_map/ppermute | solution.py:9
  27.4 8.1 %collective-permute-start.5 = (f32[]{:T(128)}, f32[]{:T(128)}, u32[]{:S(2)}, u32[]{:S(2)}) collective-permute-start(f32[]{:T(128)} %multiply_reduce_fusion), channel_id=1, source_target_pairs={{0,3},{1,2},{2,1},{3,0},{4,7},{5,6},{6,5},{7,4},{8,11},{9,10},{10,... | collective-permute-start | bytes 20 | tf_op jit(solution)/shard_map/ppermute | solution.py:9
  29.8 5.7 %collective-permute-start.4 = (f32[]{:T(128)}, f32[]{:T(128)}, u32[]{:S(2)}, u32[]{:S(2)}) collective-permute-start(f32[]{:T(128)} %multiply_reduce_fusion), channel_id=1, source_target_pairs={{0,2},{1,3},{2,0},{3,1},{4,6},{5,7},{6,4},{7,5},{8,10},{9,11},{10,... | collective-permute-start | bytes 20 | tf_op jit(solution)/shard_map/ppermute | solution.py:9
  30.6 3.6 %collective-permute-start.3 = (f32[]{:T(128)}, f32[]{:T(128)}, u32[]{:S(2)}, u32[]{:S(2)}) collective-permute-start(f32[]{:T(128)} %multiply_reduce_fusion), channel_id=1, source_target_pairs={{0,1},{1,0},{2,3},{3,2},{4,5},{5,4},{6,7},{7,6},{8,9},{9,8},{10,11... | collective-permute-start | bytes 20 | tf_op jit(solution)/shard_map/ppermute | solution.py:9

commit v2 on v1

--- a/solution.py
+++ b/solution.py
@@ -31,17 +31,9 @@
 
 def fsdp_sum(value):
     size = lax.axis_size("fsdp")
-    if size & (size - 1):
-        return lax.psum(value, "fsdp")
-    step = 1
-    while step < size:
-        radix = min(8, size // step)
-        parts = [value] + [swapped(value, "fsdp", step * k) for k in range(1, radix)]
-        while len(parts) > 1:
-            parts = [parts[i] + parts[i + 1] for i in range(0, len(parts), 2)]
-        value = parts[0]
-        step *= radix
-    return value
+    copies = jnp.broadcast_to(value, (size, 1, 128))
+    parts = lax.all_to_all(copies, "fsdp", split_axis=0, concat_axis=0, tiled=True)
+    return jnp.sum(parts[:, 0, 0])
 
 
 def per_device(pseudo_grad, params, momentum):

time: 40.1 us -> 37.3 us (0.930)
  blocking collectives: 0 us -> 12.3 us
  starting transfers between devices: 14.2 us -> 3.01 us
  between operations: 5.73 us -> 1.37 us
  waiting for transfers between devices: 14.9 us -> 14 us
  local copies, waits for them, and re-layouts: 0.01 us -> 0.66 us
  other arithmetic: 5 us -> 5.61 us
    all_to_all x0 -> x1, blocking collectives: none -> 12.3 us  [fsdp_sum(): lax.all_to_all(copies, 'fsdp', split_axis=0, concat_axis=0, tiled=True)]
    ppermute x10 -> x3, starting transfers between devices: 14.2 us -> 3.01 us  [swapped(): return lax.ppermute(value, axis, [(i, i ^ flip) for i in range(size)])]
    ppermute x10 -> x3, waiting for transfers between devices: 14.9 us -> 14 us  [swapped(): return lax.ppermute(value, axis, [(i, i ^ flip) for i in range(size)])]
    broadcast_in_dim x0 -> x1, local copies, waits for them, and re-layouts: none -> 0.65 us  [fsdp_sum(): copies = jnp.broadcast_to(value, (size, 1, 128))]
    reduce_sum x0 -> x1, other arithmetic: none -> 0.61 us  [fsdp_sum(): return jnp.sum(parts[:, 0, 0])]
  transfers between devices with their start and end apart: 10 -> 3, of which waited for: 3 -> 2; matrix products, arithmetic and copies ran while one was open for 0% -> 0% of each run, Pallas kernels for 0% -> 0%
where the time goes in v2:
time: 37.3 us; the launch traced here: 37 us
  waiting for transfers between devices  14 us (38%)
  blocking collectives  12.3 us (33%)
  other arithmetic  5.61 us (15%)
  starting transfers between devices  3.01 us (8%)
  between operations  1.37 us (4%)
  local copies, waits for them, and re-layouts  0.66 us (2%)
    ppermute x3, waiting for transfers between devices, swapped(): return lax.ppermute(value, axis, [(i, i ^ flip) for i in range(size)])  14 us
    all_to_all x1, blocking collectives, fsdp_sum(): lax.all_to_all(copies, 'fsdp', split_axis=0, concat_axis=0, tiled=True)  12.3 us
    sub x1, other arithmetic, per_device(): new_params = params - 0.7 * (clipped + 0.9 * new_momentum)  3.02 us
    ppermute x3, starting transfers between devices, swapped(): return lax.ppermute(value, axis, [(i, i ^ flip) for i in range(size)])  3.01 us
    reduce_sum x1, other arithmetic, per_device(): square_sum = fsdp_sum(jnp.sum(jnp.sum(average * average, axis=1)))  1.99 us
  transfers between devices with their start and end apart: 3, of which 2 were waited for; matrix products, arithmetic and copies ran while one was open for 0% of the time, Pallas kernels for 0%

profile of v2, /device:TPU:0, one launch (start us, length us, event | category | flops | bytes accessed | tf_op | source)
XLA Modules:
  0.0 37.0 jit_solution(98276872484655386)
XLA Ops:
  0.6 0.0 copy-start
  0.6 0.0 copy-start.1
  0.6 3.0 %collective-permute-start.1 = (bf16[32,8192]{1,0:T(8,128)(2,1)}, bf16[32,8192]{1,0:T(8,128)(2,1)S(1)}, u32[]{:S(2)}, u32[]{:S(2)}) collective-permute-start(bf16[32,8192]{1,0:T(8,128)(2,1)} %bitcast.9), channel_id=1, source_target_pairs={{0,16},{8,24},{16,0},{24,8},{1,17},{9,25},{17,1},{25,9},{2,18},{10... | collective-permute-start | bytes 1572872 | tf_op jit(solution)/shard_map/ppermute | solution.py:9
  3.7 0.0 collective-permute-start
  3.7 12.1 %collective-permute-done.1 = bf16[32,8192]{1,0:T(8,128)(2,1)S(1)} collective-permute-done((bf16[32,8192]{1,0:T(8,128)(2,1)}, bf16[32,8192]{1,0:T(8,128)(2,1)S(1)}, u32[]{:S(2)}, u32[]{:S(2)}) %collective-permute-start.1) | collective-permute-done | bytes 524320 | tf_op jit(solution)/shard_map/ppermute | solution.py:9
  15.8 0.0 collective-permute-start.2
  15.8 0.0 collective-permute-done
  15.8 1.9 %collective-permute-done.2 = bf16[32,8192]{1,0:T(8,128)(2,1)S(1)} collective-permute-done((bf16[32,8192]{1,0:T(8,128)(2,1)S(1)}, bf16[32,8192]{1,0:T(8,128)(2,1)S(1)}, u32[]{:S(2)}, u32[]{:S(2)}) %collective-permute-start.2) | collective-permute-done | bytes 524320 | tf_op jit(solution)/shard_map/ppermute | solution.py:9
  17.7 2.0 %multiply_reduce_fusion = f32[]{:T(128)} fusion(bf16[32,8192]{1,0:T(8,128)(2,1)S(1)} %collective-permute-done.2, bf16[32,8192]{1,0:T(8,128)(2,1)S(1)} %collective-permute-done.1, bf16[32,8192]{1,0:T(8,128)(2,1)S(1)} %collective-permute-done, bf16[1,32,8192]{2,1,0:T(8,128)(2,1)} %param.3), kind=kLoop, calls=%fused_computation.2 | loop fusion | flops 2621439 | bytes 2097156 | tf_op jit(solution)/shard_map/reduce_sum | solution.py:43
  19.7 0.6 %broadcast_in_dim.3 = f32[8,1,128]{2,1,0:T(1,128)S(1)} broadcast(f32[]{:T(128)} %multiply_reduce_fusion), dimensions={} | broadcast | bytes 4100 | tf_op jit(solution)/shard_map/broadcast_in_dim | solution.py:34
  20.3 12.3 %all_to_all.5 = f32[8,1,128]{2,1,0:T(1,128)S(1)} all-to-all(f32[8,1,128]{2,1,0:T(1,128)S(1)} %broadcast_in_dim.3), channel_id=1, replica_groups=mesh['replica'=4,'fsdp'=8] {'fsdp'}, dimensions={0} | all-to-all | bytes 8192 | tf_op jit(solution)/shard_map/all_to_all | solution.py:35
  32.7 0.6 %slice_reduce_fusion = f32[]{:T(128)} fusion(f32[8,1,128]{2,1,0:T(1,128)S(1)} %all_to_all.5), kind=kLoop, calls=%fused_computation.4 | loop fusion | flops 7 | bytes 36 | tf_op jit(solution)/shard_map/reduce_sum | solution.py:36
  34.0 0.0 copy-done
  34.0 0.0 copy-done.1
  34.0 3.0 %multiply_subtract_fusion = (f32[32,8192]{1,0:T(8,128)}, f32[32,8192]{1,0:T(8,128)}) fusion(f32[32,8192]{1,0:T(8,128)S(1)} %copy-done.1, f32[]{:T(128)S(6)} %mul.24, bf16[32,8192]{1,0:T(8,128)(2,1)S(1)} %collective-permute-done.2, bf16[32,8192]{1,0:T(8,128)(2,1)S(1)} %collective-permute-done.1, bf16[32,8192]{1,0:T(8,128)(2,1)S(1)} %collective-permute-done, ...), kind=kLoop, calls=%fused_computation | loop fusion | flops 3670016 | bytes 6291460 | tf_op jit(solution)/shard_map/sub | solution.py:47
Async XLA Ops:
  0.6 33.4 %copy-start = (bf16[1,32,8192]{2,1,0:T(8,128)(2,1)S(1)}, bf16[1,32,8192]{2,1,0:T(8,128)(2,1)}, u32[]{:S(2)}) copy-start(bf16[1,32,8192]{2,1,0:T(8,128)(2,1)} %param.3) | copy-start | bytes 1572868
  0.6 33.4 %copy-start.1 = (f32[32,8192]{1,0:T(8,128)S(1)}, f32[32,8192]{1,0:T(8,128)}, u32[]{:S(2)}) copy-start(f32[32,8192]{1,0:T(8,128)} %param.4) | copy-start | bytes 3145732
  0.6 15.1 %collective-permute-start.1 = (bf16[32,8192]{1,0:T(8,128)(2,1)}, bf16[32,8192]{1,0:T(8,128)(2,1)S(1)}, u32[]{:S(2)}, u32[]{:S(2)}) collective-permute-start(bf16[32,8192]{1,0:T(8,128)(2,1)} %bitcast.9), channel_id=1, source_target_pairs={{0,16},{8,24},{16,0},{24,8},{1,17},{9,25},{17,1},{25,9},{2,18},{10... | collective-permute-start | bytes 1572872 | tf_op jit(solution)/shard_map/ppermute | solution.py:9
  3.7 12.1 %collective-permute-start = (bf16[32,8192]{1,0:T(8,128)(2,1)}, bf16[32,8192]{1,0:T(8,128)(2,1)S(1)}, u32[]{:S(2)}, u32[]{:S(2)}) collective-permute-start(bf16[32,8192]{1,0:T(8,128)(2,1)} %bitcast.10), channel_id=1, source_target_pairs={{0,8},{8,0},{16,24},{24,16},{1,9},{9,1},{17,25},{25,17},{2,10},{10... | collective-permute-start | bytes 1572872 | tf_op jit(solution)/shard_map/ppermute | solution.py:9
  15.8 1.9 %collective-permute-start.2 = (bf16[32,8192]{1,0:T(8,128)(2,1)S(1)}, bf16[32,8192]{1,0:T(8,128)(2,1)S(1)}, u32[]{:S(2)}, u32[]{:S(2)}) collective-permute-start(bf16[32,8192]{1,0:T(8,128)(2,1)S(1)} %collective-permute-done.1), channel_id=1, source_target_pairs={{0,8},{8,0},{16,24},{24,16},{1,9},{9,1},{17,25},{25,17},{2,10},{10... | collective-permute-start | bytes 1572872 | tf_op jit(solution)/shard_map/ppermute | solution.py:9

commit v3 on v0

v3 whole, which is shorter than its diff:
```python
import functools

import jax
import jax.numpy as jnp
from jax import lax
from jax.experimental import pallas as pl
from jax.experimental.pallas import tpu as pltpu
from jax.sharding import PartitionSpec as P

WIDE = jnp.float32
VMEM = pl.BlockSpec(memory_space=pltpu.VMEM)
HBM = pl.BlockSpec(memory_space=pltpu.HBM)
LIMIT = 16 * 1024 * 1024


def swapped(value, axis, flip):
    size = lax.axis_size(axis)
    return lax.ppermute(value, axis, [(i, i ^ flip) for i in range(size)])


def piece_of(k, width):
    return pl.ds(pl.multiple_of((lax.axis_index("replica") ^ k) * width, width), width)


def tree(parts):
    while len(parts) > 1:
        parts = [parts[i] + parts[i + 1] for i in range(0, len(parts), 2)]
    return parts[0]


def cut_kernel(grad, *rest):
    pieces, sems = rest[:-1], rest[-1]
    width = pieces[0].shape[1]
    copies = [
        pltpu.make_async_copy(grad.at[0, :, piece_of(k, width)], piece, sems.at[k])
        for k, piece in enumerate(pieces)
    ]
    for copy in copies:
        copy.start()
    for copy in copies:
        copy.wait()


def average_kernel(*refs):
    pieces, (average, squares) = refs[:-2], refs[-2:]
    total = tree([piece[...].astype(WIDE) for piece in pieces])
    mean = total / WIDE(len(pieces))
    average[...] = mean
    row = jnp.sum(mean * mean, axis=0, keepdims=True)
    lanes = functools.reduce(
        jnp.add, [row[:, i : i + 128] for i in range(0, row.shape[1], 128)]
    )
    squares[...] = jnp.broadcast_to(lanes[None], squares.shape)


def update_kernel(count, squares, params, momentum, *refs):
    averages, (new_params, new_momentum) = refs[:-2], refs[-2:]
    square_sum = jnp.sum(squares[...], keepdims=True).reshape(1, 1)
    factor = 0.2 / jnp.sqrt(square_sum / WIDE(count) + 1e-06)
    width = averages[0].shape[1]
    for k, average in enumerate(averages):
        cols = piece_of(k, width)
        clipped = factor * average[...]
        fresh = 0.9 * momentum[:, cols] + clipped
        new_momentum[:, cols] = fresh
        new_params[:, cols] = params[:, cols] - 0.7 * (clipped + 0.9 * fresh)


def per_device(pseudo_grad, params, momentum):
    groups = lax.axis_size("replica")
    devices = groups * lax.axis_size("fsdp")
    rows, columns = params.shape
    width = columns // groups
    count = rows * lax.axis_size("fsdp") * columns
    limit = pltpu.CompilerParams(vmem_limit_bytes=LIMIT)
    piece = jax.ShapeDtypeStruct((rows, width), pseudo_grad.dtype)
    pieces = pl.pallas_call(
        cut_kernel,
        out_shape=[piece] * groups,
        in_specs=[HBM],
        out_specs=[VMEM] * groups,
        scratch_shapes=[pltpu.SemaphoreType.DMA((groups,))],
        compiler_params=limit,
    )(pseudo_grad)
    order = [k for k in range(1, groups) if k > 1] + [1]
    moved = {0: pieces[0]}
    for k in order:
        moved[k] = swapped(pieces[k], "replica", k)
    average, squares = pl.pallas_call(
        average_kernel,
        out_shape=[
            jax.ShapeDtypeStruct((rows, width), WIDE),
            jax.ShapeDtypeStruct((devices, 1, 128), WIDE),
        ],
        in_specs=[VMEM] * groups,
        out_specs=[VMEM] * 2,
        compiler_params=limit,
    )(*[moved[k] for k in range(groups)])
    averages = {0: average}
    for k in range(2, groups, 2):
        averages[k] = swapped(average, "replica", k)
    averages[1] = swapped(average, "replica", 1)
    squares = lax.all_to_all(
        squares, ("replica", "fsdp"), split_axis=0, concat_axis=0, tiled=True
    )
    squares, averages = lax.optimization_barrier((squares, averages))
    for k in range(2, groups, 2):
        averages[k + 1] = swapped(averages[k], "replica", 1)
    out = jax.ShapeDtypeStruct((rows, columns), WIDE)
    return pl.pallas_call(
        functools.partial(update_kernel, count),
        out_shape=[out, out],
        in_specs=[VMEM] * (3 + groups),
        out_specs=[VMEM] * 2,
        compiler_params=limit,
    )(squares, params, momentum, *[averages[k] for k in range(groups)])


def solution(mesh):
    placed = (P("replica", "fsdp", None), P("fsdp", None), P("fsdp", None))
    return jax.shard_map(
        per_device,
        mesh=mesh,
        in_specs=placed,
        out_specs=(P("fsdp", None), P("fsdp", None)),
        check_vma=False,
    )
```

time: 129 us -> 30.2 us (0.23)
  waiting for transfers between devices: 66.1 us -> 8.1 us
  blocking collectives: 39.5 us -> 11.9 us
  between operations: 14.5 us -> 0.66 us
  other arithmetic: 5.66 us -> 0 us
  starting transfers between devices: 0.12 us -> 4.79 us
  Pallas kernels: 0 us -> 2.17 us
    psum x1 -> x0, blocking collectives: 39.5 us -> none  [per_device(): square_sum = lax.psum(square_total(average), ('replica', 'fsdp'))]
    all_gather x2 -> x0, waiting for transfers between devices: 36.1 us -> none  [the longest x1 19 us: per_device(): lax.all_gather(fresh_params, 'replica', axis=1, tiled=True)]
    reduce_scatter x1 -> x0, waiting for transfers between devices: 29.3 us -> none  [per_device(): total = lax.psum_scatter(terms, 'replica', scatter_dimension=1, tiled=True)]
    all_to_all x0 -> x1, blocking collectives: none -> 11.9 us  [per_device(): lax.all_to_all(squares, ('replica', 'fsdp'), split_axis=0, concat_axis=0,...]
    ppermute x0 -> x6, waiting for transfers between devices: none -> 8.1 us  [swapped(): return lax.ppermute(value, axis, [(i, i ^ flip) for i in range(size)])]
    ppermute x0 -> x6, starting transfers between devices: none -> 4.79 us  [swapped(): return lax.ppermute(value, axis, [(i, i ^ flip) for i in range(size)])]
    pallas_call x0 -> x3, Pallas kernels: none -> 2.17 us  [the longest x1 1.85 us: per_device(): pl.pallas_call(functools.partial(update_kernel, count), out_shape=[out, o...]
    convert_element_type x1 -> x0, other arithmetic: 2.08 us -> none  [per_device(): terms = pseudo_grad[0].astype(jnp.float32)]
  transfers between devices with their start and end apart: 3 -> 6, of which waited for: 3 -> 3; matrix products, arithmetic and copies ran while one was open for 0% -> 0% of each run, Pallas kernels for 0% -> 0%
where the time goes in v3:
time: 30.2 us; the launch traced here: 29.9 us
  blocking collectives  11.9 us (39%)
  waiting for transfers between devices  8.1 us (27%)
  starting transfers between devices  4.79 us (16%)
  local copies, waits for them, and re-layouts  2.26 us (7%)
  Pallas kernels  2.17 us (7%)
  between operations  0.66 us (2%)
    all_to_all x1, blocking collectives, per_device(): lax.all_to_all(squares, ('replica', 'fsdp'), split_axis=0, concat_axis=0,...  11.9 us
    ppermute x6, waiting for transfers between devices, swapped(): return lax.ppermute(value, axis, [(i, i ^ flip) for i in range(size)])  8.1 us
    ppermute x6, starting transfers between devices, swapped(): return lax.ppermute(value, axis, [(i, i ^ flip) for i in range(size)])  4.79 us
    unnamed x6, local copies, waits for them, and re-layouts  2.26 us
    pallas_call x1, Pallas kernels, per_device(): pl.pallas_call(functools.partial(update_kernel, count), out_shape=[out, o...  1.85 us
  transfers between devices with their start and end apart: 6, of which 3 were waited for; matrix products, arithmetic and copies ran while one was open for 0% of the time, Pallas kernels for 0%

profile of v3, /device:TPU:0, one launch (start us, length us, event | category | flops | bytes accessed | tf_op | source)
XLA Modules:
  0.0 29.9 jit_solution(17676586283788914497)
XLA Ops:
  0.6 0.0 copy-start.2
  0.6 1.0 %copy-done.2 = bf16[1,32,8192]{2,1,0:T(8,128)(2,1)S(1)} copy-done((bf16[1,32,8192]{2,1,0:T(8,128)(2,1)S(1)}, bf16[1,32,8192]{2,1,0:T(8,128)(2,1)}, u32[]{:S(2)}) %copy-start.2) | copy-done | bytes 524312
  1.7 0.0 copy-start
  1.7 0.2 shard_map.50
  1.9 0.5 %collective-permute-start = (bf16[32,2048]{1,0:T(8,128)(2,1)S(1)}, bf16[32,2048]{1,0:T(8,128)(2,1)S(1)}, u32[]{:S(2)}, u32[]{:S(2)}) collective-permute-start(bf16[32,2048]{1,0:T(8,128)(2,1)S(1)} %get-tuple-element.13), channel_id=1, source_target_pairs={{0,8},{8,0},{16,24},{24,16},{1,9},{9,1},{17,25},{25,17},{2,10},{10... | collective-permute-start | bytes 393224 | tf_op jit(solution)/shard_map/ppermute | solution.py:18
  2.4 2.6 %collective-permute-start.1 = (bf16[32,2048]{1,0:T(8,128)(2,1)S(1)}, bf16[32,2048]{1,0:T(8,128)(2,1)S(1)}, u32[]{:S(2)}, u32[]{:S(2)}) collective-permute-start(bf16[32,2048]{1,0:T(8,128)(2,1)S(1)} %get-tuple-element.14), channel_id=1, source_target_pairs={{0,16},{8,24},{16,0},{24,8},{1,17},{9,25},{17,1},{25,9},{2,18},{10... | collective-permute-start | bytes 393224 | tf_op jit(solution)/shard_map/ppermute | solution.py:18
  5.0 0.1 collective-permute-start.2
  5.0 0.0 collective-permute-done.refs_1_
  5.0 4.3 %collective-permute-done.1.refs_2_ = bf16[32,2048]{1,0:T(8,128)(2,1)S(1)} collective-permute-done((bf16[32,2048]{1,0:T(8,128)(2,1)S(1)}, bf16[32,2048]{1,0:T(8,128)(2,1)S(1)}, u32[]{:S(2)}, u32[]{:S(2)}) %collective-permute-start.1) | collective-permute-done | bytes 131104 | tf_op jit(solution)/shard_map/ppermute | solution.py:18
  9.3 2.3 %collective-permute-done.2.refs_3_ = bf16[32,2048]{1,0:T(8,128)(2,1)S(1)} collective-permute-done((bf16[32,2048]{1,0:T(8,128)(2,1)S(1)}, bf16[32,2048]{1,0:T(8,128)(2,1)S(1)}, u32[]{:S(2)}, u32[]{:S(2)}) %collective-permute-start.2) | collective-permute-done | bytes 131104 | tf_op jit(solution)/shard_map/ppermute | solution.py:18
  11.6 0.1 shard_map.51
  11.7 1.6 %collective-permute-start.4 = (f32[32,2048]{1,0:T(8,128)S(1)}, f32[32,2048]{1,0:T(8,128)S(1)}, u32[]{:S(2)}, u32[]{:S(2)}) collective-permute-start(f32[32,2048]{1,0:T(8,128)S(1)} %get-tuple-element.19.refs_0_), channel_id=1, source_target_pairs={{0,16},{8,24},{16,0},{24,8},{1,17},{9,25},{17,1},{25,9},{2,18},{10... | collective-permute-start | bytes 786440 | tf_op jit(solution)/shard_map/ppermute | solution.py:18
  13.4 0.0 collective-permute-start.3
  13.4 11.9 %all_to_all.5.squares = f32[32,1,128]{2,1,0:T(1,128)S(1)} all-to-all(f32[32,1,128]{2,1,0:T(1,128)S(1)} %get-tuple-element.16), channel_id=1, replica_groups=mesh['replica'=4,'fsdp'=8] {'replica','fsdp'}, dimensions={0} | all-to-all | bytes 32768 | tf_op jit(solution)/shard_map/all_to_all | solution.py:103
  25.3 0.0 collective-permute-done.4.refs_2_
  25.3 0.0 collective-permute-done.3.refs_1_
  25.3 0.0 collective-permute-start.5
  25.3 1.5 %collective-permute-done.5.refs_3_ = f32[32,2048]{1,0:T(8,128)S(1)} collective-permute-done((f32[32,2048]{1,0:T(8,128)S(1)}, f32[32,2048]{1,0:T(8,128)S(1)}, u32[]{:S(2)}, u32[]{:S(2)}) %collective-permute-start.5) | collective-permute-done | bytes 262176 | tf_op jit(solution)/shard_map/ppermute | solution.py:18
  26.8 0.0 copy-done
  26.9 0.0 copy-start.1
  26.9 1.2 %copy-done.1 = f32[32,8192]{1,0:T(8,128)S(1)} copy-done((f32[32,8192]{1,0:T(8,128)S(1)}, f32[32,8192]{1,0:T(8,128)}, u32[]{:S(2)}) %copy-start.1) | copy-done | bytes 1048600
  28.1 1.9 %shard_map.52 = (f32[32,8192]{1,0:T(8,128)}, f32[32,8192]{1,0:T(8,128)}) custom-call(f32[32,1,128]{2,1,0:T(1,128)S(1)} %all_to_all.5.squares, f32[32,8192]{1,0:T(8,128)S(1)} %copy-done, f32[32,8192]{1,0:T(8,128)S(1)} %copy-done.1, f32[32,2048]{1,0:T(8,128)S(1)} %get-tuple-element.19.refs_0_, f32[32,2048]{1,0:T(8,128)S(1)} %collective-permute-done.3.refs_1_, ...), custom_call_target="tpu_custom_call" | custom-call | tf_op jit(solution)/shard_map/pallas_call | solution.py:110
Async XLA Ops:
  0.6 1.0 %copy-start.2 = (bf16[1,32,8192]{2,1,0:T(8,128)(2,1)S(1)}, bf16[1,32,8192]{2,1,0:T(8,128)(2,1)}, u32[]{:S(2)}) copy-start(bf16[1,32,8192]{2,1,0:T(8,128)(2,1)} %grad.1) | copy-start | bytes 1572868
  1.7 25.2 %copy-start = (f32[32,8192]{1,0:T(8,128)S(1)}, f32[32,8192]{1,0:T(8,128)}, u32[]{:S(2)}) copy-start(f32[32,8192]{1,0:T(8,128)} %params.1) | copy-start | bytes 3145732
  1.9 3.2 %collective-permute-start = (bf16[32,2048]{1,0:T(8,128)(2,1)S(1)}, bf16[32,2048]{1,0:T(8,128)(2,1)S(1)}, u32[]{:S(2)}, u32[]{:S(2)}) collective-permute-start(bf16[32,2048]{1,0:T(8,128)(2,1)S(1)} %get-tuple-element.13), channel_id=1, source_target_pairs={{0,8},{8,0},{16,24},{24,16},{1,9},{9,1},{17,25},{25,17},{2,10},{10... | collective-permute-start | bytes 393224 | tf_op jit(solution)/shard_map/ppermute | solution.py:18
  2.4 6.9 %collective-permute-start.1 = (bf16[32,2048]{1,0:T(8,128)(2,1)S(1)}, bf16[32,2048]{1,0:T(8,128)(2,1)S(1)}, u32[]{:S(2)}, u32[]{:S(2)}) collective-permute-start(bf16[32,2048]{1,0:T(8,128)(2,1)S(1)} %get-tuple-element.14), channel_id=1, source_target_pairs={{0,16},{8,24},{16,0},{24,8},{1,17},{9,25},{17,1},{25,9},{2,18},{10... | collective-permute-start | bytes 393224 | tf_op jit(solution)/shard_map/ppermute | solution.py:18
  5.0 6.6 %collective-permute-start.2 = (bf16[32,2048]{1,0:T(8,128)(2,1)S(1)}, bf16[32,2048]{1,0:T(8,128)(2,1)S(1)}, u32[]{:S(2)}, u32[]{:S(2)}) collective-permute-start(bf16[32,2048]{1,0:T(8,128)(2,1)S(1)} %get-tuple-element.15), channel_id=1, source_target_pairs={{0,24},{8,16},{16,8},{24,0},{1,25},{9,17},{17,9},{25,1},{2,26},{10... | collective-permute-start | bytes 393224 | tf_op jit(solution)/shard_map/ppermute | solution.py:18
  11.7 13.6 %collective-permute-start.4 = (f32[32,2048]{1,0:T(8,128)S(1)}, f32[32,2048]{1,0:T(8,128)S(1)}, u32[]{:S(2)}, u32[]{:S(2)}) collective-permute-start(f32[32,2048]{1,0:T(8,128)S(1)} %get-tuple-element.19.refs_0_), channel_id=1, source_target_pairs={{0,16},{8,24},{16,0},{24,8},{1,17},{9,25},{17,1},{25,9},{2,18},{10... | collective-permute-start | bytes 786440 | tf_op jit(solution)/shard_map/ppermute | solution.py:18
  13.4 12.0 %collective-permute-start.3 = (f32[32,2048]{1,0:T(8,128)S(1)}, f32[32,2048]{1,0:T(8,128)S(1)}, u32[]{:S(2)}, u32[]{:S(2)}) collective-permute-start(f32[32,2048]{1,0:T(8,128)S(1)} %get-tuple-element.19.refs_0_), channel_id=1, source_target_pairs={{0,8},{8,0},{16,24},{24,16},{1,9},{9,1},{17,25},{25,17},{2,10},{10... | collective-permute-start | bytes 786440 | tf_op jit(solution)/shard_map/ppermute | solution.py:18
  25.3 1.5 %collective-permute-start.5 = (f32[32,2048]{1,0:T(8,128)S(1)}, f32[32,2048]{1,0:T(8,128)S(1)}, u32[]{:S(2)}, u32[]{:S(2)}) collective-permute-start(f32[32,2048]{1,0:T(8,128)S(1)} %collective-permute-done.4.refs_2_), channel_id=1, source_target_pairs={{0,8},{8,0},{16,24},{24,16},{1,9},{9,1},{17,25},{25,17},{2,10},{10... | collective-permute-start | bytes 786440 | tf_op jit(solution)/shard_map/ppermute | solution.py:18
  26.9 1.2 %copy-start.1 = (f32[32,8192]{1,0:T(8,128)S(1)}, f32[32,8192]{1,0:T(8,128)}, u32[]{:S(2)}) copy-start(f32[32,8192]{1,0:T(8,128)} %momentum.1) | copy-start | bytes 3145732

commit v4 on v3

--- a/solution.py
+++ b/solution.py
@@ -53,17 +53,58 @@
     squares[...] = jnp.broadcast_to(lanes[None], squares.shape)
 
 
-def update_kernel(count, squares, params, momentum, *refs):
-    averages, (new_params, new_momentum) = refs[:-2], refs[-2:]
+def fetch_kernel(*refs):
+    half = (len(refs) - 1) // 2
+    copies = [
+        pltpu.make_async_copy(refs[i], refs[half + i], refs[-1].at[i])
+        for i in range(half)
+    ]
+    for copy in copies:
+        copy.start()
+    for copy in copies:
+        copy.wait()
+
+
+def update_kernel(count, flips, passed, squares, params, momentum, *refs):
+    averages, refs = refs[: len(flips)], refs[len(flips) + passed :]
+    new_params, new_momentum, params_out, momentum_out, sems = refs
     square_sum = jnp.sum(squares[...], keepdims=True).reshape(1, 1)
     factor = 0.2 / jnp.sqrt(square_sum / WIDE(count) + 1e-06)
     width = averages[0].shape[1]
-    for k, average in enumerate(averages):
+    copies = []
+    for i, (k, average) in enumerate(zip(flips, averages)):
         cols = piece_of(k, width)
         clipped = factor * average[...]
         fresh = 0.9 * momentum[:, cols] + clipped
-        new_momentum[:, cols] = fresh
-        new_params[:, cols] = params[:, cols] - 0.7 * (clipped + 0.9 * fresh)
+        momentum_out[i] = fresh
+        params_out[i] = params[:, cols] - 0.7 * (clipped + 0.9 * fresh)
+        copies += [
+            pltpu.make_async_copy(momentum_out.at[i], new_momentum.at[:, cols], sems.at[0, i]),
+            pltpu.make_async_copy(params_out.at[i], new_params.at[:, cols], sems.at[1, i]),
+        ]
+        copies[-2].start()
+        copies[-1].start()
+    for copy in copies:
+        copy.wait()
+
+
+def update(count, flips, averages, squares, params, momentum, earlier=()):
+    rows, width = averages[0].shape
+    out = jax.ShapeDtypeStruct(params.shape, WIDE)
+    first = 3 + len(flips)
+    return pl.pallas_call(
+        functools.partial(update_kernel, count, flips, len(earlier)),
+        out_shape=[out, out],
+        in_specs=[VMEM] * first + [HBM] * len(earlier),
+        out_specs=[HBM] * 2,
+        scratch_shapes=[
+            pltpu.VMEM((len(flips), rows, width), WIDE),
+            pltpu.VMEM((len(flips), rows, width), WIDE),
+            pltpu.SemaphoreType.DMA((2, len(flips))),
+        ],
+        input_output_aliases={first + i: i for i in range(len(earlier))},
+        compiler_params=pltpu.CompilerParams(vmem_limit_bytes=LIMIT),
+    )(squares, params, momentum, *averages, *earlier)
 
 
 def per_device(pseudo_grad, params, momentum):
@@ -82,10 +123,20 @@
         scratch_shapes=[pltpu.SemaphoreType.DMA((groups,))],
         compiler_params=limit,
     )(pseudo_grad)
-    order = [k for k in range(1, groups) if k > 1] + [1]
-    moved = {0: pieces[0]}
-    for k in order:
-        moved[k] = swapped(pieces[k], "replica", k)
+    pieces, params, momentum = lax.optimization_barrier((pieces, params, momentum))
+    kept = jax.ShapeDtypeStruct(params.shape, WIDE)
+    params, momentum = pl.pallas_call(
+        fetch_kernel,
+        out_shape=[kept, kept],
+        in_specs=[HBM] * 2,
+        out_specs=[VMEM] * 2,
+        scratch_shapes=[pltpu.SemaphoreType.DMA((2,))],
+        compiler_params=limit,
+        cost_estimate=pl.CostEstimate(flops=0, bytes_accessed=8 * params.size, transcendentals=0),
+    )(params, momentum)
+    moved = {k: swapped(pieces[k], "replica", k) for k in range(2, groups)}
+    near, params, momentum = lax.optimization_barrier((pieces[1], params, momentum))
+    moved.update({0: pieces[0], 1: swapped(near, "replica", 1)})
     average, squares = pl.pallas_call(
         average_kernel,
         out_shape=[
@@ -106,14 +157,14 @@
     squares, averages = lax.optimization_barrier((squares, averages))
     for k in range(2, groups, 2):
         averages[k + 1] = swapped(averages[k], "replica", 1)
-    out = jax.ShapeDtypeStruct((rows, columns), WIDE)
-    return pl.pallas_call(
-        functools.partial(update_kernel, count),
-        out_shape=[out, out],
-        in_specs=[VMEM] * (3 + groups),
-        out_specs=[VMEM] * 2,
-        compiler_params=limit,
-    )(squares, params, momentum, *[averages[k] for k in range(groups)])
+    here = [k for k in range(groups) if k < 2 or k % 2 == 0]
+    late = [k for k in range(groups) if k not in here]
+    outs = update(count, here, [averages[k] for k in here], squares, params, momentum)
+    if late:
+        outs = update(
+            count, late, [averages[k] for k in late], squares, params, momentum, outs
+        )
+    return outs
 
 
 def solution(mesh):

time: 30.2 us -> 27.3 us (0.904)
  waiting for transfers between devices: 8.1 us -> 3.09 us
  local copies, waits for them, and re-layouts: 2.26 us -> 3.48 us
  Pallas kernels: 2.17 us -> 2.91 us
    ppermute x6, waiting for transfers between devices: 8.1 us -> 3.09 us  [swapped(): return lax.ppermute(value, axis, [(i, i ^ flip) for i in range(size)])]
    unnamed x6, local copies, waits for them, and re-layouts: 2.26 us -> 3.48 us
    pallas_call x1 -> x3, Pallas kernels: 1.85 us -> 2.59 us  [the longest x2 2.43 us: update(): pl.pallas_call(functools.partial(update_kernel, count, flips, len(earlier...]
  transfers between devices with their start and end apart: 6 -> 6, of which waited for: 3 -> 3; matrix products, arithmetic and copies ran while one was open for 0% -> 0% of each run, Pallas kernels for 0% -> 6%
where the time goes in v4:
time: 27.3 us; the launch traced here: 27.1 us
  blocking collectives  11.8 us (43%)
  starting transfers between devices  5.06 us (19%)
  local copies, waits for them, and re-layouts  3.48 us (13%)
  waiting for transfers between devices  3.09 us (11%)
  Pallas kernels  2.91 us (11%)
  between operations  0.68 us (2%)
    all_to_all x1, blocking collectives, per_device(): lax.all_to_all(squares, ('replica', 'fsdp'), split_axis=0, concat_axis=0,...  11.8 us
    ppermute x6, starting transfers between devices, swapped(): return lax.ppermute(value, axis, [(i, i ^ flip) for i in range(size)])  5.06 us
    unnamed x6, local copies, waits for them, and re-layouts  3.48 us
    ppermute x6, waiting for transfers between devices, swapped(): return lax.ppermute(value, axis, [(i, i ^ flip) for i in range(size)])  3.09 us
    pallas_call x2, Pallas kernels, update(): pl.pallas_call(functools.partial(update_kernel, count, flips, len(earlier...  2.43 us
  transfers between devices with their start and end apart: 6, of which 3 were waited for; matrix products, arithmetic and copies ran while one was open for 0% of the time, Pallas kernels for 6%

profile of v4, /device:TPU:0, one launch (start us, length us, event | category | flops | bytes accessed | tf_op | source)
XLA Modules:
  0.0 27.1 jit_solution(12913720437716896479)
XLA Ops:
  0.6 0.0 copy-start.2
  0.6 1.0 %copy-done.2 = bf16[1,32,8192]{2,1,0:T(8,128)(2,1)S(1)} copy-done((bf16[1,32,8192]{2,1,0:T(8,128)(2,1)S(1)}, bf16[1,32,8192]{2,1,0:T(8,128)(2,1)}, u32[]{:S(2)}) %copy-start.2) | copy-done | bytes 524312
  1.7 0.2 shard_map.50
  1.9 3.0 %collective-permute-start.1 = (bf16[32,2048]{1,0:T(8,128)(2,1)S(1)}, bf16[32,2048]{1,0:T(8,128)(2,1)S(1)}, u32[]{:S(2)}, u32[]{:S(2)}) collective-permute-start(bf16[32,2048]{1,0:T(8,128)(2,1)S(1)} %get-tuple-element.36), channel_id=1, source_target_pairs={{0,16},{8,24},{16,0},{24,8},{1,17},{9,25},{17,1},{25,9},{2,18},{10... | collective-permute-start | bytes 393224 | tf_op jit(solution)/shard_map/ppermute | solution.py:18
  4.9 0.0 collective-permute-start.2
  4.9 0.0 copy-start
  4.9 1.2 %copy-done = f32[32,8192]{1,0:T(8,128)S(1)} copy-done((f32[32,8192]{1,0:T(8,128)S(1)}, f32[32,8192]{1,0:T(8,128)}, u32[]{:S(2)}) %copy-start) | copy-done | bytes 1048600
  6.1 0.0 copy-start.1
  6.1 1.2 %copy-done.1 = f32[32,8192]{1,0:T(8,128)S(1)} copy-done((f32[32,8192]{1,0:T(8,128)S(1)}, f32[32,8192]{1,0:T(8,128)}, u32[]{:S(2)}) %copy-start.1) | copy-done | bytes 1048600
  7.3 0.2 shard_map.51
  7.5 0.3 collective-permute-start
  7.8 1.1 %collective-permute-done.1.refs_2_ = bf16[32,2048]{1,0:T(8,128)(2,1)S(1)} collective-permute-done((bf16[32,2048]{1,0:T(8,128)(2,1)S(1)}, bf16[32,2048]{1,0:T(8,128)(2,1)S(1)}, u32[]{:S(2)}, u32[]{:S(2)}) %collective-permute-start.1) | collective-permute-done | bytes 131104 | tf_op jit(solution)/shard_map/ppermute | solution.py:18
  8.8 1.9 %collective-permute-done.2.refs_3_ = bf16[32,2048]{1,0:T(8,128)(2,1)S(1)} collective-permute-done((bf16[32,2048]{1,0:T(8,128)(2,1)S(1)}, bf16[32,2048]{1,0:T(8,128)(2,1)S(1)}, u32[]{:S(2)}, u32[]{:S(2)}) %collective-permute-start.2) | collective-permute-done | bytes 131104 | tf_op jit(solution)/shard_map/ppermute | solution.py:18
  10.7 0.0 collective-permute-done.refs_1_
  10.7 0.1 shard_map.52
  10.9 1.1 %collective-permute-start.4 = (f32[32,2048]{1,0:T(8,128)S(1)}, f32[32,2048]{1,0:T(8,128)S(1)}, u32[]{:S(2)}, u32[]{:S(2)}) collective-permute-start(f32[32,2048]{1,0:T(8,128)S(1)} %get-tuple-element.44.refs_0_), channel_id=1, source_target_pairs={{0,16},{8,24},{16,0},{24,8},{1,17},{9,25},{17,1},{25,9},{2,18},{10... | collective-permute-start | bytes 786440 | tf_op jit(solution)/shard_map/ppermute | solution.py:18
  12.0 0.7 %collective-permute-start.3 = (f32[32,2048]{1,0:T(8,128)S(1)}, f32[32,2048]{1,0:T(8,128)S(1)}, u32[]{:S(2)}, u32[]{:S(2)}) collective-permute-start(f32[32,2048]{1,0:T(8,128)S(1)} %get-tuple-element.44.refs_0_), channel_id=1, source_target_pairs={{0,8},{8,0},{16,24},{24,16},{1,9},{9,1},{17,25},{25,17},{2,10},{10... | collective-permute-start | bytes 786440 | tf_op jit(solution)/shard_map/ppermute | solution.py:18
  12.7 11.8 %all_to_all.5.squares = f32[32,1,128]{2,1,0:T(1,128)S(1)} all-to-all(f32[32,1,128]{2,1,0:T(1,128)S(1)} %get-tuple-element.38), channel_id=1, replica_groups=mesh['replica'=4,'fsdp'=8] {'replica','fsdp'}, dimensions={0} | all-to-all | bytes 32768 | tf_op jit(solution)/shard_map/all_to_all | solution.py:154
  24.5 0.0 collective-permute-done.4.refs_2_
  24.5 0.0 collective-permute-done.3.refs_1_
  24.5 0.0 collective-permute-start.5
  24.5 1.4 %shard_map.53 = (f32[32,8192]{1,0:T(8,128)}, f32[32,8192]{1,0:T(8,128)}) custom-call(f32[32,1,128]{2,1,0:T(1,128)S(1)} %all_to_all.5.squares, f32[32,8192]{1,0:T(8,128)S(1)} %get-tuple-element.41.params, f32[32,8192]{1,0:T(8,128)S(1)} %get-tuple-element.42.momentum, f32[32,2048]{1,0:T(8,128)S(1)} %get-tuple-element.44.refs_0_, ...), custom_call_target="tpu_custom_call" | custom-call | tf_op jit(solution)/shard_map/pallas_call | solution.py:95
  25.9 0.1 collective-permute-done.5.refs_0_
  26.0 1.0 %shard_map.54 = (f32[32,8192]{1,0:T(8,128)}, f32[32,8192]{1,0:T(8,128)}) custom-call(f32[32,1,128]{2,1,0:T(1,128)S(1)} %all_to_all.5.squares, f32[32,8192]{1,0:T(8,128)S(1)} %get-tuple-element.41.params, f32[32,8192]{1,0:T(8,128)S(1)} %get-tuple-element.42.momentum, ...), custom_call_target="tpu_custom_call", output_to_operand_aliasing={{0}: (4, {}), {1}: (5, {})} | custom-call | tf_op jit(solution)/shard_map/pallas_call | solution.py:95
Async XLA Ops:
  0.6 1.0 %copy-start.2 = (bf16[1,32,8192]{2,1,0:T(8,128)(2,1)S(1)}, bf16[1,32,8192]{2,1,0:T(8,128)(2,1)}, u32[]{:S(2)}) copy-start(bf16[1,32,8192]{2,1,0:T(8,128)(2,1)} %grad.1) | copy-start | bytes 1572868
  1.9 6.9 %collective-permute-start.1 = (bf16[32,2048]{1,0:T(8,128)(2,1)S(1)}, bf16[32,2048]{1,0:T(8,128)(2,1)S(1)}, u32[]{:S(2)}, u32[]{:S(2)}) collective-permute-start(bf16[32,2048]{1,0:T(8,128)(2,1)S(1)} %get-tuple-element.36), channel_id=1, source_target_pairs={{0,16},{8,24},{16,0},{24,8},{1,17},{9,25},{17,1},{25,9},{2,18},{10... | collective-permute-start | bytes 393224 | tf_op jit(solution)/shard_map/ppermute | solution.py:18
  4.9 5.9 %collective-permute-start.2 = (bf16[32,2048]{1,0:T(8,128)(2,1)S(1)}, bf16[32,2048]{1,0:T(8,128)(2,1)S(1)}, u32[]{:S(2)}, u32[]{:S(2)}) collective-permute-start(bf16[32,2048]{1,0:T(8,128)(2,1)S(1)} %get-tuple-element.37), channel_id=1, source_target_pairs={{0,24},{8,16},{16,8},{24,0},{1,25},{9,17},{17,9},{25,1},{2,26},{10... | collective-permute-start | bytes 393224 | tf_op jit(solution)/shard_map/ppermute | solution.py:18
  4.9 1.2 %copy-start = (f32[32,8192]{1,0:T(8,128)S(1)}, f32[32,8192]{1,0:T(8,128)}, u32[]{:S(2)}) copy-start(f32[32,8192]{1,0:T(8,128)} %refs_0_) | copy-start | bytes 3145732
  6.1 1.2 %copy-start.1 = (f32[32,8192]{1,0:T(8,128)S(1)}, f32[32,8192]{1,0:T(8,128)}, u32[]{:S(2)}) copy-start(f32[32,8192]{1,0:T(8,128)} %refs_1_) | copy-start | bytes 3145732
  7.5 3.2 %collective-permute-start = (bf16[32,2048]{1,0:T(8,128)(2,1)S(1)}, bf16[32,2048]{1,0:T(8,128)(2,1)S(1)}, u32[]{:S(2)}, u32[]{:S(2)}) collective-permute-start(bf16[32,2048]{1,0:T(8,128)(2,1)S(1)} %get-tuple-element.35), channel_id=1, source_target_pairs={{0,8},{8,0},{16,24},{24,16},{1,9},{9,1},{17,25},{25,17},{2,10},{10... | collective-permute-start | bytes 393224 | tf_op jit(solution)/shard_map/ppermute | solution.py:18
  10.9 13.6 %collective-permute-start.4 = (f32[32,2048]{1,0:T(8,128)S(1)}, f32[32,2048]{1,0:T(8,128)S(1)}, u32[]{:S(2)}, u32[]{:S(2)}) collective-permute-start(f32[32,2048]{1,0:T(8,128)S(1)} %get-tuple-element.44.refs_0_), channel_id=1, source_target_pairs={{0,16},{8,24},{16,0},{24,8},{1,17},{9,25},{17,1},{25,9},{2,18},{10... | collective-permute-start | bytes 786440 | tf_op jit(solution)/shard_map/ppermute | solution.py:18
  12.0 12.5 %collective-permute-start.3 = (f32[32,2048]{1,0:T(8,128)S(1)}, f32[32,2048]{1,0:T(8,128)S(1)}, u32[]{:S(2)}, u32[]{:S(2)}) collective-permute-start(f32[32,2048]{1,0:T(8,128)S(1)} %get-tuple-element.44.refs_0_), channel_id=1, source_target_pairs={{0,8},{8,0},{16,24},{24,16},{1,9},{9,1},{17,25},{25,17},{2,10},{10... | collective-permute-start | bytes 786440 | tf_op jit(solution)/shard_map/ppermute | solution.py:18
  24.5 1.5 %collective-permute-start.5 = (f32[32,2048]{1,0:T(8,128)S(1)}, f32[32,2048]{1,0:T(8,128)S(1)}, u32[]{:S(2)}, u32[]{:S(2)}) collective-permute-start(f32[32,2048]{1,0:T(8,128)S(1)} %collective-permute-done.4.refs_2_), channel_id=1, source_target_pairs={{0,8},{8,0},{16,24},{24,16},{1,9},{9,1},{17,25},{25,17},{2,10},{10... | collective-permute-start | bytes 786440 | tf_op jit(solution)/shard_map/ppermute | solution.py:18

commit v5 on v4

--- a/solution.py
+++ b/solution.py
@@ -50,7 +50,11 @@
     lanes = functools.reduce(
         jnp.add, [row[:, i : i + 128] for i in range(0, row.shape[1], 128)]
     )
-    squares[...] = jnp.broadcast_to(lanes[None], squares.shape)
+    squares[...] = lanes
+
+
+def add_kernel(left, right, out):
+    out[...] = left[...] + right[...]
 
 
 def fetch_kernel(*refs):
@@ -65,10 +69,10 @@
         copy.wait()
 
 
-def update_kernel(count, flips, passed, squares, params, momentum, *refs):
-    averages, refs = refs[: len(flips)], refs[len(flips) + passed :]
+def update_kernel(count, flips, near, far, params, momentum, *refs):
+    averages, refs = refs[: len(flips)], refs[len(flips) :]
     new_params, new_momentum, params_out, momentum_out, sems = refs
-    square_sum = jnp.sum(squares[...], keepdims=True).reshape(1, 1)
+    square_sum = jnp.sum(near[...] + far[...], axis=1, keepdims=True)
     factor = 0.2 / jnp.sqrt(square_sum / WIDE(count) + 1e-06)
     width = averages[0].shape[1]
     copies = []
@@ -88,28 +92,36 @@
         copy.wait()
 
 
-def update(count, flips, averages, squares, params, momentum, earlier=()):
+def update(count, averages, near, far, params, momentum):
+    flips = sorted(averages)
     rows, width = averages[0].shape
     out = jax.ShapeDtypeStruct(params.shape, WIDE)
-    first = 3 + len(flips)
     return pl.pallas_call(
-        functools.partial(update_kernel, count, flips, len(earlier)),
+        functools.partial(update_kernel, count, flips),
         out_shape=[out, out],
-        in_specs=[VMEM] * first + [HBM] * len(earlier),
+        in_specs=[VMEM] * (4 + len(flips)),
         out_specs=[HBM] * 2,
         scratch_shapes=[
             pltpu.VMEM((len(flips), rows, width), WIDE),
             pltpu.VMEM((len(flips), rows, width), WIDE),
             pltpu.SemaphoreType.DMA((2, len(flips))),
         ],
-        input_output_aliases={first + i: i for i in range(len(earlier))},
         compiler_params=pltpu.CompilerParams(vmem_limit_bytes=LIMIT),
-    )(squares, params, momentum, *averages, *earlier)
+    )(near, far, params, momentum, *[averages[k] for k in flips])
+
+
+def add(left, right):
+    return pl.pallas_call(
+        add_kernel,
+        out_shape=jax.ShapeDtypeStruct(left.shape, left.dtype),
+        in_specs=[VMEM] * 2,
+        out_specs=VMEM,
+        compiler_params=pltpu.CompilerParams(vmem_limit_bytes=LIMIT),
+    )(left, right)
 
 
 def per_device(pseudo_grad, params, momentum):
     groups = lax.axis_size("replica")
-    devices = groups * lax.axis_size("fsdp")
     rows, columns = params.shape
     width = columns // groups
     count = rows * lax.axis_size("fsdp") * columns
@@ -141,7 +153,7 @@
         average_kernel,
         out_shape=[
             jax.ShapeDtypeStruct((rows, width), WIDE),
-            jax.ShapeDtypeStruct((devices, 1, 128), WIDE),
+            jax.ShapeDtypeStruct((1, 128), WIDE),
         ],
         in_specs=[VMEM] * groups,
         out_specs=[VMEM] * 2,
@@ -150,21 +162,24 @@
     averages = {0: average}
     for k in range(2, groups, 2):
         averages[k] = swapped(average, "replica", k)
-    averages[1] = swapped(average, "replica", 1)
-    squares = lax.all_to_all(
-        squares, ("replica", "fsdp"), split_axis=0, concat_axis=0, tiled=True
-    )
-    squares, averages = lax.optimization_barrier((squares, averages))
+    near, far = squares, jnp.zeros_like(squares)
+    steps = [
+        (axis, 1 << i)
+        for axis in ("fsdp", "replica")
+        for i in range((lax.axis_size(axis) - 1).bit_length())
+    ]
+    for i, (axis, flip) in enumerate(steps):
+        if i:
+            near = add(near, far)
+        if i == 1:
+            near, average = lax.optimization_barrier((near, average))
+            averages[1] = swapped(average, "replica", 1)
+        if i == len(steps) - 1:
+            near, averages = lax.optimization_barrier((near, averages))
+        far = swapped(near, axis, flip)
     for k in range(2, groups, 2):
         averages[k + 1] = swapped(averages[k], "replica", 1)
-    here = [k for k in range(groups) if k < 2 or k % 2 == 0]
-    late = [k for k in range(groups) if k not in here]
-    outs = update(count, here, [averages[k] for k in here], squares, params, momentum)
-    if late:
-        outs = update(
-            count, late, [averages[k] for k in late], squares, params, momentum, outs
-        )
-    return outs
+    return update(count, averages, near, far, params, momentum)
 
 
 def solution(mesh):

time: 27.3 us -> 29.2 us (1.070)
  blocking collectives: 11.8 us -> 0 us
  waiting for transfers between devices: 3.09 us -> 11.6 us
  starting transfers between devices: 5.06 us -> 11.2 us
  Pallas kernels: 2.91 us -> 2 us
    all_to_all x1 -> x0, blocking collectives: 11.8 us -> none  [per_device(): lax.all_to_all(squares, ('replica', 'fsdp'), split_axis=0, concat_axis=0,...]
    ppermute x6 -> x11, waiting for transfers between devices: 3.09 us -> 11.6 us  [swapped(): return lax.ppermute(value, axis, [(i, i ^ flip) for i in range(size)])]
    ppermute x6 -> x11, starting transfers between devices: 5.06 us -> 11.2 us  [swapped(): return lax.ppermute(value, axis, [(i, i ^ flip) for i in range(size)])]
    pallas_call x2 -> x5, Pallas kernels: 2.43 us -> 1.53 us  [the longest x1 1.52 us: update(): pl.pallas_call(functools.partial(update_kernel, count, flips), out_shape=...]
  transfers between devices with their start and end apart: 6 -> 11, of which waited for: 3 -> 7; matrix products, arithmetic and copies ran while one was open for 0% -> 0% of each run, Pallas kernels for 6% -> 1%
where the time goes in v5:
time: 29.2 us; the launch traced here: 28.9 us
  waiting for transfers between devices  11.6 us (40%)
  starting transfers between devices  11.2 us (38%)
  local copies, waits for them, and re-layouts  3.48 us (12%)
  Pallas kernels  2 us (7%)
  between operations  0.67 us (2%)
    ppermute x11, waiting for transfers between devices, swapped(): return lax.ppermute(value, axis, [(i, i ^ flip) for i in range(size)])  11.6 us
    ppermute x11, starting transfers between devices, swapped(): return lax.ppermute(value, axis, [(i, i ^ flip) for i in range(size)])  11.2 us
    unnamed x6, local copies, waits for them, and re-layouts  3.48 us
    pallas_call x1, Pallas kernels, update(): pl.pallas_call(functools.partial(update_kernel, count, flips), out_shape=...  1.52 us
  transfers between devices with their start and end apart: 11, of which 7 were waited for; matrix products, arithmetic and copies ran while one was open for 0% of the time, Pallas kernels for 1%

profile of v5, /device:TPU:0, one launch (start us, length us, event | category | flops | bytes accessed | tf_op | source)
XLA Modules:
  0.0 28.9 jit_solution(13641673371904171902)
XLA Ops:
  0.6 0.0 copy-start.2
  0.6 1.0 %copy-done.2 = bf16[1,32,8192]{2,1,0:T(8,128)(2,1)S(1)} copy-done((bf16[1,32,8192]{2,1,0:T(8,128)(2,1)S(1)}, bf16[1,32,8192]{2,1,0:T(8,128)(2,1)}, u32[]{:S(2)}) %copy-start.2) | copy-done | bytes 524312
  1.7 0.2 shard_map.50
  1.9 3.0 %collective-permute-start.1 = (bf16[32,2048]{1,0:T(8,128)(2,1)S(1)}, bf16[32,2048]{1,0:T(8,128)(2,1)S(1)}, u32[]{:S(2)}, u32[]{:S(2)}) collective-permute-start(bf16[32,2048]{1,0:T(8,128)(2,1)S(1)} %get-tuple-element.36), channel_id=1, source_target_pairs={{0,16},{8,24},{16,0},{24,8},{1,17},{9,25},{17,1},{25,9},{2,18},{10... | collective-permute-start | bytes 393224 | tf_op jit(solution)/shard_map/ppermute | solution.py:18
  4.9 0.0 collective-permute-start.2
  4.9 0.0 copy-start
  4.9 1.2 %copy-done = f32[32,8192]{1,0:T(8,128)S(1)} copy-done((f32[32,8192]{1,0:T(8,128)S(1)}, f32[32,8192]{1,0:T(8,128)}, u32[]{:S(2)}) %copy-start) | copy-done | bytes 1048600
  6.1 0.0 copy-start.1
  6.1 1.2 %copy-done.1 = f32[32,8192]{1,0:T(8,128)S(1)} copy-done((f32[32,8192]{1,0:T(8,128)S(1)}, f32[32,8192]{1,0:T(8,128)}, u32[]{:S(2)}) %copy-start.1) | copy-done | bytes 1048600
  7.3 0.2 shard_map.51
  7.5 0.3 collective-permute-start
  7.8 1.1 %collective-permute-done.1.refs_2_ = bf16[32,2048]{1,0:T(8,128)(2,1)S(1)} collective-permute-done((bf16[32,2048]{1,0:T(8,128)(2,1)S(1)}, bf16[32,2048]{1,0:T(8,128)(2,1)S(1)}, u32[]{:S(2)}, u32[]{:S(2)}) %collective-permute-start.1) | collective-permute-done | bytes 131104 | tf_op jit(solution)/shard_map/ppermute | solution.py:18
  8.8 1.9 %collective-permute-done.2.refs_3_ = bf16[32,2048]{1,0:T(8,128)(2,1)S(1)} collective-permute-done((bf16[32,2048]{1,0:T(8,128)(2,1)S(1)}, bf16[32,2048]{1,0:T(8,128)(2,1)S(1)}, u32[]{:S(2)}, u32[]{:S(2)}) %collective-permute-start.2) | collective-permute-done | bytes 131104 | tf_op jit(solution)/shard_map/ppermute | solution.py:18
  10.7 0.0 collective-permute-done.refs_1_
  10.7 0.1 shard_map.52
  10.9 1.5 %collective-permute-start.3 = (f32[1,128]{1,0:T(1,128)S(1)}, f32[1,128]{1,0:T(1,128)S(1)}, u32[]{:S(2)}, u32[]{:S(2)}) collective-permute-start(f32[1,128]{1,0:T(1,128)S(1)} %get-tuple-element.38.left), channel_id=1, source_target_pairs={{0,1},{1,0},{2,3},{3,2},{4,5},{5,4},{6,7},{7,6},{8,9},{9,8},{10,11... | collective-permute-start | bytes 1544 | tf_op jit(solution)/shard_map/ppermute | solution.py:18
  12.4 1.1 %collective-permute-start.8 = (f32[32,2048]{1,0:T(8,128)S(1)}, f32[32,2048]{1,0:T(8,128)S(1)}, u32[]{:S(2)}, u32[]{:S(2)}) collective-permute-start(f32[32,2048]{1,0:T(8,128)S(1)} %get-tuple-element.45.refs_0_), channel_id=1, source_target_pairs={{0,16},{8,24},{16,0},{24,8},{1,17},{9,25},{17,1},{25,9},{2,18},{10... | collective-permute-start | bytes 786440 | tf_op jit(solution)/shard_map/ppermute | solution.py:18
  13.5 1.0 %collective-permute-done.3.right = f32[1,128]{1,0:T(1,128)S(1)} collective-permute-done((f32[1,128]{1,0:T(1,128)S(1)}, f32[1,128]{1,0:T(1,128)S(1)}, u32[]{:S(2)}, u32[]{:S(2)}) %collective-permute-start.3) | collective-permute-done | bytes 544 | tf_op jit(solution)/shard_map/ppermute | solution.py:18
  14.5 0.0 collective-permute-start.7
  14.5 1.5 %collective-permute-start.4 = (f32[1,128]{1,0:T(1,128)S(1)}, f32[1,128]{1,0:T(1,128)S(1)}, u32[]{:S(2)}, u32[]{:S(2)}) collective-permute-start(f32[1,128]{1,0:T(1,128)S(1)} %shard_map.53.left), channel_id=1, source_target_pairs={{0,2},{1,3},{2,0},{3,1},{4,6},{5,7},{6,4},{7,5},{8,10},{9,11},{10,... | collective-permute-start | bytes 1544 | tf_op jit(solution)/shard_map/ppermute | solution.py:18
  16.0 2.0 %collective-permute-done.4.right = f32[1,128]{1,0:T(1,128)S(1)} collective-permute-done((f32[1,128]{1,0:T(1,128)S(1)}, f32[1,128]{1,0:T(1,128)S(1)}, u32[]{:S(2)}, u32[]{:S(2)}) %collective-permute-start.4) | collective-permute-done | bytes 544 | tf_op jit(solution)/shard_map/ppermute | solution.py:18
  18.0 2.5 %collective-permute-start.5 = (f32[1,128]{1,0:T(1,128)S(1)}, f32[1,128]{1,0:T(1,128)S(1)}, u32[]{:S(2)}, u32[]{:S(2)}) collective-permute-start(f32[1,128]{1,0:T(1,128)S(1)} %shard_map.54.left), channel_id=1, source_target_pairs={{0,4},{1,5},{2,6},{3,7},{4,0},{5,1},{6,2},{7,3},{8,12},{9,13},{10,... | collective-permute-start | bytes 1544 | tf_op jit(solution)/shard_map/ppermute | solution.py:18
  20.5 1.9 %collective-permute-done.5.right = f32[1,128]{1,0:T(1,128)S(1)} collective-permute-done((f32[1,128]{1,0:T(1,128)S(1)}, f32[1,128]{1,0:T(1,128)S(1)}, u32[]{:S(2)}, u32[]{:S(2)}) %collective-permute-start.5) | collective-permute-done | bytes 544 | tf_op jit(solution)/shard_map/ppermute | solution.py:18
  22.5 0.0 collective-permute-start.6
  22.5 1.1 %collective-permute-done.6.right = f32[1,128]{1,0:T(1,128)S(1)} collective-permute-done((f32[1,128]{1,0:T(1,128)S(1)}, f32[1,128]{1,0:T(1,128)S(1)}, u32[]{:S(2)}, u32[]{:S(2)}) %collective-permute-start.6) | collective-permute-done | bytes 544 | tf_op jit(solution)/shard_map/ppermute | solution.py:18
  23.6 0.0 collective-permute-done.8.refs_2_
  23.6 0.0 collective-permute-done.7.refs_1_
  23.6 0.3 collective-permute-start.10
  23.9 1.0 %collective-permute-start.9 = (f32[1,128]{1,0:T(1,128)S(1)}, f32[1,128]{1,0:T(1,128)S(1)}, u32[]{:S(2)}, u32[]{:S(2)}) collective-permute-start(f32[1,128]{1,0:T(1,128)S(1)} %shard_map.56.near), channel_id=1, source_target_pairs={{0,16},{8,24},{16,0},{24,8},{1,17},{9,25},{17,1},{25,9},{2,18},{10... | collective-permute-start | bytes 1544 | tf_op jit(solution)/shard_map/ppermute | solution.py:18
  24.9 2.5 %collective-permute-done.9.far = f32[1,128]{1,0:T(1,128)S(1)} collective-permute-done((f32[1,128]{1,0:T(1,128)S(1)}, f32[1,128]{1,0:T(1,128)S(1)}, u32[]{:S(2)}, u32[]{:S(2)}) %collective-permute-start.9) | collective-permute-done | bytes 544 | tf_op jit(solution)/shard_map/ppermute | solution.py:18
  27.4 0.0 collective-permute-done.10.refs_3_
  27.4 1.5 %shard_map.57 = (f32[32,8192]{1,0:T(8,128)}, f32[32,8192]{1,0:T(8,128)}) custom-call(f32[1,128]{1,0:T(1,128)S(1)} %shard_map.56.near, f32[1,128]{1,0:T(1,128)S(1)} %collective-permute-done.9.far, f32[32,8192]{1,0:T(8,128)S(1)} %get-tuple-element.43.params, f32[32,8192]{1,0:T(8,128)S(1)} %get-tuple-element.44.momentum, ...), custom_call_target="tpu_custom_call" | custom-call | tf_op jit(solution)/shard_map/pallas_call | solution.py:99
  (4 shorter events, 0.0 us)
Async XLA Ops:
  0.6 1.0 %copy-start.2 = (bf16[1,32,8192]{2,1,0:T(8,128)(2,1)S(1)}, bf16[1,32,8192]{2,1,0:T(8,128)(2,1)}, u32[]{:S(2)}) copy-start(bf16[1,32,8192]{2,1,0:T(8,128)(2,1)} %grad.1) | copy-start | bytes 1572868
  1.9 6.9 %collective-permute-start.1 = (bf16[32,2048]{1,0:T(8,128)(2,1)S(1)}, bf16[32,2048]{1,0:T(8,128)(2,1)S(1)}, u32[]{:S(2)}, u32[]{:S(2)}) collective-permute-start(bf16[32,2048]{1,0:T(8,128)(2,1)S(1)} %get-tuple-element.36), channel_id=1, source_target_pairs={{0,16},{8,24},{16,0},{24,8},{1,17},{9,25},{17,1},{25,9},{2,18},{10... | collective-permute-start | bytes 393224 | tf_op jit(solution)/shard_map/ppermute | solution.py:18
  4.9 5.9 %collective-permute-start.2 = (bf16[32,2048]{1,0:T(8,128)(2,1)S(1)}, bf16[32,2048]{1,0:T(8,128)(2,1)S(1)}, u32[]{:S(2)}, u32[]{:S(2)}) collective-permute-start(bf16[32,2048]{1,0:T(8,128)(2,1)S(1)} %get-tuple-element.37), channel_id=1, source_target_pairs={{0,24},{8,16},{16,8},{24,0},{1,25},{9,17},{17,9},{25,1},{2,26},{10... | collective-permute-start | bytes 393224 | tf_op jit(solution)/shard_map/ppermute | solution.py:18
  4.9 1.2 %copy-start = (f32[32,8192]{1,0:T(8,128)S(1)}, f32[32,8192]{1,0:T(8,128)}, u32[]{:S(2)}) copy-start(f32[32,8192]{1,0:T(8,128)} %refs_0_) | copy-start | bytes 3145732
  6.1 1.2 %copy-start.1 = (f32[32,8192]{1,0:T(8,128)S(1)}, f32[32,8192]{1,0:T(8,128)}, u32[]{:S(2)}) copy-start(f32[32,8192]{1,0:T(8,128)} %refs_1_) | copy-start | bytes 3145732
  7.5 3.2 %collective-permute-start = (bf16[32,2048]{1,0:T(8,128)(2,1)S(1)}, bf16[32,2048]{1,0:T(8,128)(2,1)S(1)}, u32[]{:S(2)}, u32[]{:S(2)}) collective-permute-start(bf16[32,2048]{1,0:T(8,128)(2,1)S(1)} %get-tuple-element.35), channel_id=1, source_target_pairs={{0,8},{8,0},{16,24},{24,16},{1,9},{9,1},{17,25},{25,17},{2,10},{10... | collective-permute-start | bytes 393224 | tf_op jit(solution)/shard_map/ppermute | solution.py:18
  10.9 3.6 %collective-permute-start.3 = (f32[1,128]{1,0:T(1,128)S(1)}, f32[1,128]{1,0:T(1,128)S(1)}, u32[]{:S(2)}, u32[]{:S(2)}) collective-permute-start(f32[1,128]{1,0:T(1,128)S(1)} %get-tuple-element.38.left), channel_id=1, source_target_pairs={{0,1},{1,0},{2,3},{3,2},{4,5},{5,4},{6,7},{7,6},{8,9},{9,8},{10,11... | collective-permute-start | bytes 1544 | tf_op jit(solution)/shard_map/ppermute | solution.py:18
  12.4 11.2 %collective-permute-start.8 = (f32[32,2048]{1,0:T(8,128)S(1)}, f32[32,2048]{1,0:T(8,128)S(1)}, u32[]{:S(2)}, u32[]{:S(2)}) collective-permute-start(f32[32,2048]{1,0:T(8,128)S(1)} %get-tuple-element.45.refs_0_), channel_id=1, source_target_pairs={{0,16},{8,24},{16,0},{24,8},{1,17},{9,25},{17,1},{25,9},{2,18},{10... | collective-permute-start | bytes 786440 | tf_op jit(solution)/shard_map/ppermute | solution.py:18
  14.5 9.1 %collective-permute-start.7 = (f32[32,2048]{1,0:T(8,128)S(1)}, f32[32,2048]{1,0:T(8,128)S(1)}, u32[]{:S(2)}, u32[]{:S(2)}) collective-permute-start(f32[32,2048]{1,0:T(8,128)S(1)} %get-tuple-element.45.refs_0_), channel_id=1, source_target_pairs={{0,8},{8,0},{16,24},{24,16},{1,9},{9,1},{17,25},{25,17},{2,10},{10... | collective-permute-start | bytes 786440 | tf_op jit(solution)/shard_map/ppermute | solution.py:18
  14.5 3.5 %collective-permute-start.4 = (f32[1,128]{1,0:T(1,128)S(1)}, f32[1,128]{1,0:T(1,128)S(1)}, u32[]{:S(2)}, u32[]{:S(2)}) collective-permute-start(f32[1,128]{1,0:T(1,128)S(1)} %shard_map.53.left), channel_id=1, source_target_pairs={{0,2},{1,3},{2,0},{3,1},{4,6},{5,7},{6,4},{7,5},{8,10},{9,11},{10,... | collective-permute-start | bytes 1544 | tf_op jit(solution)/shard_map/ppermute | solution.py:18
  18.0 4.4 %collective-permute-start.5 = (f32[1,128]{1,0:T(1,128)S(1)}, f32[1,128]{1,0:T(1,128)S(1)}, u32[]{:S(2)}, u32[]{:S(2)}) collective-permute-start(f32[1,128]{1,0:T(1,128)S(1)} %shard_map.54.left), channel_id=1, source_target_pairs={{0,4},{1,5},{2,6},{3,7},{4,0},{5,1},{6,2},{7,3},{8,12},{9,13},{10,... | collective-permute-start | bytes 1544 | tf_op jit(solution)/shard_map/ppermute | solution.py:18
  22.5 1.1 %collective-permute-start.6 = (f32[1,128]{1,0:T(1,128)S(1)}, f32[1,128]{1,0:T(1,128)S(1)}, u32[]{:S(2)}, u32[]{:S(2)}) collective-permute-start(f32[1,128]{1,0:T(1,128)S(1)} %shard_map.55.left), channel_id=1, source_target_pairs={{0,8},{8,0},{16,24},{24,16},{1,9},{9,1},{17,25},{25,17},{2,10},{10... | collective-permute-start | bytes 1544 | tf_op jit(solution)/shard_map/ppermute | solution.py:18
  23.6 3.8 %collective-permute-start.10 = (f32[32,2048]{1,0:T(8,128)S(1)}, f32[32,2048]{1,0:T(8,128)S(1)}, u32[]{:S(2)}, u32[]{:S(2)}) collective-permute-start(f32[32,2048]{1,0:T(8,128)S(1)} %collective-permute-done.8.refs_2_), channel_id=1, source_target_pairs={{0,8},{8,0},{16,24},{24,16},{1,9},{9,1},{17,25},{25,17},{2,10},{10... | collective-permute-start | bytes 786440 | tf_op jit(solution)/shard_map/ppermute | solution.py:18
  23.9 3.5 %collective-permute-start.9 = (f32[1,128]{1,0:T(1,128)S(1)}, f32[1,128]{1,0:T(1,128)S(1)}, u32[]{:S(2)}, u32[]{:S(2)}) collective-permute-start(f32[1,128]{1,0:T(1,128)S(1)} %shard_map.56.near), channel_id=1, source_target_pairs={{0,16},{8,24},{16,0},{24,8},{1,17},{9,25},{17,1},{25,9},{2,18},{10... | collective-permute-start | bytes 1544 | tf_op jit(solution)/shard_map/ppermute | solution.py:18

commit v6 on v4

--- a/solution.py
+++ b/solution.py
@@ -41,16 +41,27 @@
         copy.wait()
 
 
-def average_kernel(*refs):
-    pieces, (average, squares) = refs[:-2], refs[-2:]
-    total = tree([piece[...].astype(WIDE) for piece in pieces])
-    mean = total / WIDE(len(pieces))
+def pair_kernel(own, own_mate, other, other_mate, own_sum, other_sum):
+    own_sum[...] = own[...].astype(WIDE) + own_mate[...].astype(WIDE)
+    other_sum[...] = other[...].astype(WIDE) + other_mate[...].astype(WIDE)
+
+
+def average_kernel(groups, *refs):
+    own, pieces, (average, squares) = refs[0], refs[1:-2], refs[-2:]
+    pairs = [own[...]]
+    for i in range(0, len(pieces), 2):
+        pairs.append(pieces[i][...].astype(WIDE) + pieces[i + 1][...].astype(WIDE))
+    mean = tree(pairs) / WIDE(groups)
     average[...] = mean
     row = jnp.sum(mean * mean, axis=0, keepdims=True)
     lanes = functools.reduce(
         jnp.add, [row[:, i : i + 128] for i in range(0, row.shape[1], 128)]
     )
     squares[...] = jnp.broadcast_to(lanes[None], squares.shape)
+
+
+def join_kernel(groups, here, there, average):
+    average[...] = (here[...] + there[...]) / WIDE(groups)
 
 
 def fetch_kernel(*refs):
@@ -107,55 +118,67 @@
     )(squares, params, momentum, *averages, *earlier)
 
 
+def call(kernel, out_shape, *args, scratch=()):
+    return pl.pallas_call(
+        kernel,
+        out_shape=out_shape,
+        in_specs=[VMEM] * len(args),
+        out_specs=jax.tree.map(lambda _: VMEM, out_shape),
+        scratch_shapes=scratch,
+        compiler_params=pltpu.CompilerParams(vmem_limit_bytes=LIMIT),
+    )(*args)
+
+
 def per_device(pseudo_grad, params, momentum):
     groups = lax.axis_size("replica")
     devices = groups * lax.axis_size("fsdp")
     rows, columns = params.shape
     width = columns // groups
     count = rows * lax.axis_size("fsdp") * columns
-    limit = pltpu.CompilerParams(vmem_limit_bytes=LIMIT)
     piece = jax.ShapeDtypeStruct((rows, width), pseudo_grad.dtype)
-    pieces = pl.pallas_call(
-        cut_kernel,
-        out_shape=[piece] * groups,
-        in_specs=[HBM],
-        out_specs=[VMEM] * groups,
-        scratch_shapes=[pltpu.SemaphoreType.DMA((groups,))],
-        compiler_params=limit,
-    )(pseudo_grad)
-    pieces, params, momentum = lax.optimization_barrier((pieces, params, momentum))
-    kept = jax.ShapeDtypeStruct(params.shape, WIDE)
-    params, momentum = pl.pallas_call(
-        fetch_kernel,
-        out_shape=[kept, kept],
-        in_specs=[HBM] * 2,
-        out_specs=[VMEM] * 2,
-        scratch_shapes=[pltpu.SemaphoreType.DMA((2,))],
-        compiler_params=limit,
-        cost_estimate=pl.CostEstimate(flops=0, bytes_accessed=8 * params.size, transcendentals=0),
-    )(params, momentum)
-    moved = {k: swapped(pieces[k], "replica", k) for k in range(2, groups)}
-    near, params, momentum = lax.optimization_barrier((pieces[1], params, momentum))
-    moved.update({0: pieces[0], 1: swapped(near, "replica", 1)})
-    average, squares = pl.pallas_call(
-        average_kernel,
-        out_shape=[
-            jax.ShapeDtypeStruct((rows, width), WIDE),
-            jax.ShapeDtypeStruct((devices, 1, 128), WIDE),
-        ],
-        in_specs=[VMEM] * groups,
-        out_specs=[VMEM] * 2,
-        compiler_params=limit,
-    )(*[moved[k] for k in range(groups)])
-    averages = {0: average}
-    for k in range(2, groups, 2):
-        averages[k] = swapped(average, "replica", k)
-    averages[1] = swapped(average, "replica", 1)
+    wide_piece = jax.ShapeDtypeStruct((rows, width), WIDE)
+    others = range(2, groups, 2)
+
+    pieces = call(
+        cut_kernel, [piece] * groups, pseudo_grad,
+        scratch=[pltpu.SemaphoreType.DMA((groups,))],
+    )
+    direct = {k: swapped(pieces[k], "replica", k) for k in others}
+    near = {k: swapped(pieces[k + 1], "replica", 1) for k in others}
+    near, last = lax.optimization_barrier((near, pieces[1]))
+    relayed = {k: swapped(near[k], "replica", k) for k in others}
+    direct, momentum = lax.optimization_barrier((direct, momentum))
+    mate = swapped(last, "replica", 1)
+    (momentum,) = call(
+        fetch_kernel, [jax.ShapeDtypeStruct(params.shape, WIDE)], momentum,
+        scratch=[pltpu.SemaphoreType.DMA((1,))],
+    )
+    own_sum, other_sum = call(
+        pair_kernel, [wide_piece] * 2,
+        pieces[0], mate, pieces[2 % groups], near.get(2, mate),
+    )
+    averages = {}
+    if groups == 4:
+        own_sum, momentum = lax.optimization_barrier((own_sum, momentum))
+        across = swapped(own_sum, "replica", 2)
+    averages[0], squares = call(
+        functools.partial(average_kernel, groups),
+        [wide_piece, jax.ShapeDtypeStruct((devices, 1, 128), WIDE)],
+        own_sum, *[x[k] for k in others for x in (direct, relayed)],
+    )
+    averages[1] = swapped(averages[0], "replica", 1)
+    if groups != 4:
+        averages.update({k: swapped(averages[0], "replica", k) for k in others})
     squares = lax.all_to_all(
         squares, ("replica", "fsdp"), split_axis=0, concat_axis=0, tiled=True
     )
+    if groups == 4:
+        squares, across = lax.optimization_barrier((squares, across))
+        averages[2] = call(
+            functools.partial(join_kernel, groups), wide_piece, other_sum, across
+        )
     squares, averages = lax.optimization_barrier((squares, averages))
-    for k in range(2, groups, 2):
+    for k in others:
         averages[k + 1] = swapped(averages[k], "replica", 1)
     here = [k for k in range(groups) if k < 2 or k % 2 == 0]
     late = [k for k in range(groups) if k not in here]

time: 27.3 us -> 28.1 us (1.029)
  starting transfers between devices: 5.06 us -> 6.67 us
  local copies, waits for them, and re-layouts: 3.48 us -> 2.27 us
  blocking collectives: 11.8 us -> 12.3 us
    ppermute x6 -> x7, starting transfers between devices: 5.06 us -> 6.67 us  [swapped(): return lax.ppermute(value, axis, [(i, i ^ flip) for i in range(size)])]
    unnamed x6, local copies, waits for them, and re-layouts: 3.48 us -> 2.27 us
    all_to_all x1, blocking collectives: 11.8 us -> 12.3 us  [per_device(): lax.all_to_all(squares, ('replica', 'fsdp'), split_axis=0, concat_axis=0,...]
    ppermute x6 -> x7, waiting for transfers between devices: 3.09 us -> 3.02 us  [swapped(): return lax.ppermute(value, axis, [(i, i ^ flip) for i in range(size)])]
  transfers between devices with their start and end apart: 6 -> 7, of which waited for: 3 -> 2; matrix products, arithmetic and copies ran while one was open for 0% -> 0% of each run, Pallas kernels for 6% -> 6%
where the time goes in v6:
time: 28.1 us; the launch traced here: 27.8 us
  blocking collectives  12.3 us (44%)
  starting transfers between devices  6.67 us (24%)
  waiting for transfers between devices  3.02 us (11%)
  Pallas kernels  2.89 us (10%)
  local copies, waits for them, and re-layouts  2.27 us (8%)
  between operations  0.73 us (3%)
    all_to_all x1, blocking collectives, per_device(): lax.all_to_all(squares, ('replica', 'fsdp'), split_axis=0, concat_axis=0,...  12.3 us
    ppermute x7, starting transfers between devices, swapped(): return lax.ppermute(value, axis, [(i, i ^ flip) for i in range(size)])  6.67 us
    ppermute x7, waiting for transfers between devices, swapped(): return lax.ppermute(value, axis, [(i, i ^ flip) for i in range(size)])  3.02 us
    pallas_call x2, Pallas kernels, update(): pl.pallas_call(functools.partial(update_kernel, count, flips, len(earlier...  2.43 us
    unnamed x6, local copies, waits for them, and re-layouts  2.27 us
  transfers between devices with their start and end apart: 7, of which 2 were waited for; matrix products, arithmetic and copies ran while one was open for 0% of the time, Pallas kernels for 6%

profile of v6, /device:TPU:0, one launch (start us, length us, event | category | flops | bytes accessed | tf_op | source)
XLA Modules:
  0.0 27.8 jit_solution(14904265612962099803)
XLA Ops:
  0.6 0.0 copy-start.2
  0.6 1.0 %copy-done.2 = bf16[1,32,8192]{2,1,0:T(8,128)(2,1)S(1)} copy-done((bf16[1,32,8192]{2,1,0:T(8,128)(2,1)S(1)}, bf16[1,32,8192]{2,1,0:T(8,128)(2,1)}, u32[]{:S(2)}) %copy-start.2) | copy-done | bytes 524312
  1.7 0.2 shard_map.50
  1.9 0.5 %collective-permute-start = (bf16[32,2048]{1,0:T(8,128)(2,1)S(1)}, bf16[32,2048]{1,0:T(8,128)(2,1)S(1)}, u32[]{:S(2)}, u32[]{:S(2)}) collective-permute-start(bf16[32,2048]{1,0:T(8,128)(2,1)S(1)} %get-tuple-element.25), channel_id=1, source_target_pairs={{0,8},{8,0},{16,24},{24,16},{1,9},{9,1},{17,25},{25,17},{2,10},{10... | collective-permute-start | bytes 393224 | tf_op jit(solution)/shard_map/ppermute | solution.py:18
  2.4 2.6 %collective-permute-start.2 = (bf16[32,2048]{1,0:T(8,128)(2,1)S(1)}, bf16[32,2048]{1,0:T(8,128)(2,1)S(1)}, u32[]{:S(2)}, u32[]{:S(2)}) collective-permute-start(bf16[32,2048]{1,0:T(8,128)(2,1)S(1)} %get-tuple-element.28.other), channel_id=1, source_target_pairs={{0,16},{8,24},{16,0},{24,8},{1,17},{9,25},{17,1},{25,9},{2,18},{10... | collective-permute-start | bytes 393224 | tf_op jit(solution)/shard_map/ppermute | solution.py:18
  5.0 0.0 collective-permute-done.other_mate
  5.0 0.2 collective-permute-start.1
  5.1 1.3 %collective-permute-start.3 = (bf16[32,2048]{1,0:T(8,128)(2,1)S(1)}, bf16[32,2048]{1,0:T(8,128)(2,1)S(1)}, u32[]{:S(2)}, u32[]{:S(2)}) collective-permute-start(bf16[32,2048]{1,0:T(8,128)(2,1)S(1)} %collective-permute-done.other_mate), channel_id=1, source_target_pairs={{0,16},{8,24},{16,0},{24,8},{1,17},{9,25},{17,1},{25,9},{2,18},{10... | collective-permute-start | bytes 393224 | tf_op jit(solution)/shard_map/ppermute | solution.py:18
  6.4 2.9 %collective-permute-done.2.refs_1_ = bf16[32,2048]{1,0:T(8,128)(2,1)S(1)} collective-permute-done((bf16[32,2048]{1,0:T(8,128)(2,1)S(1)}, bf16[32,2048]{1,0:T(8,128)(2,1)S(1)}, u32[]{:S(2)}, u32[]{:S(2)}) %collective-permute-start.2) | collective-permute-done | bytes 131104 | tf_op jit(solution)/shard_map/ppermute | solution.py:18
  9.3 0.0 copy-start.1
  9.3 1.2 %copy-done.1 = f32[32,8192]{1,0:T(8,128)S(1)} copy-done((f32[32,8192]{1,0:T(8,128)S(1)}, f32[32,8192]{1,0:T(8,128)}, u32[]{:S(2)}) %copy-start.1) | copy-done | bytes 1048600
  10.5 0.1 shard_map.52.momentum
  10.6 0.0 copy-start
  10.6 0.0 collective-permute-done.1.own_mate
  10.6 0.1 shard_map.51
  10.7 2.0 %collective-permute-start.4 = (f32[32,2048]{1,0:T(8,128)S(1)}, f32[32,2048]{1,0:T(8,128)S(1)}, u32[]{:S(2)}, u32[]{:S(2)}) collective-permute-start(f32[32,2048]{1,0:T(8,128)S(1)} %get-tuple-element.32.refs_0_), channel_id=1, source_target_pairs={{0,16},{8,24},{16,0},{24,8},{1,17},{9,25},{17,1},{25,9},{2,18},{10... | collective-permute-start | bytes 786440 | tf_op jit(solution)/shard_map/ppermute | solution.py:18
  12.7 0.0 collective-permute-done.3.refs_2_
  12.7 0.1 shard_map.53
  12.8 0.1 collective-permute-start.5
  12.9 12.3 %all_to_all.5.squares = f32[32,1,128]{2,1,0:T(1,128)S(1)} all-to-all(f32[32,1,128]{2,1,0:T(1,128)S(1)} %get-tuple-element.34), channel_id=1, replica_groups=mesh['replica'=4,'fsdp'=8] {'replica','fsdp'}, dimensions={0} | all-to-all | bytes 32768 | tf_op jit(solution)/shard_map/all_to_all | solution.py:172
  25.2 0.0 collective-permute-done.4.there
  25.2 0.0 collective-permute-done.5.refs_1_
  25.2 0.1 collective-permute-start.6
  25.3 0.0 copy-done
  25.3 1.4 %shard_map.55 = (f32[32,8192]{1,0:T(8,128)}, f32[32,8192]{1,0:T(8,128)}) custom-call(f32[32,1,128]{2,1,0:T(1,128)S(1)} %all_to_all.5.squares, f32[32,8192]{1,0:T(8,128)S(1)} %copy-done, f32[32,8192]{1,0:T(8,128)S(1)} %shard_map.52.momentum, f32[32,2048]{1,0:T(8,128)S(1)} %get-tuple-element.42.refs_0_, f32[32,2048]{1,0:T(8,128)S(1)} %collective-permute-done.5.refs_1_, ...), custom_call_target="tpu_custom_call" | custom-call | tf_op jit(solution)/shard_map/pallas_call | solution.py:106
  26.7 0.1 collective-permute-done.6.refs_0_
  26.8 1.0 %shard_map.56 = (f32[32,8192]{1,0:T(8,128)}, f32[32,8192]{1,0:T(8,128)}) custom-call(f32[32,1,128]{2,1,0:T(1,128)S(1)} %all_to_all.5.squares, f32[32,8192]{1,0:T(8,128)S(1)} %copy-done, f32[32,8192]{1,0:T(8,128)S(1)} %shard_map.52.momentum, f32[32,2048]{1,0:T(8,128)S(1)} %collective-permute-done.6.refs_0_, ...), custom_call_target="tpu_custom_call", output_to_operand_aliasing={{0}: (4, {}), {1}: (5, {})} | custom-call | tf_op jit(solution)/shard_map/pallas_call | solution.py:106
  (1 shorter events, 0.0 us)
Async XLA Ops:
  0.6 1.0 %copy-start.2 = (bf16[1,32,8192]{2,1,0:T(8,128)(2,1)S(1)}, bf16[1,32,8192]{2,1,0:T(8,128)(2,1)}, u32[]{:S(2)}) copy-start(bf16[1,32,8192]{2,1,0:T(8,128)(2,1)} %grad.1) | copy-start | bytes 1572868
  1.9 3.1 %collective-permute-start = (bf16[32,2048]{1,0:T(8,128)(2,1)S(1)}, bf16[32,2048]{1,0:T(8,128)(2,1)S(1)}, u32[]{:S(2)}, u32[]{:S(2)}) collective-permute-start(bf16[32,2048]{1,0:T(8,128)(2,1)S(1)} %get-tuple-element.25), channel_id=1, source_target_pairs={{0,8},{8,0},{16,24},{24,16},{1,9},{9,1},{17,25},{25,17},{2,10},{10... | collective-permute-start | bytes 393224 | tf_op jit(solution)/shard_map/ppermute | solution.py:18
  2.4 6.9 %collective-permute-start.2 = (bf16[32,2048]{1,0:T(8,128)(2,1)S(1)}, bf16[32,2048]{1,0:T(8,128)(2,1)S(1)}, u32[]{:S(2)}, u32[]{:S(2)}) collective-permute-start(bf16[32,2048]{1,0:T(8,128)(2,1)S(1)} %get-tuple-element.28.other), channel_id=1, source_target_pairs={{0,16},{8,24},{16,0},{24,8},{1,17},{9,25},{17,1},{25,9},{2,18},{10... | collective-permute-start | bytes 393224 | tf_op jit(solution)/shard_map/ppermute | solution.py:18
  5.0 5.7 %collective-permute-start.1 = (bf16[32,2048]{1,0:T(8,128)(2,1)S(1)}, bf16[32,2048]{1,0:T(8,128)(2,1)S(1)}, u32[]{:S(2)}, u32[]{:S(2)}) collective-permute-start(bf16[32,2048]{1,0:T(8,128)(2,1)S(1)} %get-tuple-element.27), channel_id=1, source_target_pairs={{0,8},{8,0},{16,24},{24,16},{1,9},{9,1},{17,25},{25,17},{2,10},{10... | collective-permute-start | bytes 393224 | tf_op jit(solution)/shard_map/ppermute | solution.py:18
  5.1 7.6 %collective-permute-start.3 = (bf16[32,2048]{1,0:T(8,128)(2,1)S(1)}, bf16[32,2048]{1,0:T(8,128)(2,1)S(1)}, u32[]{:S(2)}, u32[]{:S(2)}) collective-permute-start(bf16[32,2048]{1,0:T(8,128)(2,1)S(1)} %collective-permute-done.other_mate), channel_id=1, source_target_pairs={{0,16},{8,24},{16,0},{24,8},{1,17},{9,25},{17,1},{25,9},{2,18},{10... | collective-permute-start | bytes 393224 | tf_op jit(solution)/shard_map/ppermute | solution.py:18
  9.3 1.2 %copy-start.1 = (f32[32,8192]{1,0:T(8,128)S(1)}, f32[32,8192]{1,0:T(8,128)}, u32[]{:S(2)}) copy-start(f32[32,8192]{1,0:T(8,128)} %refs_0_) | copy-start | bytes 3145732
  10.6 14.7 %copy-start = (f32[32,8192]{1,0:T(8,128)S(1)}, f32[32,8192]{1,0:T(8,128)}, u32[]{:S(2)}) copy-start(f32[32,8192]{1,0:T(8,128)} %params.3) | copy-start | bytes 3145732
  10.7 14.5 %collective-permute-start.4 = (f32[32,2048]{1,0:T(8,128)S(1)}, f32[32,2048]{1,0:T(8,128)S(1)}, u32[]{:S(2)}, u32[]{:S(2)}) collective-permute-start(f32[32,2048]{1,0:T(8,128)S(1)} %get-tuple-element.32.refs_0_), channel_id=1, source_target_pairs={{0,16},{8,24},{16,0},{24,8},{1,17},{9,25},{17,1},{25,9},{2,18},{10... | collective-permute-start | bytes 786440 | tf_op jit(solution)/shard_map/ppermute | solution.py:18
  12.8 12.4 %collective-permute-start.5 = (f32[32,2048]{1,0:T(8,128)S(1)}, f32[32,2048]{1,0:T(8,128)S(1)}, u32[]{:S(2)}, u32[]{:S(2)}) collective-permute-start(f32[32,2048]{1,0:T(8,128)S(1)} %get-tuple-element.42.refs_0_), channel_id=1, source_target_pairs={{0,8},{8,0},{16,24},{24,16},{1,9},{9,1},{17,25},{25,17},{2,10},{10... | collective-permute-start | bytes 786440 | tf_op jit(solution)/shard_map/ppermute | solution.py:18
  25.2 1.6 %collective-permute-start.6 = (f32[32,2048]{1,0:T(8,128)S(1)}, f32[32,2048]{1,0:T(8,128)S(1)}, u32[]{:S(2)}, u32[]{:S(2)}) collective-permute-start(f32[32,2048]{1,0:T(8,128)S(1)} %shard_map.54.refs_2_), channel_id=1, source_target_pairs={{0,8},{8,0},{16,24},{24,16},{1,9},{9,1},{17,25},{25,17},{2,10},{10... | collective-permute-start | bytes 786440 | tf_op jit(solution)/shard_map/ppermute | solution.py:18

commit v7 on v4

--- a/solution.py
+++ b/solution.py
@@ -152,7 +152,7 @@
         averages[k] = swapped(average, "replica", k)
     averages[1] = swapped(average, "replica", 1)
     squares = lax.all_to_all(
-        squares, ("replica", "fsdp"), split_axis=0, concat_axis=0, tiled=True
+        squares, ("fsdp", "replica"), split_axis=0, concat_axis=0, tiled=True
     )
     squares, averages = lax.optimization_barrier((squares, averages))
     for k in range(2, groups, 2):

time: 27.3 us -> 27.4 us (level)
  no operation moved by 1% of the time
where the time goes in v7:
time: 27.4 us; the launch traced here: 27.1 us
  blocking collectives  11.9 us (43%)
  starting transfers between devices  5.06 us (18%)
  local copies, waits for them, and re-layouts  3.48 us (13%)
  waiting for transfers between devices  3.09 us (11%)
  Pallas kernels  2.91 us (11%)
  between operations  0.68 us (2%)
    all_to_all x1, blocking collectives, per_device(): lax.all_to_all(squares, ('fsdp', 'replica'), split_axis=0, concat_axis=0,...  11.9 us
    ppermute x6, starting transfers between devices, swapped(): return lax.ppermute(value, axis, [(i, i ^ flip) for i in range(size)])  5.06 us
    unnamed x6, local copies, waits for them, and re-layouts  3.48 us
    ppermute x6, waiting for transfers between devices, swapped(): return lax.ppermute(value, axis, [(i, i ^ flip) for i in range(size)])  3.09 us
    pallas_call x2, Pallas kernels, update(): pl.pallas_call(functools.partial(update_kernel, count, flips, len(earlier...  2.43 us
  transfers between devices with their start and end apart: 6, of which 3 were waited for; matrix products, arithmetic and copies ran while one was open for 0% of the time, Pallas kernels for 6%

profile of v7, /device:TPU:0, one launch (start us, length us, event | category | flops | bytes accessed | tf_op | source)
XLA Modules:
  0.0 27.1 jit_solution(574264947389886260)
XLA Ops:
  0.6 0.0 copy-start.2
  0.6 1.0 %copy-done.2 = bf16[1,32,8192]{2,1,0:T(8,128)(2,1)S(1)} copy-done((bf16[1,32,8192]{2,1,0:T(8,128)(2,1)S(1)}, bf16[1,32,8192]{2,1,0:T(8,128)(2,1)}, u32[]{:S(2)}) %copy-start.2) | copy-done | bytes 524312
  1.7 0.2 shard_map.50
  1.9 3.0 %collective-permute-start.1 = (bf16[32,2048]{1,0:T(8,128)(2,1)S(1)}, bf16[32,2048]{1,0:T(8,128)(2,1)S(1)}, u32[]{:S(2)}, u32[]{:S(2)}) collective-permute-start(bf16[32,2048]{1,0:T(8,128)(2,1)S(1)} %get-tuple-element.36), channel_id=1, source_target_pairs={{0,16},{8,24},{16,0},{24,8},{1,17},{9,25},{17,1},{25,9},{2,18},{10... | collective-permute-start | bytes 393224 | tf_op jit(solution)/shard_map/ppermute | solution.py:18
  4.9 0.0 collective-permute-start.2
  4.9 0.0 copy-start
  4.9 1.2 %copy-done = f32[32,8192]{1,0:T(8,128)S(1)} copy-done((f32[32,8192]{1,0:T(8,128)S(1)}, f32[32,8192]{1,0:T(8,128)}, u32[]{:S(2)}) %copy-start) | copy-done | bytes 1048600
  6.1 0.0 copy-start.1
  6.1 1.2 %copy-done.1 = f32[32,8192]{1,0:T(8,128)S(1)} copy-done((f32[32,8192]{1,0:T(8,128)S(1)}, f32[32,8192]{1,0:T(8,128)}, u32[]{:S(2)}) %copy-start.1) | copy-done | bytes 1048600
  7.3 0.2 shard_map.51
  7.5 0.3 collective-permute-start
  7.8 1.1 %collective-permute-done.1.refs_2_ = bf16[32,2048]{1,0:T(8,128)(2,1)S(1)} collective-permute-done((bf16[32,2048]{1,0:T(8,128)(2,1)S(1)}, bf16[32,2048]{1,0:T(8,128)(2,1)S(1)}, u32[]{:S(2)}, u32[]{:S(2)}) %collective-permute-start.1) | collective-permute-done | bytes 131104 | tf_op jit(solution)/shard_map/ppermute | solution.py:18
  8.8 1.9 %collective-permute-done.2.refs_3_ = bf16[32,2048]{1,0:T(8,128)(2,1)S(1)} collective-permute-done((bf16[32,2048]{1,0:T(8,128)(2,1)S(1)}, bf16[32,2048]{1,0:T(8,128)(2,1)S(1)}, u32[]{:S(2)}, u32[]{:S(2)}) %collective-permute-start.2) | collective-permute-done | bytes 131104 | tf_op jit(solution)/shard_map/ppermute | solution.py:18
  10.7 0.0 collective-permute-done.refs_1_
  10.7 0.1 shard_map.52
  10.9 1.1 %collective-permute-start.4 = (f32[32,2048]{1,0:T(8,128)S(1)}, f32[32,2048]{1,0:T(8,128)S(1)}, u32[]{:S(2)}, u32[]{:S(2)}) collective-permute-start(f32[32,2048]{1,0:T(8,128)S(1)} %get-tuple-element.44.refs_0_), channel_id=1, source_target_pairs={{0,16},{8,24},{16,0},{24,8},{1,17},{9,25},{17,1},{25,9},{2,18},{10... | collective-permute-start | bytes 786440 | tf_op jit(solution)/shard_map/ppermute | solution.py:18
  12.0 0.7 %collective-permute-start.3 = (f32[32,2048]{1,0:T(8,128)S(1)}, f32[32,2048]{1,0:T(8,128)S(1)}, u32[]{:S(2)}, u32[]{:S(2)}) collective-permute-start(f32[32,2048]{1,0:T(8,128)S(1)} %get-tuple-element.44.refs_0_), channel_id=1, source_target_pairs={{0,8},{8,0},{16,24},{24,16},{1,9},{9,1},{17,25},{25,17},{2,10},{10... | collective-permute-start | bytes 786440 | tf_op jit(solution)/shard_map/ppermute | solution.py:18
  12.7 11.9 %all_to_all.5.squares = f32[32,1,128]{2,1,0:T(1,128)S(1)} all-to-all(f32[32,1,128]{2,1,0:T(1,128)S(1)} %get-tuple-element.38), channel_id=1, replica_groups=mesh['replica'=4,'fsdp'=8] {'fsdp','replica'}, dimensions={0} | all-to-all | bytes 32768 | tf_op jit(solution)/shard_map/all_to_all | solution.py:154
  24.5 0.0 collective-permute-done.4.refs_2_
  24.5 0.0 collective-permute-done.3.refs_1_
  24.5 0.0 collective-permute-start.5
  24.5 1.4 %shard_map.53 = (f32[32,8192]{1,0:T(8,128)}, f32[32,8192]{1,0:T(8,128)}) custom-call(f32[32,1,128]{2,1,0:T(1,128)S(1)} %all_to_all.5.squares, f32[32,8192]{1,0:T(8,128)S(1)} %get-tuple-element.41.params, f32[32,8192]{1,0:T(8,128)S(1)} %get-tuple-element.42.momentum, f32[32,2048]{1,0:T(8,128)S(1)} %get-tuple-element.44.refs_0_, ...), custom_call_target="tpu_custom_call" | custom-call | tf_op jit(solution)/shard_map/pallas_call | solution.py:95
  26.0 0.1 collective-permute-done.5.refs_0_
  26.1 1.0 %shard_map.54 = (f32[32,8192]{1,0:T(8,128)}, f32[32,8192]{1,0:T(8,128)}) custom-call(f32[32,1,128]{2,1,0:T(1,128)S(1)} %all_to_all.5.squares, f32[32,8192]{1,0:T(8,128)S(1)} %get-tuple-element.41.params, f32[32,8192]{1,0:T(8,128)S(1)} %get-tuple-element.42.momentum, ...), custom_call_target="tpu_custom_call", output_to_operand_aliasing={{0}: (4, {}), {1}: (5, {})} | custom-call | tf_op jit(solution)/shard_map/pallas_call | solution.py:95
Async XLA Ops:
  0.6 1.0 %copy-start.2 = (bf16[1,32,8192]{2,1,0:T(8,128)(2,1)S(1)}, bf16[1,32,8192]{2,1,0:T(8,128)(2,1)}, u32[]{:S(2)}) copy-start(bf16[1,32,8192]{2,1,0:T(8,128)(2,1)} %grad.1) | copy-start | bytes 1572868
  1.9 6.9 %collective-permute-start.1 = (bf16[32,2048]{1,0:T(8,128)(2,1)S(1)}, bf16[32,2048]{1,0:T(8,128)(2,1)S(1)}, u32[]{:S(2)}, u32[]{:S(2)}) collective-permute-start(bf16[32,2048]{1,0:T(8,128)(2,1)S(1)} %get-tuple-element.36), channel_id=1, source_target_pairs={{0,16},{8,24},{16,0},{24,8},{1,17},{9,25},{17,1},{25,9},{2,18},{10... | collective-permute-start | bytes 393224 | tf_op jit(solution)/shard_map/ppermute | solution.py:18
  4.9 5.9 %collective-permute-start.2 = (bf16[32,2048]{1,0:T(8,128)(2,1)S(1)}, bf16[32,2048]{1,0:T(8,128)(2,1)S(1)}, u32[]{:S(2)}, u32[]{:S(2)}) collective-permute-start(bf16[32,2048]{1,0:T(8,128)(2,1)S(1)} %get-tuple-element.37), channel_id=1, source_target_pairs={{0,24},{8,16},{16,8},{24,0},{1,25},{9,17},{17,9},{25,1},{2,26},{10... | collective-permute-start | bytes 393224 | tf_op jit(solution)/shard_map/ppermute | solution.py:18
  4.9 1.2 %copy-start = (f32[32,8192]{1,0:T(8,128)S(1)}, f32[32,8192]{1,0:T(8,128)}, u32[]{:S(2)}) copy-start(f32[32,8192]{1,0:T(8,128)} %refs_0_) | copy-start | bytes 3145732
  6.1 1.2 %copy-start.1 = (f32[32,8192]{1,0:T(8,128)S(1)}, f32[32,8192]{1,0:T(8,128)}, u32[]{:S(2)}) copy-start(f32[32,8192]{1,0:T(8,128)} %refs_1_) | copy-start | bytes 3145732
  7.5 3.2 %collective-permute-start = (bf16[32,2048]{1,0:T(8,128)(2,1)S(1)}, bf16[32,2048]{1,0:T(8,128)(2,1)S(1)}, u32[]{:S(2)}, u32[]{:S(2)}) collective-permute-start(bf16[32,2048]{1,0:T(8,128)(2,1)S(1)} %get-tuple-element.35), channel_id=1, source_target_pairs={{0,8},{8,0},{16,24},{24,16},{1,9},{9,1},{17,25},{25,17},{2,10},{10... | collective-permute-start | bytes 393224 | tf_op jit(solution)/shard_map/ppermute | solution.py:18
  10.9 13.7 %collective-permute-start.4 = (f32[32,2048]{1,0:T(8,128)S(1)}, f32[32,2048]{1,0:T(8,128)S(1)}, u32[]{:S(2)}, u32[]{:S(2)}) collective-permute-start(f32[32,2048]{1,0:T(8,128)S(1)} %get-tuple-element.44.refs_0_), channel_id=1, source_target_pairs={{0,16},{8,24},{16,0},{24,8},{1,17},{9,25},{17,1},{25,9},{2,18},{10... | collective-permute-start | bytes 786440 | tf_op jit(solution)/shard_map/ppermute | solution.py:18
  12.0 12.6 %collective-permute-start.3 = (f32[32,2048]{1,0:T(8,128)S(1)}, f32[32,2048]{1,0:T(8,128)S(1)}, u32[]{:S(2)}, u32[]{:S(2)}) collective-permute-start(f32[32,2048]{1,0:T(8,128)S(1)} %get-tuple-element.44.refs_0_), channel_id=1, source_target_pairs={{0,8},{8,0},{16,24},{24,16},{1,9},{9,1},{17,25},{25,17},{2,10},{10... | collective-permute-start | bytes 786440 | tf_op jit(solution)/shard_map/ppermute | solution.py:18
  24.5 1.5 %collective-permute-start.5 = (f32[32,2048]{1,0:T(8,128)S(1)}, f32[32,2048]{1,0:T(8,128)S(1)}, u32[]{:S(2)}, u32[]{:S(2)}) collective-permute-start(f32[32,2048]{1,0:T(8,128)S(1)} %collective-permute-done.4.refs_2_), channel_id=1, source_target_pairs={{0,8},{8,0},{16,24},{24,16},{1,9},{9,1},{17,25},{25,17},{2,10},{10... | collective-permute-start | bytes 786440 | tf_op jit(solution)/shard_map/ppermute | solution.py:18

commit v8 on v5

--- a/solution.py
+++ b/solution.py
@@ -11,6 +11,7 @@
 VMEM = pl.BlockSpec(memory_space=pltpu.VMEM)
 HBM = pl.BlockSpec(memory_space=pltpu.HBM)
 LIMIT = 16 * 1024 * 1024
+LINE = 2
 
 
 def swapped(value, axis, flip):
@@ -24,7 +25,7 @@
 
 def tree(parts):
     while len(parts) > 1:
-        parts = [parts[i] + parts[i + 1] for i in range(0, len(parts), 2)]
+        parts = [functools.reduce(jnp.add, parts[i : i + 2]) for i in range(0, len(parts), 2)]
     return parts[0]
 
 
@@ -53,8 +54,13 @@
     squares[...] = lanes
 
 
-def add_kernel(left, right, out):
-    out[...] = left[...] + right[...]
+def add_kernel(*refs):
+    refs[-1][...] = tree([ref[...] for ref in refs[:-1]])
+
+
+def pick_kernel(own, *refs):
+    first = lax.axis_index("fsdp") < LINE
+    refs[-1][...] = jnp.where(first, own[...], functools.reduce(jnp.add, [ref[...] for ref in refs[:-1]]))
 
 
 def fetch_kernel(*refs):
@@ -110,14 +116,24 @@
     )(near, far, params, momentum, *[averages[k] for k in flips])
 
 
-def add(left, right):
+def small(kernel, *args):
     return pl.pallas_call(
-        add_kernel,
-        out_shape=jax.ShapeDtypeStruct(left.shape, left.dtype),
-        in_specs=[VMEM] * 2,
+        kernel,
+        out_shape=jax.ShapeDtypeStruct(args[0].shape, args[0].dtype),
+        in_specs=[VMEM] * len(args),
         out_specs=VMEM,
         compiler_params=pltpu.CompilerParams(vmem_limit_bytes=LIMIT),
-    )(left, right)
+    )(*args)
+
+
+def line_sends(value, back):
+    size = lax.axis_size("fsdp")
+    moves = [[(f + m, f) for f in range(LINE)] for m in range(LINE, size, LINE)]
+    moves.reverse()
+    return [
+        lax.ppermute(value, "fsdp", [(b, a) if back else (a, b) for a, b in move])
+        for move in moves
+    ]
 
 
 def per_device(pseudo_grad, params, momentum):
@@ -159,21 +175,21 @@
         out_specs=[VMEM] * 2,
         compiler_params=limit,
     )(*[moved[k] for k in range(groups)])
-    averages = {0: average}
+    parts = line_sends(squares, False)
+    averages = {0: average, 1: swapped(average, "replica", 1)}
     for k in range(2, groups, 2):
         averages[k] = swapped(average, "replica", k)
-    near, far = squares, jnp.zeros_like(squares)
-    steps = [
-        (axis, 1 << i)
-        for axis in ("fsdp", "replica")
-        for i in range((lax.axis_size(axis) - 1).bit_length())
-    ]
+    parts = [squares] + parts
+    while len(parts) > 4:
+        parts = [small(add_kernel, *parts[:4])] + parts[4:]
+    total = small(add_kernel, *parts)
+    near = small(pick_kernel, total, *line_sends(total, True))
+    steps = [("fsdp", 1 << i) for i in range((LINE - 1).bit_length())]
+    steps += [("replica", 1 << i) for i in range((groups - 1).bit_length())]
+    far = None
     for i, (axis, flip) in enumerate(steps):
-        if i:
-            near = add(near, far)
-        if i == 1:
-            near, average = lax.optimization_barrier((near, average))
-            averages[1] = swapped(average, "replica", 1)
+        if far is not None:
+            near = small(add_kernel, near, far)
         if i == len(steps) - 1:
             near, averages = lax.optimization_barrier((near, averages))
         far = swapped(near, axis, flip)

time: 29.2 us -> 38 us (1.30)
  waiting for transfers between devices: 11.6 us -> 16.5 us
  starting transfers between devices: 11.2 us -> 14.9 us
    ppermute x0 -> x6, starting transfers between devices: none -> 7.72 us  [line_sends(): lax.ppermute(value, 'fsdp', [(b, a) if back else (a, b) for a, b in move])]
    ppermute x0 -> x6, waiting for transfers between devices: none -> 7.19 us  [line_sends(): lax.ppermute(value, 'fsdp', [(b, a) if back else (a, b) for a, b in move])]
    ppermute x11 -> x9, starting transfers between devices: 11.2 us -> 7.21 us  [swapped(): return lax.ppermute(value, axis, [(i, i ^ flip) for i in range(size)])]
    ppermute x11 -> x9, waiting for transfers between devices: 11.6 us -> 9.31 us  [swapped(): return lax.ppermute(value, axis, [(i, i ^ flip) for i in range(size)])]
  transfers between devices with their start and end apart: 11 -> 15, of which waited for: 7 -> 9; matrix products, arithmetic and copies ran while one was open for 0% -> 0% of each run, Pallas kernels for 1% -> 0%
where the time goes in v8:
time: 38 us; the launch traced here: 37.7 us
  waiting for transfers between devices  16.5 us (43%)
  starting transfers between devices  14.9 us (39%)
  local copies, waits for them, and re-layouts  3.48 us (9%)
  Pallas kernels  2 us (5%)
  between operations  0.74 us (2%)
    ppermute x9, waiting for transfers between devices, swapped(): return lax.ppermute(value, axis, [(i, i ^ flip) for i in range(size)])  9.31 us
    ppermute x6, starting transfers between devices, line_sends(): lax.ppermute(value, 'fsdp', [(b, a) if back else (a, b) for a, b in move])  7.72 us
    ppermute x9, starting transfers between devices, swapped(): return lax.ppermute(value, axis, [(i, i ^ flip) for i in range(size)])  7.21 us
    ppermute x6, waiting for transfers between devices, line_sends(): lax.ppermute(value, 'fsdp', [(b, a) if back else (a, b) for a, b in move])  7.19 us
    unnamed x6, local copies, waits for them, and re-layouts  3.48 us
    pallas_call x1, Pallas kernels, update(): pl.pallas_call(functools.partial(update_kernel, count, flips), out_shape=...  1.52 us
  transfers between devices with their start and end apart: 15, of which 9 were waited for; matrix products, arithmetic and copies ran while one was open for 0% of the time, Pallas kernels for 0%

profile of v8, /device:TPU:0, one launch (start us, length us, event | category | flops | bytes accessed | tf_op | source)
XLA Modules:
  0.0 37.7 jit_solution(16889891307407821259)
XLA Ops:
  0.6 0.0 copy-start.2
  0.6 1.0 %copy-done.2 = bf16[1,32,8192]{2,1,0:T(8,128)(2,1)S(1)} copy-done((bf16[1,32,8192]{2,1,0:T(8,128)(2,1)S(1)}, bf16[1,32,8192]{2,1,0:T(8,128)(2,1)}, u32[]{:S(2)}) %copy-start.2) | copy-done | bytes 524312
  1.7 0.2 shard_map.50
  1.9 3.0 %collective-permute-start.1 = (bf16[32,2048]{1,0:T(8,128)(2,1)S(1)}, bf16[32,2048]{1,0:T(8,128)(2,1)S(1)}, u32[]{:S(2)}, u32[]{:S(2)}) collective-permute-start(bf16[32,2048]{1,0:T(8,128)(2,1)S(1)} %get-tuple-element.34), channel_id=1, source_target_pairs={{0,16},{8,24},{16,0},{24,8},{1,17},{9,25},{17,1},{25,9},{2,18},{10... | collective-permute-start | bytes 393224 | tf_op jit(solution)/shard_map/ppermute | solution.py:19
  4.9 0.0 collective-permute-start.2
  4.9 0.0 copy-start
  4.9 1.2 %copy-done = f32[32,8192]{1,0:T(8,128)S(1)} copy-done((f32[32,8192]{1,0:T(8,128)S(1)}, f32[32,8192]{1,0:T(8,128)}, u32[]{:S(2)}) %copy-start) | copy-done | bytes 1048600
  6.1 0.0 copy-start.1
  6.1 1.2 %copy-done.1 = f32[32,8192]{1,0:T(8,128)S(1)} copy-done((f32[32,8192]{1,0:T(8,128)S(1)}, f32[32,8192]{1,0:T(8,128)}, u32[]{:S(2)}) %copy-start.1) | copy-done | bytes 1048600
  7.3 0.2 shard_map.51
  7.5 0.3 collective-permute-start
  7.8 1.1 %collective-permute-done.1.refs_2_ = bf16[32,2048]{1,0:T(8,128)(2,1)S(1)} collective-permute-done((bf16[32,2048]{1,0:T(8,128)(2,1)S(1)}, bf16[32,2048]{1,0:T(8,128)(2,1)S(1)}, u32[]{:S(2)}, u32[]{:S(2)}) %collective-permute-start.1) | collective-permute-done | bytes 131104 | tf_op jit(solution)/shard_map/ppermute | solution.py:19
  8.8 1.9 %collective-permute-done.2.refs_3_ = bf16[32,2048]{1,0:T(8,128)(2,1)S(1)} collective-permute-done((bf16[32,2048]{1,0:T(8,128)(2,1)S(1)}, bf16[32,2048]{1,0:T(8,128)(2,1)S(1)}, u32[]{:S(2)}, u32[]{:S(2)}) %collective-permute-start.2) | collective-permute-done | bytes 131104 | tf_op jit(solution)/shard_map/ppermute | solution.py:19
  10.7 0.0 collective-permute-done.refs_1_
  10.7 0.1 shard_map.52
  10.9 1.1 %collective-permute-start.12 = (f32[32,2048]{1,0:T(8,128)S(1)}, f32[32,2048]{1,0:T(8,128)S(1)}, u32[]{:S(2)}, u32[]{:S(2)}) collective-permute-start(f32[32,2048]{1,0:T(8,128)S(1)} %get-tuple-element.41.refs_0_), channel_id=1, source_target_pairs={{0,16},{8,24},{16,0},{24,8},{1,17},{9,25},{17,1},{25,9},{2,18},{10... | collective-permute-start | bytes 786440 | tf_op jit(solution)/shard_map/ppermute | solution.py:19
  12.0 0.7 %collective-permute-start.11 = (f32[32,2048]{1,0:T(8,128)S(1)}, f32[32,2048]{1,0:T(8,128)S(1)}, u32[]{:S(2)}, u32[]{:S(2)}) collective-permute-start(f32[32,2048]{1,0:T(8,128)S(1)} %get-tuple-element.41.refs_0_), channel_id=1, source_target_pairs={{0,8},{8,0},{16,24},{24,16},{1,9},{9,1},{17,25},{25,17},{2,10},{10... | collective-permute-start | bytes 786440 | tf_op jit(solution)/shard_map/ppermute | solution.py:19
  12.7 1.3 %collective-permute-start.5 = (f32[1,128]{1,0:T(1,128)S(1)}, f32[1,128]{1,0:T(1,128)S(1)}, u32[]{:S(2)}, u32[]{:S(2)}) collective-permute-start(f32[1,128]{1,0:T(1,128)S(1)} %get-tuple-element.36.refs_0_), channel_id=1, source_target_pairs={{2,0},{3,1},{10,8},{11,9},{18,16},{19,17},{26,24},{27,25}} | collective-permute-start | bytes 1544 | tf_op jit(solution)/shard_map/ppermute | solution.py:134
  13.9 1.3 %collective-permute-start.4 = (f32[1,128]{1,0:T(1,128)S(1)}, f32[1,128]{1,0:T(1,128)S(1)}, u32[]{:S(2)}, u32[]{:S(2)}) collective-permute-start(f32[1,128]{1,0:T(1,128)S(1)} %get-tuple-element.36.refs_0_), channel_id=1, source_target_pairs={{4,0},{5,1},{12,8},{13,9},{20,16},{21,17},{28,24},{29,25}} | collective-permute-start | bytes 1544 | tf_op jit(solution)/shard_map/ppermute | solution.py:134
  15.2 1.3 %collective-permute-start.3 = (f32[1,128]{1,0:T(1,128)S(1)}, f32[1,128]{1,0:T(1,128)S(1)}, u32[]{:S(2)}, u32[]{:S(2)}) collective-permute-start(f32[1,128]{1,0:T(1,128)S(1)} %get-tuple-element.36.refs_0_), channel_id=1, source_target_pairs={{6,0},{7,1},{14,8},{15,9},{22,16},{23,17},{30,24},{31,25}} | collective-permute-start | bytes 1544 | tf_op jit(solution)/shard_map/ppermute | solution.py:134
  16.5 1.5 %collective-permute-done.5.refs_3_ = f32[1,128]{1,0:T(1,128)S(1)} collective-permute-done((f32[1,128]{1,0:T(1,128)S(1)}, f32[1,128]{1,0:T(1,128)S(1)}, u32[]{:S(2)}, u32[]{:S(2)}) %collective-permute-start.5) | collective-permute-done | bytes 544 | tf_op jit(solution)/shard_map/ppermute | solution.py:134
  18.1 2.2 %collective-permute-done.4.refs_2_ = f32[1,128]{1,0:T(1,128)S(1)} collective-permute-done((f32[1,128]{1,0:T(1,128)S(1)}, f32[1,128]{1,0:T(1,128)S(1)}, u32[]{:S(2)}, u32[]{:S(2)}) %collective-permute-start.4) | collective-permute-done | bytes 544 | tf_op jit(solution)/shard_map/ppermute | solution.py:134
  20.3 2.2 %collective-permute-done.3.refs_1_ = f32[1,128]{1,0:T(1,128)S(1)} collective-permute-done((f32[1,128]{1,0:T(1,128)S(1)}, f32[1,128]{1,0:T(1,128)S(1)}, u32[]{:S(2)}, u32[]{:S(2)}) %collective-permute-start.3) | collective-permute-done | bytes 544 | tf_op jit(solution)/shard_map/ppermute | solution.py:134
  22.5 1.3 %collective-permute-start.8 = (f32[1,128]{1,0:T(1,128)S(1)}, f32[1,128]{1,0:T(1,128)S(1)}, u32[]{:S(2)}, u32[]{:S(2)}) collective-permute-start(f32[1,128]{1,0:T(1,128)S(1)} %shard_map.53.own), channel_id=1, source_target_pairs={{0,2},{1,3},{8,10},{9,11},{16,18},{17,19},{24,26},{25,27}} | collective-permute-start | bytes 1544 | tf_op jit(solution)/shard_map/ppermute | solution.py:134
  23.8 1.3 %collective-permute-start.7 = (f32[1,128]{1,0:T(1,128)S(1)}, f32[1,128]{1,0:T(1,128)S(1)}, u32[]{:S(2)}, u32[]{:S(2)}) collective-permute-start(f32[1,128]{1,0:T(1,128)S(1)} %shard_map.53.own), channel_id=1, source_target_pairs={{0,4},{1,5},{8,12},{9,13},{16,20},{17,21},{24,28},{25,29}} | collective-permute-start | bytes 1544 | tf_op jit(solution)/shard_map/ppermute | solution.py:134
  25.1 1.3 %collective-permute-start.6 = (f32[1,128]{1,0:T(1,128)S(1)}, f32[1,128]{1,0:T(1,128)S(1)}, u32[]{:S(2)}, u32[]{:S(2)}) collective-permute-start(f32[1,128]{1,0:T(1,128)S(1)} %shard_map.53.own), channel_id=1, source_target_pairs={{0,6},{1,7},{8,14},{9,15},{16,22},{17,23},{24,30},{25,31}} | collective-permute-start | bytes 1544 | tf_op jit(solution)/shard_map/ppermute | solution.py:134
  26.4 0.0 collective-permute-done.8.refs_2_
  26.4 0.0 collective-permute-done.7.refs_1_
  26.4 1.3 %collective-permute-done.6.refs_0_ = f32[1,128]{1,0:T(1,128)S(1)} collective-permute-done((f32[1,128]{1,0:T(1,128)S(1)}, f32[1,128]{1,0:T(1,128)S(1)}, u32[]{:S(2)}, u32[]{:S(2)}) %collective-permute-start.6) | collective-permute-done | bytes 544 | tf_op jit(solution)/shard_map/ppermute | solution.py:134
  27.6 1.5 %collective-permute-start.9 = (f32[1,128]{1,0:T(1,128)S(1)}, f32[1,128]{1,0:T(1,128)S(1)}, u32[]{:S(2)}, u32[]{:S(2)}) collective-permute-start(f32[1,128]{1,0:T(1,128)S(1)} %shard_map.54.refs_0_), channel_id=1, source_target_pairs={{0,1},{1,0},{2,3},{3,2},{4,5},{5,4},{6,7},{7,6},{8,9},{9,8},{10,11... | collective-permute-start | bytes 1544 | tf_op jit(solution)/shard_map/ppermute | solution.py:19
  29.2 2.0 %collective-permute-done.9.refs_1_ = f32[1,128]{1,0:T(1,128)S(1)} collective-permute-done((f32[1,128]{1,0:T(1,128)S(1)}, f32[1,128]{1,0:T(1,128)S(1)}, u32[]{:S(2)}, u32[]{:S(2)}) %collective-permute-start.9) | collective-permute-done | bytes 544 | tf_op jit(solution)/shard_map/ppermute | solution.py:19
  31.2 0.0 collective-permute-start.10
  31.2 1.1 %collective-permute-done.10.refs_1_ = f32[1,128]{1,0:T(1,128)S(1)} collective-permute-done((f32[1,128]{1,0:T(1,128)S(1)}, f32[1,128]{1,0:T(1,128)S(1)}, u32[]{:S(2)}, u32[]{:S(2)}) %collective-permute-start.10) | collective-permute-done | bytes 544 | tf_op jit(solution)/shard_map/ppermute | solution.py:19
  32.3 0.0 collective-permute-done.12.refs_2_
  32.3 0.0 collective-permute-done.11.refs_1_
  32.3 0.3 collective-permute-start.14
  32.6 0.4 collective-permute-start.13
  33.0 3.2 %collective-permute-done.13.far = f32[1,128]{1,0:T(1,128)S(1)} collective-permute-done((f32[1,128]{1,0:T(1,128)S(1)}, f32[1,128]{1,0:T(1,128)S(1)}, u32[]{:S(2)}, u32[]{:S(2)}) %collective-permute-start.13) | collective-permute-done | bytes 544 | tf_op jit(solution)/shard_map/ppermute | solution.py:19
  36.1 0.0 collective-permute-done.14.refs_3_
  36.1 1.5 %shard_map.57 = (f32[32,8192]{1,0:T(8,128)}, f32[32,8192]{1,0:T(8,128)}) custom-call(f32[1,128]{1,0:T(1,128)S(1)} %shard_map.56.near, f32[1,128]{1,0:T(1,128)S(1)} %collective-permute-done.13.far, f32[32,8192]{1,0:T(8,128)S(1)} %get-tuple-element.39.params, f32[32,8192]{1,0:T(8,128)S(1)} %get-tuple-element.40.momentum, ...), custom_call_target="tpu_custom_call" | custom-call | tf_op jit(solution)/shard_map/pallas_call | solution.py:105
  (4 shorter events, 0.0 us)
Async XLA Ops:
  0.6 1.0 %copy-start.2 = (bf16[1,32,8192]{2,1,0:T(8,128)(2,1)S(1)}, bf16[1,32,8192]{2,1,0:T(8,128)(2,1)}, u32[]{:S(2)}) copy-start(bf16[1,32,8192]{2,1,0:T(8,128)(2,1)} %grad.1) | copy-start | bytes 1572868
  1.9 6.9 %collective-permute-start.1 = (bf16[32,2048]{1,0:T(8,128)(2,1)S(1)}, bf16[32,2048]{1,0:T(8,128)(2,1)S(1)}, u32[]{:S(2)}, u32[]{:S(2)}) collective-permute-start(bf16[32,2048]{1,0:T(8,128)(2,1)S(1)} %get-tuple-element.34), channel_id=1, source_target_pairs={{0,16},{8,24},{16,0},{24,8},{1,17},{9,25},{17,1},{25,9},{2,18},{10... | collective-permute-start | bytes 393224 | tf_op jit(solution)/shard_map/ppermute | solution.py:19
  4.9 5.9 %collective-permute-start.2 = (bf16[32,2048]{1,0:T(8,128)(2,1)S(1)}, bf16[32,2048]{1,0:T(8,128)(2,1)S(1)}, u32[]{:S(2)}, u32[]{:S(2)}) collective-permute-start(bf16[32,2048]{1,0:T(8,128)(2,1)S(1)} %get-tuple-element.35), channel_id=1, source_target_pairs={{0,24},{8,16},{16,8},{24,0},{1,25},{9,17},{17,9},{25,1},{2,26},{10... | collective-permute-start | bytes 393224 | tf_op jit(solution)/shard_map/ppermute | solution.py:19
  4.9 1.2 %copy-start = (f32[32,8192]{1,0:T(8,128)S(1)}, f32[32,8192]{1,0:T(8,128)}, u32[]{:S(2)}) copy-start(f32[32,8192]{1,0:T(8,128)} %refs_0_) | copy-start | bytes 3145732
  6.1 1.2 %copy-start.1 = (f32[32,8192]{1,0:T(8,128)S(1)}, f32[32,8192]{1,0:T(8,128)}, u32[]{:S(2)}) copy-start(f32[32,8192]{1,0:T(8,128)} %refs_1_) | copy-start | bytes 3145732
  7.5 3.2 %collective-permute-start = (bf16[32,2048]{1,0:T(8,128)(2,1)S(1)}, bf16[32,2048]{1,0:T(8,128)(2,1)S(1)}, u32[]{:S(2)}, u32[]{:S(2)}) collective-permute-start(bf16[32,2048]{1,0:T(8,128)(2,1)S(1)} %get-tuple-element.33), channel_id=1, source_target_pairs={{0,8},{8,0},{16,24},{24,16},{1,9},{9,1},{17,25},{25,17},{2,10},{10... | collective-permute-start | bytes 393224 | tf_op jit(solution)/shard_map/ppermute | solution.py:19
  10.9 21.5 %collective-permute-start.12 = (f32[32,2048]{1,0:T(8,128)S(1)}, f32[32,2048]{1,0:T(8,128)S(1)}, u32[]{:S(2)}, u32[]{:S(2)}) collective-permute-start(f32[32,2048]{1,0:T(8,128)S(1)} %get-tuple-element.41.refs_0_), channel_id=1, source_target_pairs={{0,16},{8,24},{16,0},{24,8},{1,17},{9,25},{17,1},{25,9},{2,18},{10... | collective-permute-start | bytes 786440 | tf_op jit(solution)/shard_map/ppermute | solution.py:19
  12.0 20.4 %collective-permute-start.11 = (f32[32,2048]{1,0:T(8,128)S(1)}, f32[32,2048]{1,0:T(8,128)S(1)}, u32[]{:S(2)}, u32[]{:S(2)}) collective-permute-start(f32[32,2048]{1,0:T(8,128)S(1)} %get-tuple-element.41.refs_0_), channel_id=1, source_target_pairs={{0,8},{8,0},{16,24},{24,16},{1,9},{9,1},{17,25},{25,17},{2,10},{10... | collective-permute-start | bytes 786440 | tf_op jit(solution)/shard_map/ppermute | solution.py:19
  12.7 5.4 %collective-permute-start.5 = (f32[1,128]{1,0:T(1,128)S(1)}, f32[1,128]{1,0:T(1,128)S(1)}, u32[]{:S(2)}, u32[]{:S(2)}) collective-permute-start(f32[1,128]{1,0:T(1,128)S(1)} %get-tuple-element.36.refs_0_), channel_id=1, source_target_pairs={{2,0},{3,1},{10,8},{11,9},{18,16},{19,17},{26,24},{27,25}} | collective-permute-start | bytes 1544 | tf_op jit(solution)/shard_map/ppermute | solution.py:134
  13.9 6.3 %collective-permute-start.4 = (f32[1,128]{1,0:T(1,128)S(1)}, f32[1,128]{1,0:T(1,128)S(1)}, u32[]{:S(2)}, u32[]{:S(2)}) collective-permute-start(f32[1,128]{1,0:T(1,128)S(1)} %get-tuple-element.36.refs_0_), channel_id=1, source_target_pairs={{4,0},{5,1},{12,8},{13,9},{20,16},{21,17},{28,24},{29,25}} | collective-permute-start | bytes 1544 | tf_op jit(solution)/shard_map/ppermute | solution.py:134
  15.2 7.2 %collective-permute-start.3 = (f32[1,128]{1,0:T(1,128)S(1)}, f32[1,128]{1,0:T(1,128)S(1)}, u32[]{:S(2)}, u32[]{:S(2)}) collective-permute-start(f32[1,128]{1,0:T(1,128)S(1)} %get-tuple-element.36.refs_0_), channel_id=1, source_target_pairs={{6,0},{7,1},{14,8},{15,9},{22,16},{23,17},{30,24},{31,25}} | collective-permute-start | bytes 1544 | tf_op jit(solution)/shard_map/ppermute | solution.py:134
  22.5 3.9 %collective-permute-start.8 = (f32[1,128]{1,0:T(1,128)S(1)}, f32[1,128]{1,0:T(1,128)S(1)}, u32[]{:S(2)}, u32[]{:S(2)}) collective-permute-start(f32[1,128]{1,0:T(1,128)S(1)} %shard_map.53.own), channel_id=1, source_target_pairs={{0,2},{1,3},{8,10},{9,11},{16,18},{17,19},{24,26},{25,27}} | collective-permute-start | bytes 1544 | tf_op jit(solution)/shard_map/ppermute | solution.py:134
  23.8 2.6 %collective-permute-start.7 = (f32[1,128]{1,0:T(1,128)S(1)}, f32[1,128]{1,0:T(1,128)S(1)}, u32[]{:S(2)}, u32[]{:S(2)}) collective-permute-start(f32[1,128]{1,0:T(1,128)S(1)} %shard_map.53.own), channel_id=1, source_target_pairs={{0,4},{1,5},{8,12},{9,13},{16,20},{17,21},{24,28},{25,29}} | collective-permute-start | bytes 1544 | tf_op jit(solution)/shard_map/ppermute | solution.py:134
  25.1 2.6 %collective-permute-start.6 = (f32[1,128]{1,0:T(1,128)S(1)}, f32[1,128]{1,0:T(1,128)S(1)}, u32[]{:S(2)}, u32[]{:S(2)}) collective-permute-start(f32[1,128]{1,0:T(1,128)S(1)} %shard_map.53.own), channel_id=1, source_target_pairs={{0,6},{1,7},{8,14},{9,15},{16,22},{17,23},{24,30},{25,31}} | collective-permute-start | bytes 1544 | tf_op jit(solution)/shard_map/ppermute | solution.py:134
  27.6 3.5 %collective-permute-start.9 = (f32[1,128]{1,0:T(1,128)S(1)}, f32[1,128]{1,0:T(1,128)S(1)}, u32[]{:S(2)}, u32[]{:S(2)}) collective-permute-start(f32[1,128]{1,0:T(1,128)S(1)} %shard_map.54.refs_0_), channel_id=1, source_target_pairs={{0,1},{1,0},{2,3},{3,2},{4,5},{5,4},{6,7},{7,6},{8,9},{9,8},{10,11... | collective-permute-start | bytes 1544 | tf_op jit(solution)/shard_map/ppermute | solution.py:19
  31.2 1.1 %collective-permute-start.10 = (f32[1,128]{1,0:T(1,128)S(1)}, f32[1,128]{1,0:T(1,128)S(1)}, u32[]{:S(2)}, u32[]{:S(2)}) collective-permute-start(f32[1,128]{1,0:T(1,128)S(1)} %shard_map.55.refs_0_), channel_id=1, source_target_pairs={{0,8},{8,0},{16,24},{24,16},{1,9},{9,1},{17,25},{25,17},{2,10},{10... | collective-permute-start | bytes 1544 | tf_op jit(solution)/shard_map/ppermute | solution.py:19
  32.3 3.8 %collective-permute-start.14 = (f32[32,2048]{1,0:T(8,128)S(1)}, f32[32,2048]{1,0:T(8,128)S(1)}, u32[]{:S(2)}, u32[]{:S(2)}) collective-permute-start(f32[32,2048]{1,0:T(8,128)S(1)} %collective-permute-done.12.refs_2_), channel_id=1, source_target_pairs={{0,8},{8,0},{16,24},{24,16},{1,9},{9,1},{17,25},{25,17},{2,10},{10... | collective-permute-start | bytes 786440 | tf_op jit(solution)/shard_map/ppermute | solution.py:19
  32.6 3.5 %collective-permute-start.13 = (f32[1,128]{1,0:T(1,128)S(1)}, f32[1,128]{1,0:T(1,128)S(1)}, u32[]{:S(2)}, u32[]{:S(2)}) collective-permute-start(f32[1,128]{1,0:T(1,128)S(1)} %shard_map.56.near), channel_id=1, source_target_pairs={{0,16},{8,24},{16,0},{24,8},{1,17},{9,25},{17,1},{25,9},{2,18},{10... | collective-permute-start | bytes 1544 | tf_op jit(solution)/shard_map/ppermute | solution.py:19

commit v9 on v6

--- a/solution.py
+++ b/solution.py
@@ -60,8 +60,9 @@
     squares[...] = jnp.broadcast_to(lanes[None], squares.shape)
 
 
-def join_kernel(groups, here, there, average):
-    average[...] = (here[...] + there[...]) / WIDE(groups)
+def join_kernel(groups, here, there, there_mate, average):
+    pair = there[...].astype(WIDE) + there_mate[...].astype(WIDE)
+    average[...] = (here[...] + pair) / WIDE(groups)
 
 
 def fetch_kernel(*refs):
@@ -143,30 +144,28 @@
         cut_kernel, [piece] * groups, pseudo_grad,
         scratch=[pltpu.SemaphoreType.DMA((groups,))],
     )
-    direct = {k: swapped(pieces[k], "replica", k) for k in others}
-    near = {k: swapped(pieces[k + 1], "replica", 1) for k in others}
-    near, last = lax.optimization_barrier((near, pieces[1]))
-    relayed = {k: swapped(near[k], "replica", k) for k in others}
-    direct, momentum = lax.optimization_barrier((direct, momentum))
-    mate = swapped(last, "replica", 1)
+    direct = {k: swapped(pieces[k], "replica", k) for k in range(2, groups)}
     (momentum,) = call(
         fetch_kernel, [jax.ShapeDtypeStruct(params.shape, WIDE)], momentum,
         scratch=[pltpu.SemaphoreType.DMA((1,))],
     )
+    (zero, one, three), momentum = lax.optimization_barrier(
+        ((pieces[0], pieces[1], pieces[3 % groups]), momentum)
+    )
+    mate = swapped(one, "replica", 1)
+    mates_other = swapped(three, "replica", 1) if groups == 4 else mate
     own_sum, other_sum = call(
-        pair_kernel, [wide_piece] * 2,
-        pieces[0], mate, pieces[2 % groups], near.get(2, mate),
+        pair_kernel, [wide_piece] * 2, pieces[0], mate, pieces[2 % groups], mates_other
     )
     averages = {}
     if groups == 4:
-        own_sum, momentum = lax.optimization_barrier((own_sum, momentum))
-        across = swapped(own_sum, "replica", 2)
+        zero, mate, direct[2] = lax.optimization_barrier((zero, mate, direct[2]))
+        across = [swapped(x, "replica", 2) for x in (zero, mate)]
     averages[0], squares = call(
         functools.partial(average_kernel, groups),
         [wide_piece, jax.ShapeDtypeStruct((devices, 1, 128), WIDE)],
-        own_sum, *[x[k] for k in others for x in (direct, relayed)],
-    )
-    averages[1] = swapped(averages[0], "replica", 1)
+        own_sum, *[direct[k] for k in range(2, groups)],
+    )
     if groups != 4:
         averages.update({k: swapped(averages[0], "replica", k) for k in others})
     squares = lax.all_to_all(
@@ -175,13 +174,13 @@
     if groups == 4:
         squares, across = lax.optimization_barrier((squares, across))
         averages[2] = call(
-            functools.partial(join_kernel, groups), wide_piece, other_sum, across
+            functools.partial(join_kernel, groups), wide_piece, other_sum, *across
         )
     squares, averages = lax.optimization_barrier((squares, averages))
-    for k in others:
+    here = range(0, groups, 2)
+    late = range(1, groups, 2)
+    for k in here:
         averages[k + 1] = swapped(averages[k], "replica", 1)
-    here = [k for k in range(groups) if k < 2 or k % 2 == 0]
-    late = [k for k in range(groups) if k not in here]
     outs = update(count, here, [averages[k] for k in here], squares, params, momentum)
     if late:
         outs = update(

time: 28.1 us -> 27.7 us (0.986)
  waiting for transfers between devices: 3.02 us -> 3.58 us
  blocking collectives: 12.3 us -> 11.8 us
  starting transfers between devices: 6.67 us -> 6.2 us
    ppermute x7 -> x8, waiting for transfers between devices: 3.02 us -> 3.58 us  [swapped(): return lax.ppermute(value, axis, [(i, i ^ flip) for i in range(size)])]
    ppermute x7 -> x8, starting transfers between devices: 6.67 us -> 6.2 us  [swapped(): return lax.ppermute(value, axis, [(i, i ^ flip) for i in range(size)])]
    all_to_all x1, blocking collectives: 12.3 us -> 11.8 us  [per_device(): lax.all_to_all(squares, ('replica', 'fsdp'), split_axis=0, concat_axis=0,...]
  transfers between devices with their start and end apart: 7 -> 8, of which waited for: 2 -> 3; matrix products, arithmetic and copies ran while one was open for 0% -> 0% of each run, Pallas kernels for 6% -> 5%
where the time goes in v9:
time: 27.7 us; the launch traced here: 27.5 us
  blocking collectives  11.8 us (43%)
  starting transfers between devices  6.2 us (22%)
  waiting for transfers between devices  3.58 us (13%)
  Pallas kernels  2.91 us (11%)
  local copies, waits for them, and re-layouts  2.27 us (8%)
  between operations  0.71 us (3%)
    all_to_all x1, blocking collectives, per_device(): lax.all_to_all(squares, ('replica', 'fsdp'), split_axis=0, concat_axis=0,...  11.8 us
    ppermute x8, starting transfers between devices, swapped(): return lax.ppermute(value, axis, [(i, i ^ flip) for i in range(size)])  6.2 us
    ppermute x8, waiting for transfers between devices, swapped(): return lax.ppermute(value, axis, [(i, i ^ flip) for i in range(size)])  3.58 us
    pallas_call x2, Pallas kernels, update(): pl.pallas_call(functools.partial(update_kernel, count, flips, len(earlier...  2.44 us
    unnamed x6, local copies, waits for them, and re-layouts  2.27 us
  transfers between devices with their start and end apart: 8, of which 3 were waited for; matrix products, arithmetic and copies ran while one was open for 0% of the time, Pallas kernels for 5%

profile of v9, /device:TPU:0, one launch (start us, length us, event | category | flops | bytes accessed | tf_op | source)
XLA Modules:
  0.0 27.5 jit_solution(4540037523695812871)
XLA Ops:
  0.6 0.0 copy-start.2
  0.6 1.0 %copy-done.2 = bf16[1,32,8192]{2,1,0:T(8,128)(2,1)S(1)} copy-done((bf16[1,32,8192]{2,1,0:T(8,128)(2,1)S(1)}, bf16[1,32,8192]{2,1,0:T(8,128)(2,1)}, u32[]{:S(2)}) %copy-start.2) | copy-done | bytes 524312
  1.7 0.2 shard_map.50
  1.9 3.0 %collective-permute-start.2 = (bf16[32,2048]{1,0:T(8,128)(2,1)S(1)}, bf16[32,2048]{1,0:T(8,128)(2,1)S(1)}, u32[]{:S(2)}, u32[]{:S(2)}) collective-permute-start(bf16[32,2048]{1,0:T(8,128)(2,1)S(1)} %get-tuple-element.29.other), channel_id=1, source_target_pairs={{0,16},{8,24},{16,0},{24,8},{1,17},{9,25},{17,1},{25,9},{2,18},{10... | collective-permute-start | bytes 393224 | tf_op jit(solution)/shard_map/ppermute | solution.py:18
  4.9 0.0 copy-start.1
  4.9 1.2 %copy-done.1 = f32[32,8192]{1,0:T(8,128)S(1)} copy-done((f32[32,8192]{1,0:T(8,128)S(1)}, f32[32,8192]{1,0:T(8,128)}, u32[]{:S(2)}) %copy-start.1) | copy-done | bytes 1048600
  6.1 0.1 shard_map.51.momentum
  6.2 0.0 copy-start
  6.2 0.1 collective-permute-start
  6.3 0.5 %collective-permute-start.1 = (bf16[32,2048]{1,0:T(8,128)(2,1)S(1)}, bf16[32,2048]{1,0:T(8,128)(2,1)S(1)}, u32[]{:S(2)}, u32[]{:S(2)}) collective-permute-start(bf16[32,2048]{1,0:T(8,128)(2,1)S(1)} %get-tuple-element.30), channel_id=1, source_target_pairs={{0,8},{8,0},{16,24},{24,16},{1,9},{9,1},{17,25},{25,17},{2,10},{10... | collective-permute-start | bytes 393224 | tf_op jit(solution)/shard_map/ppermute | solution.py:18
  6.8 0.0 collective-permute-start.3
  6.8 1.6 %collective-permute-done.2.refs_1_ = bf16[32,2048]{1,0:T(8,128)(2,1)S(1)} collective-permute-done((bf16[32,2048]{1,0:T(8,128)(2,1)S(1)}, bf16[32,2048]{1,0:T(8,128)(2,1)S(1)}, u32[]{:S(2)}, u32[]{:S(2)}) %collective-permute-start.2) | collective-permute-done | bytes 131104 | tf_op jit(solution)/shard_map/ppermute | solution.py:18
  8.4 0.0 collective-permute-done.own_mate
  8.4 2.0 %collective-permute-start.4 = (bf16[32,2048]{1,0:T(8,128)(2,1)S(1)}, bf16[32,2048]{1,0:T(8,128)(2,1)S(1)}, u32[]{:S(2)}, u32[]{:S(2)}) collective-permute-start(bf16[32,2048]{1,0:T(8,128)(2,1)S(1)} %get-tuple-element.35.own), channel_id=1, source_target_pairs={{0,16},{8,24},{16,0},{24,8},{1,17},{9,25},{17,1},{25,9},{2,18},{10... | collective-permute-start | bytes 393224 | tf_op jit(solution)/shard_map/ppermute | solution.py:18
  10.4 0.0 collective-permute-start.5
  10.4 0.0 collective-permute-done.1.other_mate
  10.4 0.1 shard_map.52
  10.5 1.8 %collective-permute-done.3.refs_2_ = bf16[32,2048]{1,0:T(8,128)(2,1)S(1)} collective-permute-done((bf16[32,2048]{1,0:T(8,128)(2,1)S(1)}, bf16[32,2048]{1,0:T(8,128)(2,1)S(1)}, u32[]{:S(2)}, u32[]{:S(2)}) %collective-permute-start.3) | collective-permute-done | bytes 131104 | tf_op jit(solution)/shard_map/ppermute | solution.py:18
  12.3 0.1 shard_map.53
  12.4 11.8 %all_to_all.5.squares = f32[32,1,128]{2,1,0:T(1,128)S(1)} all-to-all(f32[32,1,128]{2,1,0:T(1,128)S(1)} %get-tuple-element.34), channel_id=1, replica_groups=mesh['replica'=4,'fsdp'=8] {'replica','fsdp'}, dimensions={0} | all-to-all | bytes 32768 | tf_op jit(solution)/shard_map/all_to_all | solution.py:171
  24.3 0.0 collective-permute-done.4.there
  24.3 0.0 collective-permute-done.5.there_mate
  24.3 0.1 collective-permute-start.6
  24.4 0.5 %collective-permute-start.7 = (f32[32,2048]{1,0:T(8,128)S(1)}, f32[32,2048]{1,0:T(8,128)S(1)}, u32[]{:S(2)}, u32[]{:S(2)}) collective-permute-start(f32[32,2048]{1,0:T(8,128)S(1)} %shard_map.54.refs_1_), channel_id=1, source_target_pairs={{0,8},{8,0},{16,24},{24,16},{1,9},{9,1},{17,25},{25,17},{2,10},{10... | collective-permute-start | bytes 786440 | tf_op jit(solution)/shard_map/ppermute | solution.py:18
  24.9 0.0 copy-done
  24.9 1.2 %shard_map.55 = (f32[32,8192]{1,0:T(8,128)}, f32[32,8192]{1,0:T(8,128)}) custom-call(f32[32,1,128]{2,1,0:T(1,128)S(1)} %all_to_all.5.squares, f32[32,8192]{1,0:T(8,128)S(1)} %copy-done, f32[32,8192]{1,0:T(8,128)S(1)} %shard_map.51.momentum, f32[32,2048]{1,0:T(8,128)S(1)} %get-tuple-element.44.refs_0_, f32[32,2048]{1,0:T(8,128)S(1)} %shard_map.54.refs_1_), custom_call_target="tpu_custom_call" | custom-call | tf_op jit(solution)/shard_map/pallas_call | solution.py:107
  26.1 0.0 collective-permute-done.6.refs_0_
  26.1 0.2 collective-permute-done.7.refs_1_
  26.3 1.2 %shard_map.56 = (f32[32,8192]{1,0:T(8,128)}, f32[32,8192]{1,0:T(8,128)}) custom-call(f32[32,1,128]{2,1,0:T(1,128)S(1)} %all_to_all.5.squares, f32[32,8192]{1,0:T(8,128)S(1)} %copy-done, f32[32,8192]{1,0:T(8,128)S(1)} %shard_map.51.momentum, f32[32,2048]{1,0:T(8,128)S(1)} %collective-permute-done.6.refs_0_, ...), custom_call_target="tpu_custom_call", output_to_operand_aliasing={{0}: (5, {}), {1}: (6, {})} | custom-call | tf_op jit(solution)/shard_map/pallas_call | solution.py:107
  (1 shorter events, 0.0 us)
Async XLA Ops:
  0.6 1.0 %copy-start.2 = (bf16[1,32,8192]{2,1,0:T(8,128)(2,1)S(1)}, bf16[1,32,8192]{2,1,0:T(8,128)(2,1)}, u32[]{:S(2)}) copy-start(bf16[1,32,8192]{2,1,0:T(8,128)(2,1)} %grad.1) | copy-start | bytes 1572868
  1.9 6.5 %collective-permute-start.2 = (bf16[32,2048]{1,0:T(8,128)(2,1)S(1)}, bf16[32,2048]{1,0:T(8,128)(2,1)S(1)}, u32[]{:S(2)}, u32[]{:S(2)}) collective-permute-start(bf16[32,2048]{1,0:T(8,128)(2,1)S(1)} %get-tuple-element.29.other), channel_id=1, source_target_pairs={{0,16},{8,24},{16,0},{24,8},{1,17},{9,25},{17,1},{25,9},{2,18},{10... | collective-permute-start | bytes 393224 | tf_op jit(solution)/shard_map/ppermute | solution.py:18
  4.9 1.2 %copy-start.1 = (f32[32,8192]{1,0:T(8,128)S(1)}, f32[32,8192]{1,0:T(8,128)}, u32[]{:S(2)}) copy-start(f32[32,8192]{1,0:T(8,128)} %refs_0_.1) | copy-start | bytes 3145732
  6.2 18.7 %copy-start = (f32[32,8192]{1,0:T(8,128)S(1)}, f32[32,8192]{1,0:T(8,128)}, u32[]{:S(2)}) copy-start(f32[32,8192]{1,0:T(8,128)} %params.3) | copy-start | bytes 3145732
  6.2 2.2 %collective-permute-start = (bf16[32,2048]{1,0:T(8,128)(2,1)S(1)}, bf16[32,2048]{1,0:T(8,128)(2,1)S(1)}, u32[]{:S(2)}, u32[]{:S(2)}) collective-permute-start(bf16[32,2048]{1,0:T(8,128)(2,1)S(1)} %get-tuple-element.28), channel_id=1, source_target_pairs={{0,8},{8,0},{16,24},{24,16},{1,9},{9,1},{17,25},{25,17},{2,10},{10... | collective-permute-start | bytes 393224 | tf_op jit(solution)/shard_map/ppermute | solution.py:18
  6.3 4.2 %collective-permute-start.1 = (bf16[32,2048]{1,0:T(8,128)(2,1)S(1)}, bf16[32,2048]{1,0:T(8,128)(2,1)S(1)}, u32[]{:S(2)}, u32[]{:S(2)}) collective-permute-start(bf16[32,2048]{1,0:T(8,128)(2,1)S(1)} %get-tuple-element.30), channel_id=1, source_target_pairs={{0,8},{8,0},{16,24},{24,16},{1,9},{9,1},{17,25},{25,17},{2,10},{10... | collective-permute-start | bytes 393224 | tf_op jit(solution)/shard_map/ppermute | solution.py:18
  6.8 5.5 %collective-permute-start.3 = (bf16[32,2048]{1,0:T(8,128)(2,1)S(1)}, bf16[32,2048]{1,0:T(8,128)(2,1)S(1)}, u32[]{:S(2)}, u32[]{:S(2)}) collective-permute-start(bf16[32,2048]{1,0:T(8,128)(2,1)S(1)} %get-tuple-element.30), channel_id=1, source_target_pairs={{0,24},{8,16},{16,8},{24,0},{1,25},{9,17},{17,9},{25,1},{2,26},{10... | collective-permute-start | bytes 393224 | tf_op jit(solution)/shard_map/ppermute | solution.py:18
  8.4 15.9 %collective-permute-start.4 = (bf16[32,2048]{1,0:T(8,128)(2,1)S(1)}, bf16[32,2048]{1,0:T(8,128)(2,1)S(1)}, u32[]{:S(2)}, u32[]{:S(2)}) collective-permute-start(bf16[32,2048]{1,0:T(8,128)(2,1)S(1)} %get-tuple-element.35.own), channel_id=1, source_target_pairs={{0,16},{8,24},{16,0},{24,8},{1,17},{9,25},{17,1},{25,9},{2,18},{10... | collective-permute-start | bytes 393224 | tf_op jit(solution)/shard_map/ppermute | solution.py:18
  10.4 13.9 %collective-permute-start.5 = (bf16[32,2048]{1,0:T(8,128)(2,1)S(1)}, bf16[32,2048]{1,0:T(8,128)(2,1)S(1)}, u32[]{:S(2)}, u32[]{:S(2)}) collective-permute-start(bf16[32,2048]{1,0:T(8,128)(2,1)S(1)} %collective-permute-done.own_mate), channel_id=1, source_target_pairs={{0,16},{8,24},{16,0},{24,8},{1,17},{9,25},{17,1},{25,9},{2,18},{10... | collective-permute-start | bytes 393224 | tf_op jit(solution)/shard_map/ppermute | solution.py:18
  24.3 1.8 %collective-permute-start.6 = (f32[32,2048]{1,0:T(8,128)S(1)}, f32[32,2048]{1,0:T(8,128)S(1)}, u32[]{:S(2)}, u32[]{:S(2)}) collective-permute-start(f32[32,2048]{1,0:T(8,128)S(1)} %get-tuple-element.44.refs_0_), channel_id=1, source_target_pairs={{0,8},{8,0},{16,24},{24,16},{1,9},{9,1},{17,25},{25,17},{2,10},{10... | collective-permute-start | bytes 786440 | tf_op jit(solution)/shard_map/ppermute | solution.py:18
  24.4 1.9 %collective-permute-start.7 = (f32[32,2048]{1,0:T(8,128)S(1)}, f32[32,2048]{1,0:T(8,128)S(1)}, u32[]{:S(2)}, u32[]{:S(2)}) collective-permute-start(f32[32,2048]{1,0:T(8,128)S(1)} %shard_map.54.refs_1_), channel_id=1, source_target_pairs={{0,8},{8,0},{16,24},{24,16},{1,9},{9,1},{17,25},{25,17},{2,10},{10... | collective-permute-start | bytes 786440 | tf_op jit(solution)/shard_map/ppermute | solution.py:18

commit v10 on v7

--- a/solution.py
+++ b/solution.py
@@ -151,8 +151,15 @@
     for k in range(2, groups, 2):
         averages[k] = swapped(average, "replica", k)
     averages[1] = swapped(average, "replica", 1)
+    middle = lax.axis_size("fsdp") // 2 + 1
+    members = sorted(range(devices), key=lambda i: i != middle)
     squares = lax.all_to_all(
-        squares, ("fsdp", "replica"), split_axis=0, concat_axis=0, tiled=True
+        squares,
+        ("replica", "fsdp"),
+        split_axis=0,
+        concat_axis=0,
+        axis_index_groups=[members],
+        tiled=True,
     )
     squares, averages = lax.optimization_barrier((squares, averages))
     for k in range(2, groups, 2):

time: 27.4 us -> 27.4 us (level)
  no operation moved by 1% of the time
where the time goes in v10:
time: 27.4 us; the launch traced here: 27.1 us
  blocking collectives  11.9 us (43%)
  starting transfers between devices  5.06 us (18%)
  local copies, waits for them, and re-layouts  3.48 us (13%)
  waiting for transfers between devices  3.09 us (11%)
  Pallas kernels  2.91 us (11%)
  between operations  0.68 us (2%)
    all_to_all x1, blocking collectives, per_device(): lax.all_to_all(squares, ('replica', 'fsdp'), split_axis=0, concat_axis=0,...  11.9 us
    ppermute x6, starting transfers between devices, swapped(): return lax.ppermute(value, axis, [(i, i ^ flip) for i in range(size)])  5.06 us
    unnamed x6, local copies, waits for them, and re-layouts  3.48 us
    ppermute x6, waiting for transfers between devices, swapped(): return lax.ppermute(value, axis, [(i, i ^ flip) for i in range(size)])  3.09 us
    pallas_call x2, Pallas kernels, update(): pl.pallas_call(functools.partial(update_kernel, count, flips, len(earlier...  2.43 us
  transfers between devices with their start and end apart: 6, of which 3 were waited for; matrix products, arithmetic and copies ran while one was open for 0% of the time, Pallas kernels for 6%

profile of v10, /device:TPU:0, one launch (start us, length us, event | category | flops | bytes accessed | tf_op | source)
XLA Modules:
  0.0 27.1 jit_solution(4522539587750259373)
XLA Ops:
  0.6 0.0 copy-start.2
  0.6 1.0 %copy-done.2 = bf16[1,32,8192]{2,1,0:T(8,128)(2,1)S(1)} copy-done((bf16[1,32,8192]{2,1,0:T(8,128)(2,1)S(1)}, bf16[1,32,8192]{2,1,0:T(8,128)(2,1)}, u32[]{:S(2)}) %copy-start.2) | copy-done | bytes 524312
  1.7 0.2 shard_map.50
  1.9 3.0 %collective-permute-start.1 = (bf16[32,2048]{1,0:T(8,128)(2,1)S(1)}, bf16[32,2048]{1,0:T(8,128)(2,1)S(1)}, u32[]{:S(2)}, u32[]{:S(2)}) collective-permute-start(bf16[32,2048]{1,0:T(8,128)(2,1)S(1)} %get-tuple-element.36), channel_id=1, source_target_pairs={{0,16},{8,24},{16,0},{24,8},{1,17},{9,25},{17,1},{25,9},{2,18},{10... | collective-permute-start | bytes 393224 | tf_op jit(solution)/shard_map/ppermute | solution.py:18
  4.9 0.0 collective-permute-start.2
  4.9 0.0 copy-start
  4.9 1.2 %copy-done = f32[32,8192]{1,0:T(8,128)S(1)} copy-done((f32[32,8192]{1,0:T(8,128)S(1)}, f32[32,8192]{1,0:T(8,128)}, u32[]{:S(2)}) %copy-start) | copy-done | bytes 1048600
  6.1 0.0 copy-start.1
  6.1 1.2 %copy-done.1 = f32[32,8192]{1,0:T(8,128)S(1)} copy-done((f32[32,8192]{1,0:T(8,128)S(1)}, f32[32,8192]{1,0:T(8,128)}, u32[]{:S(2)}) %copy-start.1) | copy-done | bytes 1048600
  7.3 0.2 shard_map.51
  7.5 0.3 collective-permute-start
  7.8 1.1 %collective-permute-done.1.refs_2_ = bf16[32,2048]{1,0:T(8,128)(2,1)S(1)} collective-permute-done((bf16[32,2048]{1,0:T(8,128)(2,1)S(1)}, bf16[32,2048]{1,0:T(8,128)(2,1)S(1)}, u32[]{:S(2)}, u32[]{:S(2)}) %collective-permute-start.1) | collective-permute-done | bytes 131104 | tf_op jit(solution)/shard_map/ppermute | solution.py:18
  8.8 1.9 %collective-permute-done.2.refs_3_ = bf16[32,2048]{1,0:T(8,128)(2,1)S(1)} collective-permute-done((bf16[32,2048]{1,0:T(8,128)(2,1)S(1)}, bf16[32,2048]{1,0:T(8,128)(2,1)S(1)}, u32[]{:S(2)}, u32[]{:S(2)}) %collective-permute-start.2) | collective-permute-done | bytes 131104 | tf_op jit(solution)/shard_map/ppermute | solution.py:18
  10.7 0.0 collective-permute-done.refs_1_
  10.7 0.1 shard_map.52
  10.9 1.1 %collective-permute-start.4 = (f32[32,2048]{1,0:T(8,128)S(1)}, f32[32,2048]{1,0:T(8,128)S(1)}, u32[]{:S(2)}, u32[]{:S(2)}) collective-permute-start(f32[32,2048]{1,0:T(8,128)S(1)} %get-tuple-element.44.refs_0_), channel_id=1, source_target_pairs={{0,16},{8,24},{16,0},{24,8},{1,17},{9,25},{17,1},{25,9},{2,18},{10... | collective-permute-start | bytes 786440 | tf_op jit(solution)/shard_map/ppermute | solution.py:18
  12.0 0.7 %collective-permute-start.3 = (f32[32,2048]{1,0:T(8,128)S(1)}, f32[32,2048]{1,0:T(8,128)S(1)}, u32[]{:S(2)}, u32[]{:S(2)}) collective-permute-start(f32[32,2048]{1,0:T(8,128)S(1)} %get-tuple-element.44.refs_0_), channel_id=1, source_target_pairs={{0,8},{8,0},{16,24},{24,16},{1,9},{9,1},{17,25},{25,17},{2,10},{10... | collective-permute-start | bytes 786440 | tf_op jit(solution)/shard_map/ppermute | solution.py:18
  12.7 11.9 %all_to_all.5.squares = f32[32,1,128]{2,1,0:T(1,128)S(1)} all-to-all(f32[32,1,128]{2,1,0:T(1,128)S(1)} %get-tuple-element.38), channel_id=1, replica_groups={{5,0,1,2,3,4,6,7,8,9,10,11,12,13,14,15,16,17,18,19,20,21,22,23,24,25,26..., dimensions={0} | all-to-all | bytes 32768 | tf_op jit(solution)/shard_map/all_to_all | solution.py:156
  24.6 0.0 collective-permute-done.4.refs_2_
  24.6 0.0 collective-permute-done.3.refs_1_
  24.6 0.0 collective-permute-start.5
  24.6 1.4 %shard_map.53 = (f32[32,8192]{1,0:T(8,128)}, f32[32,8192]{1,0:T(8,128)}) custom-call(f32[32,1,128]{2,1,0:T(1,128)S(1)} %all_to_all.5.squares, f32[32,8192]{1,0:T(8,128)S(1)} %get-tuple-element.41.params, f32[32,8192]{1,0:T(8,128)S(1)} %get-tuple-element.42.momentum, f32[32,2048]{1,0:T(8,128)S(1)} %get-tuple-element.44.refs_0_, ...), custom_call_target="tpu_custom_call" | custom-call | tf_op jit(solution)/shard_map/pallas_call | solution.py:95
  26.0 0.1 collective-permute-done.5.refs_0_
  26.1 1.0 %shard_map.54 = (f32[32,8192]{1,0:T(8,128)}, f32[32,8192]{1,0:T(8,128)}) custom-call(f32[32,1,128]{2,1,0:T(1,128)S(1)} %all_to_all.5.squares, f32[32,8192]{1,0:T(8,128)S(1)} %get-tuple-element.41.params, f32[32,8192]{1,0:T(8,128)S(1)} %get-tuple-element.42.momentum, ...), custom_call_target="tpu_custom_call", output_to_operand_aliasing={{0}: (4, {}), {1}: (5, {})} | custom-call | tf_op jit(solution)/shard_map/pallas_call | solution.py:95
Async XLA Ops:
  0.6 1.0 %copy-start.2 = (bf16[1,32,8192]{2,1,0:T(8,128)(2,1)S(1)}, bf16[1,32,8192]{2,1,0:T(8,128)(2,1)}, u32[]{:S(2)}) copy-start(bf16[1,32,8192]{2,1,0:T(8,128)(2,1)} %grad.1) | copy-start | bytes 1572868
  1.9 6.9 %collective-permute-start.1 = (bf16[32,2048]{1,0:T(8,128)(2,1)S(1)}, bf16[32,2048]{1,0:T(8,128)(2,1)S(1)}, u32[]{:S(2)}, u32[]{:S(2)}) collective-permute-start(bf16[32,2048]{1,0:T(8,128)(2,1)S(1)} %get-tuple-element.36), channel_id=1, source_target_pairs={{0,16},{8,24},{16,0},{24,8},{1,17},{9,25},{17,1},{25,9},{2,18},{10... | collective-permute-start | bytes 393224 | tf_op jit(solution)/shard_map/ppermute | solution.py:18
  4.9 5.9 %collective-permute-start.2 = (bf16[32,2048]{1,0:T(8,128)(2,1)S(1)}, bf16[32,2048]{1,0:T(8,128)(2,1)S(1)}, u32[]{:S(2)}, u32[]{:S(2)}) collective-permute-start(bf16[32,2048]{1,0:T(8,128)(2,1)S(1)} %get-tuple-element.37), channel_id=1, source_target_pairs={{0,24},{8,16},{16,8},{24,0},{1,25},{9,17},{17,9},{25,1},{2,26},{10... | collective-permute-start | bytes 393224 | tf_op jit(solution)/shard_map/ppermute | solution.py:18
  4.9 1.2 %copy-start = (f32[32,8192]{1,0:T(8,128)S(1)}, f32[32,8192]{1,0:T(8,128)}, u32[]{:S(2)}) copy-start(f32[32,8192]{1,0:T(8,128)} %refs_0_) | copy-start | bytes 3145732
  6.1 1.2 %copy-start.1 = (f32[32,8192]{1,0:T(8,128)S(1)}, f32[32,8192]{1,0:T(8,128)}, u32[]{:S(2)}) copy-start(f32[32,8192]{1,0:T(8,128)} %refs_1_) | copy-start | bytes 3145732
  7.5 3.2 %collective-permute-start = (bf16[32,2048]{1,0:T(8,128)(2,1)S(1)}, bf16[32,2048]{1,0:T(8,128)(2,1)S(1)}, u32[]{:S(2)}, u32[]{:S(2)}) collective-permute-start(bf16[32,2048]{1,0:T(8,128)(2,1)S(1)} %get-tuple-element.35), channel_id=1, source_target_pairs={{0,8},{8,0},{16,24},{24,16},{1,9},{9,1},{17,25},{25,17},{2,10},{10... | collective-permute-start | bytes 393224 | tf_op jit(solution)/shard_map/ppermute | solution.py:18
  10.9 13.7 %collective-permute-start.4 = (f32[32,2048]{1,0:T(8,128)S(1)}, f32[32,2048]{1,0:T(8,128)S(1)}, u32[]{:S(2)}, u32[]{:S(2)}) collective-permute-start(f32[32,2048]{1,0:T(8,128)S(1)} %get-tuple-element.44.refs_0_), channel_id=1, source_target_pairs={{0,16},{8,24},{16,0},{24,8},{1,17},{9,25},{17,1},{25,9},{2,18},{10... | collective-permute-start | bytes 786440 | tf_op jit(solution)/shard_map/ppermute | solution.py:18
  12.0 12.6 %collective-permute-start.3 = (f32[32,2048]{1,0:T(8,128)S(1)}, f32[32,2048]{1,0:T(8,128)S(1)}, u32[]{:S(2)}, u32[]{:S(2)}) collective-permute-start(f32[32,2048]{1,0:T(8,128)S(1)} %get-tuple-element.44.refs_0_), channel_id=1, source_target_pairs={{0,8},{8,0},{16,24},{24,16},{1,9},{9,1},{17,25},{25,17},{2,10},{10... | collective-permute-start | bytes 786440 | tf_op jit(solution)/shard_map/ppermute | solution.py:18
  24.6 1.5 %collective-permute-start.5 = (f32[32,2048]{1,0:T(8,128)S(1)}, f32[32,2048]{1,0:T(8,128)S(1)}, u32[]{:S(2)}, u32[]{:S(2)}) collective-permute-start(f32[32,2048]{1,0:T(8,128)S(1)} %collective-permute-done.4.refs_2_), channel_id=1, source_target_pairs={{0,8},{8,0},{16,24},{24,16},{1,9},{9,1},{17,25},{25,17},{2,10},{10... | collective-permute-start | bytes 786440 | tf_op jit(solution)/shard_map/ppermute | solution.py:18

commit v11 on v4

--- a/solution.py
+++ b/solution.py
@@ -28,17 +28,34 @@
     return parts[0]
 
 
-def cut_kernel(grad, *rest):
-    pieces, sems = rest[:-1], rest[-1]
-    width = pieces[0].shape[1]
+def cut_kernel(flips, arrays, *refs):
+    grad, sems = refs[0], refs[-1]
+    outs = refs[1 + arrays : -1]
+    moves = [(grad.at[0, :, piece_of(k, outs[0].shape[1])], out) for k, out in zip(flips, outs)]
+    moves += list(zip(refs[1 : 1 + arrays], outs[len(flips) :]))
     copies = [
-        pltpu.make_async_copy(grad.at[0, :, piece_of(k, width)], piece, sems.at[k])
-        for k, piece in enumerate(pieces)
+        pltpu.make_async_copy(source, out, sems.at[i])
+        for i, (source, out) in enumerate(moves)
     ]
     for copy in copies:
         copy.start()
     for copy in copies:
         copy.wait()
+
+
+def cut(grad, width, flips, *arrays):
+    piece = jax.ShapeDtypeStruct((grad.shape[1], width), grad.dtype)
+    out_shape = [piece] * len(flips) + [jax.ShapeDtypeStruct(x.shape, x.dtype) for x in arrays]
+    held = [pltpu.with_memory_space_constraint(x, pltpu.HBM) for x in (grad, *arrays)]
+    outs = pl.pallas_call(
+        functools.partial(cut_kernel, flips, len(arrays)),
+        out_shape=out_shape,
+        in_specs=[HBM] * len(held),
+        out_specs=[VMEM] * len(out_shape),
+        scratch_shapes=[pltpu.SemaphoreType.DMA((len(out_shape),))],
+        compiler_params=pltpu.CompilerParams(vmem_limit_bytes=LIMIT),
+    )(*held)
+    return dict(zip(flips, outs)), outs[len(flips) :]
 
 
 def average_kernel(*refs):
@@ -51,18 +68,6 @@
         jnp.add, [row[:, i : i + 128] for i in range(0, row.shape[1], 128)]
     )
     squares[...] = jnp.broadcast_to(lanes[None], squares.shape)
-
-
-def fetch_kernel(*refs):
-    half = (len(refs) - 1) // 2
-    copies = [
-        pltpu.make_async_copy(refs[i], refs[half + i], refs[-1].at[i])
-        for i in range(half)
-    ]
-    for copy in copies:
-        copy.start()
-    for copy in copies:
-        copy.wait()
 
 
 def update_kernel(count, flips, passed, squares, params, momentum, *refs):
@@ -114,29 +119,13 @@
     width = columns // groups
     count = rows * lax.axis_size("fsdp") * columns
     limit = pltpu.CompilerParams(vmem_limit_bytes=LIMIT)
-    piece = jax.ShapeDtypeStruct((rows, width), pseudo_grad.dtype)
-    pieces = pl.pallas_call(
-        cut_kernel,
-        out_shape=[piece] * groups,
-        in_specs=[HBM],
-        out_specs=[VMEM] * groups,
-        scratch_shapes=[pltpu.SemaphoreType.DMA((groups,))],
-        compiler_params=limit,
-    )(pseudo_grad)
-    pieces, params, momentum = lax.optimization_barrier((pieces, params, momentum))
-    kept = jax.ShapeDtypeStruct(params.shape, WIDE)
-    params, momentum = pl.pallas_call(
-        fetch_kernel,
-        out_shape=[kept, kept],
-        in_specs=[HBM] * 2,
-        out_specs=[VMEM] * 2,
-        scratch_shapes=[pltpu.SemaphoreType.DMA((2,))],
-        compiler_params=limit,
-        cost_estimate=pl.CostEstimate(flops=0, bytes_accessed=8 * params.size, transcendentals=0),
-    )(params, momentum)
+    pieces, _ = cut(pseudo_grad, width, range(2, groups))
+    pieces, pseudo_grad, params, momentum = lax.optimization_barrier(
+        (pieces, pseudo_grad, params, momentum)
+    )
     moved = {k: swapped(pieces[k], "replica", k) for k in range(2, groups)}
-    near, params, momentum = lax.optimization_barrier((pieces[1], params, momentum))
-    moved.update({0: pieces[0], 1: swapped(near, "replica", 1)})
+    near, (params, momentum) = cut(pseudo_grad, width, range(2), params, momentum)
+    moved.update({0: near[0], 1: swapped(near[1], "replica", 1)})
     average, squares = pl.pallas_call(
         average_kernel,
         out_shape=[

time: 27.3 us -> 27 us (0.989)
  local copies, waits for them, and re-layouts: 3.48 us -> 0 us
  Pallas kernels: 2.91 us -> 5.26 us
  waiting for transfers between devices: 3.09 us -> 3.99 us
    unnamed x6 -> x0, local copies, waits for them, and re-layouts: 3.48 us -> none
    pallas_call x2, Pallas kernels: 0.36 us -> 2.72 us  [cut(): pl.pallas_call(functools.partial(cut_kernel, flips, len(arrays)), out_sha...]
    ppermute x6, waiting for transfers between devices: 3.09 us -> 3.99 us  [swapped(): return lax.ppermute(value, axis, [(i, i ^ flip) for i in range(size)])]
  transfers between devices with their start and end apart: 6 -> 6, of which waited for: 3 -> 3; matrix products, arithmetic and copies ran while one was open for 0% -> 0% of each run, Pallas kernels for 6% -> 12%
where the time goes in v11:
time: 27 us; the launch traced here: 26.8 us
  blocking collectives  11.8 us (44%)
  Pallas kernels  5.26 us (19%)
  starting transfers between devices  5.06 us (19%)
  waiting for transfers between devices  3.99 us (15%)
  between operations  0.67 us (2%)
    all_to_all x1, blocking collectives, per_device(): lax.all_to_all(squares, ('replica', 'fsdp'), split_axis=0, concat_axis=0,...  11.8 us
    ppermute x6, starting transfers between devices, swapped(): return lax.ppermute(value, axis, [(i, i ^ flip) for i in range(size)])  5.06 us
    ppermute x6, waiting for transfers between devices, swapped(): return lax.ppermute(value, axis, [(i, i ^ flip) for i in range(size)])  3.99 us
    pallas_call x2, Pallas kernels, cut(): pl.pallas_call(functools.partial(cut_kernel, flips, len(arrays)), out_sha...  2.72 us
    pallas_call x2, Pallas kernels, update(): pl.pallas_call(functools.partial(update_kernel, count, flips, len(earlier...  2.43 us
  transfers between devices with their start and end apart: 6, of which 3 were waited for; matrix products, arithmetic and copies ran while one was open for 0% of the time, Pallas kernels for 12%

profile of v11, /device:TPU:0, one launch (start us, length us, event | category | flops | bytes accessed | tf_op | source)
XLA Modules:
  0.0 26.8 jit_solution(13026220438811682142)
XLA Ops:
  0.6 1.0 %shard_map.50 = (bf16[32,2048]{1,0:T(8,128)(2,1)S(1)}, bf16[32,2048]{1,0:T(8,128)(2,1)S(1)}) custom-call(bf16[1,32,8192]{2,1,0:T(8,128)(2,1)} %refs_0_.2), custom_call_target="tpu_custom_call" | custom-call | tf_op jit(solution)/shard_map/pallas_call | solution.py:50
  1.6 3.0 %collective-permute-start.1 = (bf16[32,2048]{1,0:T(8,128)(2,1)S(1)}, bf16[32,2048]{1,0:T(8,128)(2,1)S(1)}, u32[]{:S(2)}, u32[]{:S(2)}) collective-permute-start(bf16[32,2048]{1,0:T(8,128)(2,1)S(1)} %get-tuple-element.28), channel_id=1, source_target_pairs={{0,16},{8,24},{16,0},{24,8},{1,17},{9,25},{17,1},{25,9},{2,18},{10... | collective-permute-start | bytes 393224 | tf_op jit(solution)/shard_map/ppermute | solution.py:18
  4.6 0.0 collective-permute-start.2
  4.6 1.7 %shard_map.51 = (bf16[32,2048]{1,0:T(8,128)(2,1)S(1)}, bf16[32,2048]{1,0:T(8,128)(2,1)S(1)}, f32[32,8192]{1,0:T(8,128)S(1)}, f32[32,8192]{1,0:T(8,128)S(1)}) custom-call(bf16[1,32,8192]{2,1,0:T(8,128)(2,1)} %refs_0_.2, f32[32,8192]{1,0:T(8,128)} %refs_1_, f32[32,8192]{1,0:T(8,128)} %refs_2_), custom_call_target="tpu_custom_call" | custom-call | tf_op jit(solution)/shard_map/pallas_call | solution.py:50
  6.4 0.3 collective-permute-start
  6.6 2.0 %collective-permute-done.1.refs_2_ = bf16[32,2048]{1,0:T(8,128)(2,1)S(1)} collective-permute-done((bf16[32,2048]{1,0:T(8,128)(2,1)S(1)}, bf16[32,2048]{1,0:T(8,128)(2,1)S(1)}, u32[]{:S(2)}, u32[]{:S(2)}) %collective-permute-start.1) | collective-permute-done | bytes 131104 | tf_op jit(solution)/shard_map/ppermute | solution.py:18
  8.6 1.9 %collective-permute-done.2.refs_3_ = bf16[32,2048]{1,0:T(8,128)(2,1)S(1)} collective-permute-done((bf16[32,2048]{1,0:T(8,128)(2,1)S(1)}, bf16[32,2048]{1,0:T(8,128)(2,1)S(1)}, u32[]{:S(2)}, u32[]{:S(2)}) %collective-permute-start.2) | collective-permute-done | bytes 131104 | tf_op jit(solution)/shard_map/ppermute | solution.py:18
  10.5 0.0 collective-permute-done.refs_1_
  10.5 0.1 shard_map.52
  10.6 1.1 %collective-permute-start.4 = (f32[32,2048]{1,0:T(8,128)S(1)}, f32[32,2048]{1,0:T(8,128)S(1)}, u32[]{:S(2)}, u32[]{:S(2)}) collective-permute-start(f32[32,2048]{1,0:T(8,128)S(1)} %get-tuple-element.36.refs_0_), channel_id=1, source_target_pairs={{0,16},{8,24},{16,0},{24,8},{1,17},{9,25},{17,1},{25,9},{2,18},{10... | collective-permute-start | bytes 786440 | tf_op jit(solution)/shard_map/ppermute | solution.py:18
  11.7 0.7 %collective-permute-start.3 = (f32[32,2048]{1,0:T(8,128)S(1)}, f32[32,2048]{1,0:T(8,128)S(1)}, u32[]{:S(2)}, u32[]{:S(2)}) collective-permute-start(f32[32,2048]{1,0:T(8,128)S(1)} %get-tuple-element.36.refs_0_), channel_id=1, source_target_pairs={{0,8},{8,0},{16,24},{24,16},{1,9},{9,1},{17,25},{25,17},{2,10},{10... | collective-permute-start | bytes 786440 | tf_op jit(solution)/shard_map/ppermute | solution.py:18
  12.4 11.8 %all_to_all.5.squares = f32[32,1,128]{2,1,0:T(1,128)S(1)} all-to-all(f32[32,1,128]{2,1,0:T(1,128)S(1)} %get-tuple-element.30), channel_id=1, replica_groups=mesh['replica'=4,'fsdp'=8] {'replica','fsdp'}, dimensions={0} | all-to-all | bytes 32768 | tf_op jit(solution)/shard_map/all_to_all | solution.py:143
  24.2 0.0 collective-permute-done.4.refs_2_
  24.3 0.0 collective-permute-done.3.refs_1_
  24.3 0.0 collective-permute-start.5
  24.3 1.4 %shard_map.53 = (f32[32,8192]{1,0:T(8,128)}, f32[32,8192]{1,0:T(8,128)}) custom-call(f32[32,1,128]{2,1,0:T(1,128)S(1)} %all_to_all.5.squares, f32[32,8192]{1,0:T(8,128)S(1)} %get-tuple-element.33.params, f32[32,8192]{1,0:T(8,128)S(1)} %get-tuple-element.34.momentum, f32[32,2048]{1,0:T(8,128)S(1)} %get-tuple-element.36.refs_0_, ...), custom_call_target="tpu_custom_call" | custom-call | tf_op jit(solution)/shard_map/pallas_call | solution.py:100
  25.7 0.1 collective-permute-done.5.refs_0_
  25.8 1.0 %shard_map.54 = (f32[32,8192]{1,0:T(8,128)}, f32[32,8192]{1,0:T(8,128)}) custom-call(f32[32,1,128]{2,1,0:T(1,128)S(1)} %all_to_all.5.squares, f32[32,8192]{1,0:T(8,128)S(1)} %get-tuple-element.33.params, f32[32,8192]{1,0:T(8,128)S(1)} %get-tuple-element.34.momentum, ...), custom_call_target="tpu_custom_call", output_to_operand_aliasing={{0}: (4, {}), {1}: (5, {})} | custom-call | tf_op jit(solution)/shard_map/pallas_call | solution.py:100
Async XLA Ops:
  1.6 6.9 %collective-permute-start.1 = (bf16[32,2048]{1,0:T(8,128)(2,1)S(1)}, bf16[32,2048]{1,0:T(8,128)(2,1)S(1)}, u32[]{:S(2)}, u32[]{:S(2)}) collective-permute-start(bf16[32,2048]{1,0:T(8,128)(2,1)S(1)} %get-tuple-element.28), channel_id=1, source_target_pairs={{0,16},{8,24},{16,0},{24,8},{1,17},{9,25},{17,1},{25,9},{2,18},{10... | collective-permute-start | bytes 393224 | tf_op jit(solution)/shard_map/ppermute | solution.py:18
  4.6 5.9 %collective-permute-start.2 = (bf16[32,2048]{1,0:T(8,128)(2,1)S(1)}, bf16[32,2048]{1,0:T(8,128)(2,1)S(1)}, u32[]{:S(2)}, u32[]{:S(2)}) collective-permute-start(bf16[32,2048]{1,0:T(8,128)(2,1)S(1)} %get-tuple-element.29), channel_id=1, source_target_pairs={{0,24},{8,16},{16,8},{24,0},{1,25},{9,17},{17,9},{25,1},{2,26},{10... | collective-permute-start | bytes 393224 | tf_op jit(solution)/shard_map/ppermute | solution.py:18
  6.4 4.1 %collective-permute-start = (bf16[32,2048]{1,0:T(8,128)(2,1)S(1)}, bf16[32,2048]{1,0:T(8,128)(2,1)S(1)}, u32[]{:S(2)}, u32[]{:S(2)}) collective-permute-start(bf16[32,2048]{1,0:T(8,128)(2,1)S(1)} %get-tuple-element.27), channel_id=1, source_target_pairs={{0,8},{8,0},{16,24},{24,16},{1,9},{9,1},{17,25},{25,17},{2,10},{10... | collective-permute-start | bytes 393224 | tf_op jit(solution)/shard_map/ppermute | solution.py:18
  10.6 13.6 %collective-permute-start.4 = (f32[32,2048]{1,0:T(8,128)S(1)}, f32[32,2048]{1,0:T(8,128)S(1)}, u32[]{:S(2)}, u32[]{:S(2)}) collective-permute-start(f32[32,2048]{1,0:T(8,128)S(1)} %get-tuple-element.36.refs_0_), channel_id=1, source_target_pairs={{0,16},{8,24},{16,0},{24,8},{1,17},{9,25},{17,1},{25,9},{2,18},{10... | collective-permute-start | bytes 786440 | tf_op jit(solution)/shard_map/ppermute | solution.py:18
  11.7 12.5 %collective-permute-start.3 = (f32[32,2048]{1,0:T(8,128)S(1)}, f32[32,2048]{1,0:T(8,128)S(1)}, u32[]{:S(2)}, u32[]{:S(2)}) collective-permute-start(f32[32,2048]{1,0:T(8,128)S(1)} %get-tuple-element.36.refs_0_), channel_id=1, source_target_pairs={{0,8},{8,0},{16,24},{24,16},{1,9},{9,1},{17,25},{25,17},{2,10},{10... | collective-permute-start | bytes 786440 | tf_op jit(solution)/shard_map/ppermute | solution.py:18
  24.3 1.5 %collective-permute-start.5 = (f32[32,2048]{1,0:T(8,128)S(1)}, f32[32,2048]{1,0:T(8,128)S(1)}, u32[]{:S(2)}, u32[]{:S(2)}) collective-permute-start(f32[32,2048]{1,0:T(8,128)S(1)} %collective-permute-done.4.refs_2_), channel_id=1, source_target_pairs={{0,8},{8,0},{16,24},{24,16},{1,9},{9,1},{17,25},{25,17},{2,10},{10... | collective-permute-start | bytes 786440 | tf_op jit(solution)/shard_map/ppermute | solution.py:18

commit v12 on v11

v12 whole, which is shorter than its diff:
```python
import functools

import jax
import jax.numpy as jnp
from jax import lax
from jax.experimental import pallas as pl
from jax.experimental.pallas import tpu as pltpu
from jax.sharding import PartitionSpec as P

WIDE = jnp.float32
VMEM = pl.BlockSpec(memory_space=pltpu.VMEM)
HBM = pl.BlockSpec(memory_space=pltpu.HBM)
LIMIT = 16 * 1024 * 1024


def swapped(value, axis, flip):
    size = lax.axis_size(axis)
    return lax.ppermute(value, axis, [(i, i ^ flip) for i in range(size)])


def piece_of(k, width):
    return pl.ds(pl.multiple_of((lax.axis_index("replica") ^ k) * width, width), width)


SIDE = 128
TOP = 2.0**7.5
KNEE = 2.0**-4


def encode(value):
    size = jnp.abs(value)
    scale = jnp.maximum(jnp.max(size, axis=1, keepdims=True), 1e-30)
    scale = scale.astype(jnp.bfloat16).astype(WIDE)
    unit = size * (TOP / scale)
    power = unit
    for _ in range(4):
        power = power * power
    code = jnp.where(unit < KNEE, unit * KNEE**15, power)
    code = jnp.where(value < 0, -code, code).astype(jnp.bfloat16)
    side = jnp.broadcast_to(scale, (value.shape[0], SIDE)).astype(jnp.bfloat16)
    return jnp.concatenate([code, side], axis=1)


def decode(code):
    width = code.shape[1] - SIDE
    scale = code[:, width : width + 1].astype(WIDE)
    power = code[:, :width].astype(WIDE)
    size = jnp.abs(power)
    root = jnp.exp(jnp.log(jnp.maximum(size, KNEE**16)) * (1 / 16))
    unit = jnp.where(size < KNEE**16, size * KNEE**-15, root) * (scale * (1 / TOP))
    return jnp.where(power < 0, -unit, unit)


def tree(parts):
    while len(parts) > 1:
        parts = [parts[i] + parts[i + 1] for i in range(0, len(parts), 2)]
    return parts[0]


def copy_all(moves, sems):
    copies = [
        pltpu.make_async_copy(source, out, sems.at[i])
        for i, (source, out) in enumerate(moves)
    ]
    for copy in copies:
        copy.start()
    for copy in copies:
        copy.wait()


def cut_kernel(flips, grad, *refs):
    outs, sems = refs[:-1], refs[-1]
    width = outs[0].shape[2]
    copy_all(
        [
            (grad.at[0, :, piece_of(k, width)], out.at[i])
            for group, out in zip(flips, outs)
            for i, k in enumerate(group)
        ],
        sems,
    )


def read_kernel(*refs):
    count = len(refs) // 2
    copy_all(list(zip(refs[:count], refs[count:-1])), refs[-1])


def call(kernel, out_shape, *args, held=False, copies=0):
    if held:
        args = [pltpu.with_memory_space_constraint(x, pltpu.HBM) for x in args]
    return pl.pallas_call(
        kernel,
        out_shape=out_shape,
        in_specs=[HBM if held else VMEM] * len(args),
        out_specs=[VMEM] * len(out_shape),
        scratch_shapes=[pltpu.SemaphoreType.DMA((copies,))] if copies else (),
        compiler_params=pltpu.CompilerParams(vmem_limit_bytes=LIMIT),
    )(*args)


def cut(grad, width, *flips):
    out_shape = [
        jax.ShapeDtypeStruct((len(group), grad.shape[1], width), grad.dtype)
        for group in flips
    ]
    kernel = functools.partial(cut_kernel, flips)
    return call(kernel, out_shape, grad, held=True, copies=sum(map(len, flips)))


def read(*arrays):
    out_shape = [jax.ShapeDtypeStruct(x.shape, x.dtype) for x in arrays]
    return call(read_kernel, out_shape, *arrays, held=True, copies=len(arrays))


def squares_of(mean, squares):
    row = jnp.sum(mean * mean, axis=0, keepdims=True)
    lanes = functools.reduce(
        jnp.add, [row[:, i : i + 128] for i in range(0, row.shape[1], 128)]
    )
    squares[...] = jnp.broadcast_to(lanes[None], squares.shape)


def average_kernel(*refs):
    pieces, (average, squares) = refs[:-2], refs[-2:]
    total = tree([piece[...].astype(WIDE) for piece in pieces])
    mean = total / WIDE(len(pieces))
    average[...] = mean
    squares_of(mean, squares)


def pair_kernel(own, mate, first, second, sums):
    for i, code in enumerate((first, second)):
        code[...] = encode(own[i].astype(WIDE) + mate[i].astype(WIDE))
        sums[i] = decode(code[...])


def join_kernel(groups, sums, code, average, squares):
    mean = (sums[0] + decode(code[...])) / WIDE(groups)
    average[...] = mean
    squares_of(mean, squares)


def write_out(count, flips, means, squares, params, momentum, refs):
    new_params, new_momentum, params_out, momentum_out, sems = refs
    square_sum = jnp.sum(squares[...], keepdims=True).reshape(1, 1)
    factor = 0.2 / jnp.sqrt(square_sum / WIDE(count) + 1e-06)
    width = params_out.shape[2]
    copies = []
    for i, (k, mean) in enumerate(zip(flips, means)):
        cols = piece_of(k, width)
        clipped = factor * mean()
        fresh = 0.9 * momentum[:, cols] + clipped
        momentum_out[i] = fresh
        params_out[i] = params[:, cols] - 0.7 * (clipped + 0.9 * fresh)
        copies += [
            pltpu.make_async_copy(momentum_out.at[i], new_momentum.at[:, cols], sems.at[0, i]),
            pltpu.make_async_copy(params_out.at[i], new_params.at[:, cols], sems.at[1, i]),
        ]
        copies[-2].start()
        copies[-1].start()
    for copy in copies:
        copy.wait()


def update_kernel(count, flips, passed, squares, params, momentum, *refs):
    means = [functools.partial(ref.__getitem__, ...) for ref in refs[: len(flips)]]
    write_out(count, flips, means, squares, params, momentum, refs[len(flips) + passed :])


def final_kernel(count, groups, squares, params, momentum, average, own, mate, one, two, three, *refs):
    def joined(sums, i, code):
        return lambda: (sums[i] + decode(code[...])) / WIDE(groups)

    means = [
        functools.partial(average.__getitem__, ...),
        joined(mate, 0, one),
        joined(own, 1, two),
        joined(mate, 1, three),
    ]
    write_out(count, range(groups), means, squares, params, momentum, refs)


def update(kernel, flips, width, args, earlier=()):
    shape = args[1].shape
    out = jax.ShapeDtypeStruct(shape, WIDE)
    return pl.pallas_call(
        kernel,
        out_shape=[out, out],
        in_specs=[VMEM] * len(args) + [HBM] * len(earlier),
        out_specs=[HBM] * 2,
        scratch_shapes=[
            pltpu.VMEM((len(flips), shape[0], width), WIDE),
            pltpu.VMEM((len(flips), shape[0], width), WIDE),
            pltpu.SemaphoreType.DMA((2, len(flips))),
        ],
        input_output_aliases={len(args) + i: i for i in range(len(earlier))},
        compiler_params=pltpu.CompilerParams(vmem_limit_bytes=LIMIT),
    )(*args, *earlier)


def all_squares(squares):
    return lax.all_to_all(
        squares, ("replica", "fsdp"), split_axis=0, concat_axis=0, tiled=True
    )


def two_chips(pseudo_grad, params, momentum, width, count, square_rows):
    groups = lax.axis_size("replica")
    rows = params.shape[0]
    code = jax.ShapeDtypeStruct((rows, width + SIDE), jnp.bfloat16)
    sums = jax.ShapeDtypeStruct((2, rows, width), WIDE)
    own, others = cut(pseudo_grad, width, (0, 2), (1, 3))
    mate = swapped(others, "replica", 1)
    code_own, code_far, own_sums = call(pair_kernel, [code, code, sums], own, mate)
    urgent = swapped(code_far, "replica", 2)
    mate_sums = swapped(own_sums, "replica", 1)
    code_own, code_far, params, momentum = lax.optimization_barrier(
        (code_own, code_far, params, momentum)
    )
    params, momentum = read(params, momentum)
    code_own, code_far, params, momentum = lax.optimization_barrier(
        (code_own, code_far, params, momentum)
    )
    one = swapped(code_far, "replica", 3)
    two = swapped(code_own, "replica", 2)
    three = swapped(code_own, "replica", 3)
    average, squares = call(
        functools.partial(join_kernel, groups),
        [jax.ShapeDtypeStruct((rows, width), WIDE), square_rows],
        own_sums, urgent,
    )
    squares = all_squares(squares)
    squares, one, two, three, mate_sums = lax.optimization_barrier(
        (squares, one, two, three, mate_sums)
    )
    return update(
        functools.partial(final_kernel, count, groups), range(groups), width,
        (squares, params, momentum, average, own_sums, mate_sums, one, two, three),
    )


def per_device(pseudo_grad, params, momentum):
    groups = lax.axis_size("replica")
    devices = groups * lax.axis_size("fsdp")
    rows, columns = params.shape
    width = columns // groups
    count = rows * lax.axis_size("fsdp") * columns
    square_rows = jax.ShapeDtypeStruct((devices, 1, 128), WIDE)
    if groups == 4:
        return two_chips(pseudo_grad, params, momentum, width, count, square_rows)
    (pieces,) = cut(pseudo_grad, width, range(groups))
    params, momentum = read(params, momentum)
    moved = [swapped(pieces[k], "replica", k) if k else pieces[k] for k in range(groups)]
    average, squares = call(
        average_kernel, [jax.ShapeDtypeStruct((rows, width), WIDE), square_rows], *moved
    )
    averages = {0: average, 1: swapped(average, "replica", 1)}
    for k in range(2, groups, 2):
        averages[k] = swapped(average, "replica", k)
    squares = all_squares(squares)
    squares, averages = lax.optimization_barrier((squares, averages))
    for k in range(2, groups, 2):
        averages[k + 1] = swapped(averages[k], "replica", 1)
    here = [k for k in range(groups) if k < 2 or k % 2 == 0]
    late = [k for k in range(groups) if k not in here]
    outs = ()
    for flips in (here, late):
        if flips:
            outs = update(
                functools.partial(update_kernel, count, flips, len(outs)), flips, width,
                (squares, params, momentum, *[averages[k] for k in flips]), outs,
            )
    return outs


def solution(mesh):
    placed = (P("replica", "fsdp", None), P("fsdp", None), P("fsdp", None))
    return jax.shard_map(
        per_device,
        mesh=mesh,
        in_specs=placed,
        out_specs=(P("fsdp", None), P("fsdp", None)),
        check_vma=False,
    )
```

time: 27 us -> 29.9 us (1.11)
  blocking collectives: 11.8 us -> 0 us
  starting transfers between devices: 5.06 us -> 12.2 us
  waiting for transfers between devices: 3.99 us -> 9.07 us
  Pallas kernels: 5.26 us -> 7.16 us
  local copies, waits for them, and re-layouts: 0 us -> 0.59 us
    all_to_all x1 -> x0, blocking collectives: 11.8 us -> none  [per_device(): lax.all_to_all(squares, ('replica', 'fsdp'), split_axis=0, concat_axis=0,...]
    all_to_all x0 -> x1, starting transfers between devices: none -> 6.78 us  [all_squares(): lax.all_to_all(squares, ('replica', 'fsdp'), split_axis=0, concat_axis=0,...]
    all_to_all x0 -> x1, waiting for transfers between devices: none -> 5.1 us  [all_squares(): lax.all_to_all(squares, ('replica', 'fsdp'), split_axis=0, concat_axis=0,...]
    pallas_call x5, Pallas kernels: 5.26 us -> 7.16 us  [the longest x4 4.2 us: call(): pl.pallas_call(kernel, out_shape=out_shape, in_specs=[HBM if held else VM...]
    unnamed x0 -> x2, local copies, waits for them, and re-layouts: none -> 0.59 us
    ppermute x6, starting transfers between devices: 5.06 us -> 5.37 us  [swapped(): return lax.ppermute(value, axis, [(i, i ^ flip) for i in range(size)])]
  transfers between devices with their start and end apart: 6 -> 7, of which waited for: 3 -> 4; matrix products, arithmetic and copies ran while one was open for 0% -> 0% of each run, Pallas kernels for 12% -> 6%
where the time goes in v12:
time: 29.9 us; the launch traced here: 29.7 us
  starting transfers between devices  12.2 us (41%)
  waiting for transfers between devices  9.07 us (30%)
  Pallas kernels  7.16 us (24%)
  between operations  0.69 us (2%)
  local copies, waits for them, and re-layouts  0.59 us (2%)
    all_to_all x1, starting transfers between devices, all_squares(): lax.all_to_all(squares, ('replica', 'fsdp'), split_axis=0, concat_axis=0,...  6.78 us
    ppermute x6, starting transfers between devices, swapped(): return lax.ppermute(value, axis, [(i, i ^ flip) for i in range(size)])  5.37 us
    all_to_all x1, waiting for transfers between devices, all_squares(): lax.all_to_all(squares, ('replica', 'fsdp'), split_axis=0, concat_axis=0,...  5.1 us
    pallas_call x4, Pallas kernels, call(): pl.pallas_call(kernel, out_shape=out_shape, in_specs=[HBM if held else VM...  4.2 us
    ppermute x6, waiting for transfers between devices, swapped(): return lax.ppermute(value, axis, [(i, i ^ flip) for i in range(size)])  3.97 us
    pallas_call x1, Pallas kernels, update(): pl.pallas_call(kernel, out_shape=[out, out], in_specs=[VMEM] * len(args)...  2.96 us
  transfers between devices with their start and end apart: 7, of which 4 were waited for; matrix products, arithmetic and copies ran while one was open for 0% of the time, Pallas kernels for 6%

profile of v12, /device:TPU:0, one launch (start us, length us, event | category | flops | bytes accessed | tf_op | source)
XLA Modules:
  0.0 29.7 jit_solution(4833789775663010210)
XLA Ops:
  0.6 1.1 %shard_map.50 = (bf16[2,32,2048]{2,1,0:T(8,128)(2,1)S(1)}, bf16[2,32,2048]{2,1,0:T(8,128)(2,1)S(1)}) custom-call(bf16[1,32,8192]{2,1,0:T(8,128)(2,1)} %grad.1), custom_call_target="tpu_custom_call" | custom-call | tf_op jit(solution)/shard_map/pallas_call | solution.py:92
  1.8 0.5 %collective-permute-start = (bf16[2,32,2048]{2,1,0:T(8,128)(2,1)S(1)}, bf16[2,32,2048]{2,1,0:T(8,128)(2,1)S(1)}, u32[]{:S(2)}, u32[]{:S(2)}) collective-permute-start(bf16[2,32,2048]{2,1,0:T(8,128)(2,1)S(1)} %get-tuple-element.25), channel_id=1, source_target_pairs={{0,8},{8,0},{16,24},{24,16},{1,9},{9,1},{17,25},{25,17},{2,10},{10... | collective-permute-start | bytes 786440 | tf_op jit(solution)/shard_map/ppermute | solution.py:18
  2.3 1.2 %collective-permute-done.mate = bf16[2,32,2048]{2,1,0:T(8,128)(2,1)S(1)} collective-permute-done((bf16[2,32,2048]{2,1,0:T(8,128)(2,1)S(1)}, bf16[2,32,2048]{2,1,0:T(8,128)(2,1)S(1)}, u32[]{:S(2)}, u32[]{:S(2)}) %collective-permute-start) | collective-permute-done | bytes 262176 | tf_op jit(solution)/shard_map/ppermute | solution.py:18
  3.5 1.2 %shard_map.51 = (bf16[32,2176]{1,0:T(8,128)(2,1)}, bf16[32,2176]{1,0:T(8,128)(2,1)}, f32[2,32,2048]{2,1,0:T(8,128)S(1)}) custom-call(bf16[2,32,2048]{2,1,0:T(8,128)(2,1)S(1)} %get-tuple-element.24.own, bf16[2,32,2048]{2,1,0:T(8,128)(2,1)S(1)} %collective-permute-done.mate), custom_call_target="tpu_custom_call" | custom-call | tf_op jit(solution)/shard_map/pallas_call | solution.py:92
  4.7 0.4 %collective-permute-start.5 = (f32[2,32,2048]{2,1,0:T(8,128)S(1)}, f32[2,32,2048]{2,1,0:T(8,128)S(1)}, u32[]{:S(2)}, u32[]{:S(2)}) collective-permute-start(f32[2,32,2048]{2,1,0:T(8,128)S(1)} %get-tuple-element.26.sums.own), channel_id=1, source_target_pairs={{0,8},{8,0},{16,24},{24,16},{1,9},{9,1},{17,25},{25,17},{2,10},{10... | collective-permute-start | bytes 1572872 | tf_op jit(solution)/shard_map/ppermute | solution.py:18
  5.1 2.6 %collective-permute-start.1 = (bf16[32,2176]{1,0:T(8,128)(2,1)}, bf16[32,2176]{1,0:T(8,128)(2,1)S(1)}, u32[]{:S(2)}, u32[]{:S(2)}) collective-permute-start(bf16[32,2176]{1,0:T(8,128)(2,1)} %get-tuple-element.36), channel_id=1, source_target_pairs={{0,16},{8,24},{16,0},{24,8},{1,17},{9,25},{17,1},{25,9},{2,18},{10... | collective-permute-start | bytes 417800 | tf_op jit(solution)/shard_map/ppermute | solution.py:18
  7.7 1.6 %shard_map.53 = (f32[32,8192]{1,0:T(8,128)S(1)}, f32[32,8192]{1,0:T(8,128)S(1)}) custom-call(f32[32,8192]{1,0:T(8,128)} %refs_0_, f32[32,8192]{1,0:T(8,128)} %refs_1_), custom_call_target="tpu_custom_call" | custom-call | tf_op jit(solution)/shard_map/pallas_call | solution.py:92
  9.3 0.1 collective-permute-start.2
  9.4 1.7 %collective-permute-start.4 = (bf16[32,2176]{1,0:T(8,128)(2,1)}, bf16[32,2176]{1,0:T(8,128)(2,1)}, u32[]{:S(2)}, u32[]{:S(2)}) collective-permute-start(bf16[32,2176]{1,0:T(8,128)(2,1)} %get-tuple-element.37), channel_id=1, source_target_pairs={{0,24},{8,16},{16,8},{24,0},{1,25},{9,17},{17,9},{25,1},{2,26},{10... | collective-permute-start | bytes 417800 | tf_op jit(solution)/shard_map/ppermute | solution.py:18
  11.1 0.0 collective-permute-start.3
  11.1 1.0 %collective-permute-done.1.code = bf16[32,2176]{1,0:T(8,128)(2,1)S(1)} collective-permute-done((bf16[32,2176]{1,0:T(8,128)(2,1)}, bf16[32,2176]{1,0:T(8,128)(2,1)S(1)}, u32[]{:S(2)}, u32[]{:S(2)}) %collective-permute-start.1) | collective-permute-done | bytes 139296 | tf_op jit(solution)/shard_map/ppermute | solution.py:18
  12.1 0.3 shard_map.52
  12.4 0.0 copy-start
  12.4 0.6 %copy-done = f32[32,1,128]{2,1,0:T(1,128)} copy-done((f32[32,1,128]{2,1,0:T(1,128)}, f32[32,1,128]{2,1,0:T(1,128)S(1)}, u32[]{:S(2)}) %copy-start) | copy-done | bytes 16408
  13.0 6.8 %all-to-all-start = ((f32[32,1,128]{2,1,0:T(1,128)}), f32[32,1,128]{2,1,0:T(1,128)}, u32[]{:S(2)}, u32[]{:S(2)}) async-start(f32[32,1,128]{2,1,0:T(1,128)} %copy-done), calls=%async_computation | async-start | bytes 32768 | tf_op jit(solution)/shard_map/all_to_all | solution.py:203
  19.8 0.0 collective-permute-done.2.one
  19.8 0.0 collective-permute-done.4.three
  19.8 1.8 %collective-permute-done.3.two = bf16[32,2176]{1,0:T(8,128)(2,1)} collective-permute-done((bf16[32,2176]{1,0:T(8,128)(2,1)}, bf16[32,2176]{1,0:T(8,128)(2,1)}, u32[]{:S(2)}, u32[]{:S(2)}) %collective-permute-start.3) | collective-permute-done | bytes 139296 | tf_op jit(solution)/shard_map/ppermute | solution.py:18
  21.6 5.1 %all-to-all-done.squares = f32[32,1,128]{2,1,0:T(1,128)} async-done(((f32[32,1,128]{2,1,0:T(1,128)}), f32[32,1,128]{2,1,0:T(1,128)}, u32[]{:S(2)}, u32[]{:S(2)}) %all-to-all-start) | async-done | bytes 16416 | tf_op jit(solution)/shard_map/all_to_all | solution.py:203
  26.7 0.0 collective-permute-done.5.mate
  26.7 3.0 %shard_map.54 = (f32[32,8192]{1,0:T(8,128)}, f32[32,8192]{1,0:T(8,128)}) custom-call(f32[32,1,128]{2,1,0:T(1,128)} %all-to-all-done.squares, f32[32,8192]{1,0:T(8,128)S(1)} %get-tuple-element.39.params, f32[32,8192]{1,0:T(8,128)S(1)} %get-tuple-element.40.momentum, f32[32,2048]{1,0:T(8,128)S(1)} %get-tuple-element.41.average, ...), custom_call_target="tpu_custom_call" | custom-call | tf_op jit(solution)/shard_map/pallas_call | solution.py:187
Async XLA Ops:
  1.8 1.7 %collective-permute-start = (bf16[2,32,2048]{2,1,0:T(8,128)(2,1)S(1)}, bf16[2,32,2048]{2,1,0:T(8,128)(2,1)S(1)}, u32[]{:S(2)}, u32[]{:S(2)}) collective-permute-start(bf16[2,32,2048]{2,1,0:T(8,128)(2,1)S(1)} %get-tuple-element.25), channel_id=1, source_target_pairs={{0,8},{8,0},{16,24},{24,16},{1,9},{9,1},{17,25},{25,17},{2,10},{10... | collective-permute-start | bytes 786440 | tf_op jit(solution)/shard_map/ppermute | solution.py:18
  4.7 22.0 %collective-permute-start.5 = (f32[2,32,2048]{2,1,0:T(8,128)S(1)}, f32[2,32,2048]{2,1,0:T(8,128)S(1)}, u32[]{:S(2)}, u32[]{:S(2)}) collective-permute-start(f32[2,32,2048]{2,1,0:T(8,128)S(1)} %get-tuple-element.26.sums.own), channel_id=1, source_target_pairs={{0,8},{8,0},{16,24},{24,16},{1,9},{9,1},{17,25},{25,17},{2,10},{10... | collective-permute-start | bytes 1572872 | tf_op jit(solution)/shard_map/ppermute | solution.py:18
  5.1 7.0 %collective-permute-start.1 = (bf16[32,2176]{1,0:T(8,128)(2,1)}, bf16[32,2176]{1,0:T(8,128)(2,1)S(1)}, u32[]{:S(2)}, u32[]{:S(2)}) collective-permute-start(bf16[32,2176]{1,0:T(8,128)(2,1)} %get-tuple-element.36), channel_id=1, source_target_pairs={{0,16},{8,24},{16,0},{24,8},{1,17},{9,25},{17,1},{25,9},{2,18},{10... | collective-permute-start | bytes 417800 | tf_op jit(solution)/shard_map/ppermute | solution.py:18
  9.3 10.5 %collective-permute-start.2 = (bf16[32,2176]{1,0:T(8,128)(2,1)}, bf16[32,2176]{1,0:T(8,128)(2,1)S(1)}, u32[]{:S(2)}, u32[]{:S(2)}) collective-permute-start(bf16[32,2176]{1,0:T(8,128)(2,1)} %get-tuple-element.36), channel_id=1, source_target_pairs={{0,24},{8,16},{16,8},{24,0},{1,25},{9,17},{17,9},{25,1},{2,26},{10... | collective-permute-start | bytes 417800 | tf_op jit(solution)/shard_map/ppermute | solution.py:18
  9.4 10.4 %collective-permute-start.4 = (bf16[32,2176]{1,0:T(8,128)(2,1)}, bf16[32,2176]{1,0:T(8,128)(2,1)}, u32[]{:S(2)}, u32[]{:S(2)}) collective-permute-start(bf16[32,2176]{1,0:T(8,128)(2,1)} %get-tuple-element.37), channel_id=1, source_target_pairs={{0,24},{8,16},{16,8},{24,0},{1,25},{9,17},{17,9},{25,1},{2,26},{10... | collective-permute-start | bytes 417800 | tf_op jit(solution)/shard_map/ppermute | solution.py:18
  11.1 10.5 %collective-permute-start.3 = (bf16[32,2176]{1,0:T(8,128)(2,1)}, bf16[32,2176]{1,0:T(8,128)(2,1)}, u32[]{:S(2)}, u32[]{:S(2)}) collective-permute-start(bf16[32,2176]{1,0:T(8,128)(2,1)} %get-tuple-element.37), channel_id=1, source_target_pairs={{0,16},{8,24},{16,0},{24,8},{1,17},{9,25},{17,1},{25,9},{2,18},{10... | collective-permute-start | bytes 417800 | tf_op jit(solution)/shard_map/ppermute | solution.py:18
  12.4 0.6 %copy-start = (f32[32,1,128]{2,1,0:T(1,128)}, f32[32,1,128]{2,1,0:T(1,128)S(1)}, u32[]{:S(2)}) copy-start(f32[32,1,128]{2,1,0:T(1,128)S(1)} %get-tuple-element.28) | copy-start | bytes 49156
  13.0 13.7 %all-to-all-start = ((f32[32,1,128]{2,1,0:T(1,128)}), f32[32,1,128]{2,1,0:T(1,128)}, u32[]{:S(2)}, u32[]{:S(2)}) async-start(f32[32,1,128]{2,1,0:T(1,128)} %copy-done), calls=%async_computation | async-start | bytes 32768 | tf_op jit(solution)/shard_map/all_to_all | solution.py:203

commit v13 on v11

--- a/solution.py
+++ b/solution.py
@@ -70,8 +70,8 @@
     squares[...] = jnp.broadcast_to(lanes[None], squares.shape)
 
 
-def update_kernel(count, flips, passed, squares, params, momentum, *refs):
-    averages, refs = refs[: len(flips)], refs[len(flips) + passed :]
+def update_kernel(count, flips, squares, params, momentum, *refs):
+    averages, refs = refs[: len(flips)], refs[len(flips) :]
     new_params, new_momentum, params_out, momentum_out, sems = refs
     square_sum = jnp.sum(squares[...], keepdims=True).reshape(1, 1)
     factor = 0.2 / jnp.sqrt(square_sum / WIDE(count) + 1e-06)
@@ -93,23 +93,21 @@
         copy.wait()
 
 
-def update(count, flips, averages, squares, params, momentum, earlier=()):
+def update(count, flips, averages, squares, params, momentum):
     rows, width = averages[0].shape
     out = jax.ShapeDtypeStruct(params.shape, WIDE)
-    first = 3 + len(flips)
     return pl.pallas_call(
-        functools.partial(update_kernel, count, flips, len(earlier)),
+        functools.partial(update_kernel, count, flips),
         out_shape=[out, out],
-        in_specs=[VMEM] * first + [HBM] * len(earlier),
+        in_specs=[VMEM] * (3 + len(flips)),
         out_specs=[HBM] * 2,
         scratch_shapes=[
             pltpu.VMEM((len(flips), rows, width), WIDE),
             pltpu.VMEM((len(flips), rows, width), WIDE),
             pltpu.SemaphoreType.DMA((2, len(flips))),
         ],
-        input_output_aliases={first + i: i for i in range(len(earlier))},
         compiler_params=pltpu.CompilerParams(vmem_limit_bytes=LIMIT),
-    )(squares, params, momentum, *averages, *earlier)
+    )(squares, params, momentum, *averages)
 
 
 def per_device(pseudo_grad, params, momentum):
@@ -143,17 +141,11 @@
     squares = lax.all_to_all(
         squares, ("replica", "fsdp"), split_axis=0, concat_axis=0, tiled=True
     )
-    squares, averages = lax.optimization_barrier((squares, averages))
     for k in range(2, groups, 2):
         averages[k + 1] = swapped(averages[k], "replica", 1)
-    here = [k for k in range(groups) if k < 2 or k % 2 == 0]
-    late = [k for k in range(groups) if k not in here]
-    outs = update(count, here, [averages[k] for k in here], squares, params, momentum)
-    if late:
-        outs = update(
-            count, late, [averages[k] for k in late], squares, params, momentum, outs
-        )
-    return outs
+    return update(
+        count, range(groups), [averages[k] for k in range(groups)], squares, params, momentum
+    )
 
 
 def solution(mesh):

time: 27 us -> 34.1 us (1.26)
  waiting for transfers between devices: 3.99 us -> 10.6 us
  blocking collectives: 11.8 us -> 13.2 us
  Pallas kernels: 5.26 us -> 4.43 us
    ppermute x6, waiting for transfers between devices: 3.99 us -> 10.6 us  [swapped(): return lax.ppermute(value, axis, [(i, i ^ flip) for i in range(size)])]
    all_to_all x1, blocking collectives: 11.8 us -> 13.2 us  [per_device(): lax.all_to_all(squares, ('replica', 'fsdp'), split_axis=0, concat_axis=0,...]
    pallas_call x2 -> x1, Pallas kernels: 2.43 us -> 1.6 us  [update(): pl.pallas_call(functools.partial(update_kernel, count, flips), out_shape=...]
  transfers between devices with their start and end apart: 6 -> 6, of which waited for: 3 -> 3; matrix products, arithmetic and copies ran while one was open for 0% -> 0% of each run, Pallas kernels for 12% -> 5%
where the time goes in v13:
time: 34.1 us; the launch traced here: 33.9 us
  blocking collectives  13.2 us (39%)
  waiting for transfers between devices  10.6 us (31%)
  starting transfers between devices  5.06 us (15%)
  Pallas kernels  4.43 us (13%)
  between operations  0.65 us (2%)
    all_to_all x1, blocking collectives, per_device(): lax.all_to_all(squares, ('replica', 'fsdp'), split_axis=0, concat_axis=0,...  13.2 us
    ppermute x6, waiting for transfers between devices, swapped(): return lax.ppermute(value, axis, [(i, i ^ flip) for i in range(size)])  10.6 us
    ppermute x6, starting transfers between devices, swapped(): return lax.ppermute(value, axis, [(i, i ^ flip) for i in range(size)])  5.06 us
    pallas_call x2, Pallas kernels, cut(): pl.pallas_call(functools.partial(cut_kernel, flips, len(arrays)), out_sha...  2.72 us
    pallas_call x1, Pallas kernels, update(): pl.pallas_call(functools.partial(update_kernel, count, flips), out_shape=...  1.6 us
  transfers between devices with their start and end apart: 6, of which 3 were waited for; matrix products, arithmetic and copies ran while one was open for 0% of the time, Pallas kernels for 5%

profile of v13, /device:TPU:0, one launch (start us, length us, event | category | flops | bytes accessed | tf_op | source)
XLA Modules:
  0.0 33.9 jit_solution(16364457953817786025)
XLA Ops:
  0.6 1.0 %shard_map.50 = (bf16[32,2048]{1,0:T(8,128)(2,1)S(1)}, bf16[32,2048]{1,0:T(8,128)(2,1)S(1)}) custom-call(bf16[1,32,8192]{2,1,0:T(8,128)(2,1)} %refs_0_.2), custom_call_target="tpu_custom_call" | custom-call | tf_op jit(solution)/shard_map/pallas_call | solution.py:50
  1.6 3.0 %collective-permute-start.1 = (bf16[32,2048]{1,0:T(8,128)(2,1)S(1)}, bf16[32,2048]{1,0:T(8,128)(2,1)S(1)}, u32[]{:S(2)}, u32[]{:S(2)}) collective-permute-start(bf16[32,2048]{1,0:T(8,128)(2,1)S(1)} %get-tuple-element.22), channel_id=1, source_target_pairs={{0,16},{8,24},{16,0},{24,8},{1,17},{9,25},{17,1},{25,9},{2,18},{10... | collective-permute-start | bytes 393224 | tf_op jit(solution)/shard_map/ppermute | solution.py:18
  4.6 0.0 collective-permute-start.2
  4.6 1.7 %shard_map.51 = (bf16[32,2048]{1,0:T(8,128)(2,1)S(1)}, bf16[32,2048]{1,0:T(8,128)(2,1)S(1)}, f32[32,8192]{1,0:T(8,128)S(1)}, f32[32,8192]{1,0:T(8,128)S(1)}) custom-call(bf16[1,32,8192]{2,1,0:T(8,128)(2,1)} %refs_0_.2, f32[32,8192]{1,0:T(8,128)} %refs_1_, f32[32,8192]{1,0:T(8,128)} %refs_2_), custom_call_target="tpu_custom_call" | custom-call | tf_op jit(solution)/shard_map/pallas_call | solution.py:50
  6.4 0.3 collective-permute-start
  6.6 2.0 %collective-permute-done.1.refs_2_ = bf16[32,2048]{1,0:T(8,128)(2,1)S(1)} collective-permute-done((bf16[32,2048]{1,0:T(8,128)(2,1)S(1)}, bf16[32,2048]{1,0:T(8,128)(2,1)S(1)}, u32[]{:S(2)}, u32[]{:S(2)}) %collective-permute-start.1) | collective-permute-done | bytes 131104 | tf_op jit(solution)/shard_map/ppermute | solution.py:18
  8.6 1.9 %collective-permute-done.2.refs_3_ = bf16[32,2048]{1,0:T(8,128)(2,1)S(1)} collective-permute-done((bf16[32,2048]{1,0:T(8,128)(2,1)S(1)}, bf16[32,2048]{1,0:T(8,128)(2,1)S(1)}, u32[]{:S(2)}, u32[]{:S(2)}) %collective-permute-start.2) | collective-permute-done | bytes 131104 | tf_op jit(solution)/shard_map/ppermute | solution.py:18
  10.5 0.0 collective-permute-done.refs_1_
  10.5 0.1 shard_map.52
  10.6 1.1 %collective-permute-start.4 = (f32[32,2048]{1,0:T(8,128)S(1)}, f32[32,2048]{1,0:T(8,128)S(1)}, u32[]{:S(2)}, u32[]{:S(2)}) collective-permute-start(f32[32,2048]{1,0:T(8,128)S(1)} %get-tuple-element.27.refs_0_), channel_id=1, source_target_pairs={{0,16},{8,24},{16,0},{24,8},{1,17},{9,25},{17,1},{25,9},{2,18},{10... | collective-permute-start | bytes 786440 | tf_op jit(solution)/shard_map/ppermute | solution.py:18
  11.7 0.7 %collective-permute-start.3 = (f32[32,2048]{1,0:T(8,128)S(1)}, f32[32,2048]{1,0:T(8,128)S(1)}, u32[]{:S(2)}, u32[]{:S(2)}) collective-permute-start(f32[32,2048]{1,0:T(8,128)S(1)} %get-tuple-element.27.refs_0_), channel_id=1, source_target_pairs={{0,8},{8,0},{16,24},{24,16},{1,9},{9,1},{17,25},{25,17},{2,10},{10... | collective-permute-start | bytes 786440 | tf_op jit(solution)/shard_map/ppermute | solution.py:18
  12.4 6.8 %collective-permute-done.4.refs_2_ = f32[32,2048]{1,0:T(8,128)S(1)} collective-permute-done((f32[32,2048]{1,0:T(8,128)S(1)}, f32[32,2048]{1,0:T(8,128)S(1)}, u32[]{:S(2)}, u32[]{:S(2)}) %collective-permute-start.4) | collective-permute-done | bytes 262176 | tf_op jit(solution)/shard_map/ppermute | solution.py:18
  19.2 0.0 collective-permute-start.5
  19.2 13.2 %all_to_all.5.squares = f32[32,1,128]{2,1,0:T(1,128)S(1)} all-to-all(f32[32,1,128]{2,1,0:T(1,128)S(1)} %get-tuple-element.24), channel_id=1, replica_groups=mesh['replica'=4,'fsdp'=8] {'replica','fsdp'}, dimensions={0} | all-to-all | bytes 32768 | tf_op jit(solution)/shard_map/all_to_all | solution.py:141
  32.3 0.0 collective-permute-done.3.refs_1_
  32.3 0.0 collective-permute-done.5.refs_3_
  32.3 1.6 %shard_map.53 = (f32[32,8192]{1,0:T(8,128)}, f32[32,8192]{1,0:T(8,128)}) custom-call(f32[32,1,128]{2,1,0:T(1,128)S(1)} %all_to_all.5.squares, f32[32,8192]{1,0:T(8,128)S(1)} %get-tuple-element.25.params, f32[32,8192]{1,0:T(8,128)S(1)} %get-tuple-element.26.momentum, f32[32,2048]{1,0:T(8,128)S(1)} %get-tuple-element.27.refs_0_, ...), custom_call_target="tpu_custom_call" | custom-call | tf_op jit(solution)/shard_map/pallas_call | solution.py:99
Async XLA Ops:
  1.6 6.9 %collective-permute-start.1 = (bf16[32,2048]{1,0:T(8,128)(2,1)S(1)}, bf16[32,2048]{1,0:T(8,128)(2,1)S(1)}, u32[]{:S(2)}, u32[]{:S(2)}) collective-permute-start(bf16[32,2048]{1,0:T(8,128)(2,1)S(1)} %get-tuple-element.22), channel_id=1, source_target_pairs={{0,16},{8,24},{16,0},{24,8},{1,17},{9,25},{17,1},{25,9},{2,18},{10... | collective-permute-start | bytes 393224 | tf_op jit(solution)/shard_map/ppermute | solution.py:18
  4.6 5.9 %collective-permute-start.2 = (bf16[32,2048]{1,0:T(8,128)(2,1)S(1)}, bf16[32,2048]{1,0:T(8,128)(2,1)S(1)}, u32[]{:S(2)}, u32[]{:S(2)}) collective-permute-start(bf16[32,2048]{1,0:T(8,128)(2,1)S(1)} %get-tuple-element.23), channel_id=1, source_target_pairs={{0,24},{8,16},{16,8},{24,0},{1,25},{9,17},{17,9},{25,1},{2,26},{10... | collective-permute-start | bytes 393224 | tf_op jit(solution)/shard_map/ppermute | solution.py:18
  6.4 4.1 %collective-permute-start = (bf16[32,2048]{1,0:T(8,128)(2,1)S(1)}, bf16[32,2048]{1,0:T(8,128)(2,1)S(1)}, u32[]{:S(2)}, u32[]{:S(2)}) collective-permute-start(bf16[32,2048]{1,0:T(8,128)(2,1)S(1)} %get-tuple-element.21), channel_id=1, source_target_pairs={{0,8},{8,0},{16,24},{24,16},{1,9},{9,1},{17,25},{25,17},{2,10},{10... | collective-permute-start | bytes 393224 | tf_op jit(solution)/shard_map/ppermute | solution.py:18
  10.6 8.5 %collective-permute-start.4 = (f32[32,2048]{1,0:T(8,128)S(1)}, f32[32,2048]{1,0:T(8,128)S(1)}, u32[]{:S(2)}, u32[]{:S(2)}) collective-permute-start(f32[32,2048]{1,0:T(8,128)S(1)} %get-tuple-element.27.refs_0_), channel_id=1, source_target_pairs={{0,16},{8,24},{16,0},{24,8},{1,17},{9,25},{17,1},{25,9},{2,18},{10... | collective-permute-start | bytes 786440 | tf_op jit(solution)/shard_map/ppermute | solution.py:18
  11.7 20.6 %collective-permute-start.3 = (f32[32,2048]{1,0:T(8,128)S(1)}, f32[32,2048]{1,0:T(8,128)S(1)}, u32[]{:S(2)}, u32[]{:S(2)}) collective-permute-start(f32[32,2048]{1,0:T(8,128)S(1)} %get-tuple-element.27.refs_0_), channel_id=1, source_target_pairs={{0,8},{8,0},{16,24},{24,16},{1,9},{9,1},{17,25},{25,17},{2,10},{10... | collective-permute-start | bytes 786440 | tf_op jit(solution)/shard_map/ppermute | solution.py:18
  19.2 13.2 %collective-permute-start.5 = (f32[32,2048]{1,0:T(8,128)S(1)}, f32[32,2048]{1,0:T(8,128)S(1)}, u32[]{:S(2)}, u32[]{:S(2)}) collective-permute-start(f32[32,2048]{1,0:T(8,128)S(1)} %collective-permute-done.4.refs_2_), channel_id=1, source_target_pairs={{0,8},{8,0},{16,24},{24,16},{1,9},{9,1},{17,25},{25,17},{2,10},{10... | collective-permute-start | bytes 786440 | tf_op jit(solution)/shard_map/ppermute | solution.py:18

commit v14 on v12

--- a/solution.py
+++ b/solution.py
@@ -46,7 +46,9 @@
     scale = code[:, width : width + 1].astype(WIDE)
     power = code[:, :width].astype(WIDE)
     size = jnp.abs(power)
-    root = jnp.exp(jnp.log(jnp.maximum(size, KNEE**16)) * (1 / 16))
+    root = jnp.maximum(size, KNEE**16)
+    for _ in range(4):
+        root = lax.rsqrt(root)
     unit = jnp.where(size < KNEE**16, size * KNEE**-15, root) * (scale * (1 / TOP))
     return jnp.where(power < 0, -unit, unit)
 
@@ -129,16 +131,29 @@
     squares_of(mean, squares)
 
 
-def pair_kernel(own, mate, first, second, sums):
-    for i, code in enumerate((first, second)):
-        code[...] = encode(own[i].astype(WIDE) + mate[i].astype(WIDE))
-        sums[i] = decode(code[...])
-
-
-def join_kernel(groups, sums, code, average, squares):
-    mean = (sums[0] + decode(code[...])) / WIDE(groups)
+def pair_sum(own, mate, i):
+    return own[i].astype(WIDE) + mate[i].astype(WIDE)
+
+
+def urgent_kernel(own, mate, code):
+    code[...] = encode(pair_sum(own, mate, 1))
+
+
+def pair_kernel(own, mate, urgent, code, sum_own, sum_far):
+    code[...] = encode(pair_sum(own, mate, 0))
+    sum_own[...] = decode(code[...])
+    sum_far[...] = decode(urgent[...])
+
+
+def first_kernel(groups, sums, code, average, squares):
+    mean = (sums[...] + decode(code[...])) / WIDE(groups)
     average[...] = mean
     squares_of(mean, squares)
+
+
+def join_kernel(groups, *refs):
+    for sums, code, average in zip(refs[:3], refs[3:6], refs[6:]):
+        average[...] = (sums[...] + decode(code[...])) / WIDE(groups)
 
 
 def write_out(count, flips, means, squares, params, momentum, refs):
@@ -168,19 +183,6 @@
     write_out(count, flips, means, squares, params, momentum, refs[len(flips) + passed :])
 
 
-def final_kernel(count, groups, squares, params, momentum, average, own, mate, one, two, three, *refs):
-    def joined(sums, i, code):
-        return lambda: (sums[i] + decode(code[...])) / WIDE(groups)
-
-    means = [
-        functools.partial(average.__getitem__, ...),
-        joined(mate, 0, one),
-        joined(own, 1, two),
-        joined(mate, 1, three),
-    ]
-    write_out(count, range(groups), means, squares, params, momentum, refs)
-
-
 def update(kernel, flips, width, args, earlier=()):
     shape = args[1].shape
     out = jax.ShapeDtypeStruct(shape, WIDE)
@@ -209,34 +211,37 @@
     groups = lax.axis_size("replica")
     rows = params.shape[0]
     code = jax.ShapeDtypeStruct((rows, width + SIDE), jnp.bfloat16)
-    sums = jax.ShapeDtypeStruct((2, rows, width), WIDE)
+    piece = jax.ShapeDtypeStruct((rows, width), WIDE)
     own, others = cut(pseudo_grad, width, (0, 2), (1, 3))
     mate = swapped(others, "replica", 1)
-    code_own, code_far, own_sums = call(pair_kernel, [code, code, sums], own, mate)
+    (code_far,) = call(urgent_kernel, [code], own, mate)
     urgent = swapped(code_far, "replica", 2)
-    mate_sums = swapped(own_sums, "replica", 1)
-    code_own, code_far, params, momentum = lax.optimization_barrier(
-        (code_own, code_far, params, momentum)
+    own, mate, code_far, params, momentum = lax.optimization_barrier(
+        (own, mate, code_far, params, momentum)
     )
     params, momentum = read(params, momentum)
-    code_own, code_far, params, momentum = lax.optimization_barrier(
-        (code_own, code_far, params, momentum)
-    )
+    own, mate, code_far, params, momentum = lax.optimization_barrier(
+        (own, mate, code_far, params, momentum)
+    )
+    code_own, sum_own, sum_far = call(
+        pair_kernel, [code, piece, piece], own, mate, code_far
+    )
+    mate_own, mate_far = (swapped(x, "replica", 1) for x in (sum_own, sum_far))
     one = swapped(code_far, "replica", 3)
     two = swapped(code_own, "replica", 2)
     three = swapped(code_own, "replica", 3)
     average, squares = call(
-        functools.partial(join_kernel, groups),
-        [jax.ShapeDtypeStruct((rows, width), WIDE), square_rows],
-        own_sums, urgent,
+        functools.partial(first_kernel, groups), [piece, square_rows], sum_own, urgent
     )
     squares = all_squares(squares)
-    squares, one, two, three, mate_sums = lax.optimization_barrier(
-        (squares, one, two, three, mate_sums)
-    )
+    joined = call(
+        functools.partial(join_kernel, groups), [piece] * 3,
+        mate_own, sum_far, mate_far, one, two, three,
+    )
+    flips = range(groups)
     return update(
-        functools.partial(final_kernel, count, groups), range(groups), width,
-        (squares, params, momentum, average, own_sums, mate_sums, one, two, three),
+        functools.partial(update_kernel, count, flips, 0), flips, width,
+        (squares, params, momentum, average, *joined),
     )
 
 

time: 29.9 us -> 29.7 us (level)
  waiting for transfers between devices: 9.07 us -> 4.35 us
  local copies, waits for them, and re-layouts: 0.59 us -> 3.89 us
  Pallas kernels: 7.16 us -> 8.47 us
  starting transfers between devices: 12.2 us -> 11.9 us
    all_to_all x1, waiting for transfers between devices: 5.1 us -> 0.01 us  [all_squares(): lax.all_to_all(squares, ('replica', 'fsdp'), split_axis=0, concat_axis=0,...]
    unnamed x2 -> x10, local copies, waits for them, and re-layouts: 0.59 us -> 3.89 us
    pallas_call x4 -> x6, Pallas kernels: 4.2 us -> 6.15 us  [call(): pl.pallas_call(kernel, out_shape=out_shape, in_specs=[HBM if held else VM...]
    pallas_call x1, Pallas kernels: 2.96 us -> 2.32 us  [update(): pl.pallas_call(kernel, out_shape=[out, out], in_specs=[VMEM] * len(args)...]
    all_to_all x1, starting transfers between devices: 6.78 us -> 6.2 us  [all_squares(): lax.all_to_all(squares, ('replica', 'fsdp'), split_axis=0, concat_axis=0,...]
    ppermute x6 -> x7, waiting for transfers between devices: 3.97 us -> 4.34 us  [swapped(): return lax.ppermute(value, axis, [(i, i ^ flip) for i in range(size)])]
    ppermute x6 -> x7, starting transfers between devices: 5.37 us -> 5.73 us  [swapped(): return lax.ppermute(value, axis, [(i, i ^ flip) for i in range(size)])]
  transfers between devices with their start and end apart: 7 -> 8, of which waited for: 4 -> 3; matrix products, arithmetic and copies ran while one was open for 0% -> 0% of each run, Pallas kernels for 6% -> 16%
where the time goes in v14:
time: 29.7 us; the launch traced here: 29.3 us
  starting transfers between devices  11.9 us (40%)
  Pallas kernels  8.47 us (29%)
  waiting for transfers between devices  4.35 us (15%)
  local copies, waits for them, and re-layouts  3.89 us (13%)
  between operations  0.7 us (2%)
    all_to_all x1, starting transfers between devices, all_squares(): lax.all_to_all(squares, ('replica', 'fsdp'), split_axis=0, concat_axis=0,...  6.2 us
    pallas_call x6, Pallas kernels, call(): pl.pallas_call(kernel, out_shape=out_shape, in_specs=[HBM if held else VM...  6.15 us
    ppermute x7, starting transfers between devices, swapped(): return lax.ppermute(value, axis, [(i, i ^ flip) for i in range(size)])  5.73 us
    ppermute x7, waiting for transfers between devices, swapped(): return lax.ppermute(value, axis, [(i, i ^ flip) for i in range(size)])  4.34 us
    unnamed x10, local copies, waits for them, and re-layouts  3.89 us
    pallas_call x1, Pallas kernels, update(): pl.pallas_call(kernel, out_shape=[out, out], in_specs=[VMEM] * len(args)...  2.32 us
  transfers between devices with their start and end apart: 8, of which 3 were waited for; matrix products, arithmetic and copies ran while one was open for 0% of the time, Pallas kernels for 16%

profile of v14, /device:TPU:0, one launch (start us, length us, event | category | flops | bytes accessed | tf_op | source)
XLA Modules:
  0.0 29.3 jit_solution(7546808901453921330)
XLA Ops:
  0.6 1.1 %shard_map.50 = (bf16[2,32,2048]{2,1,0:T(8,128)(2,1)S(1)}, bf16[2,32,2048]{2,1,0:T(8,128)(2,1)S(1)}) custom-call(bf16[1,32,8192]{2,1,0:T(8,128)(2,1)} %grad.1), custom_call_target="tpu_custom_call" | custom-call | tf_op jit(solution)/shard_map/pallas_call | solution.py:94
  1.8 0.5 %collective-permute-start = (bf16[2,32,2048]{2,1,0:T(8,128)(2,1)S(1)}, bf16[2,32,2048]{2,1,0:T(8,128)(2,1)S(1)}, u32[]{:S(2)}, u32[]{:S(2)}) collective-permute-start(bf16[2,32,2048]{2,1,0:T(8,128)(2,1)S(1)} %get-tuple-element.25), channel_id=1, source_target_pairs={{0,8},{8,0},{16,24},{24,16},{1,9},{9,1},{17,25},{25,17},{2,10},{10... | collective-permute-start | bytes 786440 | tf_op jit(solution)/shard_map/ppermute | solution.py:18
  2.3 1.2 %collective-permute-done.mate = bf16[2,32,2048]{2,1,0:T(8,128)(2,1)S(1)} collective-permute-done((bf16[2,32,2048]{2,1,0:T(8,128)(2,1)S(1)}, bf16[2,32,2048]{2,1,0:T(8,128)(2,1)S(1)}, u32[]{:S(2)}, u32[]{:S(2)}) %collective-permute-start) | collective-permute-done | bytes 262176 | tf_op jit(solution)/shard_map/ppermute | solution.py:18
  3.5 0.2 shard_map.51.urgent
  3.7 2.9 %collective-permute-start.1 = (bf16[32,2176]{1,0:T(8,128)(2,1)S(1)}, bf16[32,2176]{1,0:T(8,128)(2,1)S(1)}, u32[]{:S(2)}, u32[]{:S(2)}) collective-permute-start(bf16[32,2176]{1,0:T(8,128)(2,1)S(1)} %shard_map.51.urgent), channel_id=1, source_target_pairs={{0,16},{8,24},{16,0},{24,8},{1,17},{9,25},{17,1},{25,9},{2,18},{10... | collective-permute-start | bytes 417800 | tf_op jit(solution)/shard_map/ppermute | solution.py:18
  6.6 1.6 %shard_map.52 = (f32[32,8192]{1,0:T(8,128)S(1)}, f32[32,8192]{1,0:T(8,128)S(1)}) custom-call(f32[32,8192]{1,0:T(8,128)} %refs_0_, f32[32,8192]{1,0:T(8,128)} %refs_1_), custom_call_target="tpu_custom_call" | custom-call | tf_op jit(solution)/shard_map/pallas_call | solution.py:94
  8.2 1.1 %shard_map.53 = (bf16[32,2176]{1,0:T(8,128)(2,1)}, f32[32,2048]{1,0:T(8,128)S(1)}, f32[32,2048]{1,0:T(8,128)S(1)}) custom-call(bf16[2,32,2048]{2,1,0:T(8,128)(2,1)S(1)} %get-tuple-element.33.own, bf16[2,32,2048]{2,1,0:T(8,128)(2,1)S(1)} %collective-permute-done.mate, bf16[32,2176]{1,0:T(8,128)(2,1)S(1)} %shard_map.51.urgent), custom_call_target="tpu_custom_call" | custom-call | tf_op jit(solution)/shard_map/pallas_call | solution.py:94
  9.3 0.0 collective-permute-start.2
  9.3 0.5 %collective-permute-start.3 = (f32[32,2048]{1,0:T(8,128)S(1)}, f32[32,2048]{1,0:T(8,128)S(1)}, u32[]{:S(2)}, u32[]{:S(2)}) collective-permute-start(f32[32,2048]{1,0:T(8,128)S(1)} %get-tuple-element.41.refs_1_), channel_id=1, source_target_pairs={{0,8},{8,0},{16,24},{24,16},{1,9},{9,1},{17,25},{25,17},{2,10},{10... | collective-permute-start | bytes 786440 | tf_op jit(solution)/shard_map/ppermute | solution.py:18
  9.9 0.0 collective-permute-start.6
  9.9 1.6 %collective-permute-start.5 = (bf16[32,2176]{1,0:T(8,128)(2,1)}, bf16[32,2176]{1,0:T(8,128)(2,1)}, u32[]{:S(2)}, u32[]{:S(2)}) collective-permute-start(bf16[32,2176]{1,0:T(8,128)(2,1)} %get-tuple-element.42), channel_id=1, source_target_pairs={{0,16},{8,24},{16,0},{24,8},{1,17},{9,25},{17,1},{25,9},{2,18},{10... | collective-permute-start | bytes 417800 | tf_op jit(solution)/shard_map/ppermute | solution.py:18
  11.5 0.0 collective-permute-done.1.code
  11.5 0.1 collective-permute-start.4
  11.6 0.3 %shard_map.54 = (f32[32,2048]{1,0:T(8,128)S(1)}, f32[32,1,128]{2,1,0:T(1,128)S(1)}) custom-call(f32[32,2048]{1,0:T(8,128)S(1)} %get-tuple-element.36.sums, bf16[32,2176]{1,0:T(8,128)(2,1)S(1)} %collective-permute-done.1.code), custom_call_target="tpu_custom_call" | custom-call | tf_op jit(solution)/shard_map/pallas_call | solution.py:94
  11.9 0.0 copy-start.4
  11.9 0.6 %copy-done.4 = f32[32,1,128]{2,1,0:T(1,128)} copy-done((f32[32,1,128]{2,1,0:T(1,128)}, f32[32,1,128]{2,1,0:T(1,128)S(1)}, u32[]{:S(2)}) %copy-start.4) | copy-done | bytes 16408
  12.5 6.2 %all-to-all-start = ((f32[32,1,128]{2,1,0:T(1,128)}), f32[32,1,128]{2,1,0:T(1,128)}, u32[]{:S(2)}, u32[]{:S(2)}) async-start(f32[32,1,128]{2,1,0:T(1,128)} %copy-done.4), calls=%async_computation | async-start | bytes 32768 | tf_op jit(solution)/shard_map/all_to_all | solution.py:205
  18.7 0.0 collective-permute-done.6.refs_5_
  18.8 0.6 %collective-permute-done.5.refs_4_ = bf16[32,2176]{1,0:T(8,128)(2,1)} collective-permute-done((bf16[32,2176]{1,0:T(8,128)(2,1)}, bf16[32,2176]{1,0:T(8,128)(2,1)}, u32[]{:S(2)}, u32[]{:S(2)}) %collective-permute-start.5) | collective-permute-done | bytes 139296 | tf_op jit(solution)/shard_map/ppermute | solution.py:18
  19.3 2.6 %collective-permute-done.4.refs_3_ = bf16[32,2176]{1,0:T(8,128)(2,1)} collective-permute-done((bf16[32,2176]{1,0:T(8,128)(2,1)S(1)}, bf16[32,2176]{1,0:T(8,128)(2,1)}, u32[]{:S(2)}, u32[]{:S(2)}) %collective-permute-start.4) | collective-permute-done | bytes 139296 | tf_op jit(solution)/shard_map/ppermute | solution.py:18
  21.9 0.0 collective-permute-done.2.refs_0_
  21.9 0.0 copy-start
  21.9 0.7 %copy-done = f32[32,2048]{1,0:T(8,128)} copy-done((f32[32,2048]{1,0:T(8,128)}, f32[32,2048]{1,0:T(8,128)S(1)}, u32[]{:S(2)}) %copy-start) | copy-done | bytes 262168
  22.6 0.0 collective-permute-done.3.refs_2_
  22.6 0.0 copy-start.2
  22.6 0.7 %copy-done.2 = f32[32,2048]{1,0:T(8,128)} copy-done((f32[32,2048]{1,0:T(8,128)}, f32[32,2048]{1,0:T(8,128)S(1)}, u32[]{:S(2)}) %copy-start.2) | copy-done | bytes 262168
  23.3 0.0 copy-start.1
  23.3 0.9 %copy-done.1 = f32[32,2048]{1,0:T(8,128)S(1)} copy-done((f32[32,2048]{1,0:T(8,128)S(1)}, f32[32,2048]{1,0:T(8,128)}, u32[]{:S(2)}) %copy-start.1) | copy-done | bytes 262168
  24.3 0.0 copy-start.3
  24.3 0.9 %copy-done.3 = f32[32,2048]{1,0:T(8,128)S(1)} copy-done((f32[32,2048]{1,0:T(8,128)S(1)}, f32[32,2048]{1,0:T(8,128)}, u32[]{:S(2)}) %copy-start.3) | copy-done | bytes 262168
  25.2 1.8 %shard_map.55 = (f32[32,2048]{1,0:T(8,128)S(1)}, f32[32,2048]{1,0:T(8,128)S(1)}, f32[32,2048]{1,0:T(8,128)S(1)}) custom-call(f32[32,2048]{1,0:T(8,128)S(1)} %copy-done.1, f32[32,2048]{1,0:T(8,128)S(1)} %get-tuple-element.41.refs_1_, f32[32,2048]{1,0:T(8,128)S(1)} %copy-done.3, bf16[32,2176]{1,0:T(8,128)(2,1)} %collective-permute-done.4.refs_3_, ...), custom_call_target="tpu_custom_call" | custom-call | tf_op jit(solution)/shard_map/pallas_call | solution.py:94
  27.0 0.0 all-to-all-done.squares
  27.0 2.3 %shard_map.56 = (f32[32,8192]{1,0:T(8,128)}, f32[32,8192]{1,0:T(8,128)}) custom-call(f32[32,1,128]{2,1,0:T(1,128)} %all-to-all-done.squares, f32[32,8192]{1,0:T(8,128)S(1)} %get-tuple-element.38.params, f32[32,8192]{1,0:T(8,128)S(1)} %get-tuple-element.39.momentum, f32[32,2048]{1,0:T(8,128)S(1)} %get-tuple-element.40.refs_0_, ...), custom_call_target="tpu_custom_call" | custom-call | tf_op jit(solution)/shard_map/pallas_call | solution.py:189
Async XLA Ops:
  1.8 1.7 %collective-permute-start = (bf16[2,32,2048]{2,1,0:T(8,128)(2,1)S(1)}, bf16[2,32,2048]{2,1,0:T(8,128)(2,1)S(1)}, u32[]{:S(2)}, u32[]{:S(2)}) collective-permute-start(bf16[2,32,2048]{2,1,0:T(8,128)(2,1)S(1)} %get-tuple-element.25), channel_id=1, source_target_pairs={{0,8},{8,0},{16,24},{24,16},{1,9},{9,1},{17,25},{25,17},{2,10},{10... | collective-permute-start | bytes 786440 | tf_op jit(solution)/shard_map/ppermute | solution.py:18
  3.7 7.8 %collective-permute-start.1 = (bf16[32,2176]{1,0:T(8,128)(2,1)S(1)}, bf16[32,2176]{1,0:T(8,128)(2,1)S(1)}, u32[]{:S(2)}, u32[]{:S(2)}) collective-permute-start(bf16[32,2176]{1,0:T(8,128)(2,1)S(1)} %shard_map.51.urgent), channel_id=1, source_target_pairs={{0,16},{8,24},{16,0},{24,8},{1,17},{9,25},{17,1},{25,9},{2,18},{10... | collective-permute-start | bytes 417800 | tf_op jit(solution)/shard_map/ppermute | solution.py:18
  9.3 12.6 %collective-permute-start.2 = (f32[32,2048]{1,0:T(8,128)S(1)}, f32[32,2048]{1,0:T(8,128)S(1)}, u32[]{:S(2)}, u32[]{:S(2)}) collective-permute-start(f32[32,2048]{1,0:T(8,128)S(1)} %get-tuple-element.36.sums), channel_id=1, source_target_pairs={{0,8},{8,0},{16,24},{24,16},{1,9},{9,1},{17,25},{25,17},{2,10},{10... | collective-permute-start | bytes 786440 | tf_op jit(solution)/shard_map/ppermute | solution.py:18
  9.3 13.3 %collective-permute-start.3 = (f32[32,2048]{1,0:T(8,128)S(1)}, f32[32,2048]{1,0:T(8,128)S(1)}, u32[]{:S(2)}, u32[]{:S(2)}) collective-permute-start(f32[32,2048]{1,0:T(8,128)S(1)} %get-tuple-element.41.refs_1_), channel_id=1, source_target_pairs={{0,8},{8,0},{16,24},{24,16},{1,9},{9,1},{17,25},{25,17},{2,10},{10... | collective-permute-start | bytes 786440 | tf_op jit(solution)/shard_map/ppermute | solution.py:18
  9.9 8.9 %collective-permute-start.6 = (bf16[32,2176]{1,0:T(8,128)(2,1)}, bf16[32,2176]{1,0:T(8,128)(2,1)}, u32[]{:S(2)}, u32[]{:S(2)}) collective-permute-start(bf16[32,2176]{1,0:T(8,128)(2,1)} %get-tuple-element.42), channel_id=1, source_target_pairs={{0,24},{8,16},{16,8},{24,0},{1,25},{9,17},{17,9},{25,1},{2,26},{10... | collective-permute-start | bytes 417800 | tf_op jit(solution)/shard_map/ppermute | solution.py:18
  9.9 9.5 %collective-permute-start.5 = (bf16[32,2176]{1,0:T(8,128)(2,1)}, bf16[32,2176]{1,0:T(8,128)(2,1)}, u32[]{:S(2)}, u32[]{:S(2)}) collective-permute-start(bf16[32,2176]{1,0:T(8,128)(2,1)} %get-tuple-element.42), channel_id=1, source_target_pairs={{0,16},{8,24},{16,0},{24,8},{1,17},{9,25},{17,1},{25,9},{2,18},{10... | collective-permute-start | bytes 417800 | tf_op jit(solution)/shard_map/ppermute | solution.py:18
  11.5 10.4 %collective-permute-start.4 = (bf16[32,2176]{1,0:T(8,128)(2,1)S(1)}, bf16[32,2176]{1,0:T(8,128)(2,1)}, u32[]{:S(2)}, u32[]{:S(2)}) collective-permute-start(bf16[32,2176]{1,0:T(8,128)(2,1)S(1)} %shard_map.51.urgent), channel_id=1, source_target_pairs={{0,24},{8,16},{16,8},{24,0},{1,25},{9,17},{17,9},{25,1},{2,26},{10... | collective-permute-start | bytes 417800 | tf_op jit(solution)/shard_map/ppermute | solution.py:18
  11.9 0.6 %copy-start.4 = (f32[32,1,128]{2,1,0:T(1,128)}, f32[32,1,128]{2,1,0:T(1,128)S(1)}, u32[]{:S(2)}) copy-start(f32[32,1,128]{2,1,0:T(1,128)S(1)} %get-tuple-element.37) | copy-start | bytes 49156
  12.5 14.5 %all-to-all-start = ((f32[32,1,128]{2,1,0:T(1,128)}), f32[32,1,128]{2,1,0:T(1,128)}, u32[]{:S(2)}, u32[]{:S(2)}) async-start(f32[32,1,128]{2,1,0:T(1,128)} %copy-done.4), calls=%async_computation | async-start | bytes 32768 | tf_op jit(solution)/shard_map/all_to_all | solution.py:205
  21.9 0.7 %copy-start = (f32[32,2048]{1,0:T(8,128)}, f32[32,2048]{1,0:T(8,128)S(1)}, u32[]{:S(2)}) copy-start(f32[32,2048]{1,0:T(8,128)S(1)} %collective-permute-done.2.refs_0_) | copy-start | bytes 786436
  22.6 0.7 %copy-start.2 = (f32[32,2048]{1,0:T(8,128)}, f32[32,2048]{1,0:T(8,128)S(1)}, u32[]{:S(2)}) copy-start(f32[32,2048]{1,0:T(8,128)S(1)} %collective-permute-done.3.refs_2_) | copy-start | bytes 786436
  23.3 0.9 %copy-start.1 = (f32[32,2048]{1,0:T(8,128)S(1)}, f32[32,2048]{1,0:T(8,128)}, u32[]{:S(2)}) copy-start(f32[32,2048]{1,0:T(8,128)} %copy-done) | copy-start | bytes 786436
  24.3 0.9 %copy-start.3 = (f32[32,2048]{1,0:T(8,128)S(1)}, f32[32,2048]{1,0:T(8,128)}, u32[]{:S(2)}) copy-start(f32[32,2048]{1,0:T(8,128)} %copy-done.2) | copy-start | bytes 786436

commit v15 on v11

--- a/solution.py
+++ b/solution.py
@@ -60,14 +60,18 @@
 
 def average_kernel(*refs):
     pieces, (average, squares) = refs[:-2], refs[-2:]
-    total = tree([piece[...].astype(WIDE) for piece in pieces])
-    mean = total / WIDE(len(pieces))
+    mean = tree([piece[...].astype(WIDE) for piece in pieces]) / WIDE(len(pieces))
     average[...] = mean
     row = jnp.sum(mean * mean, axis=0, keepdims=True)
     lanes = functools.reduce(
         jnp.add, [row[:, i : i + 128] for i in range(0, row.shape[1], 128)]
     )
     squares[...] = jnp.broadcast_to(lanes[None], squares.shape)
+
+
+def join_kernel(*refs):
+    pieces = [piece[...].astype(WIDE) for piece in refs[:-1]]
+    refs[-1][...] = tree(pieces) / WIDE(len(pieces))
 
 
 def update_kernel(count, flips, passed, squares, params, momentum, *refs):
@@ -124,8 +128,17 @@
         (pieces, pseudo_grad, params, momentum)
     )
     moved = {k: swapped(pieces[k], "replica", k) for k in range(2, groups)}
-    near, (params, momentum) = cut(pseudo_grad, width, range(2), params, momentum)
+    near, (params,) = cut(pseudo_grad, width, range(2), params)
     moved.update({0: near[0], 1: swapped(near[1], "replica", 1)})
+    again = {}
+    if groups == 4:
+        near, params, momentum = lax.optimization_barrier((near, params, momentum))
+        _, (momentum,) = cut(pseudo_grad, width, (), momentum)
+        near, params, momentum = lax.optimization_barrier((near, params, momentum))
+        again = {k: swapped(near[k ^ 2], "replica", k) for k in (2, 3)}
+        again[1] = swapped(pieces[3], "replica", 1)
+    else:
+        _, (momentum,) = cut(pseudo_grad, width, (), momentum)
     average, squares = pl.pallas_call(
         average_kernel,
         out_shape=[
@@ -137,16 +150,23 @@
         compiler_params=limit,
     )(*[moved[k] for k in range(groups)])
     averages = {0: average}
-    for k in range(2, groups, 2):
-        averages[k] = swapped(average, "replica", k)
-    averages[1] = swapped(average, "replica", 1)
+    if groups != 4:
+        averages.update({k: swapped(average, "replica", k) for k in range(2, groups, 2)})
     squares = lax.all_to_all(
         squares, ("replica", "fsdp"), split_axis=0, concat_axis=0, tiled=True
     )
-    squares, averages = lax.optimization_barrier((squares, averages))
-    for k in range(2, groups, 2):
+    squares, averages, again = lax.optimization_barrier((squares, averages, again))
+    if groups == 4:
+        averages[2] = pl.pallas_call(
+            join_kernel,
+            out_shape=jax.ShapeDtypeStruct((rows, width), WIDE),
+            in_specs=[VMEM] * groups,
+            out_specs=VMEM,
+            compiler_params=limit,
+        )(again[2], again[3], pieces[2], again[1])
+    for k in range(0, groups, 2):
         averages[k + 1] = swapped(averages[k], "replica", 1)
-    here = [k for k in range(groups) if k < 2 or k % 2 == 0]
+    here = [k for k in range(groups) if k % 2 == 0]
     late = [k for k in range(groups) if k not in here]
     outs = update(count, here, [averages[k] for k in here], squares, params, momentum)
     if late:

time: 27 us -> 27.8 us (1.030)
  blocking collectives: 11.8 us -> 0 us
  starting transfers between devices: 5.06 us -> 12 us
  waiting for transfers between devices: 3.99 us -> 7.92 us
  Pallas kernels: 5.26 us -> 6.91 us
    all_to_all x1 -> x0, blocking collectives: 11.8 us -> none  [per_device(): lax.all_to_all(squares, ('replica', 'fsdp'), split_axis=0, concat_axis=0,...]
    all_to_all x0 -> x1, waiting for transfers between devices: none -> 7.01 us  [per_device(): lax.all_to_all(squares, ('replica', 'fsdp'), split_axis=0, concat_axis=0,...]
    all_to_all x0 -> x1, starting transfers between devices: none -> 5.97 us  [per_device(): lax.all_to_all(squares, ('replica', 'fsdp'), split_axis=0, concat_axis=0,...]
    ppermute x6 -> x8, waiting for transfers between devices: 3.99 us -> 0.91 us  [swapped(): return lax.ppermute(value, axis, [(i, i ^ flip) for i in range(size)])]
    ppermute x6 -> x8, starting transfers between devices: 5.06 us -> 6.04 us  [swapped(): return lax.ppermute(value, axis, [(i, i ^ flip) for i in range(size)])]
    pallas_call x2 -> x3, Pallas kernels: 2.72 us -> 3.62 us  [cut(): pl.pallas_call(functools.partial(cut_kernel, flips, len(arrays)), out_sha...]
    pallas_call x1, Pallas kernels: 0.11 us -> 0.78 us  [per_device(): pl.pallas_call(average_kernel, out_shape=[jax.ShapeDtypeStruct((rows, wid...]
  transfers between devices with their start and end apart: 6 -> 9, of which waited for: 3 -> 3; matrix products, arithmetic and copies ran while one was open for 0% -> 0% of each run, Pallas kernels for 12% -> 17%
where the time goes in v15:
time: 27.8 us; the launch traced here: 27.6 us
  starting transfers between devices  12 us (43%)
  waiting for transfers between devices  7.92 us (28%)
  Pallas kernels  6.91 us (25%)
  between operations  0.72 us (3%)
    all_to_all x1, waiting for transfers between devices, per_device(): lax.all_to_all(squares, ('replica', 'fsdp'), split_axis=0, concat_axis=0,...  7.01 us
    ppermute x8, starting transfers between devices, swapped(): return lax.ppermute(value, axis, [(i, i ^ flip) for i in range(size)])  6.04 us
    all_to_all x1, starting transfers between devices, per_device(): lax.all_to_all(squares, ('replica', 'fsdp'), split_axis=0, concat_axis=0,...  5.97 us
    pallas_call x3, Pallas kernels, cut(): pl.pallas_call(functools.partial(cut_kernel, flips, len(arrays)), out_sha...  3.62 us
    pallas_call x2, Pallas kernels, update(): pl.pallas_call(functools.partial(update_kernel, count, flips, len(earlier...  2.44 us
    ppermute x8, waiting for transfers between devices, swapped(): return lax.ppermute(value, axis, [(i, i ^ flip) for i in range(size)])  0.91 us
    pallas_call x1, Pallas kernels, per_device(): pl.pallas_call(average_kernel, out_shape=[jax.ShapeDtypeStruct((rows, wid...  0.78 us
  transfers between devices with their start and end apart: 9, of which 3 were waited for; matrix products, arithmetic and copies ran while one was open for 0% of the time, Pallas kernels for 17%

profile of v15, /device:TPU:0, one launch (start us, length us, event | category | flops | bytes accessed | tf_op | source)
XLA Modules:
  0.0 27.6 jit_solution(14946200144078189512)
XLA Ops:
  0.6 1.0 %shard_map.50 = (bf16[32,2048]{1,0:T(8,128)(2,1)S(1)}, bf16[32,2048]{1,0:T(8,128)(2,1)S(1)}) custom-call(bf16[1,32,8192]{2,1,0:T(8,128)(2,1)} %refs_0_.3), custom_call_target="tpu_custom_call" | custom-call | tf_op jit(solution)/shard_map/pallas_call | solution.py:50
  1.6 3.0 %collective-permute-start.1 = (bf16[32,2048]{1,0:T(8,128)(2,1)S(1)}, bf16[32,2048]{1,0:T(8,128)(2,1)S(1)}, u32[]{:S(2)}, u32[]{:S(2)}) collective-permute-start(bf16[32,2048]{1,0:T(8,128)(2,1)S(1)} %get-tuple-element.35.refs_2_), channel_id=1, source_target_pairs={{0,16},{8,24},{16,0},{24,8},{1,17},{9,25},{17,1},{25,9},{2,18},{10... | collective-permute-start | bytes 393224 | tf_op jit(solution)/shard_map/ppermute | solution.py:18
  4.6 0.0 collective-permute-start.2
  4.6 1.4 %shard_map.51 = (bf16[32,2048]{1,0:T(8,128)(2,1)S(1)}, bf16[32,2048]{1,0:T(8,128)(2,1)S(1)}, f32[32,8192]{1,0:T(8,128)S(1)}) custom-call(bf16[1,32,8192]{2,1,0:T(8,128)(2,1)} %refs_0_.3, f32[32,8192]{1,0:T(8,128)} %refs_1_), custom_call_target="tpu_custom_call" | custom-call | tf_op jit(solution)/shard_map/pallas_call | solution.py:50
  6.0 0.3 collective-permute-start
  6.3 0.3 %collective-permute-start.3 = (bf16[32,2048]{1,0:T(8,128)(2,1)S(1)}, bf16[32,2048]{1,0:T(8,128)(2,1)S(1)}, u32[]{:S(2)}, u32[]{:S(2)}) collective-permute-start(bf16[32,2048]{1,0:T(8,128)(2,1)S(1)} %get-tuple-element.36), channel_id=1, source_target_pairs={{0,8},{8,0},{16,24},{24,16},{1,9},{9,1},{17,25},{25,17},{2,10},{10... | collective-permute-start | bytes 393224 | tf_op jit(solution)/shard_map/ppermute | solution.py:18
  6.6 1.2 %shard_map.53.momentum = f32[32,8192]{1,0:T(8,128)S(1)} custom-call(bf16[1,32,8192]{2,1,0:T(8,128)(2,1)} %refs_0_.3, f32[32,8192]{1,0:T(8,128)} %refs_1_.1), custom_call_target="tpu_custom_call" | custom-call | tf_op jit(solution)/shard_map/pallas_call | solution.py:50
  7.9 1.8 %collective-permute-start.4 = (bf16[32,2048]{1,0:T(8,128)(2,1)S(1)}, bf16[32,2048]{1,0:T(8,128)(2,1)S(1)}, u32[]{:S(2)}, u32[]{:S(2)}) collective-permute-start(bf16[32,2048]{1,0:T(8,128)(2,1)S(1)} %get-tuple-element.45.refs_0_), channel_id=1, source_target_pairs={{0,16},{8,24},{16,0},{24,8},{1,17},{9,25},{17,1},{25,9},{2,18},{10... | collective-permute-start | bytes 393224 | tf_op jit(solution)/shard_map/ppermute | solution.py:18
  9.6 0.0 collective-permute-done.1.refs_2_
  9.6 0.1 collective-permute-start.5
  9.8 0.7 %collective-permute-done.2.refs_3_ = bf16[32,2048]{1,0:T(8,128)(2,1)S(1)} collective-permute-done((bf16[32,2048]{1,0:T(8,128)(2,1)S(1)}, bf16[32,2048]{1,0:T(8,128)(2,1)S(1)}, u32[]{:S(2)}, u32[]{:S(2)}) %collective-permute-start.2) | collective-permute-done | bytes 131104 | tf_op jit(solution)/shard_map/ppermute | solution.py:18
  10.5 0.0 collective-permute-done.refs_1_
  10.5 0.8 %shard_map.52 = (f32[32,2048]{1,0:T(8,128)S(1)}, f32[32,1,128]{2,1,0:T(1,128)}) custom-call(bf16[32,2048]{1,0:T(8,128)(2,1)S(1)} %get-tuple-element.45.refs_0_, bf16[32,2048]{1,0:T(8,128)(2,1)S(1)} %collective-permute-done.refs_1_, bf16[32,2048]{1,0:T(8,128)(2,1)S(1)} %collective-permute-done.1.refs_2_, bf16[32,2048]{1,0:T(8,128)(2,1)S(1)} %collective-permute-done.2.refs_3_), custom_call_target="tpu_custom_call" | custom-call | tf_op jit(solution)/shard_map/pallas_call | solution.py:142
  11.3 6.0 %all-to-all-start = ((f32[32,1,128]{2,1,0:T(1,128)}), f32[32,1,128]{2,1,0:T(1,128)S(1)}, u32[]{:S(2)}, u32[]{:S(2)}) async-start(f32[32,1,128]{2,1,0:T(1,128)} %get-tuple-element.37), calls=%async_computation | async-start | bytes 32768 | tf_op jit(solution)/shard_map/all_to_all | solution.py:155
  17.3 0.0 collective-permute-done.3.refs_3_
  17.3 0.0 collective-permute-done.4.refs_0_
  17.3 0.0 collective-permute-done.5.refs_1_
  17.3 7.0 %all-to-all-done.squares = f32[32,1,128]{2,1,0:T(1,128)S(1)} async-done(((f32[32,1,128]{2,1,0:T(1,128)}), f32[32,1,128]{2,1,0:T(1,128)S(1)}, u32[]{:S(2)}, u32[]{:S(2)}) %all-to-all-start) | async-done | bytes 16416 | tf_op jit(solution)/shard_map/all_to_all | solution.py:155
  24.3 0.1 shard_map.54.refs_1_
  24.4 0.1 collective-permute-start.7
  24.5 0.5 %collective-permute-start.6 = (f32[32,2048]{1,0:T(8,128)S(1)}, f32[32,2048]{1,0:T(8,128)S(1)}, u32[]{:S(2)}, u32[]{:S(2)}) collective-permute-start(f32[32,2048]{1,0:T(8,128)S(1)} %get-tuple-element.50.refs_0_), channel_id=1, source_target_pairs={{0,8},{8,0},{16,24},{24,16},{1,9},{9,1},{17,25},{25,17},{2,10},{10... | collective-permute-start | bytes 786440 | tf_op jit(solution)/shard_map/ppermute | solution.py:18
  24.9 1.2 %shard_map.55 = (f32[32,8192]{1,0:T(8,128)}, f32[32,8192]{1,0:T(8,128)}) custom-call(f32[32,1,128]{2,1,0:T(1,128)S(1)} %all-to-all-done.squares, f32[32,8192]{1,0:T(8,128)S(1)} %get-tuple-element.48.params, f32[32,8192]{1,0:T(8,128)S(1)} %shard_map.53.momentum, f32[32,2048]{1,0:T(8,128)S(1)} %get-tuple-element.50.refs_0_, f32[32,2048]{1,0:T(8,128)S(1)} %shard_map.54.refs_1_), custom_call_target="tpu_custom_call" | custom-call | tf_op jit(solution)/shard_map/pallas_call | solution.py:104
  26.2 0.0 collective-permute-done.7.refs_1_
  26.2 0.2 collective-permute-done.6.refs_0_
  26.3 1.2 %shard_map.56 = (f32[32,8192]{1,0:T(8,128)}, f32[32,8192]{1,0:T(8,128)}) custom-call(f32[32,1,128]{2,1,0:T(1,128)S(1)} %all-to-all-done.squares, f32[32,8192]{1,0:T(8,128)S(1)} %get-tuple-element.48.params, f32[32,8192]{1,0:T(8,128)S(1)} %shard_map.53.momentum, ...), custom_call_target="tpu_custom_call", output_to_operand_aliasing={{0}: (5, {}), {1}: (6, {})} | custom-call | tf_op jit(solution)/shard_map/pallas_call | solution.py:104
Async XLA Ops:
  1.6 8.0 %collective-permute-start.1 = (bf16[32,2048]{1,0:T(8,128)(2,1)S(1)}, bf16[32,2048]{1,0:T(8,128)(2,1)S(1)}, u32[]{:S(2)}, u32[]{:S(2)}) collective-permute-start(bf16[32,2048]{1,0:T(8,128)(2,1)S(1)} %get-tuple-element.35.refs_2_), channel_id=1, source_target_pairs={{0,16},{8,24},{16,0},{24,8},{1,17},{9,25},{17,1},{25,9},{2,18},{10... | collective-permute-start | bytes 393224 | tf_op jit(solution)/shard_map/ppermute | solution.py:18
  4.6 5.9 %collective-permute-start.2 = (bf16[32,2048]{1,0:T(8,128)(2,1)S(1)}, bf16[32,2048]{1,0:T(8,128)(2,1)S(1)}, u32[]{:S(2)}, u32[]{:S(2)}) collective-permute-start(bf16[32,2048]{1,0:T(8,128)(2,1)S(1)} %get-tuple-element.36), channel_id=1, source_target_pairs={{0,24},{8,16},{16,8},{24,0},{1,25},{9,17},{17,9},{25,1},{2,26},{10... | collective-permute-start | bytes 393224 | tf_op jit(solution)/shard_map/ppermute | solution.py:18
  6.0 4.5 %collective-permute-start = (bf16[32,2048]{1,0:T(8,128)(2,1)S(1)}, bf16[32,2048]{1,0:T(8,128)(2,1)S(1)}, u32[]{:S(2)}, u32[]{:S(2)}) collective-permute-start(bf16[32,2048]{1,0:T(8,128)(2,1)S(1)} %get-tuple-element.46), channel_id=1, source_target_pairs={{0,8},{8,0},{16,24},{24,16},{1,9},{9,1},{17,25},{25,17},{2,10},{10... | collective-permute-start | bytes 393224 | tf_op jit(solution)/shard_map/ppermute | solution.py:18
  6.3 11.0 %collective-permute-start.3 = (bf16[32,2048]{1,0:T(8,128)(2,1)S(1)}, bf16[32,2048]{1,0:T(8,128)(2,1)S(1)}, u32[]{:S(2)}, u32[]{:S(2)}) collective-permute-start(bf16[32,2048]{1,0:T(8,128)(2,1)S(1)} %get-tuple-element.36), channel_id=1, source_target_pairs={{0,8},{8,0},{16,24},{24,16},{1,9},{9,1},{17,25},{25,17},{2,10},{10... | collective-permute-start | bytes 393224 | tf_op jit(solution)/shard_map/ppermute | solution.py:18
  7.9 9.4 %collective-permute-start.4 = (bf16[32,2048]{1,0:T(8,128)(2,1)S(1)}, bf16[32,2048]{1,0:T(8,128)(2,1)S(1)}, u32[]{:S(2)}, u32[]{:S(2)}) collective-permute-start(bf16[32,2048]{1,0:T(8,128)(2,1)S(1)} %get-tuple-element.45.refs_0_), channel_id=1, source_target_pairs={{0,16},{8,24},{16,0},{24,8},{1,17},{9,25},{17,1},{25,9},{2,18},{10... | collective-permute-start | bytes 393224 | tf_op jit(solution)/shard_map/ppermute | solution.py:18
  9.6 7.6 %collective-permute-start.5 = (bf16[32,2048]{1,0:T(8,128)(2,1)S(1)}, bf16[32,2048]{1,0:T(8,128)(2,1)S(1)}, u32[]{:S(2)}, u32[]{:S(2)}) collective-permute-start(bf16[32,2048]{1,0:T(8,128)(2,1)S(1)} %get-tuple-element.46), channel_id=1, source_target_pairs={{0,24},{8,16},{16,8},{24,0},{1,25},{9,17},{17,9},{25,1},{2,26},{10... | collective-permute-start | bytes 393224 | tf_op jit(solution)/shard_map/ppermute | solution.py:18
  11.3 13.0 %all-to-all-start = ((f32[32,1,128]{2,1,0:T(1,128)}), f32[32,1,128]{2,1,0:T(1,128)S(1)}, u32[]{:S(2)}, u32[]{:S(2)}) async-start(f32[32,1,128]{2,1,0:T(1,128)} %get-tuple-element.37), calls=%async_computation | async-start | bytes 32768 | tf_op jit(solution)/shard_map/all_to_all | solution.py:155
  24.4 1.8 %collective-permute-start.7 = (f32[32,2048]{1,0:T(8,128)S(1)}, f32[32,2048]{1,0:T(8,128)S(1)}, u32[]{:S(2)}, u32[]{:S(2)}) collective-permute-start(f32[32,2048]{1,0:T(8,128)S(1)} %shard_map.54.refs_1_), channel_id=1, source_target_pairs={{0,8},{8,0},{16,24},{24,16},{1,9},{9,1},{17,25},{25,17},{2,10},{10... | collective-permute-start | bytes 786440 | tf_op jit(solution)/shard_map/ppermute | solution.py:18
  24.5 1.9 %collective-permute-start.6 = (f32[32,2048]{1,0:T(8,128)S(1)}, f32[32,2048]{1,0:T(8,128)S(1)}, u32[]{:S(2)}, u32[]{:S(2)}) collective-permute-start(f32[32,2048]{1,0:T(8,128)S(1)} %get-tuple-element.50.refs_0_), channel_id=1, source_target_pairs={{0,8},{8,0},{16,24},{24,16},{1,9},{9,1},{17,25},{25,17},{2,10},{10... | collective-permute-start | bytes 786440 | tf_op jit(solution)/shard_map/ppermute | solution.py:18

commit v16 on v15

--- a/solution.py
+++ b/solution.py
@@ -58,9 +58,14 @@
     return dict(zip(flips, outs)), outs[len(flips) :]
 
 
-def average_kernel(*refs):
-    pieces, (average, squares) = refs[:-2], refs[-2:]
-    mean = tree([piece[...].astype(WIDE) for piece in pieces]) / WIDE(len(pieces))
+def average_kernel(groups, *refs):
+    pieces, rest = refs[:groups], refs[groups:]
+    if len(rest) > 2:
+        first, second, average, squares, other_sum = rest
+        other_sum[...] = first[...].astype(WIDE) + second[...].astype(WIDE)
+    else:
+        average, squares = rest
+    mean = tree([piece[...].astype(WIDE) for piece in pieces]) / WIDE(groups)
     average[...] = mean
     row = jnp.sum(mean * mean, axis=0, keepdims=True)
     lanes = functools.reduce(
@@ -69,9 +74,9 @@
     squares[...] = jnp.broadcast_to(lanes[None], squares.shape)
 
 
-def join_kernel(*refs):
-    pieces = [piece[...].astype(WIDE) for piece in refs[:-1]]
-    refs[-1][...] = tree(pieces) / WIDE(len(pieces))
+def join_kernel(groups, here, first, second, average):
+    there = first[...].astype(WIDE) + second[...].astype(WIDE)
+    average[...] = (here[...] + there) / WIDE(groups)
 
 
 def update_kernel(count, flips, passed, squares, params, momentum, *refs):
@@ -139,31 +144,35 @@
         again[1] = swapped(pieces[3], "replica", 1)
     else:
         _, (momentum,) = cut(pseudo_grad, width, (), momentum)
-    average, squares = pl.pallas_call(
-        average_kernel,
-        out_shape=[
-            jax.ShapeDtypeStruct((rows, width), WIDE),
-            jax.ShapeDtypeStruct((devices, 1, 128), WIDE),
-        ],
-        in_specs=[VMEM] * groups,
-        out_specs=[VMEM] * 2,
+    wide_piece = jax.ShapeDtypeStruct((rows, width), WIDE)
+    parts = [moved[k] for k in range(groups)]
+    out_shape = [wide_piece, jax.ShapeDtypeStruct((devices, 1, 128), WIDE)]
+    if groups == 4:
+        parts += [pieces[2], again.pop(1)]
+        out_shape += [wide_piece]
+    average, squares, *other_sum = pl.pallas_call(
+        functools.partial(average_kernel, groups),
+        out_shape=out_shape,
+        in_specs=[VMEM] * len(parts),
+        out_specs=[VMEM] * len(out_shape),
         compiler_params=limit,
-    )(*[moved[k] for k in range(groups)])
+    )(*parts)
     averages = {0: average}
     if groups != 4:
         averages.update({k: swapped(average, "replica", k) for k in range(2, groups, 2)})
     squares = lax.all_to_all(
         squares, ("replica", "fsdp"), split_axis=0, concat_axis=0, tiled=True
     )
-    squares, averages, again = lax.optimization_barrier((squares, averages, again))
+    squares, again = lax.optimization_barrier((squares, again))
     if groups == 4:
         averages[2] = pl.pallas_call(
-            join_kernel,
-            out_shape=jax.ShapeDtypeStruct((rows, width), WIDE),
-            in_specs=[VMEM] * groups,
+            functools.partial(join_kernel, groups),
+            out_shape=wide_piece,
+            in_specs=[VMEM] * 3,
             out_specs=VMEM,
             compiler_params=limit,
-        )(again[2], again[3], pieces[2], again[1])
+        )(*other_sum, again[2], again[3])
+    squares, averages = lax.optimization_barrier((squares, averages))
     for k in range(0, groups, 2):
         averages[k + 1] = swapped(averages[k], "replica", 1)
     here = [k for k in range(groups) if k % 2 == 0]

time: 27.8 us -> 27.8 us (level)
  no operation moved by 1% of the time
where the time goes in v16:
time: 27.8 us; the launch traced here: 27.6 us
  starting transfers between devices  12 us (43%)
  waiting for transfers between devices  7.94 us (29%)
  Pallas kernels  6.89 us (25%)
  between operations  0.71 us (3%)
    all_to_all x1, waiting for transfers between devices, per_device(): lax.all_to_all(squares, ('replica', 'fsdp'), split_axis=0, concat_axis=0,...  7.02 us
    ppermute x8, starting transfers between devices, swapped(): return lax.ppermute(value, axis, [(i, i ^ flip) for i in range(size)])  6.04 us
    all_to_all x1, starting transfers between devices, per_device(): lax.all_to_all(squares, ('replica', 'fsdp'), split_axis=0, concat_axis=0,...  5.97 us
    pallas_call x3, Pallas kernels, cut(): pl.pallas_call(functools.partial(cut_kernel, flips, len(arrays)), out_sha...  3.62 us
    pallas_call x2, Pallas kernels, update(): pl.pallas_call(functools.partial(update_kernel, count, flips, len(earlier...  2.44 us
    ppermute x8, waiting for transfers between devices, swapped(): return lax.ppermute(value, axis, [(i, i ^ flip) for i in range(size)])  0.92 us
    pallas_call x1, Pallas kernels, per_device(): pl.pallas_call(functools.partial(average_kernel, groups), out_shape=out_s...  0.78 us
  transfers between devices with their start and end apart: 9, of which 3 were waited for; matrix products, arithmetic and copies ran while one was open for 0% of the time, Pallas kernels for 17%

profile of v16, /device:TPU:0, one launch (start us, length us, event | category | flops | bytes accessed | tf_op | source)
XLA Modules:
  0.0 27.6 jit_solution(5026392193689957448)
XLA Ops:
  0.6 1.0 %shard_map.50 = (bf16[32,2048]{1,0:T(8,128)(2,1)S(1)}, bf16[32,2048]{1,0:T(8,128)(2,1)S(1)}) custom-call(bf16[1,32,8192]{2,1,0:T(8,128)(2,1)} %refs_0_.3), custom_call_target="tpu_custom_call" | custom-call | tf_op jit(solution)/shard_map/pallas_call | solution.py:50
  1.6 3.0 %collective-permute-start.1 = (bf16[32,2048]{1,0:T(8,128)(2,1)S(1)}, bf16[32,2048]{1,0:T(8,128)(2,1)S(1)}, u32[]{:S(2)}, u32[]{:S(2)}) collective-permute-start(bf16[32,2048]{1,0:T(8,128)(2,1)S(1)} %get-tuple-element.37.refs_4_), channel_id=1, source_target_pairs={{0,16},{8,24},{16,0},{24,8},{1,17},{9,25},{17,1},{25,9},{2,18},{10... | collective-permute-start | bytes 393224 | tf_op jit(solution)/shard_map/ppermute | solution.py:18
  4.6 0.0 collective-permute-start.3
  4.6 0.2 collective-permute-start.2
  4.8 1.4 %shard_map.51 = (bf16[32,2048]{1,0:T(8,128)(2,1)S(1)}, bf16[32,2048]{1,0:T(8,128)(2,1)S(1)}, f32[32,8192]{1,0:T(8,128)S(1)}) custom-call(bf16[1,32,8192]{2,1,0:T(8,128)(2,1)} %refs_0_.3, f32[32,8192]{1,0:T(8,128)} %refs_1_), custom_call_target="tpu_custom_call" | custom-call | tf_op jit(solution)/shard_map/pallas_call | solution.py:50
  6.2 0.4 %collective-permute-start = (bf16[32,2048]{1,0:T(8,128)(2,1)S(1)}, bf16[32,2048]{1,0:T(8,128)(2,1)S(1)}, u32[]{:S(2)}, u32[]{:S(2)}) collective-permute-start(bf16[32,2048]{1,0:T(8,128)(2,1)S(1)} %get-tuple-element.47), channel_id=1, source_target_pairs={{0,8},{8,0},{16,24},{24,16},{1,9},{9,1},{17,25},{25,17},{2,10},{10... | collective-permute-start | bytes 393224 | tf_op jit(solution)/shard_map/ppermute | solution.py:18
  6.6 1.2 %shard_map.53.momentum = f32[32,8192]{1,0:T(8,128)S(1)} custom-call(bf16[1,32,8192]{2,1,0:T(8,128)(2,1)} %refs_0_.3, f32[32,8192]{1,0:T(8,128)} %refs_1_.1), custom_call_target="tpu_custom_call" | custom-call | tf_op jit(solution)/shard_map/pallas_call | solution.py:50
  7.9 1.7 %collective-permute-start.4 = (bf16[32,2048]{1,0:T(8,128)(2,1)S(1)}, bf16[32,2048]{1,0:T(8,128)(2,1)S(1)}, u32[]{:S(2)}, u32[]{:S(2)}) collective-permute-start(bf16[32,2048]{1,0:T(8,128)(2,1)S(1)} %get-tuple-element.46.refs_0_), channel_id=1, source_target_pairs={{0,16},{8,24},{16,0},{24,8},{1,17},{9,25},{17,1},{25,9},{2,18},{10... | collective-permute-start | bytes 393224 | tf_op jit(solution)/shard_map/ppermute | solution.py:18
  9.6 0.0 collective-permute-done.1.refs_2_
  9.6 0.2 collective-permute-start.5
  9.8 0.0 collective-permute-done.3.refs_5_
  9.8 0.7 %collective-permute-done.2.refs_3_ = bf16[32,2048]{1,0:T(8,128)(2,1)S(1)} collective-permute-done((bf16[32,2048]{1,0:T(8,128)(2,1)S(1)}, bf16[32,2048]{1,0:T(8,128)(2,1)S(1)}, u32[]{:S(2)}, u32[]{:S(2)}) %collective-permute-start.2) | collective-permute-done | bytes 131104 | tf_op jit(solution)/shard_map/ppermute | solution.py:18
  10.5 0.0 collective-permute-done.refs_1_
  10.5 0.8 %shard_map.52 = (f32[32,2048]{1,0:T(8,128)S(1)}, f32[32,1,128]{2,1,0:T(1,128)}, f32[32,2048]{1,0:T(8,128)S(1)}) custom-call(bf16[32,2048]{1,0:T(8,128)(2,1)S(1)} %get-tuple-element.46.refs_0_, bf16[32,2048]{1,0:T(8,128)(2,1)S(1)} %collective-permute-done.refs_1_, bf16[32,2048]{1,0:T(8,128)(2,1)S(1)} %collective-permute-done.1.refs_2_, ...), custom_call_target="tpu_custom_call" | custom-call | tf_op jit(solution)/shard_map/pallas_call | solution.py:153
  11.3 6.0 %all-to-all-start = ((f32[32,1,128]{2,1,0:T(1,128)}), f32[32,1,128]{2,1,0:T(1,128)S(1)}, u32[]{:S(2)}, u32[]{:S(2)}) async-start(f32[32,1,128]{2,1,0:T(1,128)} %get-tuple-element.39), calls=%async_computation | async-start | bytes 32768 | tf_op jit(solution)/shard_map/all_to_all | solution.py:163
  17.3 0.0 collective-permute-done.4.first
  17.3 0.0 collective-permute-done.5.second
  17.3 7.0 %all-to-all-done.squares = f32[32,1,128]{2,1,0:T(1,128)S(1)} async-done(((f32[32,1,128]{2,1,0:T(1,128)}), f32[32,1,128]{2,1,0:T(1,128)S(1)}, u32[]{:S(2)}, u32[]{:S(2)}) %all-to-all-start) | async-done | bytes 16416 | tf_op jit(solution)/shard_map/all_to_all | solution.py:163
  24.4 0.1 collective-permute-start.6
  24.4 0.5 %collective-permute-start.7 = (f32[32,2048]{1,0:T(8,128)S(1)}, f32[32,2048]{1,0:T(8,128)S(1)}, u32[]{:S(2)}, u32[]{:S(2)}) collective-permute-start(f32[32,2048]{1,0:T(8,128)S(1)} %shard_map.54.refs_1_), channel_id=1, source_target_pairs={{0,8},{8,0},{16,24},{24,16},{1,9},{9,1},{17,25},{25,17},{2,10},{10... | collective-permute-start | bytes 786440 | tf_op jit(solution)/shard_map/ppermute | solution.py:18
  24.9 1.2 %shard_map.55 = (f32[32,8192]{1,0:T(8,128)}, f32[32,8192]{1,0:T(8,128)}) custom-call(f32[32,1,128]{2,1,0:T(1,128)S(1)} %all-to-all-done.squares, f32[32,8192]{1,0:T(8,128)S(1)} %get-tuple-element.54.params, f32[32,8192]{1,0:T(8,128)S(1)} %shard_map.53.momentum, f32[32,2048]{1,0:T(8,128)S(1)} %get-tuple-element.56.refs_0_, f32[32,2048]{1,0:T(8,128)S(1)} %shard_map.54.refs_1_), custom_call_target="tpu_custom_call" | custom-call | tf_op jit(solution)/shard_map/pallas_call | solution.py:109
  26.2 0.0 collective-permute-done.6.refs_0_
  26.2 0.2 collective-permute-done.7.refs_1_
  26.3 1.2 %shard_map.56 = (f32[32,8192]{1,0:T(8,128)}, f32[32,8192]{1,0:T(8,128)}) custom-call(f32[32,1,128]{2,1,0:T(1,128)S(1)} %all-to-all-done.squares, f32[32,8192]{1,0:T(8,128)S(1)} %get-tuple-element.54.params, f32[32,8192]{1,0:T(8,128)S(1)} %shard_map.53.momentum, ...), custom_call_target="tpu_custom_call", output_to_operand_aliasing={{0}: (5, {}), {1}: (6, {})} | custom-call | tf_op jit(solution)/shard_map/pallas_call | solution.py:109
  (1 shorter events, 0.0 us)
Async XLA Ops:
  1.6 7.9 %collective-permute-start.1 = (bf16[32,2048]{1,0:T(8,128)(2,1)S(1)}, bf16[32,2048]{1,0:T(8,128)(2,1)S(1)}, u32[]{:S(2)}, u32[]{:S(2)}) collective-permute-start(bf16[32,2048]{1,0:T(8,128)(2,1)S(1)} %get-tuple-element.37.refs_4_), channel_id=1, source_target_pairs={{0,16},{8,24},{16,0},{24,8},{1,17},{9,25},{17,1},{25,9},{2,18},{10... | collective-permute-start | bytes 393224 | tf_op jit(solution)/shard_map/ppermute | solution.py:18
  4.6 5.1 %collective-permute-start.3 = (bf16[32,2048]{1,0:T(8,128)(2,1)S(1)}, bf16[32,2048]{1,0:T(8,128)(2,1)S(1)}, u32[]{:S(2)}, u32[]{:S(2)}) collective-permute-start(bf16[32,2048]{1,0:T(8,128)(2,1)S(1)} %get-tuple-element.38), channel_id=1, source_target_pairs={{0,8},{8,0},{16,24},{24,16},{1,9},{9,1},{17,25},{25,17},{2,10},{10... | collective-permute-start | bytes 393224 | tf_op jit(solution)/shard_map/ppermute | solution.py:18
  4.6 5.9 %collective-permute-start.2 = (bf16[32,2048]{1,0:T(8,128)(2,1)S(1)}, bf16[32,2048]{1,0:T(8,128)(2,1)S(1)}, u32[]{:S(2)}, u32[]{:S(2)}) collective-permute-start(bf16[32,2048]{1,0:T(8,128)(2,1)S(1)} %get-tuple-element.38), channel_id=1, source_target_pairs={{0,24},{8,16},{16,8},{24,0},{1,25},{9,17},{17,9},{25,1},{2,26},{10... | collective-permute-start | bytes 393224 | tf_op jit(solution)/shard_map/ppermute | solution.py:18
  6.2 4.3 %collective-permute-start = (bf16[32,2048]{1,0:T(8,128)(2,1)S(1)}, bf16[32,2048]{1,0:T(8,128)(2,1)S(1)}, u32[]{:S(2)}, u32[]{:S(2)}) collective-permute-start(bf16[32,2048]{1,0:T(8,128)(2,1)S(1)} %get-tuple-element.47), channel_id=1, source_target_pairs={{0,8},{8,0},{16,24},{24,16},{1,9},{9,1},{17,25},{25,17},{2,10},{10... | collective-permute-start | bytes 393224 | tf_op jit(solution)/shard_map/ppermute | solution.py:18
  7.9 9.4 %collective-permute-start.4 = (bf16[32,2048]{1,0:T(8,128)(2,1)S(1)}, bf16[32,2048]{1,0:T(8,128)(2,1)S(1)}, u32[]{:S(2)}, u32[]{:S(2)}) collective-permute-start(bf16[32,2048]{1,0:T(8,128)(2,1)S(1)} %get-tuple-element.46.refs_0_), channel_id=1, source_target_pairs={{0,16},{8,24},{16,0},{24,8},{1,17},{9,25},{17,1},{25,9},{2,18},{10... | collective-permute-start | bytes 393224 | tf_op jit(solution)/shard_map/ppermute | solution.py:18
  9.6 7.7 %collective-permute-start.5 = (bf16[32,2048]{1,0:T(8,128)(2,1)S(1)}, bf16[32,2048]{1,0:T(8,128)(2,1)S(1)}, u32[]{:S(2)}, u32[]{:S(2)}) collective-permute-start(bf16[32,2048]{1,0:T(8,128)(2,1)S(1)} %get-tuple-element.47), channel_id=1, source_target_pairs={{0,24},{8,16},{16,8},{24,0},{1,25},{9,17},{17,9},{25,1},{2,26},{10... | collective-permute-start | bytes 393224 | tf_op jit(solution)/shard_map/ppermute | solution.py:18
  11.3 13.0 %all-to-all-start = ((f32[32,1,128]{2,1,0:T(1,128)}), f32[32,1,128]{2,1,0:T(1,128)S(1)}, u32[]{:S(2)}, u32[]{:S(2)}) async-start(f32[32,1,128]{2,1,0:T(1,128)} %get-tuple-element.39), calls=%async_computation | async-start | bytes 32768 | tf_op jit(solution)/shard_map/all_to_all | solution.py:163
  24.4 1.8 %collective-permute-start.6 = (f32[32,2048]{1,0:T(8,128)S(1)}, f32[32,2048]{1,0:T(8,128)S(1)}, u32[]{:S(2)}, u32[]{:S(2)}) collective-permute-start(f32[32,2048]{1,0:T(8,128)S(1)} %get-tuple-element.56.refs_0_), channel_id=1, source_target_pairs={{0,8},{8,0},{16,24},{24,16},{1,9},{9,1},{17,25},{25,17},{2,10},{10... | collective-permute-start | bytes 786440 | tf_op jit(solution)/shard_map/ppermute | solution.py:18
  24.4 1.9 %collective-permute-start.7 = (f32[32,2048]{1,0:T(8,128)S(1)}, f32[32,2048]{1,0:T(8,128)S(1)}, u32[]{:S(2)}, u32[]{:S(2)}) collective-permute-start(f32[32,2048]{1,0:T(8,128)S(1)} %shard_map.54.refs_1_), channel_id=1, source_target_pairs={{0,8},{8,0},{16,24},{24,16},{1,9},{9,1},{17,25},{25,17},{2,10},{10... | collective-permute-start | bytes 786440 | tf_op jit(solution)/shard_map/ppermute | solution.py:18

commit v17 on v16

--- a/solution.py
+++ b/solution.py
@@ -79,16 +79,19 @@
     average[...] = (here[...] + there) / WIDE(groups)
 
 
-def update_kernel(count, flips, passed, squares, params, momentum, *refs):
+def factor_kernel(count, squares, factor):
+    square_sum = jnp.sum(squares[...], keepdims=True).reshape(1, 1)
+    factor[...] = jnp.broadcast_to(0.2 / jnp.sqrt(square_sum / WIDE(count) + 1e-06), factor.shape)
+
+
+def update_kernel(flips, passed, factor, params, momentum, *refs):
     averages, refs = refs[: len(flips)], refs[len(flips) + passed :]
     new_params, new_momentum, params_out, momentum_out, sems = refs
-    square_sum = jnp.sum(squares[...], keepdims=True).reshape(1, 1)
-    factor = 0.2 / jnp.sqrt(square_sum / WIDE(count) + 1e-06)
     width = averages[0].shape[1]
     copies = []
     for i, (k, average) in enumerate(zip(flips, averages)):
         cols = piece_of(k, width)
-        clipped = factor * average[...]
+        clipped = factor[:, :1] * average[...]
         fresh = 0.9 * momentum[:, cols] + clipped
         momentum_out[i] = fresh
         params_out[i] = params[:, cols] - 0.7 * (clipped + 0.9 * fresh)
@@ -102,12 +105,12 @@
         copy.wait()
 
 
-def update(count, flips, averages, squares, params, momentum, earlier=()):
+def update(flips, averages, factor, params, momentum, earlier=()):
     rows, width = averages[0].shape
     out = jax.ShapeDtypeStruct(params.shape, WIDE)
     first = 3 + len(flips)
     return pl.pallas_call(
-        functools.partial(update_kernel, count, flips, len(earlier)),
+        functools.partial(update_kernel, flips, len(earlier)),
         out_shape=[out, out],
         in_specs=[VMEM] * first + [HBM] * len(earlier),
         out_specs=[HBM] * 2,
@@ -118,7 +121,7 @@
         ],
         input_output_aliases={first + i: i for i in range(len(earlier))},
         compiler_params=pltpu.CompilerParams(vmem_limit_bytes=LIMIT),
-    )(squares, params, momentum, *averages, *earlier)
+    )(factor, params, momentum, *averages, *earlier)
 
 
 def per_device(pseudo_grad, params, momentum):
@@ -163,7 +166,14 @@
     squares = lax.all_to_all(
         squares, ("replica", "fsdp"), split_axis=0, concat_axis=0, tiled=True
     )
-    squares, again = lax.optimization_barrier((squares, again))
+    factor = pl.pallas_call(
+        functools.partial(factor_kernel, count),
+        out_shape=jax.ShapeDtypeStruct((1, 128), WIDE),
+        in_specs=[VMEM],
+        out_specs=VMEM,
+        compiler_params=limit,
+    )(squares)
+    factor, again = lax.optimization_barrier((factor, again))
     if groups == 4:
         averages[2] = pl.pallas_call(
             functools.partial(join_kernel, groups),
@@ -172,15 +182,15 @@
             out_specs=VMEM,
             compiler_params=limit,
         )(*other_sum, again[2], again[3])
-    squares, averages = lax.optimization_barrier((squares, averages))
+    factor, averages = lax.optimization_barrier((factor, averages))
     for k in range(0, groups, 2):
         averages[k + 1] = swapped(averages[k], "replica", 1)
     here = [k for k in range(groups) if k % 2 == 0]
     late = [k for k in range(groups) if k not in here]
-    outs = update(count, here, [averages[k] for k in here], squares, params, momentum)
+    outs = update(here, [averages[k] for k in here], factor, params, momentum)
     if late:
         outs = update(
-            count, late, [averages[k] for k in late], squares, params, momentum, outs
+            late, [averages[k] for k in late], factor, params, momentum, outs
         )
     return outs
 

time: 27.8 us -> 27.1 us (0.975)
  blocking collectives: 0 us -> 12.9 us
  waiting for transfers between devices: 7.94 us -> 1.02 us
  starting transfers between devices: 12 us -> 6.04 us
  Pallas kernels: 6.89 us -> 6.2 us
    all_to_all x0 -> x1, blocking collectives: none -> 12.9 us  [per_device(): lax.all_to_all(squares, ('replica', 'fsdp'), split_axis=0, concat_axis=0,...]
    all_to_all x1 -> x0, waiting for transfers between devices: 7.02 us -> none  [per_device(): lax.all_to_all(squares, ('replica', 'fsdp'), split_axis=0, concat_axis=0,...]
    all_to_all x1 -> x0, starting transfers between devices: 5.97 us -> none  [per_device(): lax.all_to_all(squares, ('replica', 'fsdp'), split_axis=0, concat_axis=0,...]
    pallas_call x1, Pallas kernels: 0.78 us -> 0.14 us  [per_device(): pl.pallas_call(functools.partial(average_kernel, groups), out_shape=out_s...]
    pallas_call x2 -> x3, Pallas kernels: 2.44 us -> 2.39 us  [the longest x2 2.23 us: update(): pl.pallas_call(functools.partial(update_kernel, flips, len(earlier)), out...]
  transfers between devices with their start and end apart: 9 -> 8, of which waited for: 3 -> 2; matrix products, arithmetic and copies ran while one was open for 0% -> 0% of each run, Pallas kernels for 17% -> 15%
where the time goes in v17:
time: 27.1 us; the launch traced here: 26.9 us
  blocking collectives  12.9 us (48%)
  Pallas kernels  6.2 us (23%)
  starting transfers between devices  6.04 us (22%)
  waiting for transfers between devices  1.02 us (4%)
  between operations  0.72 us (3%)
    all_to_all x1, blocking collectives, per_device(): lax.all_to_all(squares, ('replica', 'fsdp'), split_axis=0, concat_axis=0,...  12.9 us
    ppermute x8, starting transfers between devices, swapped(): return lax.ppermute(value, axis, [(i, i ^ flip) for i in range(size)])  6.04 us
    pallas_call x3, Pallas kernels, cut(): pl.pallas_call(functools.partial(cut_kernel, flips, len(arrays)), out_sha...  3.62 us
    pallas_call x2, Pallas kernels, update(): pl.pallas_call(functools.partial(update_kernel, flips, len(earlier)), out...  2.23 us
    ppermute x8, waiting for transfers between devices, swapped(): return lax.ppermute(value, axis, [(i, i ^ flip) for i in range(size)])  1.02 us
  transfers between devices with their start and end apart: 8, of which 2 were waited for; matrix products, arithmetic and copies ran while one was open for 0% of the time, Pallas kernels for 15%

profile of v17, /device:TPU:0, one launch (start us, length us, event | category | flops | bytes accessed | tf_op | source)
XLA Modules:
  0.0 26.9 jit_solution(5172630655145435458)
XLA Ops:
  0.6 1.0 %shard_map.50 = (bf16[32,2048]{1,0:T(8,128)(2,1)S(1)}, bf16[32,2048]{1,0:T(8,128)(2,1)S(1)}) custom-call(bf16[1,32,8192]{2,1,0:T(8,128)(2,1)} %refs_0_.3), custom_call_target="tpu_custom_call" | custom-call | tf_op jit(solution)/shard_map/pallas_call | solution.py:50
  1.6 3.0 %collective-permute-start.1 = (bf16[32,2048]{1,0:T(8,128)(2,1)S(1)}, bf16[32,2048]{1,0:T(8,128)(2,1)S(1)}, u32[]{:S(2)}, u32[]{:S(2)}) collective-permute-start(bf16[32,2048]{1,0:T(8,128)(2,1)S(1)} %get-tuple-element.37.refs_4_), channel_id=1, source_target_pairs={{0,16},{8,24},{16,0},{24,8},{1,17},{9,25},{17,1},{25,9},{2,18},{10... | collective-permute-start | bytes 393224 | tf_op jit(solution)/shard_map/ppermute | solution.py:18
  4.6 0.0 collective-permute-start.3
  4.6 0.2 collective-permute-start.2
  4.8 1.4 %shard_map.51 = (bf16[32,2048]{1,0:T(8,128)(2,1)S(1)}, bf16[32,2048]{1,0:T(8,128)(2,1)S(1)}, f32[32,8192]{1,0:T(8,128)S(1)}) custom-call(bf16[1,32,8192]{2,1,0:T(8,128)(2,1)} %refs_0_.3, f32[32,8192]{1,0:T(8,128)} %refs_1_), custom_call_target="tpu_custom_call" | custom-call | tf_op jit(solution)/shard_map/pallas_call | solution.py:50
  6.2 0.4 %collective-permute-start = (bf16[32,2048]{1,0:T(8,128)(2,1)S(1)}, bf16[32,2048]{1,0:T(8,128)(2,1)S(1)}, u32[]{:S(2)}, u32[]{:S(2)}) collective-permute-start(bf16[32,2048]{1,0:T(8,128)(2,1)S(1)} %get-tuple-element.47), channel_id=1, source_target_pairs={{0,8},{8,0},{16,24},{24,16},{1,9},{9,1},{17,25},{25,17},{2,10},{10... | collective-permute-start | bytes 393224 | tf_op jit(solution)/shard_map/ppermute | solution.py:18
  6.6 1.2 %shard_map.54.momentum = f32[32,8192]{1,0:T(8,128)S(1)} custom-call(bf16[1,32,8192]{2,1,0:T(8,128)(2,1)} %refs_0_.3, f32[32,8192]{1,0:T(8,128)} %refs_1_.1), custom_call_target="tpu_custom_call" | custom-call | tf_op jit(solution)/shard_map/pallas_call | solution.py:50
  7.9 1.7 %collective-permute-start.4 = (bf16[32,2048]{1,0:T(8,128)(2,1)S(1)}, bf16[32,2048]{1,0:T(8,128)(2,1)S(1)}, u32[]{:S(2)}, u32[]{:S(2)}) collective-permute-start(bf16[32,2048]{1,0:T(8,128)(2,1)S(1)} %get-tuple-element.46.refs_0_), channel_id=1, source_target_pairs={{0,16},{8,24},{16,0},{24,8},{1,17},{9,25},{17,1},{25,9},{2,18},{10... | collective-permute-start | bytes 393224 | tf_op jit(solution)/shard_map/ppermute | solution.py:18
  9.6 0.0 collective-permute-done.1.refs_2_
  9.6 0.2 collective-permute-start.5
  9.8 0.0 collective-permute-done.3.refs_5_
  9.8 0.7 %collective-permute-done.2.refs_3_ = bf16[32,2048]{1,0:T(8,128)(2,1)S(1)} collective-permute-done((bf16[32,2048]{1,0:T(8,128)(2,1)S(1)}, bf16[32,2048]{1,0:T(8,128)(2,1)S(1)}, u32[]{:S(2)}, u32[]{:S(2)}) %collective-permute-start.2) | collective-permute-done | bytes 131104 | tf_op jit(solution)/shard_map/ppermute | solution.py:18
  10.5 0.0 collective-permute-done.refs_1_
  10.5 0.1 shard_map.52
  10.6 12.9 %all_to_all.5.squares = f32[32,1,128]{2,1,0:T(1,128)S(1)} all-to-all(f32[32,1,128]{2,1,0:T(1,128)S(1)} %get-tuple-element.39), channel_id=1, replica_groups=mesh['replica'=4,'fsdp'=8] {'replica','fsdp'}, dimensions={0} | all-to-all | bytes 32768 | tf_op jit(solution)/shard_map/all_to_all | solution.py:166
  23.5 0.2 shard_map.53.factor
  23.7 0.0 collective-permute-done.4.first
  23.7 0.0 collective-permute-done.5.second
  23.8 0.1 collective-permute-start.6
  23.9 0.5 %collective-permute-start.7 = (f32[32,2048]{1,0:T(8,128)S(1)}, f32[32,2048]{1,0:T(8,128)S(1)}, u32[]{:S(2)}, u32[]{:S(2)}) collective-permute-start(f32[32,2048]{1,0:T(8,128)S(1)} %shard_map.55.refs_1_), channel_id=1, source_target_pairs={{0,8},{8,0},{16,24},{24,16},{1,9},{9,1},{17,25},{25,17},{2,10},{10... | collective-permute-start | bytes 786440 | tf_op jit(solution)/shard_map/ppermute | solution.py:18
  24.4 1.1 %shard_map.56 = (f32[32,8192]{1,0:T(8,128)}, f32[32,8192]{1,0:T(8,128)}) custom-call(f32[1,128]{1,0:T(1,128)S(1)} %shard_map.53.factor, f32[32,8192]{1,0:T(8,128)S(1)} %get-tuple-element.54.params, f32[32,8192]{1,0:T(8,128)S(1)} %shard_map.54.momentum, f32[32,2048]{1,0:T(8,128)S(1)} %get-tuple-element.56.refs_0_, f32[32,2048]{1,0:T(8,128)S(1)} %shard_map.55.refs_1_), custom_call_target="tpu_custom_call" | custom-call | tf_op jit(solution)/shard_map/pallas_call | solution.py:112
  25.5 0.0 collective-permute-done.6.refs_0_
  25.5 0.3 collective-permute-done.7.refs_1_
  25.8 1.1 %shard_map.57 = (f32[32,8192]{1,0:T(8,128)}, f32[32,8192]{1,0:T(8,128)}) custom-call(f32[1,128]{1,0:T(1,128)S(1)} %shard_map.53.factor, f32[32,8192]{1,0:T(8,128)S(1)} %get-tuple-element.54.params, f32[32,8192]{1,0:T(8,128)S(1)} %shard_map.54.momentum, f32[32,2048]{1,0:T(8,128)S(1)} %collective-permute-done.6.refs_0_, ...), custom_call_target="tpu_custom_call", output_to_operand_aliasing={{0}: (5, {}), {1}: (6, {})} | custom-call | tf_op jit(solution)/shard_map/pallas_call | solution.py:112
  (1 shorter events, 0.0 us)
Async XLA Ops:
  1.6 7.9 %collective-permute-start.1 = (bf16[32,2048]{1,0:T(8,128)(2,1)S(1)}, bf16[32,2048]{1,0:T(8,128)(2,1)S(1)}, u32[]{:S(2)}, u32[]{:S(2)}) collective-permute-start(bf16[32,2048]{1,0:T(8,128)(2,1)S(1)} %get-tuple-element.37.refs_4_), channel_id=1, source_target_pairs={{0,16},{8,24},{16,0},{24,8},{1,17},{9,25},{17,1},{25,9},{2,18},{10... | collective-permute-start | bytes 393224 | tf_op jit(solution)/shard_map/ppermute | solution.py:18
  4.6 5.1 %collective-permute-start.3 = (bf16[32,2048]{1,0:T(8,128)(2,1)S(1)}, bf16[32,2048]{1,0:T(8,128)(2,1)S(1)}, u32[]{:S(2)}, u32[]{:S(2)}) collective-permute-start(bf16[32,2048]{1,0:T(8,128)(2,1)S(1)} %get-tuple-element.38), channel_id=1, source_target_pairs={{0,8},{8,0},{16,24},{24,16},{1,9},{9,1},{17,25},{25,17},{2,10},{10... | collective-permute-start | bytes 393224 | tf_op jit(solution)/shard_map/ppermute | solution.py:18
  4.6 5.9 %collective-permute-start.2 = (bf16[32,2048]{1,0:T(8,128)(2,1)S(1)}, bf16[32,2048]{1,0:T(8,128)(2,1)S(1)}, u32[]{:S(2)}, u32[]{:S(2)}) collective-permute-start(bf16[32,2048]{1,0:T(8,128)(2,1)S(1)} %get-tuple-element.38), channel_id=1, source_target_pairs={{0,24},{8,16},{16,8},{24,0},{1,25},{9,17},{17,9},{25,1},{2,26},{10... | collective-permute-start | bytes 393224 | tf_op jit(solution)/shard_map/ppermute | solution.py:18
  6.2 4.3 %collective-permute-start = (bf16[32,2048]{1,0:T(8,128)(2,1)S(1)}, bf16[32,2048]{1,0:T(8,128)(2,1)S(1)}, u32[]{:S(2)}, u32[]{:S(2)}) collective-permute-start(bf16[32,2048]{1,0:T(8,128)(2,1)S(1)} %get-tuple-element.47), channel_id=1, source_target_pairs={{0,8},{8,0},{16,24},{24,16},{1,9},{9,1},{17,25},{25,17},{2,10},{10... | collective-permute-start | bytes 393224 | tf_op jit(solution)/shard_map/ppermute | solution.py:18
  7.9 15.8 %collective-permute-start.4 = (bf16[32,2048]{1,0:T(8,128)(2,1)S(1)}, bf16[32,2048]{1,0:T(8,128)(2,1)S(1)}, u32[]{:S(2)}, u32[]{:S(2)}) collective-permute-start(bf16[32,2048]{1,0:T(8,128)(2,1)S(1)} %get-tuple-element.46.refs_0_), channel_id=1, source_target_pairs={{0,16},{8,24},{16,0},{24,8},{1,17},{9,25},{17,1},{25,9},{2,18},{10... | collective-permute-start | bytes 393224 | tf_op jit(solution)/shard_map/ppermute | solution.py:18
  9.6 14.1 %collective-permute-start.5 = (bf16[32,2048]{1,0:T(8,128)(2,1)S(1)}, bf16[32,2048]{1,0:T(8,128)(2,1)S(1)}, u32[]{:S(2)}, u32[]{:S(2)}) collective-permute-start(bf16[32,2048]{1,0:T(8,128)(2,1)S(1)} %get-tuple-element.47), channel_id=1, source_target_pairs={{0,24},{8,16},{16,8},{24,0},{1,25},{9,17},{17,9},{25,1},{2,26},{10... | collective-permute-start | bytes 393224 | tf_op jit(solution)/shard_map/ppermute | solution.py:18
  23.8 1.7 %collective-permute-start.6 = (f32[32,2048]{1,0:T(8,128)S(1)}, f32[32,2048]{1,0:T(8,128)S(1)}, u32[]{:S(2)}, u32[]{:S(2)}) collective-permute-start(f32[32,2048]{1,0:T(8,128)S(1)} %get-tuple-element.56.refs_0_), channel_id=1, source_target_pairs={{0,8},{8,0},{16,24},{24,16},{1,9},{9,1},{17,25},{25,17},{2,10},{10... | collective-permute-start | bytes 786440 | tf_op jit(solution)/shard_map/ppermute | solution.py:18
  23.9 1.9 %collective-permute-start.7 = (f32[32,2048]{1,0:T(8,128)S(1)}, f32[32,2048]{1,0:T(8,128)S(1)}, u32[]{:S(2)}, u32[]{:S(2)}) collective-permute-start(f32[32,2048]{1,0:T(8,128)S(1)} %shard_map.55.refs_1_), channel_id=1, source_target_pairs={{0,8},{8,0},{16,24},{24,16},{1,9},{9,1},{17,25},{25,17},{2,10},{10... | collective-permute-start | bytes 786440 | tf_op jit(solution)/shard_map/ppermute | solution.py:18

commit v18 on v17

--- a/solution.py
+++ b/solution.py
@@ -60,13 +60,14 @@
 
 def average_kernel(groups, *refs):
     pieces, rest = refs[:groups], refs[groups:]
-    if len(rest) > 2:
-        first, second, average, squares, other_sum = rest
+    if len(rest) > 3:
+        first, second, *average, squares, other_sum = rest
         other_sum[...] = first[...].astype(WIDE) + second[...].astype(WIDE)
     else:
-        average, squares = rest
+        *average, squares = rest
     mean = tree([piece[...].astype(WIDE) for piece in pieces]) / WIDE(groups)
-    average[...] = mean
+    for i, half in enumerate(average):
+        half[...] = mean[i * half.shape[0] : (i + 1) * half.shape[0]]
     row = jnp.sum(mean * mean, axis=0, keepdims=True)
     lanes = functools.reduce(
         jnp.add, [row[:, i : i + 128] for i in range(0, row.shape[1], 128)]
@@ -84,14 +85,18 @@
     factor[...] = jnp.broadcast_to(0.2 / jnp.sqrt(square_sum / WIDE(count) + 1e-06), factor.shape)
 
 
-def update_kernel(flips, passed, factor, params, momentum, *refs):
-    averages, refs = refs[: len(flips)], refs[len(flips) + passed :]
+def update_kernel(flips, sizes, passed, factor, params, momentum, *refs):
+    averages = []
+    for size in sizes:
+        averages.append(jnp.concatenate([ref[...] for ref in refs[:size]]))
+        refs = refs[size:]
+    refs = refs[passed:]
     new_params, new_momentum, params_out, momentum_out, sems = refs
-    width = averages[0].shape[1]
+    width = params_out.shape[2]
     copies = []
     for i, (k, average) in enumerate(zip(flips, averages)):
         cols = piece_of(k, width)
-        clipped = factor[:, :1] * average[...]
+        clipped = factor[:, :1] * average
         fresh = 0.9 * momentum[:, cols] + clipped
         momentum_out[i] = fresh
         params_out[i] = params[:, cols] - 0.7 * (clipped + 0.9 * fresh)
@@ -106,11 +111,13 @@
 
 
 def update(flips, averages, factor, params, momentum, earlier=()):
-    rows, width = averages[0].shape
+    sizes = [len(average) for average in averages]
+    parts = [part for average in averages for part in average]
+    rows, width = params.shape[0], parts[0].shape[1]
     out = jax.ShapeDtypeStruct(params.shape, WIDE)
-    first = 3 + len(flips)
+    first = 3 + len(parts)
     return pl.pallas_call(
-        functools.partial(update_kernel, flips, len(earlier)),
+        functools.partial(update_kernel, flips, sizes, len(earlier)),
         out_shape=[out, out],
         in_specs=[VMEM] * first + [HBM] * len(earlier),
         out_specs=[HBM] * 2,
@@ -121,7 +128,7 @@
         ],
         input_output_aliases={first + i: i for i in range(len(earlier))},
         compiler_params=pltpu.CompilerParams(vmem_limit_bytes=LIMIT),
-    )(factor, params, momentum, *averages, *earlier)
+    )(factor, params, momentum, *parts, *earlier)
 
 
 def per_device(pseudo_grad, params, momentum):
@@ -149,20 +156,22 @@
         _, (momentum,) = cut(pseudo_grad, width, (), momentum)
     wide_piece = jax.ShapeDtypeStruct((rows, width), WIDE)
     parts = [moved[k] for k in range(groups)]
-    out_shape = [wide_piece, jax.ShapeDtypeStruct((devices, 1, 128), WIDE)]
+    half_piece = jax.ShapeDtypeStruct((rows // 2, width), WIDE)
+    out_shape = [half_piece] * 2 + [jax.ShapeDtypeStruct((devices, 1, 128), WIDE)]
     if groups == 4:
         parts += [pieces[2], again.pop(1)]
         out_shape += [wide_piece]
-    average, squares, *other_sum = pl.pallas_call(
+    low, high, squares, *other_sum = pl.pallas_call(
         functools.partial(average_kernel, groups),
         out_shape=out_shape,
         in_specs=[VMEM] * len(parts),
         out_specs=[VMEM] * len(out_shape),
         compiler_params=limit,
     )(*parts)
-    averages = {0: average}
+    averages = {0: [low, high], 1: [swapped(x, "replica", 1) for x in (low, high)]}
     if groups != 4:
-        averages.update({k: swapped(average, "replica", k) for k in range(2, groups, 2)})
+        for k in range(2, groups, 2):
+            averages[k] = [swapped(x, "replica", k) for x in (low, high)]
     squares = lax.all_to_all(
         squares, ("replica", "fsdp"), split_axis=0, concat_axis=0, tiled=True
     )
@@ -175,17 +184,18 @@
     )(squares)
     factor, again = lax.optimization_barrier((factor, again))
     if groups == 4:
-        averages[2] = pl.pallas_call(
+        joined = pl.pallas_call(
             functools.partial(join_kernel, groups),
             out_shape=wide_piece,
             in_specs=[VMEM] * 3,
             out_specs=VMEM,
             compiler_params=limit,
         )(*other_sum, again[2], again[3])
+        averages[2] = [joined]
     factor, averages = lax.optimization_barrier((factor, averages))
-    for k in range(0, groups, 2):
-        averages[k + 1] = swapped(averages[k], "replica", 1)
-    here = [k for k in range(groups) if k % 2 == 0]
+    for k in range(2, groups, 2):
+        averages[k + 1] = [swapped(x, "replica", 1) for x in averages[k]]
+    here = [k for k in range(groups) if k < 2 or k % 2 == 0]
     late = [k for k in range(groups) if k not in here]
     outs = update(here, [averages[k] for k in here], factor, params, momentum)
     if late:

time: 27.1 us -> 29.2 us (1.077)
  starting transfers between devices: 6.04 us -> 7.65 us
  waiting for transfers between devices: 1.02 us -> 2.51 us
  blocking collectives: 12.9 us -> 11.9 us
    ppermute x8 -> x9, starting transfers between devices: 6.04 us -> 7.65 us  [swapped(): return lax.ppermute(value, axis, [(i, i ^ flip) for i in range(size)])]
    ppermute x8 -> x9, waiting for transfers between devices: 1.02 us -> 2.51 us  [swapped(): return lax.ppermute(value, axis, [(i, i ^ flip) for i in range(size)])]
    all_to_all x1, blocking collectives: 12.9 us -> 11.9 us  [per_device(): lax.all_to_all(squares, ('replica', 'fsdp'), split_axis=0, concat_axis=0,...]
  transfers between devices with their start and end apart: 8 -> 9, of which waited for: 2 -> 2; matrix products, arithmetic and copies ran while one was open for 0% -> 0% of each run, Pallas kernels for 15% -> 15%
where the time goes in v18:
time: 29.2 us; the launch traced here: 29 us
  blocking collectives  11.9 us (41%)
  starting transfers between devices  7.65 us (26%)
  Pallas kernels  6.2 us (21%)
  waiting for transfers between devices  2.51 us (9%)
  between operations  0.73 us (2%)
    all_to_all x1, blocking collectives, per_device(): lax.all_to_all(squares, ('replica', 'fsdp'), split_axis=0, concat_axis=0,...  11.9 us
    ppermute x9, starting transfers between devices, swapped(): return lax.ppermute(value, axis, [(i, i ^ flip) for i in range(size)])  7.65 us
    pallas_call x3, Pallas kernels, cut(): pl.pallas_call(functools.partial(cut_kernel, flips, len(arrays)), out_sha...  3.62 us
    ppermute x9, waiting for transfers between devices, swapped(): return lax.ppermute(value, axis, [(i, i ^ flip) for i in range(size)])  2.51 us
    pallas_call x2, Pallas kernels, update(): pl.pallas_call(functools.partial(update_kernel, flips, sizes, len(earlier...  2.23 us
  transfers between devices with their start and end apart: 9, of which 2 were waited for; matrix products, arithmetic and copies ran while one was open for 0% of the time, Pallas kernels for 15%

profile of v18, /device:TPU:0, one launch (start us, length us, event | category | flops | bytes accessed | tf_op | source)
XLA Modules:
  0.0 29.0 jit_solution(9014049063230206586)
XLA Ops:
  0.6 1.0 %shard_map.50 = (bf16[32,2048]{1,0:T(8,128)(2,1)S(1)}, bf16[32,2048]{1,0:T(8,128)(2,1)S(1)}) custom-call(bf16[1,32,8192]{2,1,0:T(8,128)(2,1)} %refs_0_.3), custom_call_target="tpu_custom_call" | custom-call | tf_op jit(solution)/shard_map/pallas_call | solution.py:50
  1.6 0.5 %collective-permute-start.3 = (bf16[32,2048]{1,0:T(8,128)(2,1)S(1)}, bf16[32,2048]{1,0:T(8,128)(2,1)S(1)}, u32[]{:S(2)}, u32[]{:S(2)}) collective-permute-start(bf16[32,2048]{1,0:T(8,128)(2,1)S(1)} %get-tuple-element.42), channel_id=1, source_target_pairs={{0,8},{8,0},{16,24},{24,16},{1,9},{9,1},{17,25},{25,17},{2,10},{10... | collective-permute-start | bytes 393224 | tf_op jit(solution)/shard_map/ppermute | solution.py:18
  2.2 2.6 %collective-permute-start.2 = (bf16[32,2048]{1,0:T(8,128)(2,1)S(1)}, bf16[32,2048]{1,0:T(8,128)(2,1)S(1)}, u32[]{:S(2)}, u32[]{:S(2)}) collective-permute-start(bf16[32,2048]{1,0:T(8,128)(2,1)S(1)} %get-tuple-element.42), channel_id=1, source_target_pairs={{0,24},{8,16},{16,8},{24,0},{1,25},{9,17},{17,9},{25,1},{2,26},{10... | collective-permute-start | bytes 393224 | tf_op jit(solution)/shard_map/ppermute | solution.py:18
  4.8 0.0 collective-permute-start.1
  4.8 1.4 %shard_map.51 = (bf16[32,2048]{1,0:T(8,128)(2,1)S(1)}, bf16[32,2048]{1,0:T(8,128)(2,1)S(1)}, f32[32,8192]{1,0:T(8,128)S(1)}) custom-call(bf16[1,32,8192]{2,1,0:T(8,128)(2,1)} %refs_0_.3, f32[32,8192]{1,0:T(8,128)} %refs_1_), custom_call_target="tpu_custom_call" | custom-call | tf_op jit(solution)/shard_map/pallas_call | solution.py:50
  6.2 0.2 collective-permute-start
  6.4 1.2 %shard_map.54.momentum = f32[32,8192]{1,0:T(8,128)S(1)} custom-call(bf16[1,32,8192]{2,1,0:T(8,128)(2,1)} %refs_0_.3, f32[32,8192]{1,0:T(8,128)} %refs_1_.1), custom_call_target="tpu_custom_call" | custom-call | tf_op jit(solution)/shard_map/pallas_call | solution.py:50
  7.6 2.0 %collective-permute-start.4 = (bf16[32,2048]{1,0:T(8,128)(2,1)S(1)}, bf16[32,2048]{1,0:T(8,128)(2,1)S(1)}, u32[]{:S(2)}, u32[]{:S(2)}) collective-permute-start(bf16[32,2048]{1,0:T(8,128)(2,1)S(1)} %get-tuple-element.50.refs_0_), channel_id=1, source_target_pairs={{0,16},{8,24},{16,0},{24,8},{1,17},{9,25},{17,1},{25,9},{2,18},{10... | collective-permute-start | bytes 393224 | tf_op jit(solution)/shard_map/ppermute | solution.py:18
  9.6 2.3 %collective-permute-done.1.refs_2_ = bf16[32,2048]{1,0:T(8,128)(2,1)S(1)} collective-permute-done((bf16[32,2048]{1,0:T(8,128)(2,1)S(1)}, bf16[32,2048]{1,0:T(8,128)(2,1)S(1)}, u32[]{:S(2)}, u32[]{:S(2)}) %collective-permute-start.1) | collective-permute-done | bytes 131104 | tf_op jit(solution)/shard_map/ppermute | solution.py:18
  11.9 0.6 %collective-permute-start.5 = (bf16[32,2048]{1,0:T(8,128)(2,1)S(1)}, bf16[32,2048]{1,0:T(8,128)(2,1)S(1)}, u32[]{:S(2)}, u32[]{:S(2)}) collective-permute-start(bf16[32,2048]{1,0:T(8,128)(2,1)S(1)} %get-tuple-element.51), channel_id=1, source_target_pairs={{0,24},{8,16},{16,8},{24,0},{1,25},{9,17},{17,9},{25,1},{2,26},{10... | collective-permute-start | bytes 393224 | tf_op jit(solution)/shard_map/ppermute | solution.py:18
  12.5 0.0 collective-permute-done.3.refs_5_
  12.5 0.0 collective-permute-done.2.refs_3_
  12.5 0.0 collective-permute-done.refs_1_
  12.5 0.1 shard_map.52
  12.6 1.6 %collective-permute-start.6 = (f32[16,2048]{1,0:T(8,128)S(1)}, f32[16,2048]{1,0:T(8,128)S(1)}, u32[]{:S(2)}, u32[]{:S(2)}) collective-permute-start(f32[16,2048]{1,0:T(8,128)S(1)} %get-tuple-element.62.refs_0_), channel_id=1, source_target_pairs={{0,8},{8,0},{16,24},{24,16},{1,9},{9,1},{17,25},{25,17},{2,10},{10... | collective-permute-start | bytes 393224 | tf_op jit(solution)/shard_map/ppermute | solution.py:18
  14.2 0.1 collective-permute-start.7
  14.3 11.9 %all_to_all.5.squares = f32[32,1,128]{2,1,0:T(1,128)S(1)} all-to-all(f32[32,1,128]{2,1,0:T(1,128)S(1)} %get-tuple-element.43), channel_id=1, replica_groups=mesh['replica'=4,'fsdp'=8] {'replica','fsdp'}, dimensions={0} | all-to-all | bytes 32768 | tf_op jit(solution)/shard_map/all_to_all | solution.py:175
  26.2 0.2 shard_map.53.factor
  26.4 0.0 collective-permute-done.4.first
  26.4 0.0 collective-permute-done.5.second
  26.4 0.0 collective-permute-done.6.refs_2_
  26.4 0.0 collective-permute-done.7.refs_3_
  26.5 0.1 collective-permute-start.8
  26.5 1.3 %shard_map.56 = (f32[32,8192]{1,0:T(8,128)}, f32[32,8192]{1,0:T(8,128)}) custom-call(f32[1,128]{1,0:T(1,128)S(1)} %shard_map.53.factor, f32[32,8192]{1,0:T(8,128)S(1)} %get-tuple-element.59.params, f32[32,8192]{1,0:T(8,128)S(1)} %shard_map.54.momentum, f32[16,2048]{1,0:T(8,128)S(1)} %get-tuple-element.62.refs_0_, f32[16,2048]{1,0:T(8,128)S(1)} %get-tuple-element.63.refs_1_, ...), custom_call_target="tpu_custom_call" | custom-call | tf_op jit(solution)/shard_map/pallas_call | solution.py:119
  27.9 0.2 collective-permute-done.8.refs_0_
  28.1 0.9 %shard_map.57 = (f32[32,8192]{1,0:T(8,128)}, f32[32,8192]{1,0:T(8,128)}) custom-call(f32[1,128]{1,0:T(1,128)S(1)} %shard_map.53.factor, f32[32,8192]{1,0:T(8,128)S(1)} %get-tuple-element.59.params, f32[32,8192]{1,0:T(8,128)S(1)} %shard_map.54.momentum, f32[32,2048]{1,0:T(8,128)S(1)} %collective-permute-done.8.refs_0_, ...), custom_call_target="tpu_custom_call", output_to_operand_aliasing={{0}: (4, {}), {1}: (5, {})} | custom-call | tf_op jit(solution)/shard_map/pallas_call | solution.py:119
  (1 shorter events, 0.0 us)
Async XLA Ops:
  1.6 10.8 %collective-permute-start.3 = (bf16[32,2048]{1,0:T(8,128)(2,1)S(1)}, bf16[32,2048]{1,0:T(8,128)(2,1)S(1)}, u32[]{:S(2)}, u32[]{:S(2)}) collective-permute-start(bf16[32,2048]{1,0:T(8,128)(2,1)S(1)} %get-tuple-element.42), channel_id=1, source_target_pairs={{0,8},{8,0},{16,24},{24,16},{1,9},{9,1},{17,25},{25,17},{2,10},{10... | collective-permute-start | bytes 393224 | tf_op jit(solution)/shard_map/ppermute | solution.py:18
  2.2 10.3 %collective-permute-start.2 = (bf16[32,2048]{1,0:T(8,128)(2,1)S(1)}, bf16[32,2048]{1,0:T(8,128)(2,1)S(1)}, u32[]{:S(2)}, u32[]{:S(2)}) collective-permute-start(bf16[32,2048]{1,0:T(8,128)(2,1)S(1)} %get-tuple-element.42), channel_id=1, source_target_pairs={{0,24},{8,16},{16,8},{24,0},{1,25},{9,17},{17,9},{25,1},{2,26},{10... | collective-permute-start | bytes 393224 | tf_op jit(solution)/shard_map/ppermute | solution.py:18
  4.8 7.1 %collective-permute-start.1 = (bf16[32,2048]{1,0:T(8,128)(2,1)S(1)}, bf16[32,2048]{1,0:T(8,128)(2,1)S(1)}, u32[]{:S(2)}, u32[]{:S(2)}) collective-permute-start(bf16[32,2048]{1,0:T(8,128)(2,1)S(1)} %get-tuple-element.41.refs_4_), channel_id=1, source_target_pairs={{0,16},{8,24},{16,0},{24,8},{1,17},{9,25},{17,1},{25,9},{2,18},{10... | collective-permute-start | bytes 393224 | tf_op jit(solution)/shard_map/ppermute | solution.py:18
  6.2 6.3 %collective-permute-start = (bf16[32,2048]{1,0:T(8,128)(2,1)S(1)}, bf16[32,2048]{1,0:T(8,128)(2,1)S(1)}, u32[]{:S(2)}, u32[]{:S(2)}) collective-permute-start(bf16[32,2048]{1,0:T(8,128)(2,1)S(1)} %get-tuple-element.51), channel_id=1, source_target_pairs={{0,8},{8,0},{16,24},{24,16},{1,9},{9,1},{17,25},{25,17},{2,10},{10... | collective-permute-start | bytes 393224 | tf_op jit(solution)/shard_map/ppermute | solution.py:18
  7.6 18.8 %collective-permute-start.4 = (bf16[32,2048]{1,0:T(8,128)(2,1)S(1)}, bf16[32,2048]{1,0:T(8,128)(2,1)S(1)}, u32[]{:S(2)}, u32[]{:S(2)}) collective-permute-start(bf16[32,2048]{1,0:T(8,128)(2,1)S(1)} %get-tuple-element.50.refs_0_), channel_id=1, source_target_pairs={{0,16},{8,24},{16,0},{24,8},{1,17},{9,25},{17,1},{25,9},{2,18},{10... | collective-permute-start | bytes 393224 | tf_op jit(solution)/shard_map/ppermute | solution.py:18
  11.9 14.5 %collective-permute-start.5 = (bf16[32,2048]{1,0:T(8,128)(2,1)S(1)}, bf16[32,2048]{1,0:T(8,128)(2,1)S(1)}, u32[]{:S(2)}, u32[]{:S(2)}) collective-permute-start(bf16[32,2048]{1,0:T(8,128)(2,1)S(1)} %get-tuple-element.51), channel_id=1, source_target_pairs={{0,24},{8,16},{16,8},{24,0},{1,25},{9,17},{17,9},{25,1},{2,26},{10... | collective-permute-start | bytes 393224 | tf_op jit(solution)/shard_map/ppermute | solution.py:18
  12.6 13.8 %collective-permute-start.6 = (f32[16,2048]{1,0:T(8,128)S(1)}, f32[16,2048]{1,0:T(8,128)S(1)}, u32[]{:S(2)}, u32[]{:S(2)}) collective-permute-start(f32[16,2048]{1,0:T(8,128)S(1)} %get-tuple-element.62.refs_0_), channel_id=1, source_target_pairs={{0,8},{8,0},{16,24},{24,16},{1,9},{9,1},{17,25},{25,17},{2,10},{10... | collective-permute-start | bytes 393224 | tf_op jit(solution)/shard_map/ppermute | solution.py:18
  14.2 12.2 %collective-permute-start.7 = (f32[16,2048]{1,0:T(8,128)S(1)}, f32[16,2048]{1,0:T(8,128)S(1)}, u32[]{:S(2)}, u32[]{:S(2)}) collective-permute-start(f32[16,2048]{1,0:T(8,128)S(1)} %get-tuple-element.63.refs_1_), channel_id=1, source_target_pairs={{0,8},{8,0},{16,24},{24,16},{1,9},{9,1},{17,25},{25,17},{2,10},{10... | collective-permute-start | bytes 393224 | tf_op jit(solution)/shard_map/ppermute | solution.py:18
  26.5 1.6 %collective-permute-start.8 = (f32[32,2048]{1,0:T(8,128)S(1)}, f32[32,2048]{1,0:T(8,128)S(1)}, u32[]{:S(2)}, u32[]{:S(2)}) collective-permute-start(f32[32,2048]{1,0:T(8,128)S(1)} %shard_map.55.refs_4_), channel_id=1, source_target_pairs={{0,8},{8,0},{16,24},{24,16},{1,9},{9,1},{17,25},{25,17},{2,10},{10... | collective-permute-start | bytes 786440 | tf_op jit(solution)/shard_map/ppermute | solution.py:18

commit v19 on v18

--- a/solution.py
+++ b/solution.py
@@ -147,11 +147,13 @@
     moved.update({0: near[0], 1: swapped(near[1], "replica", 1)})
     again = {}
     if groups == 4:
-        near, params, momentum = lax.optimization_barrier((near, params, momentum))
+        near, three, params, momentum = lax.optimization_barrier(
+            (near, pieces[3], params, momentum)
+        )
         _, (momentum,) = cut(pseudo_grad, width, (), momentum)
         near, params, momentum = lax.optimization_barrier((near, params, momentum))
         again = {k: swapped(near[k ^ 2], "replica", k) for k in (2, 3)}
-        again[1] = swapped(pieces[3], "replica", 1)
+        again[1] = swapped(three, "replica", 1)
     else:
         _, (momentum,) = cut(pseudo_grad, width, (), momentum)
     wide_piece = jax.ShapeDtypeStruct((rows, width), WIDE)

time: 29.2 us -> 27.1 us (0.928)
  waiting for transfers between devices: 2.51 us -> 0.96 us
  starting transfers between devices: 7.65 us -> 6.34 us
  blocking collectives: 11.9 us -> 12.7 us
    ppermute x9, waiting for transfers between devices: 2.51 us -> 0.96 us  [swapped(): return lax.ppermute(value, axis, [(i, i ^ flip) for i in range(size)])]
    ppermute x9, starting transfers between devices: 7.65 us -> 6.34 us  [swapped(): return lax.ppermute(value, axis, [(i, i ^ flip) for i in range(size)])]
    all_to_all x1, blocking collectives: 11.9 us -> 12.7 us  [per_device(): lax.all_to_all(squares, ('replica', 'fsdp'), split_axis=0, concat_axis=0,...]
  transfers between devices with their start and end apart: 9 -> 9, of which waited for: 2 -> 2; matrix products, arithmetic and copies ran while one was open for 0% -> 0% of each run, Pallas kernels for 15% -> 16%
where the time goes in v19:
time: 27.1 us; the launch traced here: 26.9 us
  blocking collectives  12.7 us (47%)
  starting transfers between devices  6.34 us (23%)
  Pallas kernels  6.19 us (23%)
  waiting for transfers between devices  0.96 us (4%)
  between operations  0.73 us (3%)
    all_to_all x1, blocking collectives, per_device(): lax.all_to_all(squares, ('replica', 'fsdp'), split_axis=0, concat_axis=0,...  12.7 us
    ppermute x9, starting transfers between devices, swapped(): return lax.ppermute(value, axis, [(i, i ^ flip) for i in range(size)])  6.34 us
    pallas_call x3, Pallas kernels, cut(): pl.pallas_call(functools.partial(cut_kernel, flips, len(arrays)), out_sha...  3.62 us
    pallas_call x2, Pallas kernels, update(): pl.pallas_call(functools.partial(update_kernel, flips, sizes, len(earlier...  2.23 us
    ppermute x9, waiting for transfers between devices, swapped(): return lax.ppermute(value, axis, [(i, i ^ flip) for i in range(size)])  0.96 us
  transfers between devices with their start and end apart: 9, of which 2 were waited for; matrix products, arithmetic and copies ran while one was open for 0% of the time, Pallas kernels for 16%

profile of v19, /device:TPU:0, one launch (start us, length us, event | category | flops | bytes accessed | tf_op | source)
XLA Modules:
  0.0 26.9 jit_solution(13018374515073920896)
XLA Ops:
  0.6 1.0 %shard_map.50 = (bf16[32,2048]{1,0:T(8,128)(2,1)S(1)}, bf16[32,2048]{1,0:T(8,128)(2,1)S(1)}) custom-call(bf16[1,32,8192]{2,1,0:T(8,128)(2,1)} %refs_0_.3), custom_call_target="tpu_custom_call" | custom-call | tf_op jit(solution)/shard_map/pallas_call | solution.py:50
  1.6 3.0 %collective-permute-start.1 = (bf16[32,2048]{1,0:T(8,128)(2,1)S(1)}, bf16[32,2048]{1,0:T(8,128)(2,1)S(1)}, u32[]{:S(2)}, u32[]{:S(2)}) collective-permute-start(bf16[32,2048]{1,0:T(8,128)(2,1)S(1)} %get-tuple-element.42.refs_4_), channel_id=1, source_target_pairs={{0,16},{8,24},{16,0},{24,8},{1,17},{9,25},{17,1},{25,9},{2,18},{10... | collective-permute-start | bytes 393224 | tf_op jit(solution)/shard_map/ppermute | solution.py:18
  4.6 0.0 collective-permute-start.2
  4.6 1.4 %shard_map.51 = (bf16[32,2048]{1,0:T(8,128)(2,1)S(1)}, bf16[32,2048]{1,0:T(8,128)(2,1)S(1)}, f32[32,8192]{1,0:T(8,128)S(1)}) custom-call(bf16[1,32,8192]{2,1,0:T(8,128)(2,1)} %refs_0_.3, f32[32,8192]{1,0:T(8,128)} %refs_1_), custom_call_target="tpu_custom_call" | custom-call | tf_op jit(solution)/shard_map/pallas_call | solution.py:50
  6.0 0.3 collective-permute-start.3
  6.3 0.3 %collective-permute-start = (bf16[32,2048]{1,0:T(8,128)(2,1)S(1)}, bf16[32,2048]{1,0:T(8,128)(2,1)S(1)}, u32[]{:S(2)}, u32[]{:S(2)}) collective-permute-start(bf16[32,2048]{1,0:T(8,128)(2,1)S(1)} %get-tuple-element.53), channel_id=1, source_target_pairs={{0,8},{8,0},{16,24},{24,16},{1,9},{9,1},{17,25},{25,17},{2,10},{10... | collective-permute-start | bytes 393224 | tf_op jit(solution)/shard_map/ppermute | solution.py:18
  6.6 1.2 %shard_map.54.momentum = f32[32,8192]{1,0:T(8,128)S(1)} custom-call(bf16[1,32,8192]{2,1,0:T(8,128)(2,1)} %refs_0_.3, f32[32,8192]{1,0:T(8,128)} %refs_1_.1), custom_call_target="tpu_custom_call" | custom-call | tf_op jit(solution)/shard_map/pallas_call | solution.py:50
  7.9 1.8 %collective-permute-start.4 = (bf16[32,2048]{1,0:T(8,128)(2,1)S(1)}, bf16[32,2048]{1,0:T(8,128)(2,1)S(1)}, u32[]{:S(2)}, u32[]{:S(2)}) collective-permute-start(bf16[32,2048]{1,0:T(8,128)(2,1)S(1)} %get-tuple-element.52.refs_0_), channel_id=1, source_target_pairs={{0,16},{8,24},{16,0},{24,8},{1,17},{9,25},{17,1},{25,9},{2,18},{10... | collective-permute-start | bytes 393224 | tf_op jit(solution)/shard_map/ppermute | solution.py:18
  9.6 0.0 collective-permute-done.1.refs_2_
  9.6 0.1 collective-permute-start.5
  9.8 0.7 %collective-permute-done.2.refs_3_ = bf16[32,2048]{1,0:T(8,128)(2,1)S(1)} collective-permute-done((bf16[32,2048]{1,0:T(8,128)(2,1)S(1)}, bf16[32,2048]{1,0:T(8,128)(2,1)S(1)}, u32[]{:S(2)}, u32[]{:S(2)}) %collective-permute-start.2) | collective-permute-done | bytes 131104 | tf_op jit(solution)/shard_map/ppermute | solution.py:18
  10.5 0.0 collective-permute-done.3.refs_5_
  10.5 0.0 collective-permute-done.refs_1_
  10.5 0.1 shard_map.52
  10.6 0.7 %collective-permute-start.6 = (f32[16,2048]{1,0:T(8,128)S(1)}, f32[16,2048]{1,0:T(8,128)S(1)}, u32[]{:S(2)}, u32[]{:S(2)}) collective-permute-start(f32[16,2048]{1,0:T(8,128)S(1)} %get-tuple-element.64.refs_0_), channel_id=1, source_target_pairs={{0,8},{8,0},{16,24},{24,16},{1,9},{9,1},{17,25},{25,17},{2,10},{10... | collective-permute-start | bytes 393224 | tf_op jit(solution)/shard_map/ppermute | solution.py:18
  11.4 0.1 collective-permute-start.7
  11.4 12.7 %all_to_all.5.squares = f32[32,1,128]{2,1,0:T(1,128)S(1)} all-to-all(f32[32,1,128]{2,1,0:T(1,128)S(1)} %get-tuple-element.47), channel_id=1, replica_groups=mesh['replica'=4,'fsdp'=8] {'replica','fsdp'}, dimensions={0} | all-to-all | bytes 32768 | tf_op jit(solution)/shard_map/all_to_all | solution.py:177
  24.1 0.2 shard_map.53.factor
  24.3 0.0 collective-permute-done.4.first
  24.3 0.0 collective-permute-done.5.second
  24.4 0.0 collective-permute-done.6.refs_2_
  24.4 0.0 collective-permute-done.7.refs_3_
  24.4 0.1 collective-permute-start.8
  24.5 1.3 %shard_map.56 = (f32[32,8192]{1,0:T(8,128)}, f32[32,8192]{1,0:T(8,128)}) custom-call(f32[1,128]{1,0:T(1,128)S(1)} %shard_map.53.factor, f32[32,8192]{1,0:T(8,128)S(1)} %get-tuple-element.61.params, f32[32,8192]{1,0:T(8,128)S(1)} %shard_map.54.momentum, f32[16,2048]{1,0:T(8,128)S(1)} %get-tuple-element.64.refs_0_, f32[16,2048]{1,0:T(8,128)S(1)} %get-tuple-element.65.refs_1_, ...), custom_call_target="tpu_custom_call" | custom-call | tf_op jit(solution)/shard_map/pallas_call | solution.py:119
  25.8 0.2 collective-permute-done.8.refs_0_
  26.0 0.9 %shard_map.57 = (f32[32,8192]{1,0:T(8,128)}, f32[32,8192]{1,0:T(8,128)}) custom-call(f32[1,128]{1,0:T(1,128)S(1)} %shard_map.53.factor, f32[32,8192]{1,0:T(8,128)S(1)} %get-tuple-element.61.params, f32[32,8192]{1,0:T(8,128)S(1)} %shard_map.54.momentum, f32[32,2048]{1,0:T(8,128)S(1)} %collective-permute-done.8.refs_0_, ...), custom_call_target="tpu_custom_call", output_to_operand_aliasing={{0}: (4, {}), {1}: (5, {})} | custom-call | tf_op jit(solution)/shard_map/pallas_call | solution.py:119
  (1 shorter events, 0.0 us)
Async XLA Ops:
  1.6 8.0 %collective-permute-start.1 = (bf16[32,2048]{1,0:T(8,128)(2,1)S(1)}, bf16[32,2048]{1,0:T(8,128)(2,1)S(1)}, u32[]{:S(2)}, u32[]{:S(2)}) collective-permute-start(bf16[32,2048]{1,0:T(8,128)(2,1)S(1)} %get-tuple-element.42.refs_4_), channel_id=1, source_target_pairs={{0,16},{8,24},{16,0},{24,8},{1,17},{9,25},{17,1},{25,9},{2,18},{10... | collective-permute-start | bytes 393224 | tf_op jit(solution)/shard_map/ppermute | solution.py:18
  4.6 5.9 %collective-permute-start.2 = (bf16[32,2048]{1,0:T(8,128)(2,1)S(1)}, bf16[32,2048]{1,0:T(8,128)(2,1)S(1)}, u32[]{:S(2)}, u32[]{:S(2)}) collective-permute-start(bf16[32,2048]{1,0:T(8,128)(2,1)S(1)} %get-tuple-element.46), channel_id=1, source_target_pairs={{0,24},{8,16},{16,8},{24,0},{1,25},{9,17},{17,9},{25,1},{2,26},{10... | collective-permute-start | bytes 393224 | tf_op jit(solution)/shard_map/ppermute | solution.py:18
  6.0 4.5 %collective-permute-start.3 = (bf16[32,2048]{1,0:T(8,128)(2,1)S(1)}, bf16[32,2048]{1,0:T(8,128)(2,1)S(1)}, u32[]{:S(2)}, u32[]{:S(2)}) collective-permute-start(bf16[32,2048]{1,0:T(8,128)(2,1)S(1)} %get-tuple-element.46), channel_id=1, source_target_pairs={{0,8},{8,0},{16,24},{24,16},{1,9},{9,1},{17,25},{25,17},{2,10},{10... | collective-permute-start | bytes 393224 | tf_op jit(solution)/shard_map/ppermute | solution.py:18
  6.3 4.2 %collective-permute-start = (bf16[32,2048]{1,0:T(8,128)(2,1)S(1)}, bf16[32,2048]{1,0:T(8,128)(2,1)S(1)}, u32[]{:S(2)}, u32[]{:S(2)}) collective-permute-start(bf16[32,2048]{1,0:T(8,128)(2,1)S(1)} %get-tuple-element.53), channel_id=1, source_target_pairs={{0,8},{8,0},{16,24},{24,16},{1,9},{9,1},{17,25},{25,17},{2,10},{10... | collective-permute-start | bytes 393224 | tf_op jit(solution)/shard_map/ppermute | solution.py:18
  7.9 16.4 %collective-permute-start.4 = (bf16[32,2048]{1,0:T(8,128)(2,1)S(1)}, bf16[32,2048]{1,0:T(8,128)(2,1)S(1)}, u32[]{:S(2)}, u32[]{:S(2)}) collective-permute-start(bf16[32,2048]{1,0:T(8,128)(2,1)S(1)} %get-tuple-element.52.refs_0_), channel_id=1, source_target_pairs={{0,16},{8,24},{16,0},{24,8},{1,17},{9,25},{17,1},{25,9},{2,18},{10... | collective-permute-start | bytes 393224 | tf_op jit(solution)/shard_map/ppermute | solution.py:18
  9.6 14.7 %collective-permute-start.5 = (bf16[32,2048]{1,0:T(8,128)(2,1)S(1)}, bf16[32,2048]{1,0:T(8,128)(2,1)S(1)}, u32[]{:S(2)}, u32[]{:S(2)}) collective-permute-start(bf16[32,2048]{1,0:T(8,128)(2,1)S(1)} %get-tuple-element.53), channel_id=1, source_target_pairs={{0,24},{8,16},{16,8},{24,0},{1,25},{9,17},{17,9},{25,1},{2,26},{10... | collective-permute-start | bytes 393224 | tf_op jit(solution)/shard_map/ppermute | solution.py:18
  10.6 13.7 %collective-permute-start.6 = (f32[16,2048]{1,0:T(8,128)S(1)}, f32[16,2048]{1,0:T(8,128)S(1)}, u32[]{:S(2)}, u32[]{:S(2)}) collective-permute-start(f32[16,2048]{1,0:T(8,128)S(1)} %get-tuple-element.64.refs_0_), channel_id=1, source_target_pairs={{0,8},{8,0},{16,24},{24,16},{1,9},{9,1},{17,25},{25,17},{2,10},{10... | collective-permute-start | bytes 393224 | tf_op jit(solution)/shard_map/ppermute | solution.py:18
  11.4 13.0 %collective-permute-start.7 = (f32[16,2048]{1,0:T(8,128)S(1)}, f32[16,2048]{1,0:T(8,128)S(1)}, u32[]{:S(2)}, u32[]{:S(2)}) collective-permute-start(f32[16,2048]{1,0:T(8,128)S(1)} %get-tuple-element.65.refs_1_), channel_id=1, source_target_pairs={{0,8},{8,0},{16,24},{24,16},{1,9},{9,1},{17,25},{25,17},{2,10},{10... | collective-permute-start | bytes 393224 | tf_op jit(solution)/shard_map/ppermute | solution.py:18
  24.4 1.6 %collective-permute-start.8 = (f32[32,2048]{1,0:T(8,128)S(1)}, f32[32,2048]{1,0:T(8,128)S(1)}, u32[]{:S(2)}, u32[]{:S(2)}) collective-permute-start(f32[32,2048]{1,0:T(8,128)S(1)} %shard_map.55.refs_4_), channel_id=1, source_target_pairs={{0,8},{8,0},{16,24},{24,16},{1,9},{9,1},{17,25},{25,17},{2,10},{10... | collective-permute-start | bytes 786440 | tf_op jit(solution)/shard_map/ppermute | solution.py:18

commit v20 on v11

--- a/solution.py
+++ b/solution.py
@@ -70,11 +70,15 @@
     squares[...] = jnp.broadcast_to(lanes[None], squares.shape)
 
 
-def update_kernel(count, flips, passed, squares, params, momentum, *refs):
+def update_kernel(count, flips, passed, scale, params, momentum, *refs):
     averages, refs = refs[: len(flips)], refs[len(flips) + passed :]
-    new_params, new_momentum, params_out, momentum_out, sems = refs
-    square_sum = jnp.sum(squares[...], keepdims=True).reshape(1, 1)
-    factor = 0.2 / jnp.sqrt(square_sum / WIDE(count) + 1e-06)
+    new_params, new_momentum, factor_out, params_out, momentum_out, sems = refs
+    if passed:
+        factor = scale[:, :1]
+    else:
+        square_sum = jnp.sum(scale[...], keepdims=True).reshape(1, 1)
+        factor = 0.2 / jnp.sqrt(square_sum / WIDE(count) + 1e-06)
+    factor_out[...] = jnp.broadcast_to(factor, factor_out.shape)
     width = averages[0].shape[1]
     copies = []
     for i, (k, average) in enumerate(zip(flips, averages)):
@@ -93,15 +97,15 @@
         copy.wait()
 
 
-def update(count, flips, averages, squares, params, momentum, earlier=()):
+def update(count, flips, averages, scale, params, momentum, earlier=()):
     rows, width = averages[0].shape
     out = jax.ShapeDtypeStruct(params.shape, WIDE)
     first = 3 + len(flips)
     return pl.pallas_call(
         functools.partial(update_kernel, count, flips, len(earlier)),
-        out_shape=[out, out],
+        out_shape=[out, out, jax.ShapeDtypeStruct((1, 128), WIDE)],
         in_specs=[VMEM] * first + [HBM] * len(earlier),
-        out_specs=[HBM] * 2,
+        out_specs=[HBM, HBM, VMEM],
         scratch_shapes=[
             pltpu.VMEM((len(flips), rows, width), WIDE),
             pltpu.VMEM((len(flips), rows, width), WIDE),
@@ -109,7 +113,7 @@
         ],
         input_output_aliases={first + i: i for i in range(len(earlier))},
         compiler_params=pltpu.CompilerParams(vmem_limit_bytes=LIMIT),
-    )(squares, params, momentum, *averages, *earlier)
+    )(scale, params, momentum, *averages, *earlier)
 
 
 def per_device(pseudo_grad, params, momentum):
@@ -148,12 +152,14 @@
         averages[k + 1] = swapped(averages[k], "replica", 1)
     here = [k for k in range(groups) if k < 2 or k % 2 == 0]
     late = [k for k in range(groups) if k not in here]
-    outs = update(count, here, [averages[k] for k in here], squares, params, momentum)
+    *outs, factor = update(
+        count, here, [averages[k] for k in here], squares, params, momentum
+    )
     if late:
-        outs = update(
-            count, late, [averages[k] for k in late], squares, params, momentum, outs
+        *outs, factor = update(
+            count, late, [averages[k] for k in late], factor, params, momentum, outs
         )
-    return outs
+    return tuple(outs)
 
 
 def solution(mesh):

time: 27 us -> 27.4 us (1.015)
  Pallas kernels: 5.26 us -> 5.7 us
    pallas_call x2, Pallas kernels: 2.43 us -> 2.87 us  [update(): pl.pallas_call(functools.partial(update_kernel, count, flips, len(earlier...]
  transfers between devices with their start and end apart: 6 -> 6, of which waited for: 3 -> 3; matrix products, arithmetic and copies ran while one was open for 0% -> 0% of each run, Pallas kernels for 12% -> 11%
where the time goes in v20:
time: 27.4 us; the launch traced here: 27.3 us
  blocking collectives  11.8 us (43%)
  Pallas kernels  5.7 us (21%)
  starting transfers between devices  5.06 us (18%)
  waiting for transfers between devices  3.99 us (15%)
  between operations  0.67 us (2%)
    all_to_all x1, blocking collectives, per_device(): lax.all_to_all(squares, ('replica', 'fsdp'), split_axis=0, concat_axis=0,...  11.8 us
    ppermute x6, starting transfers between devices, swapped(): return lax.ppermute(value, axis, [(i, i ^ flip) for i in range(size)])  5.06 us
    ppermute x6, waiting for transfers between devices, swapped(): return lax.ppermute(value, axis, [(i, i ^ flip) for i in range(size)])  3.99 us
    pallas_call x2, Pallas kernels, update(): pl.pallas_call(functools.partial(update_kernel, count, flips, len(earlier...  2.87 us
    pallas_call x2, Pallas kernels, cut(): pl.pallas_call(functools.partial(cut_kernel, flips, len(arrays)), out_sha...  2.72 us
  transfers between devices with their start and end apart: 6, of which 3 were waited for; matrix products, arithmetic and copies ran while one was open for 0% of the time, Pallas kernels for 11%

profile of v20, /device:TPU:0, one launch (start us, length us, event | category | flops | bytes accessed | tf_op | source)
XLA Modules:
  0.0 27.3 jit_solution(13435567561030064809)
XLA Ops:
  0.6 1.0 %shard_map.50 = (bf16[32,2048]{1,0:T(8,128)(2,1)S(1)}, bf16[32,2048]{1,0:T(8,128)(2,1)S(1)}) custom-call(bf16[1,32,8192]{2,1,0:T(8,128)(2,1)} %refs_0_.2), custom_call_target="tpu_custom_call" | custom-call | tf_op jit(solution)/shard_map/pallas_call | solution.py:50
  1.6 3.0 %collective-permute-start.1 = (bf16[32,2048]{1,0:T(8,128)(2,1)S(1)}, bf16[32,2048]{1,0:T(8,128)(2,1)S(1)}, u32[]{:S(2)}, u32[]{:S(2)}) collective-permute-start(bf16[32,2048]{1,0:T(8,128)(2,1)S(1)} %get-tuple-element.31), channel_id=1, source_target_pairs={{0,16},{8,24},{16,0},{24,8},{1,17},{9,25},{17,1},{25,9},{2,18},{10... | collective-permute-start | bytes 393224 | tf_op jit(solution)/shard_map/ppermute | solution.py:18
  4.6 0.0 collective-permute-start.2
  4.6 1.7 %shard_map.51 = (bf16[32,2048]{1,0:T(8,128)(2,1)S(1)}, bf16[32,2048]{1,0:T(8,128)(2,1)S(1)}, f32[32,8192]{1,0:T(8,128)S(1)}, f32[32,8192]{1,0:T(8,128)S(1)}) custom-call(bf16[1,32,8192]{2,1,0:T(8,128)(2,1)} %refs_0_.2, f32[32,8192]{1,0:T(8,128)} %refs_1_, f32[32,8192]{1,0:T(8,128)} %refs_2_), custom_call_target="tpu_custom_call" | custom-call | tf_op jit(solution)/shard_map/pallas_call | solution.py:50
  6.4 0.3 collective-permute-start
  6.6 2.0 %collective-permute-done.1.refs_2_ = bf16[32,2048]{1,0:T(8,128)(2,1)S(1)} collective-permute-done((bf16[32,2048]{1,0:T(8,128)(2,1)S(1)}, bf16[32,2048]{1,0:T(8,128)(2,1)S(1)}, u32[]{:S(2)}, u32[]{:S(2)}) %collective-permute-start.1) | collective-permute-done | bytes 131104 | tf_op jit(solution)/shard_map/ppermute | solution.py:18
  8.6 1.9 %collective-permute-done.2.refs_3_ = bf16[32,2048]{1,0:T(8,128)(2,1)S(1)} collective-permute-done((bf16[32,2048]{1,0:T(8,128)(2,1)S(1)}, bf16[32,2048]{1,0:T(8,128)(2,1)S(1)}, u32[]{:S(2)}, u32[]{:S(2)}) %collective-permute-start.2) | collective-permute-done | bytes 131104 | tf_op jit(solution)/shard_map/ppermute | solution.py:18
  10.5 0.0 collective-permute-done.refs_1_
  10.5 0.1 shard_map.52
  10.6 1.1 %collective-permute-start.4 = (f32[32,2048]{1,0:T(8,128)S(1)}, f32[32,2048]{1,0:T(8,128)S(1)}, u32[]{:S(2)}, u32[]{:S(2)}) collective-permute-start(f32[32,2048]{1,0:T(8,128)S(1)} %get-tuple-element.38.refs_0_), channel_id=1, source_target_pairs={{0,16},{8,24},{16,0},{24,8},{1,17},{9,25},{17,1},{25,9},{2,18},{10... | collective-permute-start | bytes 786440 | tf_op jit(solution)/shard_map/ppermute | solution.py:18
  11.7 0.7 %collective-permute-start.3 = (f32[32,2048]{1,0:T(8,128)S(1)}, f32[32,2048]{1,0:T(8,128)S(1)}, u32[]{:S(2)}, u32[]{:S(2)}) collective-permute-start(f32[32,2048]{1,0:T(8,128)S(1)} %get-tuple-element.38.refs_0_), channel_id=1, source_target_pairs={{0,8},{8,0},{16,24},{24,16},{1,9},{9,1},{17,25},{25,17},{2,10},{10... | collective-permute-start | bytes 786440 | tf_op jit(solution)/shard_map/ppermute | solution.py:18
  12.4 11.8 %all_to_all.5.scale = f32[32,1,128]{2,1,0:T(1,128)S(1)} all-to-all(f32[32,1,128]{2,1,0:T(1,128)S(1)} %get-tuple-element.33), channel_id=1, replica_groups=mesh['replica'=4,'fsdp'=8] {'replica','fsdp'}, dimensions={0} | all-to-all | bytes 32768 | tf_op jit(solution)/shard_map/all_to_all | solution.py:147
  24.2 0.0 collective-permute-done.4.refs_2_
  24.3 0.0 collective-permute-done.3.refs_1_
  24.3 0.0 collective-permute-start.5
  24.3 1.4 %shard_map.53 = (f32[32,8192]{1,0:T(8,128)}, f32[32,8192]{1,0:T(8,128)}, f32[1,128]{1,0:T(1,128)S(1)}) custom-call(f32[32,1,128]{2,1,0:T(1,128)S(1)} %all_to_all.5.scale, f32[32,8192]{1,0:T(8,128)S(1)} %get-tuple-element.36.params, f32[32,8192]{1,0:T(8,128)S(1)} %get-tuple-element.37.momentum, f32[32,2048]{1,0:T(8,128)S(1)} %get-tuple-element.38.refs_0_, ...), custom_call_target="tpu_custom_call" | custom-call | tf_op jit(solution)/shard_map/pallas_call | solution.py:104
  25.7 0.1 collective-permute-done.5.refs_0_
  25.8 1.5 %shard_map.54 = (f32[32,8192]{1,0:T(8,128)}, f32[32,8192]{1,0:T(8,128)}, f32[1,128]{1,0:T(1,128)}) custom-call(f32[1,128]{1,0:T(1,128)S(1)} %get-tuple-element.41.scale, f32[32,8192]{1,0:T(8,128)S(1)} %get-tuple-element.36.params, f32[32,8192]{1,0:T(8,128)S(1)} %get-tuple-element.37.momentum, ...), custom_call_target="tpu_custom_call", output_to_operand_aliasing={{0}: (4, {}), {1}: (5, {})} | custom-call | tf_op jit(solution)/shard_map/pallas_call | solution.py:104
Async XLA Ops:
  1.6 6.9 %collective-permute-start.1 = (bf16[32,2048]{1,0:T(8,128)(2,1)S(1)}, bf16[32,2048]{1,0:T(8,128)(2,1)S(1)}, u32[]{:S(2)}, u32[]{:S(2)}) collective-permute-start(bf16[32,2048]{1,0:T(8,128)(2,1)S(1)} %get-tuple-element.31), channel_id=1, source_target_pairs={{0,16},{8,24},{16,0},{24,8},{1,17},{9,25},{17,1},{25,9},{2,18},{10... | collective-permute-start | bytes 393224 | tf_op jit(solution)/shard_map/ppermute | solution.py:18
  4.6 5.9 %collective-permute-start.2 = (bf16[32,2048]{1,0:T(8,128)(2,1)S(1)}, bf16[32,2048]{1,0:T(8,128)(2,1)S(1)}, u32[]{:S(2)}, u32[]{:S(2)}) collective-permute-start(bf16[32,2048]{1,0:T(8,128)(2,1)S(1)} %get-tuple-element.32), channel_id=1, source_target_pairs={{0,24},{8,16},{16,8},{24,0},{1,25},{9,17},{17,9},{25,1},{2,26},{10... | collective-permute-start | bytes 393224 | tf_op jit(solution)/shard_map/ppermute | solution.py:18
  6.4 4.1 %collective-permute-start = (bf16[32,2048]{1,0:T(8,128)(2,1)S(1)}, bf16[32,2048]{1,0:T(8,128)(2,1)S(1)}, u32[]{:S(2)}, u32[]{:S(2)}) collective-permute-start(bf16[32,2048]{1,0:T(8,128)(2,1)S(1)} %get-tuple-element.30), channel_id=1, source_target_pairs={{0,8},{8,0},{16,24},{24,16},{1,9},{9,1},{17,25},{25,17},{2,10},{10... | collective-permute-start | bytes 393224 | tf_op jit(solution)/shard_map/ppermute | solution.py:18
  10.6 13.6 %collective-permute-start.4 = (f32[32,2048]{1,0:T(8,128)S(1)}, f32[32,2048]{1,0:T(8,128)S(1)}, u32[]{:S(2)}, u32[]{:S(2)}) collective-permute-start(f32[32,2048]{1,0:T(8,128)S(1)} %get-tuple-element.38.refs_0_), channel_id=1, source_target_pairs={{0,16},{8,24},{16,0},{24,8},{1,17},{9,25},{17,1},{25,9},{2,18},{10... | collective-permute-start | bytes 786440 | tf_op jit(solution)/shard_map/ppermute | solution.py:18
  11.7 12.5 %collective-permute-start.3 = (f32[32,2048]{1,0:T(8,128)S(1)}, f32[32,2048]{1,0:T(8,128)S(1)}, u32[]{:S(2)}, u32[]{:S(2)}) collective-permute-start(f32[32,2048]{1,0:T(8,128)S(1)} %get-tuple-element.38.refs_0_), channel_id=1, source_target_pairs={{0,8},{8,0},{16,24},{24,16},{1,9},{9,1},{17,25},{25,17},{2,10},{10... | collective-permute-start | bytes 786440 | tf_op jit(solution)/shard_map/ppermute | solution.py:18
  24.3 1.5 %collective-permute-start.5 = (f32[32,2048]{1,0:T(8,128)S(1)}, f32[32,2048]{1,0:T(8,128)S(1)}, u32[]{:S(2)}, u32[]{:S(2)}) collective-permute-start(f32[32,2048]{1,0:T(8,128)S(1)} %collective-permute-done.4.refs_2_), channel_id=1, source_target_pairs={{0,8},{8,0},{16,24},{24,16},{1,9},{9,1},{17,25},{25,17},{2,10},{10... | collective-permute-start | bytes 786440 | tf_op jit(solution)/shard_map/ppermute | solution.py:18

commit v21 on v11

--- a/solution.py
+++ b/solution.py
@@ -123,7 +123,7 @@
     pieces, pseudo_grad, params, momentum = lax.optimization_barrier(
         (pieces, pseudo_grad, params, momentum)
     )
-    moved = {k: swapped(pieces[k], "replica", k) for k in range(2, groups)}
+    moved = {k: swapped(pieces[k], "replica", k) for k in reversed(range(2, groups))}
     near, (params, momentum) = cut(pseudo_grad, width, range(2), params, momentum)
     moved.update({0: near[0], 1: swapped(near[1], "replica", 1)})
     average, squares = pl.pallas_call(
@@ -135,7 +135,7 @@
         in_specs=[VMEM] * groups,
         out_specs=[VMEM] * 2,
         compiler_params=limit,
-    )(*[moved[k] for k in range(groups)])
+    )(*[moved[k] for k in reversed(range(groups))])
     averages = {0: average}
     for k in range(2, groups, 2):
         averages[k] = swapped(average, "replica", k)

time: 27 us -> 28.1 us (1.041)
  waiting for transfers between devices: 3.99 us -> 4.51 us
  starting transfers between devices: 5.06 us -> 5.56 us
    ppermute x6, waiting for transfers between devices: 3.99 us -> 4.51 us  [swapped(): return lax.ppermute(value, axis, [(i, i ^ flip) for i in range(size)])]
    ppermute x6, starting transfers between devices: 5.06 us -> 5.56 us  [swapped(): return lax.ppermute(value, axis, [(i, i ^ flip) for i in range(size)])]
  transfers between devices with their start and end apart: 6 -> 6, of which waited for: 3 -> 3; matrix products, arithmetic and copies ran while one was open for 0% -> 0% of each run, Pallas kernels for 12% -> 11%
where the time goes in v21:
time: 28.1 us; the launch traced here: 27.9 us
  blocking collectives  11.9 us (42%)
  starting transfers between devices  5.56 us (20%)
  Pallas kernels  5.26 us (19%)
  waiting for transfers between devices  4.51 us (16%)
  between operations  0.67 us (2%)
    all_to_all x1, blocking collectives, per_device(): lax.all_to_all(squares, ('replica', 'fsdp'), split_axis=0, concat_axis=0,...  11.9 us
    ppermute x6, starting transfers between devices, swapped(): return lax.ppermute(value, axis, [(i, i ^ flip) for i in range(size)])  5.56 us
    ppermute x6, waiting for transfers between devices, swapped(): return lax.ppermute(value, axis, [(i, i ^ flip) for i in range(size)])  4.51 us
    pallas_call x2, Pallas kernels, cut(): pl.pallas_call(functools.partial(cut_kernel, flips, len(arrays)), out_sha...  2.71 us
    pallas_call x2, Pallas kernels, update(): pl.pallas_call(functools.partial(update_kernel, count, flips, len(earlier...  2.43 us
  transfers between devices with their start and end apart: 6, of which 3 were waited for; matrix products, arithmetic and copies ran while one was open for 0% of the time, Pallas kernels for 11%

profile of v21, /device:TPU:0, one launch (start us, length us, event | category | flops | bytes accessed | tf_op | source)
XLA Modules:
  0.0 27.9 jit_solution(6008425454177645381)
XLA Ops:
  0.6 1.0 %shard_map.50 = (bf16[32,2048]{1,0:T(8,128)(2,1)S(1)}, bf16[32,2048]{1,0:T(8,128)(2,1)S(1)}) custom-call(bf16[1,32,8192]{2,1,0:T(8,128)(2,1)} %refs_0_.2), custom_call_target="tpu_custom_call" | custom-call | tf_op jit(solution)/shard_map/pallas_call | solution.py:50
  1.6 2.4 %collective-permute-start = (bf16[32,2048]{1,0:T(8,128)(2,1)S(1)}, bf16[32,2048]{1,0:T(8,128)(2,1)S(1)}, u32[]{:S(2)}, u32[]{:S(2)}) collective-permute-start(bf16[32,2048]{1,0:T(8,128)(2,1)S(1)} %get-tuple-element.23), channel_id=1, source_target_pairs={{0,24},{8,16},{16,8},{24,0},{1,25},{9,17},{17,9},{25,1},{2,26},{10... | collective-permute-start | bytes 393224 | tf_op jit(solution)/shard_map/ppermute | solution.py:18
  4.1 0.6 %collective-permute-start.1 = (bf16[32,2048]{1,0:T(8,128)(2,1)S(1)}, bf16[32,2048]{1,0:T(8,128)(2,1)S(1)}, u32[]{:S(2)}, u32[]{:S(2)}) collective-permute-start(bf16[32,2048]{1,0:T(8,128)(2,1)S(1)} %get-tuple-element.24), channel_id=1, source_target_pairs={{0,16},{8,24},{16,0},{24,8},{1,17},{9,25},{17,1},{25,9},{2,18},{10... | collective-permute-start | bytes 393224 | tf_op jit(solution)/shard_map/ppermute | solution.py:18
  4.7 1.7 %shard_map.51 = (bf16[32,2048]{1,0:T(8,128)(2,1)S(1)}, bf16[32,2048]{1,0:T(8,128)(2,1)S(1)}, f32[32,8192]{1,0:T(8,128)S(1)}, f32[32,8192]{1,0:T(8,128)S(1)}) custom-call(bf16[1,32,8192]{2,1,0:T(8,128)(2,1)} %refs_0_.2, f32[32,8192]{1,0:T(8,128)} %refs_1_, f32[32,8192]{1,0:T(8,128)} %refs_2_), custom_call_target="tpu_custom_call" | custom-call | tf_op jit(solution)/shard_map/pallas_call | solution.py:50
  6.4 0.1 collective-permute-start.2
  6.5 1.4 %collective-permute-done.refs_0_ = bf16[32,2048]{1,0:T(8,128)(2,1)S(1)} collective-permute-done((bf16[32,2048]{1,0:T(8,128)(2,1)S(1)}, bf16[32,2048]{1,0:T(8,128)(2,1)S(1)}, u32[]{:S(2)}, u32[]{:S(2)}) %collective-permute-start) | collective-permute-done | bytes 131104 | tf_op jit(solution)/shard_map/ppermute | solution.py:18
  8.0 3.0 %collective-permute-done.1.refs_1_ = bf16[32,2048]{1,0:T(8,128)(2,1)S(1)} collective-permute-done((bf16[32,2048]{1,0:T(8,128)(2,1)S(1)}, bf16[32,2048]{1,0:T(8,128)(2,1)S(1)}, u32[]{:S(2)}, u32[]{:S(2)}) %collective-permute-start.1) | collective-permute-done | bytes 131104 | tf_op jit(solution)/shard_map/ppermute | solution.py:18
  10.9 0.0 collective-permute-done.2.refs_2_
  10.9 0.1 shard_map.52
  11.1 2.4 %collective-permute-start.4 = (f32[32,2048]{1,0:T(8,128)S(1)}, f32[32,2048]{1,0:T(8,128)S(1)}, u32[]{:S(2)}, u32[]{:S(2)}) collective-permute-start(f32[32,2048]{1,0:T(8,128)S(1)} %get-tuple-element.36.refs_0_), channel_id=1, source_target_pairs={{0,16},{8,24},{16,0},{24,8},{1,17},{9,25},{17,1},{25,9},{2,18},{10... | collective-permute-start | bytes 786440 | tf_op jit(solution)/shard_map/ppermute | solution.py:18
  13.4 0.0 collective-permute-start.3
  13.4 11.9 %all_to_all.5.squares = f32[32,1,128]{2,1,0:T(1,128)S(1)} all-to-all(f32[32,1,128]{2,1,0:T(1,128)S(1)} %get-tuple-element.30), channel_id=1, replica_groups=mesh['replica'=4,'fsdp'=8] {'replica','fsdp'}, dimensions={0} | all-to-all | bytes 32768 | tf_op jit(solution)/shard_map/all_to_all | solution.py:143
  25.4 0.0 collective-permute-done.4.refs_2_
  25.4 0.0 collective-permute-done.3.refs_1_
  25.4 0.0 collective-permute-start.5
  25.4 1.4 %shard_map.53 = (f32[32,8192]{1,0:T(8,128)}, f32[32,8192]{1,0:T(8,128)}) custom-call(f32[32,1,128]{2,1,0:T(1,128)S(1)} %all_to_all.5.squares, f32[32,8192]{1,0:T(8,128)S(1)} %get-tuple-element.33.params, f32[32,8192]{1,0:T(8,128)S(1)} %get-tuple-element.34.momentum, f32[32,2048]{1,0:T(8,128)S(1)} %get-tuple-element.36.refs_0_, ...), custom_call_target="tpu_custom_call" | custom-call | tf_op jit(solution)/shard_map/pallas_call | solution.py:100
  26.8 0.1 collective-permute-done.5.refs_0_
  26.9 1.0 %shard_map.54 = (f32[32,8192]{1,0:T(8,128)}, f32[32,8192]{1,0:T(8,128)}) custom-call(f32[32,1,128]{2,1,0:T(1,128)S(1)} %all_to_all.5.squares, f32[32,8192]{1,0:T(8,128)S(1)} %get-tuple-element.33.params, f32[32,8192]{1,0:T(8,128)S(1)} %get-tuple-element.34.momentum, ...), custom_call_target="tpu_custom_call", output_to_operand_aliasing={{0}: (4, {}), {1}: (5, {})} | custom-call | tf_op jit(solution)/shard_map/pallas_call | solution.py:100
Async XLA Ops:
  1.6 6.3 %collective-permute-start = (bf16[32,2048]{1,0:T(8,128)(2,1)S(1)}, bf16[32,2048]{1,0:T(8,128)(2,1)S(1)}, u32[]{:S(2)}, u32[]{:S(2)}) collective-permute-start(bf16[32,2048]{1,0:T(8,128)(2,1)S(1)} %get-tuple-element.23), channel_id=1, source_target_pairs={{0,24},{8,16},{16,8},{24,0},{1,25},{9,17},{17,9},{25,1},{2,26},{10... | collective-permute-start | bytes 393224 | tf_op jit(solution)/shard_map/ppermute | solution.py:18
  4.1 6.9 %collective-permute-start.1 = (bf16[32,2048]{1,0:T(8,128)(2,1)S(1)}, bf16[32,2048]{1,0:T(8,128)(2,1)S(1)}, u32[]{:S(2)}, u32[]{:S(2)}) collective-permute-start(bf16[32,2048]{1,0:T(8,128)(2,1)S(1)} %get-tuple-element.24), channel_id=1, source_target_pairs={{0,16},{8,24},{16,0},{24,8},{1,17},{9,25},{17,1},{25,9},{2,18},{10... | collective-permute-start | bytes 393224 | tf_op jit(solution)/shard_map/ppermute | solution.py:18
  6.4 4.5 %collective-permute-start.2 = (bf16[32,2048]{1,0:T(8,128)(2,1)S(1)}, bf16[32,2048]{1,0:T(8,128)(2,1)S(1)}, u32[]{:S(2)}, u32[]{:S(2)}) collective-permute-start(bf16[32,2048]{1,0:T(8,128)(2,1)S(1)} %get-tuple-element.28), channel_id=1, source_target_pairs={{0,8},{8,0},{16,24},{24,16},{1,9},{9,1},{17,25},{25,17},{2,10},{10... | collective-permute-start | bytes 393224 | tf_op jit(solution)/shard_map/ppermute | solution.py:18
  11.1 14.3 %collective-permute-start.4 = (f32[32,2048]{1,0:T(8,128)S(1)}, f32[32,2048]{1,0:T(8,128)S(1)}, u32[]{:S(2)}, u32[]{:S(2)}) collective-permute-start(f32[32,2048]{1,0:T(8,128)S(1)} %get-tuple-element.36.refs_0_), channel_id=1, source_target_pairs={{0,16},{8,24},{16,0},{24,8},{1,17},{9,25},{17,1},{25,9},{2,18},{10... | collective-permute-start | bytes 786440 | tf_op jit(solution)/shard_map/ppermute | solution.py:18
  13.4 12.0 %collective-permute-start.3 = (f32[32,2048]{1,0:T(8,128)S(1)}, f32[32,2048]{1,0:T(8,128)S(1)}, u32[]{:S(2)}, u32[]{:S(2)}) collective-permute-start(f32[32,2048]{1,0:T(8,128)S(1)} %get-tuple-element.36.refs_0_), channel_id=1, source_target_pairs={{0,8},{8,0},{16,24},{24,16},{1,9},{9,1},{17,25},{25,17},{2,10},{10... | collective-permute-start | bytes 786440 | tf_op jit(solution)/shard_map/ppermute | solution.py:18
  25.4 1.5 %collective-permute-start.5 = (f32[32,2048]{1,0:T(8,128)S(1)}, f32[32,2048]{1,0:T(8,128)S(1)}, u32[]{:S(2)}, u32[]{:S(2)}) collective-permute-start(f32[32,2048]{1,0:T(8,128)S(1)} %collective-permute-done.4.refs_2_), channel_id=1, source_target_pairs={{0,8},{8,0},{16,24},{24,16},{1,9},{9,1},{17,25},{25,17},{2,10},{10... | collective-permute-start | bytes 786440 | tf_op jit(solution)/shard_map/ppermute | solution.py:18

commit v22 on v17

--- a/solution.py
+++ b/solution.py
@@ -74,9 +74,10 @@
     squares[...] = jnp.broadcast_to(lanes[None], squares.shape)
 
 
-def join_kernel(groups, here, first, second, average):
+def join_kernel(groups, own, here, first, second, averages):
     there = first[...].astype(WIDE) + second[...].astype(WIDE)
-    average[...] = (here[...] + there) / WIDE(groups)
+    averages[0] = own[...]
+    averages[1] = (here[...] + there) / WIDE(groups)
 
 
 def factor_kernel(count, squares, factor):
@@ -85,13 +86,16 @@
 
 
 def update_kernel(flips, passed, factor, params, momentum, *refs):
-    averages, refs = refs[: len(flips)], refs[len(flips) + passed :]
+    if len(refs[0].shape) == 3:
+        averages, refs = [refs[0][i] for i in range(len(flips))], refs[1 + passed :]
+    else:
+        averages, refs = [ref[...] for ref in refs[: len(flips)]], refs[len(flips) + passed :]
     new_params, new_momentum, params_out, momentum_out, sems = refs
-    width = averages[0].shape[1]
+    width = params_out.shape[2]
     copies = []
     for i, (k, average) in enumerate(zip(flips, averages)):
         cols = piece_of(k, width)
-        clipped = factor[:, :1] * average[...]
+        clipped = factor[:, :1] * average
         fresh = 0.9 * momentum[:, cols] + clipped
         momentum_out[i] = fresh
         params_out[i] = params[:, cols] - 0.7 * (clipped + 0.9 * fresh)
@@ -106,9 +110,9 @@
 
 
 def update(flips, averages, factor, params, momentum, earlier=()):
-    rows, width = averages[0].shape
+    rows, width = averages[0].shape[-2:]
     out = jax.ShapeDtypeStruct(params.shape, WIDE)
-    first = 3 + len(flips)
+    first = 3 + len(averages)
     return pl.pallas_call(
         functools.partial(update_kernel, flips, len(earlier)),
         out_shape=[out, out],
@@ -173,16 +177,18 @@
         out_specs=VMEM,
         compiler_params=limit,
     )(squares)
-    factor, again = lax.optimization_barrier((factor, again))
+    factor, again, averages = lax.optimization_barrier((factor, again, averages))
     if groups == 4:
-        averages[2] = pl.pallas_call(
+        joined = pl.pallas_call(
             functools.partial(join_kernel, groups),
-            out_shape=wide_piece,
-            in_specs=[VMEM] * 3,
+            out_shape=jax.ShapeDtypeStruct((2, rows, width), WIDE),
+            in_specs=[VMEM] * 4,
             out_specs=VMEM,
             compiler_params=limit,
-        )(*other_sum, again[2], again[3])
-    factor, averages = lax.optimization_barrier((factor, averages))
+        )(averages[0], *other_sum, again[2], again[3])
+        mates = swapped(joined, "replica", 1)
+        outs = update((0, 2), [joined], factor, params, momentum)
+        return update((1, 3), [mates], factor, params, momentum, outs)
     for k in range(0, groups, 2):
         averages[k + 1] = swapped(averages[k], "replica", 1)
     here = [k for k in range(groups) if k % 2 == 0]

time: 27.1 us -> 27.1 us (level)
  waiting for transfers between devices: 1.02 us -> 1.52 us
  starting transfers between devices: 6.04 us -> 5.55 us
    ppermute x8 -> x7, waiting for transfers between devices: 1.02 us -> 1.52 us  [swapped(): return lax.ppermute(value, axis, [(i, i ^ flip) for i in range(size)])]
    ppermute x8 -> x7, starting transfers between devices: 6.04 us -> 5.55 us  [swapped(): return lax.ppermute(value, axis, [(i, i ^ flip) for i in range(size)])]
  transfers between devices with their start and end apart: 8 -> 7, of which waited for: 2 -> 2; matrix products, arithmetic and copies ran while one was open for 0% -> 0% of each run, Pallas kernels for 15% -> 15%
where the time goes in v22:
time: 27.1 us; the launch traced here: 26.9 us
  blocking collectives  12.9 us (48%)
  Pallas kernels  6.22 us (23%)
  starting transfers between devices  5.55 us (20%)
  waiting for transfers between devices  1.52 us (6%)
  between operations  0.71 us (3%)
    all_to_all x1, blocking collectives, per_device(): lax.all_to_all(squares, ('replica', 'fsdp'), split_axis=0, concat_axis=0,...  12.9 us
    ppermute x7, starting transfers between devices, swapped(): return lax.ppermute(value, axis, [(i, i ^ flip) for i in range(size)])  5.55 us
    pallas_call x3, Pallas kernels, cut(): pl.pallas_call(functools.partial(cut_kernel, flips, len(arrays)), out_sha...  3.62 us
    pallas_call x2, Pallas kernels, update(): pl.pallas_call(functools.partial(update_kernel, flips, len(earlier)), out...  2.24 us
    ppermute x7, waiting for transfers between devices, swapped(): return lax.ppermute(value, axis, [(i, i ^ flip) for i in range(size)])  1.52 us
  transfers between devices with their start and end apart: 7, of which 2 were waited for; matrix products, arithmetic and copies ran while one was open for 0% of the time, Pallas kernels for 15%

profile of v22, /device:TPU:0, one launch (start us, length us, event | category | flops | bytes accessed | tf_op | source)
XLA Modules:
  0.0 26.9 jit_solution(13791859857821614386)
XLA Ops:
  0.6 1.0 %shard_map.50 = (bf16[32,2048]{1,0:T(8,128)(2,1)S(1)}, bf16[32,2048]{1,0:T(8,128)(2,1)S(1)}) custom-call(bf16[1,32,8192]{2,1,0:T(8,128)(2,1)} %refs_0_.3), custom_call_target="tpu_custom_call" | custom-call | tf_op jit(solution)/shard_map/pallas_call | solution.py:50
  1.6 3.0 %collective-permute-start.1 = (bf16[32,2048]{1,0:T(8,128)(2,1)S(1)}, bf16[32,2048]{1,0:T(8,128)(2,1)S(1)}, u32[]{:S(2)}, u32[]{:S(2)}) collective-permute-start(bf16[32,2048]{1,0:T(8,128)(2,1)S(1)} %get-tuple-element.35.refs_4_), channel_id=1, source_target_pairs={{0,16},{8,24},{16,0},{24,8},{1,17},{9,25},{17,1},{25,9},{2,18},{10... | collective-permute-start | bytes 393224 | tf_op jit(solution)/shard_map/ppermute | solution.py:18
  4.6 0.0 collective-permute-start.3
  4.6 0.2 collective-permute-start.2
  4.8 1.4 %shard_map.51 = (bf16[32,2048]{1,0:T(8,128)(2,1)S(1)}, bf16[32,2048]{1,0:T(8,128)(2,1)S(1)}, f32[32,8192]{1,0:T(8,128)S(1)}) custom-call(bf16[1,32,8192]{2,1,0:T(8,128)(2,1)} %refs_0_.3, f32[32,8192]{1,0:T(8,128)} %refs_1_), custom_call_target="tpu_custom_call" | custom-call | tf_op jit(solution)/shard_map/pallas_call | solution.py:50
  6.2 0.4 %collective-permute-start = (bf16[32,2048]{1,0:T(8,128)(2,1)S(1)}, bf16[32,2048]{1,0:T(8,128)(2,1)S(1)}, u32[]{:S(2)}, u32[]{:S(2)}) collective-permute-start(bf16[32,2048]{1,0:T(8,128)(2,1)S(1)} %get-tuple-element.45), channel_id=1, source_target_pairs={{0,8},{8,0},{16,24},{24,16},{1,9},{9,1},{17,25},{25,17},{2,10},{10... | collective-permute-start | bytes 393224 | tf_op jit(solution)/shard_map/ppermute | solution.py:18
  6.6 1.2 %shard_map.54.momentum = f32[32,8192]{1,0:T(8,128)S(1)} custom-call(bf16[1,32,8192]{2,1,0:T(8,128)(2,1)} %refs_0_.3, f32[32,8192]{1,0:T(8,128)} %refs_1_.1), custom_call_target="tpu_custom_call" | custom-call | tf_op jit(solution)/shard_map/pallas_call | solution.py:50
  7.9 1.7 %collective-permute-start.4 = (bf16[32,2048]{1,0:T(8,128)(2,1)S(1)}, bf16[32,2048]{1,0:T(8,128)(2,1)S(1)}, u32[]{:S(2)}, u32[]{:S(2)}) collective-permute-start(bf16[32,2048]{1,0:T(8,128)(2,1)S(1)} %get-tuple-element.44.refs_0_), channel_id=1, source_target_pairs={{0,16},{8,24},{16,0},{24,8},{1,17},{9,25},{17,1},{25,9},{2,18},{10... | collective-permute-start | bytes 393224 | tf_op jit(solution)/shard_map/ppermute | solution.py:18
  9.6 0.0 collective-permute-done.1.refs_2_
  9.6 0.2 collective-permute-start.5
  9.8 0.0 collective-permute-done.3.refs_5_
  9.8 0.7 %collective-permute-done.2.refs_3_ = bf16[32,2048]{1,0:T(8,128)(2,1)S(1)} collective-permute-done((bf16[32,2048]{1,0:T(8,128)(2,1)S(1)}, bf16[32,2048]{1,0:T(8,128)(2,1)S(1)}, u32[]{:S(2)}, u32[]{:S(2)}) %collective-permute-start.2) | collective-permute-done | bytes 131104 | tf_op jit(solution)/shard_map/ppermute | solution.py:18
  10.5 0.0 collective-permute-done.refs_1_
  10.5 0.1 shard_map.52
  10.6 12.9 %all_to_all.5.squares = f32[32,1,128]{2,1,0:T(1,128)S(1)} all-to-all(f32[32,1,128]{2,1,0:T(1,128)S(1)} %get-tuple-element.37), channel_id=1, replica_groups=mesh['replica'=4,'fsdp'=8] {'replica','fsdp'}, dimensions={0} | all-to-all | bytes 32768 | tf_op jit(solution)/shard_map/all_to_all | solution.py:170
  23.5 0.2 shard_map.53.factor
  23.7 0.0 collective-permute-done.4.first
  23.7 0.0 collective-permute-done.5.second
  23.7 0.1 shard_map.55.refs_0_
  23.8 0.1 collective-permute-start.6
  23.9 1.1 %shard_map.56 = (f32[32,8192]{1,0:T(8,128)}, f32[32,8192]{1,0:T(8,128)}) custom-call(f32[1,128]{1,0:T(1,128)S(1)} %shard_map.53.factor, f32[32,8192]{1,0:T(8,128)S(1)} %get-tuple-element.48.params, f32[32,8192]{1,0:T(8,128)S(1)} %shard_map.54.momentum, f32[2,32,2048]{2,1,0:T(8,128)S(1)} %shard_map.55.refs_0_), custom_call_target="tpu_custom_call" | custom-call | tf_op jit(solution)/shard_map/pallas_call | solution.py:116
  25.0 0.8 %collective-permute-done.6.refs_0_ = f32[2,32,2048]{2,1,0:T(8,128)S(1)} collective-permute-done((f32[2,32,2048]{2,1,0:T(8,128)S(1)}, f32[2,32,2048]{2,1,0:T(8,128)S(1)}, u32[]{:S(2)}, u32[]{:S(2)}) %collective-permute-start.6) | collective-permute-done | bytes 524320 | tf_op jit(solution)/shard_map/ppermute | solution.py:18
  25.8 1.1 %shard_map.57 = (f32[32,8192]{1,0:T(8,128)}, f32[32,8192]{1,0:T(8,128)}) custom-call(f32[1,128]{1,0:T(1,128)S(1)} %shard_map.53.factor, f32[32,8192]{1,0:T(8,128)S(1)} %get-tuple-element.48.params, f32[32,8192]{1,0:T(8,128)S(1)} %shard_map.54.momentum, ...), custom_call_target="tpu_custom_call", output_to_operand_aliasing={{0}: (4, {}), {1}: (5, {})} | custom-call | tf_op jit(solution)/shard_map/pallas_call | solution.py:116
Async XLA Ops:
  1.6 7.9 %collective-permute-start.1 = (bf16[32,2048]{1,0:T(8,128)(2,1)S(1)}, bf16[32,2048]{1,0:T(8,128)(2,1)S(1)}, u32[]{:S(2)}, u32[]{:S(2)}) collective-permute-start(bf16[32,2048]{1,0:T(8,128)(2,1)S(1)} %get-tuple-element.35.refs_4_), channel_id=1, source_target_pairs={{0,16},{8,24},{16,0},{24,8},{1,17},{9,25},{17,1},{25,9},{2,18},{10... | collective-permute-start | bytes 393224 | tf_op jit(solution)/shard_map/ppermute | solution.py:18
  4.6 5.1 %collective-permute-start.3 = (bf16[32,2048]{1,0:T(8,128)(2,1)S(1)}, bf16[32,2048]{1,0:T(8,128)(2,1)S(1)}, u32[]{:S(2)}, u32[]{:S(2)}) collective-permute-start(bf16[32,2048]{1,0:T(8,128)(2,1)S(1)} %get-tuple-element.36), channel_id=1, source_target_pairs={{0,8},{8,0},{16,24},{24,16},{1,9},{9,1},{17,25},{25,17},{2,10},{10... | collective-permute-start | bytes 393224 | tf_op jit(solution)/shard_map/ppermute | solution.py:18
  4.6 5.9 %collective-permute-start.2 = (bf16[32,2048]{1,0:T(8,128)(2,1)S(1)}, bf16[32,2048]{1,0:T(8,128)(2,1)S(1)}, u32[]{:S(2)}, u32[]{:S(2)}) collective-permute-start(bf16[32,2048]{1,0:T(8,128)(2,1)S(1)} %get-tuple-element.36), channel_id=1, source_target_pairs={{0,24},{8,16},{16,8},{24,0},{1,25},{9,17},{17,9},{25,1},{2,26},{10... | collective-permute-start | bytes 393224 | tf_op jit(solution)/shard_map/ppermute | solution.py:18
  6.2 4.3 %collective-permute-start = (bf16[32,2048]{1,0:T(8,128)(2,1)S(1)}, bf16[32,2048]{1,0:T(8,128)(2,1)S(1)}, u32[]{:S(2)}, u32[]{:S(2)}) collective-permute-start(bf16[32,2048]{1,0:T(8,128)(2,1)S(1)} %get-tuple-element.45), channel_id=1, source_target_pairs={{0,8},{8,0},{16,24},{24,16},{1,9},{9,1},{17,25},{25,17},{2,10},{10... | collective-permute-start | bytes 393224 | tf_op jit(solution)/shard_map/ppermute | solution.py:18
  7.9 15.8 %collective-permute-start.4 = (bf16[32,2048]{1,0:T(8,128)(2,1)S(1)}, bf16[32,2048]{1,0:T(8,128)(2,1)S(1)}, u32[]{:S(2)}, u32[]{:S(2)}) collective-permute-start(bf16[32,2048]{1,0:T(8,128)(2,1)S(1)} %get-tuple-element.44.refs_0_), channel_id=1, source_target_pairs={{0,16},{8,24},{16,0},{24,8},{1,17},{9,25},{17,1},{25,9},{2,18},{10... | collective-permute-start | bytes 393224 | tf_op jit(solution)/shard_map/ppermute | solution.py:18
  9.6 14.1 %collective-permute-start.5 = (bf16[32,2048]{1,0:T(8,128)(2,1)S(1)}, bf16[32,2048]{1,0:T(8,128)(2,1)S(1)}, u32[]{:S(2)}, u32[]{:S(2)}) collective-permute-start(bf16[32,2048]{1,0:T(8,128)(2,1)S(1)} %get-tuple-element.45), channel_id=1, source_target_pairs={{0,24},{8,16},{16,8},{24,0},{1,25},{9,17},{17,9},{25,1},{2,26},{10... | collective-permute-start | bytes 393224 | tf_op jit(solution)/shard_map/ppermute | solution.py:18
  23.8 2.0 %collective-permute-start.6 = (f32[2,32,2048]{2,1,0:T(8,128)S(1)}, f32[2,32,2048]{2,1,0:T(8,128)S(1)}, u32[]{:S(2)}, u32[]{:S(2)}) collective-permute-start(f32[2,32,2048]{2,1,0:T(8,128)S(1)} %shard_map.55.refs_0_), channel_id=1, source_target_pairs={{0,8},{8,0},{16,24},{24,16},{1,9},{9,1},{17,25},{25,17},{2,10},{10... | collective-permute-start | bytes 1572872 | tf_op jit(solution)/shard_map/ppermute | solution.py:18

commit v23 on v17

--- a/solution.py
+++ b/solution.py
@@ -136,17 +136,12 @@
         (pieces, pseudo_grad, params, momentum)
     )
     moved = {k: swapped(pieces[k], "replica", k) for k in range(2, groups)}
-    near, (params,) = cut(pseudo_grad, width, range(2), params)
+    near, (params, momentum) = cut(pseudo_grad, width, range(2), params, momentum)
     moved.update({0: near[0], 1: swapped(near[1], "replica", 1)})
     again = {}
     if groups == 4:
-        near, params, momentum = lax.optimization_barrier((near, params, momentum))
-        _, (momentum,) = cut(pseudo_grad, width, (), momentum)
-        near, params, momentum = lax.optimization_barrier((near, params, momentum))
         again = {k: swapped(near[k ^ 2], "replica", k) for k in (2, 3)}
         again[1] = swapped(pieces[3], "replica", 1)
-    else:
-        _, (momentum,) = cut(pseudo_grad, width, (), momentum)
     wide_piece = jax.ShapeDtypeStruct((rows, width), WIDE)
     parts = [moved[k] for k in range(groups)]
     out_shape = [wide_piece, jax.ShapeDtypeStruct((devices, 1, 128), WIDE)]

time: 27.1 us -> 28 us (1.033)
  waiting for transfers between devices: 1.02 us -> 2.69 us
  Pallas kernels: 6.2 us -> 5.29 us
  blocking collectives: 12.9 us -> 13.2 us
    ppermute x8, waiting for transfers between devices: 1.02 us -> 2.69 us  [swapped(): return lax.ppermute(value, axis, [(i, i ^ flip) for i in range(size)])]
    pallas_call x3 -> x2, Pallas kernels: 3.62 us -> 2.71 us  [cut(): pl.pallas_call(functools.partial(cut_kernel, flips, len(arrays)), out_sha...]
    all_to_all x1, blocking collectives: 12.9 us -> 13.2 us  [per_device(): lax.all_to_all(squares, ('replica', 'fsdp'), split_axis=0, concat_axis=0,...]
  transfers between devices with their start and end apart: 8 -> 8, of which waited for: 2 -> 2; matrix products, arithmetic and copies ran while one was open for 0% -> 0% of each run, Pallas kernels for 15% -> 11%
where the time goes in v23:
time: 28 us; the launch traced here: 27.8 us
  blocking collectives  13.2 us (47%)
  starting transfers between devices  5.92 us (21%)
  Pallas kernels  5.29 us (19%)
  waiting for transfers between devices  2.69 us (10%)
  between operations  0.71 us (3%)
    all_to_all x1, blocking collectives, per_device(): lax.all_to_all(squares, ('replica', 'fsdp'), split_axis=0, concat_axis=0,...  13.2 us
    ppermute x8, starting transfers between devices, swapped(): return lax.ppermute(value, axis, [(i, i ^ flip) for i in range(size)])  5.92 us
    pallas_call x2, Pallas kernels, cut(): pl.pallas_call(functools.partial(cut_kernel, flips, len(arrays)), out_sha...  2.71 us
    ppermute x8, waiting for transfers between devices, swapped(): return lax.ppermute(value, axis, [(i, i ^ flip) for i in range(size)])  2.69 us
    pallas_call x2, Pallas kernels, update(): pl.pallas_call(functools.partial(update_kernel, flips, len(earlier)), out...  2.23 us
  transfers between devices with their start and end apart: 8, of which 2 were waited for; matrix products, arithmetic and copies ran while one was open for 0% of the time, Pallas kernels for 11%

profile of v23, /device:TPU:0, one launch (start us, length us, event | category | flops | bytes accessed | tf_op | source)
XLA Modules:
  0.0 27.8 jit_solution(2794216012688545453)
XLA Ops:
  0.6 1.0 %shard_map.50 = (bf16[32,2048]{1,0:T(8,128)(2,1)S(1)}, bf16[32,2048]{1,0:T(8,128)(2,1)S(1)}) custom-call(bf16[1,32,8192]{2,1,0:T(8,128)(2,1)} %refs_0_.2), custom_call_target="tpu_custom_call" | custom-call | tf_op jit(solution)/shard_map/pallas_call | solution.py:50
  1.6 3.0 %collective-permute-start.1 = (bf16[32,2048]{1,0:T(8,128)(2,1)S(1)}, bf16[32,2048]{1,0:T(8,128)(2,1)S(1)}, u32[]{:S(2)}, u32[]{:S(2)}) collective-permute-start(bf16[32,2048]{1,0:T(8,128)(2,1)S(1)} %get-tuple-element.31.refs_4_), channel_id=1, source_target_pairs={{0,16},{8,24},{16,0},{24,8},{1,17},{9,25},{17,1},{25,9},{2,18},{10... | collective-permute-start | bytes 393224 | tf_op jit(solution)/shard_map/ppermute | solution.py:18
  4.6 0.0 collective-permute-start.3
  4.6 0.2 collective-permute-start.2
  4.8 1.7 %shard_map.51 = (bf16[32,2048]{1,0:T(8,128)(2,1)S(1)}, bf16[32,2048]{1,0:T(8,128)(2,1)S(1)}, f32[32,8192]{1,0:T(8,128)S(1)}, f32[32,8192]{1,0:T(8,128)S(1)}) custom-call(bf16[1,32,8192]{2,1,0:T(8,128)(2,1)} %refs_0_.2, f32[32,8192]{1,0:T(8,128)} %refs_1_, f32[32,8192]{1,0:T(8,128)} %refs_2_), custom_call_target="tpu_custom_call" | custom-call | tf_op jit(solution)/shard_map/pallas_call | solution.py:50
  6.6 0.4 %collective-permute-start = (bf16[32,2048]{1,0:T(8,128)(2,1)S(1)}, bf16[32,2048]{1,0:T(8,128)(2,1)S(1)}, u32[]{:S(2)}, u32[]{:S(2)}) collective-permute-start(bf16[32,2048]{1,0:T(8,128)(2,1)S(1)} %get-tuple-element.30), channel_id=1, source_target_pairs={{0,8},{8,0},{16,24},{24,16},{1,9},{9,1},{17,25},{25,17},{2,10},{10... | collective-permute-start | bytes 393224 | tf_op jit(solution)/shard_map/ppermute | solution.py:18
  6.9 1.7 %collective-permute-start.4 = (bf16[32,2048]{1,0:T(8,128)(2,1)S(1)}, bf16[32,2048]{1,0:T(8,128)(2,1)S(1)}, u32[]{:S(2)}, u32[]{:S(2)}) collective-permute-start(bf16[32,2048]{1,0:T(8,128)(2,1)S(1)} %get-tuple-element.29.refs_0_), channel_id=1, source_target_pairs={{0,16},{8,24},{16,0},{24,8},{1,17},{9,25},{17,1},{25,9},{2,18},{10... | collective-permute-start | bytes 393224 | tf_op jit(solution)/shard_map/ppermute | solution.py:18
  8.6 0.0 collective-permute-done.1.refs_2_
  8.7 0.1 collective-permute-start.5
  8.7 0.0 collective-permute-done.3.refs_5_
  8.7 2.4 %collective-permute-done.2.refs_3_ = bf16[32,2048]{1,0:T(8,128)(2,1)S(1)} collective-permute-done((bf16[32,2048]{1,0:T(8,128)(2,1)S(1)}, bf16[32,2048]{1,0:T(8,128)(2,1)S(1)}, u32[]{:S(2)}, u32[]{:S(2)}) %collective-permute-start.2) | collective-permute-done | bytes 131104 | tf_op jit(solution)/shard_map/ppermute | solution.py:18
  11.1 0.0 collective-permute-done.refs_1_
  11.1 0.1 shard_map.52
  11.3 13.2 %all_to_all.5.squares = f32[32,1,128]{2,1,0:T(1,128)S(1)} all-to-all(f32[32,1,128]{2,1,0:T(1,128)S(1)} %get-tuple-element.33), channel_id=1, replica_groups=mesh['replica'=4,'fsdp'=8] {'replica','fsdp'}, dimensions={0} | all-to-all | bytes 32768 | tf_op jit(solution)/shard_map/all_to_all | solution.py:161
  24.5 0.2 shard_map.53.factor
  24.6 0.0 collective-permute-done.4.first
  24.6 0.0 collective-permute-done.5.second
  24.7 0.1 collective-permute-start.6
  24.8 0.5 %collective-permute-start.7 = (f32[32,2048]{1,0:T(8,128)S(1)}, f32[32,2048]{1,0:T(8,128)S(1)}, u32[]{:S(2)}, u32[]{:S(2)}) collective-permute-start(f32[32,2048]{1,0:T(8,128)S(1)} %shard_map.54.refs_1_), channel_id=1, source_target_pairs={{0,8},{8,0},{16,24},{24,16},{1,9},{9,1},{17,25},{25,17},{2,10},{10... | collective-permute-start | bytes 786440 | tf_op jit(solution)/shard_map/ppermute | solution.py:18
  25.3 1.1 %shard_map.55 = (f32[32,8192]{1,0:T(8,128)}, f32[32,8192]{1,0:T(8,128)}) custom-call(f32[1,128]{1,0:T(1,128)S(1)} %shard_map.53.factor, f32[32,8192]{1,0:T(8,128)S(1)} %get-tuple-element.40.params, f32[32,8192]{1,0:T(8,128)S(1)} %get-tuple-element.41.momentum, f32[32,2048]{1,0:T(8,128)S(1)} %get-tuple-element.42.refs_0_, f32[32,2048]{1,0:T(8,128)S(1)} %shard_map.54.refs_1_), custom_call_target="tpu_custom_call" | custom-call | tf_op jit(solution)/shard_map/pallas_call | solution.py:112
  26.4 0.0 collective-permute-done.6.refs_0_
  26.4 0.3 collective-permute-done.7.refs_1_
  26.7 1.1 %shard_map.56 = (f32[32,8192]{1,0:T(8,128)}, f32[32,8192]{1,0:T(8,128)}) custom-call(f32[1,128]{1,0:T(1,128)S(1)} %shard_map.53.factor, f32[32,8192]{1,0:T(8,128)S(1)} %get-tuple-element.40.params, f32[32,8192]{1,0:T(8,128)S(1)} %get-tuple-element.41.momentum, ...), custom_call_target="tpu_custom_call", output_to_operand_aliasing={{0}: (5, {}), {1}: (6, {})} | custom-call | tf_op jit(solution)/shard_map/pallas_call | solution.py:112
  (1 shorter events, 0.0 us)
Async XLA Ops:
  1.6 7.0 %collective-permute-start.1 = (bf16[32,2048]{1,0:T(8,128)(2,1)S(1)}, bf16[32,2048]{1,0:T(8,128)(2,1)S(1)}, u32[]{:S(2)}, u32[]{:S(2)}) collective-permute-start(bf16[32,2048]{1,0:T(8,128)(2,1)S(1)} %get-tuple-element.31.refs_4_), channel_id=1, source_target_pairs={{0,16},{8,24},{16,0},{24,8},{1,17},{9,25},{17,1},{25,9},{2,18},{10... | collective-permute-start | bytes 393224 | tf_op jit(solution)/shard_map/ppermute | solution.py:18
  4.6 4.1 %collective-permute-start.3 = (bf16[32,2048]{1,0:T(8,128)(2,1)S(1)}, bf16[32,2048]{1,0:T(8,128)(2,1)S(1)}, u32[]{:S(2)}, u32[]{:S(2)}) collective-permute-start(bf16[32,2048]{1,0:T(8,128)(2,1)S(1)} %get-tuple-element.32), channel_id=1, source_target_pairs={{0,8},{8,0},{16,24},{24,16},{1,9},{9,1},{17,25},{25,17},{2,10},{10... | collective-permute-start | bytes 393224 | tf_op jit(solution)/shard_map/ppermute | solution.py:18
  4.6 6.5 %collective-permute-start.2 = (bf16[32,2048]{1,0:T(8,128)(2,1)S(1)}, bf16[32,2048]{1,0:T(8,128)(2,1)S(1)}, u32[]{:S(2)}, u32[]{:S(2)}) collective-permute-start(bf16[32,2048]{1,0:T(8,128)(2,1)S(1)} %get-tuple-element.32), channel_id=1, source_target_pairs={{0,24},{8,16},{16,8},{24,0},{1,25},{9,17},{17,9},{25,1},{2,26},{10... | collective-permute-start | bytes 393224 | tf_op jit(solution)/shard_map/ppermute | solution.py:18
  6.6 4.6 %collective-permute-start = (bf16[32,2048]{1,0:T(8,128)(2,1)S(1)}, bf16[32,2048]{1,0:T(8,128)(2,1)S(1)}, u32[]{:S(2)}, u32[]{:S(2)}) collective-permute-start(bf16[32,2048]{1,0:T(8,128)(2,1)S(1)} %get-tuple-element.30), channel_id=1, source_target_pairs={{0,8},{8,0},{16,24},{24,16},{1,9},{9,1},{17,25},{25,17},{2,10},{10... | collective-permute-start | bytes 393224 | tf_op jit(solution)/shard_map/ppermute | solution.py:18
  6.9 17.7 %collective-permute-start.4 = (bf16[32,2048]{1,0:T(8,128)(2,1)S(1)}, bf16[32,2048]{1,0:T(8,128)(2,1)S(1)}, u32[]{:S(2)}, u32[]{:S(2)}) collective-permute-start(bf16[32,2048]{1,0:T(8,128)(2,1)S(1)} %get-tuple-element.29.refs_0_), channel_id=1, source_target_pairs={{0,16},{8,24},{16,0},{24,8},{1,17},{9,25},{17,1},{25,9},{2,18},{10... | collective-permute-start | bytes 393224 | tf_op jit(solution)/shard_map/ppermute | solution.py:18
  8.7 16.0 %collective-permute-start.5 = (bf16[32,2048]{1,0:T(8,128)(2,1)S(1)}, bf16[32,2048]{1,0:T(8,128)(2,1)S(1)}, u32[]{:S(2)}, u32[]{:S(2)}) collective-permute-start(bf16[32,2048]{1,0:T(8,128)(2,1)S(1)} %get-tuple-element.30), channel_id=1, source_target_pairs={{0,24},{8,16},{16,8},{24,0},{1,25},{9,17},{17,9},{25,1},{2,26},{10... | collective-permute-start | bytes 393224 | tf_op jit(solution)/shard_map/ppermute | solution.py:18
  24.7 1.7 %collective-permute-start.6 = (f32[32,2048]{1,0:T(8,128)S(1)}, f32[32,2048]{1,0:T(8,128)S(1)}, u32[]{:S(2)}, u32[]{:S(2)}) collective-permute-start(f32[32,2048]{1,0:T(8,128)S(1)} %get-tuple-element.42.refs_0_), channel_id=1, source_target_pairs={{0,8},{8,0},{16,24},{24,16},{1,9},{9,1},{17,25},{25,17},{2,10},{10... | collective-permute-start | bytes 786440 | tf_op jit(solution)/shard_map/ppermute | solution.py:18
  24.8 1.9 %collective-permute-start.7 = (f32[32,2048]{1,0:T(8,128)S(1)}, f32[32,2048]{1,0:T(8,128)S(1)}, u32[]{:S(2)}, u32[]{:S(2)}) collective-permute-start(f32[32,2048]{1,0:T(8,128)S(1)} %shard_map.54.refs_1_), channel_id=1, source_target_pairs={{0,8},{8,0},{16,24},{24,16},{1,9},{9,1},{17,25},{25,17},{2,10},{10... | collective-permute-start | bytes 786440 | tf_op jit(solution)/shard_map/ppermute | solution.py:18

commit v24 on v17

--- a/solution.py
+++ b/solution.py
@@ -166,6 +166,8 @@
     squares = lax.all_to_all(
         squares, ("replica", "fsdp"), split_axis=0, concat_axis=0, tiled=True
     )
+    squares, averages = lax.optimization_barrier((squares, averages))
+    own_forward = swapped(averages[0], "replica", 1)
     factor = pl.pallas_call(
         functools.partial(factor_kernel, count),
         out_shape=jax.ShapeDtypeStruct((1, 128), WIDE),
@@ -183,7 +185,8 @@
             compiler_params=limit,
         )(*other_sum, again[2], again[3])
     factor, averages = lax.optimization_barrier((factor, averages))
-    for k in range(0, groups, 2):
+    averages[1] = own_forward
+    for k in range(2, groups, 2):
         averages[k + 1] = swapped(averages[k], "replica", 1)
     here = [k for k in range(groups) if k % 2 == 0]
     late = [k for k in range(groups) if k not in here]

time: 27.1 us -> 27 us (level)
  no operation moved by 1% of the time
where the time goes in v24:
time: 27 us; the launch traced here: 26.8 us
  blocking collectives  12.9 us (48%)
  Pallas kernels  6.2 us (23%)
  starting transfers between devices  6.09 us (23%)
  waiting for transfers between devices  0.9 us (3%)
  between operations  0.72 us (3%)
    all_to_all x1, blocking collectives, per_device(): lax.all_to_all(squares, ('replica', 'fsdp'), split_axis=0, concat_axis=0,...  12.9 us
    ppermute x8, starting transfers between devices, swapped(): return lax.ppermute(value, axis, [(i, i ^ flip) for i in range(size)])  6.09 us
    pallas_call x3, Pallas kernels, cut(): pl.pallas_call(functools.partial(cut_kernel, flips, len(arrays)), out_sha...  3.62 us
    pallas_call x2, Pallas kernels, update(): pl.pallas_call(functools.partial(update_kernel, flips, len(earlier)), out...  2.23 us
    ppermute x8, waiting for transfers between devices, swapped(): return lax.ppermute(value, axis, [(i, i ^ flip) for i in range(size)])  0.9 us
  transfers between devices with their start and end apart: 8, of which 2 were waited for; matrix products, arithmetic and copies ran while one was open for 0% of the time, Pallas kernels for 15%

profile of v24, /device:TPU:0, one launch (start us, length us, event | category | flops | bytes accessed | tf_op | source)
XLA Modules:
  0.0 26.8 jit_solution(414454999582718621)
XLA Ops:
  0.6 1.0 %shard_map.50 = (bf16[32,2048]{1,0:T(8,128)(2,1)S(1)}, bf16[32,2048]{1,0:T(8,128)(2,1)S(1)}) custom-call(bf16[1,32,8192]{2,1,0:T(8,128)(2,1)} %refs_0_.3), custom_call_target="tpu_custom_call" | custom-call | tf_op jit(solution)/shard_map/pallas_call | solution.py:50
  1.6 3.0 %collective-permute-start.1 = (bf16[32,2048]{1,0:T(8,128)(2,1)S(1)}, bf16[32,2048]{1,0:T(8,128)(2,1)S(1)}, u32[]{:S(2)}, u32[]{:S(2)}) collective-permute-start(bf16[32,2048]{1,0:T(8,128)(2,1)S(1)} %get-tuple-element.39.refs_4_), channel_id=1, source_target_pairs={{0,16},{8,24},{16,0},{24,8},{1,17},{9,25},{17,1},{25,9},{2,18},{10... | collective-permute-start | bytes 393224 | tf_op jit(solution)/shard_map/ppermute | solution.py:18
  4.6 0.0 collective-permute-start.3
  4.6 0.2 collective-permute-start.2
  4.8 1.4 %shard_map.51 = (bf16[32,2048]{1,0:T(8,128)(2,1)S(1)}, bf16[32,2048]{1,0:T(8,128)(2,1)S(1)}, f32[32,8192]{1,0:T(8,128)S(1)}) custom-call(bf16[1,32,8192]{2,1,0:T(8,128)(2,1)} %refs_0_.3, f32[32,8192]{1,0:T(8,128)} %refs_1_), custom_call_target="tpu_custom_call" | custom-call | tf_op jit(solution)/shard_map/pallas_call | solution.py:50
  6.2 0.4 %collective-permute-start = (bf16[32,2048]{1,0:T(8,128)(2,1)S(1)}, bf16[32,2048]{1,0:T(8,128)(2,1)S(1)}, u32[]{:S(2)}, u32[]{:S(2)}) collective-permute-start(bf16[32,2048]{1,0:T(8,128)(2,1)S(1)} %get-tuple-element.51), channel_id=1, source_target_pairs={{0,8},{8,0},{16,24},{24,16},{1,9},{9,1},{17,25},{25,17},{2,10},{10... | collective-permute-start | bytes 393224 | tf_op jit(solution)/shard_map/ppermute | solution.py:18
  6.6 1.2 %shard_map.54.momentum = f32[32,8192]{1,0:T(8,128)S(1)} custom-call(bf16[1,32,8192]{2,1,0:T(8,128)(2,1)} %refs_0_.3, f32[32,8192]{1,0:T(8,128)} %refs_1_.1), custom_call_target="tpu_custom_call" | custom-call | tf_op jit(solution)/shard_map/pallas_call | solution.py:50
  7.9 1.7 %collective-permute-start.4 = (bf16[32,2048]{1,0:T(8,128)(2,1)S(1)}, bf16[32,2048]{1,0:T(8,128)(2,1)S(1)}, u32[]{:S(2)}, u32[]{:S(2)}) collective-permute-start(bf16[32,2048]{1,0:T(8,128)(2,1)S(1)} %get-tuple-element.50.refs_0_), channel_id=1, source_target_pairs={{0,16},{8,24},{16,0},{24,8},{1,17},{9,25},{17,1},{25,9},{2,18},{10... | collective-permute-start | bytes 393224 | tf_op jit(solution)/shard_map/ppermute | solution.py:18
  9.6 0.0 collective-permute-done.1.refs_2_
  9.6 0.2 collective-permute-start.5
  9.8 0.0 collective-permute-done.3.refs_5_
  9.8 0.7 %collective-permute-done.2.refs_3_ = bf16[32,2048]{1,0:T(8,128)(2,1)S(1)} collective-permute-done((bf16[32,2048]{1,0:T(8,128)(2,1)S(1)}, bf16[32,2048]{1,0:T(8,128)(2,1)S(1)}, u32[]{:S(2)}, u32[]{:S(2)}) %collective-permute-start.2) | collective-permute-done | bytes 131104 | tf_op jit(solution)/shard_map/ppermute | solution.py:18
  10.5 0.0 collective-permute-done.refs_1_
  10.5 0.1 shard_map.52
  10.6 12.9 %all_to_all.5.squares = f32[32,1,128]{2,1,0:T(1,128)S(1)} all-to-all(f32[32,1,128]{2,1,0:T(1,128)S(1)} %get-tuple-element.41), channel_id=1, replica_groups=mesh['replica'=4,'fsdp'=8] {'replica','fsdp'}, dimensions={0} | all-to-all | bytes 32768 | tf_op jit(solution)/shard_map/all_to_all | solution.py:166
  23.5 0.2 shard_map.53.factor
  23.7 0.1 collective-permute-start.6
  23.8 0.0 collective-permute-done.4.first
  23.8 0.0 collective-permute-done.5.second
  23.9 0.5 %collective-permute-start.7 = (f32[32,2048]{1,0:T(8,128)S(1)}, f32[32,2048]{1,0:T(8,128)S(1)}, u32[]{:S(2)}, u32[]{:S(2)}) collective-permute-start(f32[32,2048]{1,0:T(8,128)S(1)} %shard_map.55.refs_1_), channel_id=1, source_target_pairs={{0,8},{8,0},{16,24},{24,16},{1,9},{9,1},{17,25},{25,17},{2,10},{10... | collective-permute-start | bytes 786440 | tf_op jit(solution)/shard_map/ppermute | solution.py:18
  24.4 1.1 %shard_map.56 = (f32[32,8192]{1,0:T(8,128)}, f32[32,8192]{1,0:T(8,128)}) custom-call(f32[1,128]{1,0:T(1,128)S(1)} %shard_map.53.factor, f32[32,8192]{1,0:T(8,128)S(1)} %get-tuple-element.58.params, f32[32,8192]{1,0:T(8,128)S(1)} %shard_map.54.momentum, f32[32,2048]{1,0:T(8,128)S(1)} %get-tuple-element.61.refs_0_, f32[32,2048]{1,0:T(8,128)S(1)} %shard_map.55.refs_1_), custom_call_target="tpu_custom_call" | custom-call | tf_op jit(solution)/shard_map/pallas_call | solution.py:112
  25.5 0.0 collective-permute-done.6.refs_0_
  25.5 0.1 collective-permute-done.7.refs_1_
  25.7 1.1 %shard_map.57 = (f32[32,8192]{1,0:T(8,128)}, f32[32,8192]{1,0:T(8,128)}) custom-call(f32[1,128]{1,0:T(1,128)S(1)} %shard_map.53.factor, f32[32,8192]{1,0:T(8,128)S(1)} %get-tuple-element.58.params, f32[32,8192]{1,0:T(8,128)S(1)} %shard_map.54.momentum, f32[32,2048]{1,0:T(8,128)S(1)} %collective-permute-done.6.refs_0_, ...), custom_call_target="tpu_custom_call", output_to_operand_aliasing={{0}: (5, {}), {1}: (6, {})} | custom-call | tf_op jit(solution)/shard_map/pallas_call | solution.py:112
  (1 shorter events, 0.0 us)
Async XLA Ops:
  1.6 7.9 %collective-permute-start.1 = (bf16[32,2048]{1,0:T(8,128)(2,1)S(1)}, bf16[32,2048]{1,0:T(8,128)(2,1)S(1)}, u32[]{:S(2)}, u32[]{:S(2)}) collective-permute-start(bf16[32,2048]{1,0:T(8,128)(2,1)S(1)} %get-tuple-element.39.refs_4_), channel_id=1, source_target_pairs={{0,16},{8,24},{16,0},{24,8},{1,17},{9,25},{17,1},{25,9},{2,18},{10... | collective-permute-start | bytes 393224 | tf_op jit(solution)/shard_map/ppermute | solution.py:18
  4.6 5.1 %collective-permute-start.3 = (bf16[32,2048]{1,0:T(8,128)(2,1)S(1)}, bf16[32,2048]{1,0:T(8,128)(2,1)S(1)}, u32[]{:S(2)}, u32[]{:S(2)}) collective-permute-start(bf16[32,2048]{1,0:T(8,128)(2,1)S(1)} %get-tuple-element.40), channel_id=1, source_target_pairs={{0,8},{8,0},{16,24},{24,16},{1,9},{9,1},{17,25},{25,17},{2,10},{10... | collective-permute-start | bytes 393224 | tf_op jit(solution)/shard_map/ppermute | solution.py:18
  4.6 5.9 %collective-permute-start.2 = (bf16[32,2048]{1,0:T(8,128)(2,1)S(1)}, bf16[32,2048]{1,0:T(8,128)(2,1)S(1)}, u32[]{:S(2)}, u32[]{:S(2)}) collective-permute-start(bf16[32,2048]{1,0:T(8,128)(2,1)S(1)} %get-tuple-element.40), channel_id=1, source_target_pairs={{0,24},{8,16},{16,8},{24,0},{1,25},{9,17},{17,9},{25,1},{2,26},{10... | collective-permute-start | bytes 393224 | tf_op jit(solution)/shard_map/ppermute | solution.py:18
  6.2 4.3 %collective-permute-start = (bf16[32,2048]{1,0:T(8,128)(2,1)S(1)}, bf16[32,2048]{1,0:T(8,128)(2,1)S(1)}, u32[]{:S(2)}, u32[]{:S(2)}) collective-permute-start(bf16[32,2048]{1,0:T(8,128)(2,1)S(1)} %get-tuple-element.51), channel_id=1, source_target_pairs={{0,8},{8,0},{16,24},{24,16},{1,9},{9,1},{17,25},{25,17},{2,10},{10... | collective-permute-start | bytes 393224 | tf_op jit(solution)/shard_map/ppermute | solution.py:18
  7.9 15.9 %collective-permute-start.4 = (bf16[32,2048]{1,0:T(8,128)(2,1)S(1)}, bf16[32,2048]{1,0:T(8,128)(2,1)S(1)}, u32[]{:S(2)}, u32[]{:S(2)}) collective-permute-start(bf16[32,2048]{1,0:T(8,128)(2,1)S(1)} %get-tuple-element.50.refs_0_), channel_id=1, source_target_pairs={{0,16},{8,24},{16,0},{24,8},{1,17},{9,25},{17,1},{25,9},{2,18},{10... | collective-permute-start | bytes 393224 | tf_op jit(solution)/shard_map/ppermute | solution.py:18
  9.6 14.2 %collective-permute-start.5 = (bf16[32,2048]{1,0:T(8,128)(2,1)S(1)}, bf16[32,2048]{1,0:T(8,128)(2,1)S(1)}, u32[]{:S(2)}, u32[]{:S(2)}) collective-permute-start(bf16[32,2048]{1,0:T(8,128)(2,1)S(1)} %get-tuple-element.51), channel_id=1, source_target_pairs={{0,24},{8,16},{16,8},{24,0},{1,25},{9,17},{17,9},{25,1},{2,26},{10... | collective-permute-start | bytes 393224 | tf_op jit(solution)/shard_map/ppermute | solution.py:18
  23.7 1.8 %collective-permute-start.6 = (f32[32,2048]{1,0:T(8,128)S(1)}, f32[32,2048]{1,0:T(8,128)S(1)}, u32[]{:S(2)}, u32[]{:S(2)}) collective-permute-start(f32[32,2048]{1,0:T(8,128)S(1)} %get-tuple-element.61.refs_0_), channel_id=1, source_target_pairs={{0,8},{8,0},{16,24},{24,16},{1,9},{9,1},{17,25},{25,17},{2,10},{10... | collective-permute-start | bytes 786440 | tf_op jit(solution)/shard_map/ppermute | solution.py:18
  23.9 1.8 %collective-permute-start.7 = (f32[32,2048]{1,0:T(8,128)S(1)}, f32[32,2048]{1,0:T(8,128)S(1)}, u32[]{:S(2)}, u32[]{:S(2)}) collective-permute-start(f32[32,2048]{1,0:T(8,128)S(1)} %shard_map.55.refs_1_), channel_id=1, source_target_pairs={{0,8},{8,0},{16,24},{24,16},{1,9},{9,1},{17,25},{25,17},{2,10},{10... | collective-permute-start | bytes 786440 | tf_op jit(solution)/shard_map/ppermute | solution.py:18
